TPU v7x, 32 devices: a whole 2x2x4 slice. The times are simulated.
32 devices in a mesh: groups: 2 (over x), dom: 8 (over z, y), rows: 2 (over core).
Axes of the slice: x: 2, y: 2, z: 4, core: 2. Of those that a mesh axis runs over, the one named last changes fastest.
Arguments:
- density: bfloat16 [4096, 2048], P(('groups', 'dom')), parts along dimension 0, may hold values from -0.25 to 0.25
- owner: int32 [32], P('groups'), parts along dimension 0, may hold values from 0 to 15, each once
- touched: int32 [16, 8], P(('groups', 'dom')), parts along dimension 0, may hold values from 0 to 15, as said below
- blocks: int32 [768, 4], P(('groups', 'dom', 'rows')), parts along dimension 0, may hold values from 0 to 7, as said below
- counts: int32 [768], P(('groups', 'dom', 'rows')), parts along dimension 0, may hold values from 2 to 4
- basis: bfloat16 [768, 512, 256], P(('groups', 'dom', 'rows')), parts along dimension 0, may hold values from -6 to 6
- points: float32 [768, 3, 256], P(('groups', 'dom', 'rows')), parts along dimension 0, may hold values from -3 to 3
- weights: float32 [768, 256], P(('groups', 'dom', 'rows')), parts along dimension 0, may hold values from 0.02 to 0.2
- centers: float32 [3, 4096], P(None, 'groups'), parts along dimension 1, may hold values from -3 to 3
- widths: float32 [4096], P('groups'), parts along dimension 0, may hold values from 0.5 to 2
Outputs:
- exchange: bfloat16 [4096, 2048], P(('groups', 'dom'), 'rows'), parts along dimension 0
There are 2 independent parts, one for each index of `groups`. A program takes and returns all parts, laid end to end along the dimension named above; each array names one. Nothing has to cross between parts.
Inputs may be any that keep to these rules, and one draw needn't show every extreme that they name: `touched`: each row holds 8 different function blocks. `blocks`: each row names 4 different positions; the batches of one dom index are 48 consecutive rows, and every position is named by some batch of each dom index. `owner`: each block row has a stored position of its own.
All inputs are finite; a program needn't handle non-finite values.
Results may differ from a plain program's by a relative error of at most 0.0034.
Values may be sent and summed in bfloat16 or wider, within the bound.
No kernel may reach another device: no remote copies, remote signals or barrier semaphores. Data moves between devices by JAX's collectives and lax.ppermute only.
A program may use at most 128 MiB of HBM per device.

v0:
```python
import math

import jax
import jax.numpy as jnp
from jax import lax
from jax.sharding import PartitionSpec as P

FB = 128
TMAX = 4
UMAX = 8


def coulomb(centre_x, centre_y, centre_z, spread, point_x, point_y, point_z):
    dist = (centre_x - point_x) ** 2 + (centre_y - point_y) ** 2 + (centre_z - point_z) ** 2
    return 1.0 / jnp.sqrt(dist + spread * spread)


def lookup_owner(owner, block_ids):
    match = block_ids[:, None] == jnp.arange(owner.shape[0], dtype=jnp.int32)[None, :]
    return jnp.sum(jnp.where(match, owner[None, :], 0), axis=1)


def answer_for(density, column_sets):
    rows_here = density.shape[0]
    sources, wanted = column_sets.shape
    blocked = density.reshape(rows_here, density.shape[1] // FB, FB)
    picked = jnp.take(blocked, column_sets.reshape(-1), axis=1)
    return picked.reshape(rows_here, sources, wanted * FB).transpose(1, 0, 2)


def spread_rows(terms, stored, block_count, sources):
    columns = terms.shape[1]
    expanded = jnp.zeros((block_count, FB, columns), jnp.float32)
    expanded = expanded.at[stored].set(terms.reshape(UMAX, FB, columns))
    return expanded.reshape(sources, block_count * FB // sources, columns)


def collect(returned, column_sets, block_count):
    sources, rows_here, columns = returned.shape
    wanted = column_sets.shape[1]
    pieces = returned.reshape(sources, rows_here, wanted, FB).transpose(1, 0, 2, 3)
    pieces = pieces.reshape(rows_here, sources * wanted, FB)
    total = jnp.zeros((rows_here, block_count, FB), jnp.float32)
    total = total.at[:, column_sets.reshape(-1)].add(pieces)
    return total.reshape(rows_here, block_count * FB)


def per_device(density, owner, touched, blocks, counts, basis, points, weights, centers, widths):
    rows_count = lax.axis_size("rows")
    rows_index = lax.axis_index("rows")
    batches = blocks.shape[0]
    block_count = owner.shape[0]
    width = TMAX * FB
    share = UMAX // rows_count
    own_set = touched[0]
    all_sets = lax.all_gather(touched, "dom", axis=0, tiled=True)
    sources = all_sets.shape[0]
    half_sets = lax.dynamic_slice_in_dim(all_sets, rows_index * share, share, 1)
    got = lax.all_to_all(
        answer_for(density, all_sets), "dom", split_axis=0, concat_axis=0, tiled=True
    )
    panel = got.reshape(block_count * FB, UMAX * FB)
    stored = lookup_owner(owner, own_set)
    tile = jnp.take(panel.reshape(block_count, FB, UMAX * FB), stored, axis=0).reshape(
        UMAX, FB, UMAX, FB
    )
    centre_blocks = centers.reshape(3, block_count, FB)
    spread_blocks = widths.reshape(block_count, FB)
    slot_ids = jnp.arange(TMAX, dtype=jnp.int32)
    group = math.gcd(batches, 8)
    turns = batches // group

    def work(total, item):
        slots, count, values, coords, quad = item
        gid = jnp.take(own_set, slots.reshape(-1), axis=0)
        active = (slot_ids[None, :] < count[:, None]).astype(jnp.float32)
        rowmask = jnp.repeat(active, FB, axis=1)[:, :, None]
        xmask = jnp.where(rowmask > 0, values, jnp.zeros_like(values))
        xweighted = (xmask.astype(jnp.float32) * quad[:, None, :]).astype(jnp.bfloat16)
        dloc = tile[slots[:, :, None], :, slots[:, None, :], :]
        dloc = dloc.transpose(0, 1, 3, 2, 4).reshape(group, width, width)
        centre = jnp.take(centre_blocks, gid, axis=1).reshape(3, group, width)
        spread = jnp.take(spread_blocks, gid, axis=0).reshape(group, width)
        vfac = coulomb(
            centre[0][:, :, None],
            centre[1][:, :, None],
            centre[2][:, :, None],
            spread[:, :, None],
            coords[:, 0][:, None, :],
            coords[:, 1][:, None, :],
            coords[:, 2][:, None, :],
        )
        gval = jnp.einsum("brc,bcg->brg", dloc, xmask, preferred_element_type=jnp.float32)
        fval = (gval * vfac * rowmask).astype(jnp.bfloat16)
        parts = jnp.einsum("brg,bcg->brc", fval, xweighted, preferred_element_type=jnp.float32)
        pieces = parts.reshape(group, TMAX, FB, TMAX, FB).transpose(0, 1, 3, 2, 4)
        total = total.at[slots[:, :, None], :, slots[:, None, :], :].add(pieces)
        return (total, None)

    items = (
        blocks.reshape(turns, group, TMAX),
        counts.reshape(turns, group),
        basis.reshape(turns, group, width, basis.shape[2]),
        points.reshape(turns, group, 3, points.shape[2]),
        weights.reshape(turns, group, weights.shape[1]),
    )
    start = jnp.zeros((UMAX, FB, UMAX, FB), jnp.float32)
    local_sum, _ = lax.scan(work, start, items)
    local_flat = local_sum.reshape(UMAX * FB, UMAX * FB)
    halved = lax.psum_scatter(local_flat, "rows", scatter_dimension=1, tiled=True)
    returned = lax.all_to_all(
        spread_rows(halved, stored, block_count, sources),
        "dom",
        split_axis=0,
        concat_axis=0,
        tiled=True,
    )
    gathered_terms = collect(returned, half_sets, block_count)
    summed = lax.psum_scatter(gathered_terms, "rows", scatter_dimension=1, tiled=True)
    return summed.astype(jnp.bfloat16)


def solution(mesh):
    in_specs = (
        P(("groups", "dom"), None),
        P("groups"),
        P(("groups", "dom"), None),
        P(("groups", "dom", "rows"), None),
        P(("groups", "dom", "rows")),
        P(("groups", "dom", "rows"), None, None),
        P(("groups", "dom", "rows"), None, None),
        P(("groups", "dom", "rows"), None),
        P(None, "groups"),
        P("groups"),
    )
    out_specs = P(("groups", "dom"), "rows")
    return jax.shard_map(
        per_device, mesh=mesh, in_specs=in_specs, out_specs=out_specs, check_vma=False
    )
```

profile of v0, /device:TPU:0, one launch (start us, length us, event | category | flops | bytes accessed | tf_op | source)
XLA Modules:
  0.0 557.6 jit_solution(10597382456933877973)
XLA Ops:
  6.5 22.3 %all-gather = s32[8,1,8]{2,1,0:T(1,128)S(1)} all-gather(s32[1,1,8]{2,1,0:T(1,128)} %bitcast.158), channel_id=1, replica_groups=mesh['groups'=2,'dom'=8,'rows'=2] {'dom'}, dimensions={0}, use_global_device_ids=true | all-gather | bytes 288 | tf_op jit(solution)/shard_map/all_gather | solution.py:56
  35.5 6.4 %copy.89 = bf16[256,64,128]{0,2,1:T(8,128)(2,1)} copy(bf16[256,64,128]{2,0,1:T(8,128)(2,1)} %bitcast.171) | data formatting | bytes 8388608 | tf_op jit(solution)/shard_map/jit(_take)/gather | solution.py:27
  52.5 89.2 %all-to-all-done = bf16[8,256,1024]{1,2,0:T(8,128)(2,1)} async-done(((bf16[8,256,1024]{1,2,0:T(8,128)(2,1)}), bf16[8,256,1024]{1,2,0:T(8,128)(2,1)}, u32[]{:S(2)}, u32[]{:S(2)}) %all-to-all-start) | async-done | bytes 4194336 | tf_op jit(solution)/shard_map/all_to_all | solution.py:59
  141.7 6.5 %copy.90 = bf16[8,256,1024]{2,1,0:T(8,128)(2,1)} copy(bf16[8,256,1024]{1,2,0:T(8,128)(2,1)} %all-to-all-done) | data formatting | bytes 8388608 | tf_op jit(solution)/shard_map/all_to_all | solution.py:59
  157.1 238.5 %while.11 = (s32[]{:T(128)}, f32[8,128,8,128]{3,1,2,0:T(8,128)}, s32[3,8,4]{2,1,0:T(8,128)S(1)}, bf16[8,128,8,128]{3,1,2,0:T(8,128)(2,1)S(1)}, s32[3,8]{1,0:T(4,...) while((s32[]{:T(128)}, f32[8,128,8,128]{3,1,2,0:T(8,128)}, ...), condition=%wide.region_3.4_spmd.clone, body=%wide.region_1.3_spmd.clone.sunk | while | flops 2167435264 | bytes 105627112 | solution.py:108
  163.4 8.1 %copy.120 = bf16[8,4,4,128,128]{4,2,3,1,0:T(4,128)(2,1)} copy(bf16[8,4,4,128,128]{4,3,2,1,0:T(8,128)(2,1)} %bitcast.163) | data formatting | bytes 8388608 | tf_op jit(solution)/shard_map/while/body/eval_jaxpr/gather | solution.py:80
  171.5 7.2 %reshape.483 = bf16[8,512,512]{2,1,0:T(8,128)(2,1)} reshape(bf16[8,4,128,4,128]{4,3,2,1,0:T(4,128)(2,1)} %bitcast.164) | data formatting | bytes 8388608 | tf_op jit(solution)/shard_map/while/body/eval_jaxpr/reshape | solution.py:81
  191.2 9.9 %reshape.485 = f32[8,4,128,4,128]{4,3,2,1,0:T(4,128)} reshape(f32[8,512,512]{2,1,0:T(8,128)} %fusion.50) | data formatting | bytes 16777216 | tf_op jit(solution)/shard_map/while/body/eval_jaxpr/reshape | solution.py:96
  201.1 7.9 %copy.121 = f32[8,4,4,128,128]{4,3,2,1,0:T(8,128)} copy(f32[8,4,4,128,128]{4,2,3,1,0:T(4,128)} %bitcast.162) | data formatting | bytes 16777216 | tf_op jit(solution)/shard_map/while/body/eval_jaxpr/transpose | solution.py:96
  209.1 27.6 %scatter_fusion = f32[8,128,8,128]{3,1,2,0:T(8,128)} fusion(f32[8,128,8,128]{3,1,2,0:T(8,128)} %get-tuple-element.285, s32[128]{0:T(128)S(1)} %reshape.481, f32[128,128,128]{2,1,0:T(8,128)} %bitcast.161), kind=kCustom, calls=%fused_computation.6.clone.clone.1 | custom fusion | flops 2097152 | bytes 25166848 | tf_op jit(solution)/shard_map/while/body/eval_jaxpr/scatter-add | solution.py:97
  243.0 8.1 %copy.120 = bf16[8,4,4,128,128]{4,2,3,1,0:T(4,128)(2,1)} copy(bf16[8,4,4,128,128]{4,3,2,1,0:T(8,128)(2,1)} %bitcast.163) | data formatting | bytes 8388608 | tf_op jit(solution)/shard_map/while/body/eval_jaxpr/gather | solution.py:80
  251.0 7.2 %reshape.483 = bf16[8,512,512]{2,1,0:T(8,128)(2,1)} reshape(bf16[8,4,128,4,128]{4,3,2,1,0:T(4,128)(2,1)} %bitcast.164) | data formatting | bytes 8388608 | tf_op jit(solution)/shard_map/while/body/eval_jaxpr/reshape | solution.py:81
  270.7 9.9 %reshape.485 = f32[8,4,128,4,128]{4,3,2,1,0:T(4,128)} reshape(f32[8,512,512]{2,1,0:T(8,128)} %fusion.50) | data formatting | bytes 16777216 | tf_op jit(solution)/shard_map/while/body/eval_jaxpr/reshape | solution.py:96
  280.7 7.9 %copy.121 = f32[8,4,4,128,128]{4,3,2,1,0:T(8,128)} copy(f32[8,4,4,128,128]{4,2,3,1,0:T(4,128)} %bitcast.162) | data formatting | bytes 16777216 | tf_op jit(solution)/shard_map/while/body/eval_jaxpr/transpose | solution.py:96
  288.6 27.5 %scatter_fusion = f32[8,128,8,128]{3,1,2,0:T(8,128)} fusion(f32[8,128,8,128]{3,1,2,0:T(8,128)} %get-tuple-element.285, s32[128]{0:T(128)S(1)} %reshape.481, f32[128,128,128]{2,1,0:T(8,128)} %bitcast.161), kind=kCustom, calls=%fused_computation.6.clone.clone.1 | custom fusion | flops 2097152 | bytes 25166848 | tf_op jit(solution)/shard_map/while/body/eval_jaxpr/scatter-add | solution.py:97
  322.5 8.1 %copy.120 = bf16[8,4,4,128,128]{4,2,3,1,0:T(4,128)(2,1)} copy(bf16[8,4,4,128,128]{4,3,2,1,0:T(8,128)(2,1)} %bitcast.163) | data formatting | bytes 8388608 | tf_op jit(solution)/shard_map/while/body/eval_jaxpr/gather | solution.py:80
  330.6 7.2 %reshape.483 = bf16[8,512,512]{2,1,0:T(8,128)(2,1)} reshape(bf16[8,4,128,4,128]{4,3,2,1,0:T(4,128)(2,1)} %bitcast.164) | data formatting | bytes 8388608 | tf_op jit(solution)/shard_map/while/body/eval_jaxpr/reshape | solution.py:81
  350.2 9.9 %reshape.485 = f32[8,4,128,4,128]{4,3,2,1,0:T(4,128)} reshape(f32[8,512,512]{2,1,0:T(8,128)} %fusion.50) | data formatting | bytes 16777216 | tf_op jit(solution)/shard_map/while/body/eval_jaxpr/reshape | solution.py:96
  360.2 7.9 %copy.121 = f32[8,4,4,128,128]{4,3,2,1,0:T(8,128)} copy(f32[8,4,4,128,128]{4,2,3,1,0:T(4,128)} %bitcast.162) | data formatting | bytes 16777216 | tf_op jit(solution)/shard_map/while/body/eval_jaxpr/transpose | solution.py:96
  368.2 27.5 %scatter_fusion = f32[8,128,8,128]{3,1,2,0:T(8,128)} fusion(f32[8,128,8,128]{3,1,2,0:T(8,128)} %get-tuple-element.285, s32[128]{0:T(128)S(1)} %reshape.481, f32[128,128,128]{2,1,0:T(8,128)} %bitcast.161), kind=kCustom, calls=%fused_computation.6.clone.clone.1 | custom fusion | flops 2097152 | bytes 25166848 | tf_op jit(solution)/shard_map/while/body/eval_jaxpr/scatter-add | solution.py:97
  403.2 11.3 %reduce-scatter.3.cloned.1.call-done = f32[1024,512]{1,0:T(8,128)} async-done(((f32[1024,1024]{1,0:T(8,128)}), f32[1024,512]{1,0:T(8,128)}) %reduce-scatter.3.cloned.1.call-update) | async-done | bytes 2097168 | tf_op jit(solution)/shard_map/reduce_scatter | solution.py:110
  426.8 93.4 %all-to-all-done.1 = f32[8,256,512]{2,1,0:T(8,128)} async-done(((f32[8,256,512]{2,1,0:T(8,128)}), f32[8,256,512]{2,1,0:T(8,128)}, u32[]{:S(2)}, u32[]{:S(2)}) %all-to-all-start.1) | async-done | bytes 4194336 | tf_op jit(solution)/shard_map/all_to_all | solution.py:111
  531.3 6.5 %scatter_fusion.2 = f32[256,16,128]{2,0,1:T(8,128)S(1)} fusion(f32[256,16,128]{2,0,1:T(8,128)S(1)} %broadcast_in_dim.117, s32[32]{0:T(128)S(1)} %fusion.27, f32[32,256,128]{2,1,0:T(8,128)} %bitcast.170), kind=kCustom, calls=%fused_computation.8 | custom fusion | flops 1048576 | bytes 12583040 | tf_op jit(solution)/shard_map/scatter-add | solution.py:44
  539.7 8.7 %reduce-scatter.5.cloned.1.call-done = f32[256,1024]{0,1:T(8,128)} async-done(((f32[256,2048]{0,1:T(8,128)}), f32[256,1024]{0,1:T(8,128)}) %reduce-scatter.5.cloned.1.call-update) | async-done | bytes 1048592 | tf_op jit(solution)/shard_map/reduce_scatter | solution.py:119
  (179 shorter events, 117.5 us)
Async XLA Ops:
  28.8 13.0 %copy-start.4 = (s32[8,1,8]{2,1,0:T(1,128)}, s32[8,1,8]{2,1,0:T(1,128)S(1)}, u32[]{:S(2)}) copy-start(s32[8,1,8]{2,1,0:T(1,128)S(1)} %all-gather) | copy-start | bytes 772
  47.3 4.8 copy-start.8
  47.3 4.9 copy-start.9
  47.3 4.9 copy-start
  47.3 4.9 copy-start.10
  47.3 94.4 %all-to-all-start = ((bf16[8,256,1024]{1,2,0:T(8,128)(2,1)}), bf16[8,256,1024]{1,2,0:T(8,128)(2,1)}, u32[]{:S(2)}, u32[]{:S(2)}) async-start(bf16[8,256,1024]{1,2,0:T(8,128)(2,1)} %fusion.26), calls=%async_computation | async-start | bytes 8388608 | tf_op jit(solution)/shard_map/all_to_all | solution.py:59
  52.0 362.5 %reduce-scatter.3.cloned.1.call-start = ((), (), s32[]{:S(2)}) async-start(), calls=%async_computation.4 | async-start | bytes 6291456 | tf_op jit(solution)/shard_map/reduce_scatter | solution.py:110
  52.5 95.7 %copy-start.6 = (s32[8]{0:T(128)}, s32[8]{0:T(128)S(1)}, u32[]{:S(2)}) copy-start(s32[8]{0:T(128)S(1)} %fusion.28) | copy-start | bytes 100
  152.4 4.7 copy-start.1
  152.4 4.7 copy-start.3
  403.2 13.8 %copy-start.7 = (s32[8]{0:T(128)S(1)}, s32[8]{0:T(128)}, u32[]{:S(2)}) copy-start(s32[8]{0:T(128)} %copy-done.6) | copy-start | bytes 100
  414.5 2.5 copy-start.2
  420.5 6.1 %copy-start.5 = (s32[8,1,8]{2,1,0:T(1,128)S(1)}, s32[8,1,8]{2,1,0:T(1,128)}, u32[]{:S(2)}) copy-start(s32[8,1,8]{2,1,0:T(1,128)} %copy-done.4) | copy-start | bytes 772
  420.5 99.7 %all-to-all-start.1 = ((f32[8,256,512]{2,1,0:T(8,128)}), f32[8,256,512]{2,1,0:T(8,128)}, u32[]{:S(2)}, u32[]{:S(2)}) async-start(f32[8,256,512]{2,1,0:T(8,128)} %bitcast.166), calls=%async_computation.2 | async-start | bytes 8388608 | tf_op jit(solution)/shard_map/all_to_all | solution.py:111
  426.5 121.9 %reduce-scatter.5.cloned.1.call-start = ((), (), s32[]{:S(2)}) async-start(), calls=%async_computation.5 | async-start | bytes 3145728 | tf_op jit(solution)/shard_map/reduce_scatter | solution.py:119
Sparse Core Ops, SparseCore 0:
  403.3 11.1 reduce-scatter.2
  539.8 8.5 reduce-scatter.4
where the time goes:
time: 561 us; the launch traced here: 558 us
  waiting for transfers between devices  203 us (36%)
  local copies, waits for them, and re-layouts  175 us (31%)
  other arithmetic  100 us (18%)
  matrix products  32.6 us (6%)
  blocking collectives  22.3 us (4%)
  between operations  13.5 us (2%)
  starting transfers between devices  10.8 us (2%)
    all_to_all x1, waiting for transfers between devices, per_device(): lax.all_to_all(spread_rows(halved, stored, block_count, sources), 'dom',...  93.4 us
    all_to_all x1, waiting for transfers between devices, per_device(): lax.all_to_all(answer_for(density, all_sets), 'dom', split_axis=0, concat...  89.2 us
    scatter-add x3, other arithmetic, work(): total = total.at[slots[:, :, None], :, slots[:, None, :], :].add(pieces)  82.6 us
    gather x6, local copies, waits for them, and re-layouts, work(): dloc = tile[slots[:, :, None], :, slots[:, None, :], :]  33.5 us
    reshape x3, local copies, waits for them, and re-layouts, work(): pieces = parts.reshape(group, TMAX, FB, TMAX, FB).transpose(0, 1, 3, 2, 4)  29.8 us
    transpose x3, local copies, waits for them, and re-layouts, work(): pieces = parts.reshape(group, TMAX, FB, TMAX, FB).transpose(0, 1, 3, 2, 4)  23.6 us
    all_gather x1, blocking collectives, per_device(): all_sets = lax.all_gather(touched, 'dom', axis=0, tiled=True)  22.3 us
    reshape x3, local copies, waits for them, and re-layouts, work(): dloc = dloc.transpose(0, 1, 3, 2, 4).reshape(group, width, width)  21.6 us
  transfers between devices with their start and end apart: 4, of which 4 were waited for; matrix products, arithmetic and copies ran while one was open for 0% of the time, Pallas kernels for 0%

commit v1 on v0

--- a/solution.py
+++ b/solution.py
@@ -1,13 +1,17 @@
+import functools
 import math
 
 import jax
 import jax.numpy as jnp
 from jax import lax
+from jax.experimental import pallas as pl
+from jax.experimental.pallas import tpu as pltpu
 from jax.sharding import PartitionSpec as P
 
 FB = 128
 TMAX = 4
 UMAX = 8
+MIB = 1024 * 1024
 
 
 def coulomb(centre_x, centre_y, centre_z, spread, point_x, point_y, point_z):
@@ -45,7 +49,7 @@
     return total.reshape(rows_here, block_count * FB)
 
 
-def per_device(density, owner, touched, blocks, counts, basis, points, weights, centers, widths):
+def per_device_any(density, owner, touched, blocks, counts, basis, points, weights, centers, widths):
     rows_count = lax.axis_size("rows")
     rows_index = lax.axis_index("rows")
     batches = blocks.shape[0]
@@ -120,6 +124,259 @@
     return summed.astype(jnp.bfloat16)
 
 
+def call(kernel, scalars, arrays, in_specs, out_shapes, out_specs, scratch, grid=(1,), cost=None, vmem=48):
+    return pl.pallas_call(
+        kernel,
+        grid_spec=pltpu.PrefetchScalarGridSpec(
+            num_scalar_prefetch=len(scalars),
+            grid=grid,
+            in_specs=in_specs,
+            out_specs=out_specs,
+            scratch_shapes=scratch,
+        ),
+        out_shape=out_shapes,
+        cost_estimate=pl.CostEstimate(flops=cost[0], bytes_accessed=cost[1], transcendentals=0),
+        compiler_params=pltpu.CompilerParams(vmem_limit_bytes=vmem * MIB),
+    )(*scalars, *arrays)
+
+
+def whole(shape):
+    return pl.BlockSpec(shape, lambda *_: (0,) * len(shape))
+
+
+def pick_kernel(sets, full, *outs):
+    for k, out in enumerate(outs):
+        for q in range(UMAX):
+            block = sets[k * UMAX + q]
+            out[:, :, q * FB : (q + 1) * FB] = full[:, :, pl.ds(pl.multiple_of(block * FB, FB), FB)]
+
+
+def pick(sets, full, peers):
+    nb, sub, cols = full.shape
+    shape = (nb, sub, UMAX * FB)
+    return call(
+        pick_kernel,
+        [sets],
+        [full],
+        [whole(full.shape)],
+        [jax.ShapeDtypeStruct(shape, full.dtype)] * peers,
+        [whole(shape)] * peers,
+        [],
+        cost=(0, 2 * nb * sub * (cols + peers * UMAX * FB)),
+    )
+
+
+def add_up(sets, terms, total):
+    total[...] = jnp.zeros(total.shape, total.dtype)
+    for k, term in enumerate(terms):
+        for q in range(UMAX):
+            cols = pl.ds(pl.multiple_of(sets[k * UMAX + q] * FB, FB), FB)
+            total[:, :, cols] += term[:, :, q * FB : (q + 1) * FB].astype(jnp.float32)
+
+
+def merge_kernel(peers, sets, *refs):
+    terms, out, total = refs[:peers], refs[peers], refs[peers + 1]
+    add_up(sets, terms, total)
+    out[...] = total[...].astype(out.dtype)
+
+
+def merge(sets, terms, cols):
+    nb, sub, wide = terms[0].shape
+    shape = (nb, sub, cols)
+    return call(
+        functools.partial(merge_kernel, len(terms)),
+        [sets],
+        terms,
+        [whole(t.shape) for t in terms],
+        jax.ShapeDtypeStruct(shape, jnp.bfloat16),
+        whole(shape),
+        [pltpu.VMEM(shape, jnp.float32)],
+        cost=(0, 2 * nb * sub * (cols + 5 * wide)),
+    )
+
+
+def finish_kernel(peers, sets, core, *refs):
+    terms, far = refs[:peers], refs[peers]
+    keep, give, total = refs[peers + 1 :]
+    add_up(sets, terms, total)
+    half = keep.shape[2]
+    for out, side in ((keep, core[0]), (give, 1 - core[0])):
+        cols = pl.ds(pl.multiple_of(side * half, FB), half)
+        out[...] = (total[:, :, cols] + far[:, :, cols].astype(jnp.float32)).astype(out.dtype)
+
+
+def finish(sets, core, terms, far):
+    nb, sub, wide = terms[0].shape
+    cols = far.shape[2]
+    shape = (nb, sub, cols // 2)
+    return call(
+        functools.partial(finish_kernel, len(terms)),
+        [sets, core],
+        [*terms, far],
+        [whole(t.shape) for t in terms] + [whole(far.shape)],
+        [jax.ShapeDtypeStruct(shape, jnp.bfloat16)] * 2,
+        [whole(shape)] * 2,
+        [pltpu.VMEM(far.shape, jnp.float32)],
+        cost=(0, 2 * nb * sub * (2 * cols + 5 * wide)),
+    )
+
+
+def batch_kernel(steps, group, pieces, local, kbs, blocks, counts, *refs):
+    xs, quads = refs[0:2], refs[2:4]
+    centre = refs[4]
+    parts = refs[5 : 5 + pieces]
+    outs = refs[5 + pieces : 5 + 2 * pieces]
+    dense, acc, sems = refs[5 + 2 * pieces :]
+    nb, sub = parts[0].shape[:2]
+    step = pl.program_id(0)
+    batches = steps * group
+
+    @pl.when(step == 0)
+    def _():
+        copies = [
+            pltpu.make_async_copy(part, dense.at[pl.ds(nb * k, nb)], sems.at[k])
+            for k, part in enumerate(parts)
+        ]
+        for copy in copies:
+            copy.start()
+        acc[...] = jnp.zeros(acc.shape, acc.dtype)
+        for copy in copies:
+            copy.wait()
+
+    def one(side, g):
+        b = side * batches + step * group + g
+        count = counts[b]
+        for live in range(2, TMAX + 1):
+
+            @pl.when(count == live)
+            def _():
+                pos = [blocks[b * TMAX + s] for s in range(live)]
+                row = [kbs[p] for p in pos]
+                col = [pl.ds(pl.multiple_of(p * FB, FB), FB) for p in pos]
+                x = xs[side][g, : live * FB, :]
+                quad = quads[side]
+                xw = (x.astype(jnp.float32) * quad[g, 3:4, :]).astype(jnp.bfloat16)
+                d = jnp.concatenate(
+                    [
+                        jnp.concatenate([dense[row[s], :, col[t]] for t in range(live)], axis=1)
+                        for s in range(live)
+                    ],
+                    axis=0,
+                )
+                gval = jnp.dot(d, x, preferred_element_type=jnp.float32)
+                fval = []
+                for s in range(live):
+                    dist = None
+                    for axis in range(3):
+                        c = centre[axis, pos[s]]
+                        c = jnp.concatenate([c] * (x.shape[1] // FB), axis=1)
+                        diff = c - quad[g, axis : axis + 1, :]
+                        dist = diff * diff if dist is None else dist + diff * diff
+                    c = centre[3, pos[s]]
+                    dist = dist + jnp.concatenate([c] * (x.shape[1] // FB), axis=1)
+                    fval.append((gval[s * sub : (s + 1) * sub] * lax.rsqrt(dist)).astype(jnp.bfloat16))
+                fval = jnp.concatenate(fval, axis=0)
+                part = lax.dot_general(
+                    fval, xw, (((1,), (1,)), ((), ())), preferred_element_type=jnp.float32
+                )
+                for s in range(live):
+                    for t in range(live):
+                        acc[row[s], :, col[t]] += part[s * sub : (s + 1) * sub, t * FB : (t + 1) * FB]
+
+    for side in (0, 1):
+
+        @pl.loop(0, group)
+        def _(g):
+            one(side, g)
+
+    @pl.when(step == steps - 1)
+    def _():
+        for k, out in enumerate(outs):
+            out[...] = acc[nb * k : nb * (k + 1)].astype(out.dtype)
+
+
+def batch_sums(kbs, blocks, counts, xs, quads, centre, parts, local):
+    batches, width, pts = xs[0].shape
+    group = math.gcd(batches, 4)
+    steps = batches // group
+    nb, sub, wide = parts[0].shape
+    pieces = len(parts)
+    out_shapes = [
+        jax.ShapeDtypeStruct(parts[0].shape, jnp.float32 if k in local else jnp.bfloat16)
+        for k in range(pieces)
+    ]
+    flops = 2 * batches * 2 * 2 * width * (width // 2) * pts
+    return call(
+        functools.partial(batch_kernel, steps, group, pieces, local),
+        [kbs, blocks, counts],
+        [*xs, *quads, centre, *parts],
+        [pl.BlockSpec((group, width, pts), lambda i, *_: (i, 0, 0))] * 2
+        + [pl.BlockSpec((group, 4, pts), lambda i, *_: (i, 0, 0))] * 2
+        + [whole(centre.shape)]
+        + [pl.BlockSpec(memory_space=pl.ANY)] * pieces,
+        out_shapes,
+        [whole(parts[0].shape)] * pieces,
+        [
+            pltpu.VMEM((nb * pieces, sub, wide), jnp.bfloat16),
+            pltpu.VMEM((nb * pieces, sub, wide), jnp.float32),
+            pltpu.SemaphoreType.DMA((pieces,)),
+        ],
+        grid=(steps,),
+        cost=(flops, 2 * batches * width * pts * 2),
+    )
+
+
+def per_device(density, owner, touched, blocks, counts, basis, points, weights, centers, widths):
+    n = lax.axis_size("dom")
+    cores = lax.axis_size("rows")
+    i = lax.axis_index("dom")
+    r = lax.axis_index("rows")
+    nb = density.shape[0] // FB
+    sub = FB // cores
+    cols = density.shape[1]
+    block_count = owner.shape[0]
+    near = n // 2
+
+    def swap(x, k):
+        return lax.ppermute(x, "dom", [(a, a ^ k) for a in range(n)])
+
+    def across(x):
+        return lax.ppermute(x, "rows", [(a, cores - 1 - a) for a in range(cores)])
+
+    own = lax.dynamic_index_in_dim(density.reshape(nb, cores, sub, cols), r, 1, keepdims=False)
+    far = swap(own, near)
+    near_sets = jnp.concatenate([touched] + [swap(touched, k) for k in range(1, near)], axis=0).reshape(-1)
+
+    quads = jnp.concatenate([points, weights[:, None, :]], axis=1)
+    tables = jnp.concatenate([blocks, counts[:, None]], axis=1)
+    basis_b, quads_b, tables_b = across(basis), across(quads), across(tables)
+    both = jnp.concatenate([tables, tables_b], axis=0)
+    slots = both[:, :TMAX].reshape(-1)
+    live = both[:, TMAX]
+
+    own_set = touched[0]
+    stored = lookup_owner(owner, own_set)
+    kbs = jnp.bitwise_xor(stored // nb, i) * nb + stored % nb
+    shaped = jnp.concatenate([centers, (widths * widths)[None]], axis=0).reshape(4, block_count, cores, sub)
+    shaped = lax.dynamic_index_in_dim(shaped, r, 2, keepdims=False)
+    centre = jnp.take(shaped, own_set, axis=1)
+    centre = jnp.broadcast_to(centre[..., None], (4, UMAX, sub, FB))
+
+    picked = pick(near_sets, own, near)
+    parts = [picked[0]] + [swap(picked[k], k) for k in range(1, near)]
+    picked = pick(near_sets, far, near)
+    parts += [picked[0]] + [swap(picked[k], k) for k in range(1, near)]
+
+    sums = batch_sums(kbs, slots, live, (basis, basis_b), (quads, quads_b), centre, parts, (0, near))
+    terms = [sums[near]] + [swap(sums[near + k], k) for k in range(1, near)]
+    far_sum = swap(merge(near_sets, terms, cols), near)
+    terms = [sums[0]] + [swap(sums[k], k) for k in range(1, near)]
+    keep, give = finish(near_sets, r.reshape(1), terms, far_sum)
+    got = across(give)
+    pair = jnp.where(r == 0, jnp.stack([keep, got], axis=1), jnp.stack([got, keep], axis=1))
+    return pair.reshape(nb * FB, cols // cores)
+
+
 def solution(mesh):
     in_specs = (
         P(("groups", "dom"), None),
@@ -134,6 +391,12 @@
         P("groups"),
     )
     out_specs = P(("groups", "dom"), "rows")
-    return jax.shard_map(
-        per_device, mesh=mesh, in_specs=in_specs, out_specs=out_specs, check_vma=False
-    )
+
+    def run(*args):
+        n, cores = mesh.shape["dom"], mesh.shape["rows"]
+        rows_here = args[0].shape[0] // (mesh.shape["groups"] * n)
+        split = rows_here % FB == 0 and cores == 2 and n >= 4 and n & (n - 1) == 0
+        body = per_device if split else per_device_any
+        return jax.shard_map(body, mesh=mesh, in_specs=in_specs, out_specs=out_specs, check_vma=False)(*args)
+
+    return run

time: 561 us -> 126 us (0.22)
  local copies, waits for them, and re-layouts: 175 us -> 7.92 us
  waiting for transfers between devices: 203 us -> 57.1 us
  other arithmetic: 100 us -> 5.35 us
  matrix products: 32.6 us -> 0 us
  Pallas kernels: 0 us -> 30 us
  blocking collectives: 22.3 us -> 0 us
  starting transfers between devices: 10.8 us -> 25.5 us
  between operations: 13.5 us -> 0.18 us
    all_to_all x2 -> x0, waiting for transfers between devices: 183 us -> none  [the longest x1 93.4 us: per_device(): lax.all_to_all(spread_rows(halved, stored, block_count, sources), 'dom',...]
    scatter-add x4 -> x0, other arithmetic: 89.1 us -> none  [the longest x3 82.6 us: work(): total = total.at[slots[:, :, None], :, slots[:, None, :], :].add(pieces)]
    reshape x20 -> x2, local copies, waits for them, and re-layouts: 58.6 us -> 0.18 us  [the longest x1 0.1 us: per_device(): slots = both[:, :TMAX].reshape(-1)]
    ppermute x0 -> x21, waiting for transfers between devices: none -> 57.1 us  [the longest x17 55.6 us: swap(): return lax.ppermute(x, 'dom', [(a, a ^ k) for a in range(n)])]
    gather x27 -> x1, local copies, waits for them, and re-layouts: 53.3 us -> 0.58 us  [per_device(): centre = jnp.take(shaped, own_set, axis=1)]
    dot_general x6 -> x0, matrix products: 32.6 us -> none  [the longest x3 16.7 us: work(): jnp.einsum('brc,bcg->brg', dloc, xmask, preferred_element_type=jnp.float32)]
    pallas_call x0 -> x5, Pallas kernels: none -> 30 us  [call(): pl.pallas_call(kernel, grid_spec=pltpu.PrefetchScalarGridSpec(num_scalar_...]
    ppermute x0 -> x21, starting transfers between devices: none -> 25.5 us  [the longest x17 24.9 us: swap(): return lax.ppermute(x, 'dom', [(a, a ^ k) for a in range(n)])]
  transfers between devices with their start and end apart: 4 -> 21, of which waited for: 4 -> 12; matrix products, arithmetic and copies ran while one was open for 0% -> 7% of each run, Pallas kernels for 0% -> 3%
where the time goes in v1:
time: 126 us
  waiting for transfers between devices  57.1 us (45%)
  Pallas kernels  30 us (24%)
  starting transfers between devices  25.5 us (20%)
  local copies, waits for them, and re-layouts  7.92 us (6%)
  other arithmetic  5.35 us (4%)
    ppermute x17, waiting for transfers between devices, swap(): return lax.ppermute(x, 'dom', [(a, a ^ k) for a in range(n)])  55.6 us
    pallas_call x5, Pallas kernels, call(): pl.pallas_call(kernel, grid_spec=pltpu.PrefetchScalarGridSpec(num_scalar_...  30 us
    ppermute x17, starting transfers between devices, swap(): return lax.ppermute(x, 'dom', [(a, a ^ k) for a in range(n)])  24.9 us
    unnamed x11, local copies, waits for them, and re-layouts  4.11 us
  transfers between devices with their start and end apart: 21, of which 12 were waited for; matrix products, arithmetic and copies ran while one was open for 7% of the time, Pallas kernels for 3%

profile of v1, /device:TPU:0, one launch (start us, length us, event | category | flops | bytes accessed | tf_op | source)
XLA Modules:
  0.0 126.1 jit_solution(4160957551390904338)
XLA Ops:
  0.5 2.6 %collective-permute-start = (s32[1,8]{1,0:T(1,128)}, s32[1,8]{1,0:T(1,128)S(1)}, u32[]{:S(2)}, u32[]{:S(2)}) collective-permute-start(s32[1,8]{1,0:T(1,128)} %param.12), channel_id=1, source_target_pairs={{0,2},{2,0},{4,6},{6,4},{8,10},{10,8},{12,14},{14,12},{1,3},{3,1},... | collective-permute-start | bytes 104 | tf_op jit(solution)/shard_map/ppermute | solution.py:341
  3.0 1.6 %collective-permute-start.1 = (s32[1,8]{1,0:T(1,128)}, s32[1,8]{1,0:T(1,128)S(1)}, u32[]{:S(2)}, u32[]{:S(2)}) collective-permute-start(s32[1,8]{1,0:T(1,128)} %param.12), channel_id=1, source_target_pairs={{0,4},{2,6},{4,0},{6,2},{8,12},{10,14},{12,8},{14,10},{1,5},{3,7},... | collective-permute-start | bytes 104 | tf_op jit(solution)/shard_map/ppermute | solution.py:341
  4.7 3.0 %collective-permute-start.9 = (bf16[2,64,2048]{2,1,0:T(8,128)(2,1)S(1)}, bf16[2,64,2048]{2,1,0:T(8,128)(2,1)S(1)}, u32[]{:S(2)}, u32[]{:S(2)}) collective-permute-start(bf16[2,64,2048]{2,1,0:T(8,128)(2,1)S(1)} %dynamic-slice_bitcast_fusion.full), channel_id=1, source_target_pairs={{0,8},{2,10},{4,12},{6,14},{8,0},{10,2},{12,4},{14,6},{1,9},{3,11}... | collective-permute-start | bytes 1572872 | tf_op jit(solution)/shard_map/ppermute | solution.py:341
  14.8 1.6 %shard_map.100 = (bf16[2,64,1024]{2,1,0:T(8,128)(2,1)S(1)}, bf16[2,64,1024]{2,1,0:T(8,128)(2,1)}, bf16[2,64,1024]{2,1,0:T(8,128)(2,1)}, bf16[2,64,1024]{2,1,0:T(8,128)(2,1)S(1)}) custom-call(s32[32]{0:T(128)S(1)} %reshape.60.sets, bf16[2,64,2048]{2,1,0:T(8,128)(2,1)S(1)} %dynamic-slice_bitcast_fusion.full), custom_call_target="tpu_custom_call" | custom-call | bytes 1572864 | tf_op jit(solution)/shard_map/pallas_call | solution.py:128
  16.4 1.5 %collective-permute-start.6 = (bf16[2,64,1024]{2,1,0:T(8,128)(2,1)}, bf16[2,64,1024]{2,1,0:T(8,128)(2,1)S(1)}, u32[]{:S(2)}, u32[]{:S(2)}) collective-permute-start(bf16[2,64,1024]{2,1,0:T(8,128)(2,1)} %get-tuple-element.24), channel_id=1, source_target_pairs={{0,2},{2,0},{4,6},{6,4},{8,10},{10,8},{12,14},{14,12},{1,3},{3,1},... | collective-permute-start | bytes 786440 | tf_op jit(solution)/shard_map/ppermute | solution.py:341
  18.0 1.6 %collective-permute-start.7 = (bf16[2,64,1024]{2,1,0:T(8,128)(2,1)}, bf16[2,64,1024]{2,1,0:T(8,128)(2,1)S(1)}, u32[]{:S(2)}, u32[]{:S(2)}) collective-permute-start(bf16[2,64,1024]{2,1,0:T(8,128)(2,1)} %get-tuple-element.25), channel_id=1, source_target_pairs={{0,4},{2,6},{4,0},{6,2},{8,12},{10,14},{12,8},{14,10},{1,5},{3,7},... | collective-permute-start | bytes 786440 | tf_op jit(solution)/shard_map/ppermute | solution.py:341
  20.4 10.4 %collective-permute-done.9.full = bf16[2,64,2048]{2,1,0:T(8,128)(2,1)S(1)} collective-permute-done((bf16[2,64,2048]{2,1,0:T(8,128)(2,1)S(1)}, bf16[2,64,2048]{2,1,0:T(8,128)(2,1)S(1)}, u32[]{:S(2)}, u32[]{:S(2)}) %collective-permute-start.9) | collective-permute-done | bytes 524320 | tf_op jit(solution)/shard_map/ppermute | solution.py:341
  30.8 1.6 %shard_map.101 = (bf16[2,64,1024]{2,1,0:T(8,128)(2,1)S(1)}, bf16[2,64,1024]{2,1,0:T(8,128)(2,1)}, bf16[2,64,1024]{2,1,0:T(8,128)(2,1)}, bf16[2,64,1024]{2,1,0:T(8,128)(2,1)}) custom-call(s32[32]{0:T(128)S(1)} %reshape.60.sets, bf16[2,64,2048]{2,1,0:T(8,128)(2,1)S(1)} %collective-permute-done.9.full), custom_call_target="tpu_custom_call" | custom-call | bytes 1572864 | tf_op jit(solution)/shard_map/pallas_call | solution.py:128
  32.4 1.6 %collective-permute-start.8 = (bf16[2,64,1024]{2,1,0:T(8,128)(2,1)S(1)}, bf16[2,64,1024]{2,1,0:T(8,128)(2,1)S(1)}, u32[]{:S(2)}, u32[]{:S(2)}) collective-permute-start(bf16[2,64,1024]{2,1,0:T(8,128)(2,1)S(1)} %get-tuple-element.26), channel_id=1, source_target_pairs={{0,6},{2,4},{4,2},{6,0},{8,14},{10,12},{12,10},{14,8},{1,7},{3,5},... | collective-permute-start | bytes 786440 | tf_op jit(solution)/shard_map/ppermute | solution.py:341
  36.6 1.6 %collective-permute-start.12 = (bf16[2,64,1024]{2,1,0:T(8,128)(2,1)}, bf16[2,64,1024]{2,1,0:T(8,128)(2,1)}, u32[]{:S(2)}, u32[]{:S(2)}) collective-permute-start(bf16[2,64,1024]{2,1,0:T(8,128)(2,1)} %get-tuple-element.30), channel_id=1, source_target_pairs={{0,6},{2,4},{4,2},{6,0},{8,14},{10,12},{12,10},{14,8},{1,7},{3,5},... | collective-permute-start | bytes 786440 | tf_op jit(solution)/shard_map/ppermute | solution.py:341
  39.2 3.3 %collective-permute-done.8.refs_8_ = bf16[2,64,1024]{2,1,0:T(8,128)(2,1)S(1)} collective-permute-done((bf16[2,64,1024]{2,1,0:T(8,128)(2,1)S(1)}, bf16[2,64,1024]{2,1,0:T(8,128)(2,1)S(1)}, u32[]{:S(2)}, u32[]{:S(2)}) %collective-permute-start.8) | collective-permute-done | bytes 262176 | tf_op jit(solution)/shard_map/ppermute | solution.py:341
  42.5 5.5 %collective-permute-done.10.refs_10_ = bf16[2,64,1024]{2,1,0:T(8,128)(2,1)S(1)} collective-permute-done((bf16[2,64,1024]{2,1,0:T(8,128)(2,1)}, bf16[2,64,1024]{2,1,0:T(8,128)(2,1)S(1)}, u32[]{:S(2)}, u32[]{:S(2)}) %collective-permute-start.10) | collective-permute-done | bytes 262176 | tf_op jit(solution)/shard_map/ppermute | solution.py:341
  48.9 4.6 %collective-permute-done.12.refs_12_ = bf16[2,64,1024]{2,1,0:T(8,128)(2,1)} collective-permute-done((bf16[2,64,1024]{2,1,0:T(8,128)(2,1)}, bf16[2,64,1024]{2,1,0:T(8,128)(2,1)}, u32[]{:S(2)}, u32[]{:S(2)}) %collective-permute-start.12) | collective-permute-done | bytes 262176 | tf_op jit(solution)/shard_map/ppermute | solution.py:341
  55.7 24.5 %shard_map.102 = (f32[2,64,1024]{2,1,0:T(8,128)S(1)}, bf16[2,64,1024]{2,1,0:T(8,128)(2,1)S(1)}, bf16[2,64,1024]{2,1,0:T(8,128)(2,1)S(1)}, bf16[2,64,1024]{2,1,0:...) custom-call(s32[8]{0:T(128)S(1)} %fusion.2.kbs, ...), custom_call_target="tpu_custom_call" | custom-call | flops 6442450944 | bytes 12582912 | tf_op jit(solution)/shard_map/pallas_call | solution.py:128
  83.8 4.8 %collective-permute-done.16.refs_1_ = bf16[2,64,1024]{2,1,0:T(8,128)(2,1)S(1)} collective-permute-done((bf16[2,64,1024]{2,1,0:T(8,128)(2,1)S(1)}, bf16[2,64,1024]{2,1,0:T(8,128)(2,1)S(1)}, u32[]{:S(2)}, u32[]{:S(2)}) %collective-permute-start.16) | collective-permute-done | bytes 262176 | tf_op jit(solution)/shard_map/ppermute | solution.py:341
  88.6 1.9 %collective-permute-done.17.refs_2_ = bf16[2,64,1024]{2,1,0:T(8,128)(2,1)S(1)} collective-permute-done((bf16[2,64,1024]{2,1,0:T(8,128)(2,1)S(1)}, bf16[2,64,1024]{2,1,0:T(8,128)(2,1)S(1)}, u32[]{:S(2)}, u32[]{:S(2)}) %collective-permute-start.17) | collective-permute-done | bytes 262176 | tf_op jit(solution)/shard_map/ppermute | solution.py:341
  90.5 4.6 %collective-permute-done.18.refs_3_ = bf16[2,64,1024]{2,1,0:T(8,128)(2,1)S(1)} collective-permute-done((bf16[2,64,1024]{2,1,0:T(8,128)(2,1)S(1)}, bf16[2,64,1024]{2,1,0:T(8,128)(2,1)S(1)}, u32[]{:S(2)}, u32[]{:S(2)}) %collective-permute-start.18) | collective-permute-done | bytes 262176 | tf_op jit(solution)/shard_map/ppermute | solution.py:341
  96.2 2.5 %collective-permute-start.19 = (bf16[2,64,2048]{2,1,0:T(8,128)(2,1)S(1)}, bf16[2,64,2048]{2,1,0:T(8,128)(2,1)S(1)}, u32[]{:S(2)}, u32[]{:S(2)}) collective-permute-start(bf16[2,64,2048]{2,1,0:T(8,128)(2,1)S(1)} %shard_map.103), channel_id=1, source_target_pairs={{0,8},{2,10},{4,12},{6,14},{8,0},{10,2},{12,4},{14,6},{1,9},{3,11}... | collective-permute-start | bytes 1572872 | tf_op jit(solution)/shard_map/ppermute | solution.py:341
  98.7 1.4 %collective-permute-start.13 = (bf16[2,64,1024]{2,1,0:T(8,128)(2,1)S(1)}, bf16[2,64,1024]{2,1,0:T(8,128)(2,1)S(1)}, u32[]{:S(2)}, u32[]{:S(2)}) collective-permute-start(bf16[2,64,1024]{2,1,0:T(8,128)(2,1)S(1)} %get-tuple-element.32), channel_id=1, source_target_pairs={{0,2},{2,0},{4,6},{6,4},{8,10},{10,8},{12,14},{14,12},{1,3},{3,1},... | collective-permute-start | bytes 786440 | tf_op jit(solution)/shard_map/ppermute | solution.py:341
  100.0 1.7 %collective-permute-start.14 = (bf16[2,64,1024]{2,1,0:T(8,128)(2,1)S(1)}, bf16[2,64,1024]{2,1,0:T(8,128)(2,1)S(1)}, u32[]{:S(2)}, u32[]{:S(2)}) collective-permute-start(bf16[2,64,1024]{2,1,0:T(8,128)(2,1)S(1)} %get-tuple-element.33), channel_id=1, source_target_pairs={{0,4},{2,6},{4,0},{6,2},{8,12},{10,14},{12,8},{14,10},{1,5},{3,7},... | collective-permute-start | bytes 786440 | tf_op jit(solution)/shard_map/ppermute | solution.py:341
  102.2 4.8 %collective-permute-done.13.refs_1_ = bf16[2,64,1024]{2,1,0:T(8,128)(2,1)S(1)} collective-permute-done((bf16[2,64,1024]{2,1,0:T(8,128)(2,1)S(1)}, bf16[2,64,1024]{2,1,0:T(8,128)(2,1)S(1)}, u32[]{:S(2)}, u32[]{:S(2)}) %collective-permute-start.13) | collective-permute-done | bytes 262176 | tf_op jit(solution)/shard_map/ppermute | solution.py:341
  107.0 9.7 %collective-permute-done.14.refs_2_ = bf16[2,64,1024]{2,1,0:T(8,128)(2,1)S(1)} collective-permute-done((bf16[2,64,1024]{2,1,0:T(8,128)(2,1)S(1)}, bf16[2,64,1024]{2,1,0:T(8,128)(2,1)S(1)}, u32[]{:S(2)}, u32[]{:S(2)}) %collective-permute-start.14) | collective-permute-done | bytes 262176 | tf_op jit(solution)/shard_map/ppermute | solution.py:341
  116.7 5.7 %collective-permute-done.15.refs_3_ = bf16[2,64,1024]{2,1,0:T(8,128)(2,1)S(1)} collective-permute-done((bf16[2,64,1024]{2,1,0:T(8,128)(2,1)S(1)}, bf16[2,64,1024]{2,1,0:T(8,128)(2,1)S(1)}, u32[]{:S(2)}, u32[]{:S(2)}) %collective-permute-start.15) | collective-permute-done | bytes 262176 | tf_op jit(solution)/shard_map/ppermute | solution.py:341
  123.7 1.5 %collective-permute-done.20 = bf16[2,64,1024]{2,1,0:T(8,128)(2,1)S(1)} collective-permute-done((bf16[2,64,1024]{2,1,0:T(8,128)(2,1)S(1)}, bf16[2,64,1024]{2,1,0:T(8,128)(2,1)S(1)}, u32[]{:S(2)}, u32[]{:S(2)}) %collective-permute-start.20) | collective-permute-done | bytes 262176 | tf_op jit(solution)/shard_map/ppermute | solution.py:344
  (62 shorter events, 22.2 us)
Async XLA Ops:
  0.0 4.6 %copy-start = (bf16[256,2048]{1,0:T(8,128)(2,1)S(1)}, bf16[256,2048]{1,0:T(8,128)(2,1)}, u32[]{:S(2)}) copy-start(bf16[256,2048]{1,0:T(8,128)(2,1)} %param.10) | copy-start | bytes 3145732
  0.0 53.5 %collective-permute-start.4 = (bf16[24,512,256]{2,1,0:T(8,128)(2,1)}, bf16[24,512,256]{2,1,0:T(8,128)(2,1)}, u32[]{:S(2)}, u32[]{:S(2)}) collective-permute-start(bf16[24,512,256]{2,1,0:T(8,128)(2,1)} %refs_0_.1), channel_id=1, source_target_pairs={{0,1},{1,0},{2,3},{3,2},{4,5},{5,4},{6,7},{7,6},{8,9},{9,8},{10,11... | collective-permute-start | bytes 18874376 | tf_op jit(solution)/shard_map/ppermute | solution.py:344
  0.5 13.5 %collective-permute-start = (s32[1,8]{1,0:T(1,128)}, s32[1,8]{1,0:T(1,128)S(1)}, u32[]{:S(2)}, u32[]{:S(2)}) collective-permute-start(s32[1,8]{1,0:T(1,128)} %param.12), channel_id=1, source_target_pairs={{0,2},{2,0},{4,6},{6,4},{8,10},{10,8},{12,14},{14,12},{1,3},{3,1},... | collective-permute-start | bytes 104 | tf_op jit(solution)/shard_map/ppermute | solution.py:341
  3.0 11.0 %collective-permute-start.1 = (s32[1,8]{1,0:T(1,128)}, s32[1,8]{1,0:T(1,128)S(1)}, u32[]{:S(2)}, u32[]{:S(2)}) collective-permute-start(s32[1,8]{1,0:T(1,128)} %param.12), channel_id=1, source_target_pairs={{0,4},{2,6},{4,0},{6,2},{8,12},{10,14},{12,8},{14,10},{1,5},{3,7},... | collective-permute-start | bytes 104 | tf_op jit(solution)/shard_map/ppermute | solution.py:341
  4.6 9.5 %collective-permute-start.2 = (s32[1,8]{1,0:T(1,128)}, s32[1,8]{1,0:T(1,128)S(1)}, u32[]{:S(2)}, u32[]{:S(2)}) collective-permute-start(s32[1,8]{1,0:T(1,128)} %param.12), channel_id=1, source_target_pairs={{0,6},{2,4},{4,2},{6,0},{8,14},{10,12},{12,10},{14,8},{1,7},{3,5},... | collective-permute-start | bytes 104 | tf_op jit(solution)/shard_map/ppermute | solution.py:341
  4.7 26.1 %collective-permute-start.9 = (bf16[2,64,2048]{2,1,0:T(8,128)(2,1)S(1)}, bf16[2,64,2048]{2,1,0:T(8,128)(2,1)S(1)}, u32[]{:S(2)}, u32[]{:S(2)}) collective-permute-start(bf16[2,64,2048]{2,1,0:T(8,128)(2,1)S(1)} %dynamic-slice_bitcast_fusion.full), channel_id=1, source_target_pairs={{0,8},{2,10},{4,12},{6,14},{8,0},{10,2},{12,4},{14,6},{1,9},{3,11}... | collective-permute-start | bytes 1572872 | tf_op jit(solution)/shard_map/ppermute | solution.py:341
  14.0 18.4 %collective-permute-start.3 = (s32[24,5]{0,1:T(8,128)S(1)}, s32[24,5]{0,1:T(8,128)S(1)}, u32[]{:S(2)}, u32[]{:S(2)}) collective-permute-start(s32[24,5]{0,1:T(8,128)S(1)} %pad_add_fusion), channel_id=1, source_target_pairs={{0,1},{1,0},{2,3},{3,2},{4,5},{5,4},{6,7},{7,6},{8,9},{9,8},{10,11... | collective-permute-start | bytes 1448 | tf_op jit(solution)/shard_map/ppermute | solution.py:344
  16.4 18.8 %collective-permute-start.6 = (bf16[2,64,1024]{2,1,0:T(8,128)(2,1)}, bf16[2,64,1024]{2,1,0:T(8,128)(2,1)S(1)}, u32[]{:S(2)}, u32[]{:S(2)}) collective-permute-start(bf16[2,64,1024]{2,1,0:T(8,128)(2,1)} %get-tuple-element.24), channel_id=1, source_target_pairs={{0,2},{2,0},{4,6},{6,4},{8,10},{10,8},{12,14},{14,12},{1,3},{3,1},... | collective-permute-start | bytes 786440 | tf_op jit(solution)/shard_map/ppermute | solution.py:341
  18.0 18.6 %collective-permute-start.7 = (bf16[2,64,1024]{2,1,0:T(8,128)(2,1)}, bf16[2,64,1024]{2,1,0:T(8,128)(2,1)S(1)}, u32[]{:S(2)}, u32[]{:S(2)}) collective-permute-start(bf16[2,64,1024]{2,1,0:T(8,128)(2,1)} %get-tuple-element.25), channel_id=1, source_target_pairs={{0,4},{2,6},{4,0},{6,2},{8,12},{10,14},{12,8},{14,10},{1,5},{3,7},... | collective-permute-start | bytes 786440 | tf_op jit(solution)/shard_map/ppermute | solution.py:341
  30.7 3.3 %collective-permute-start.5 = (f32[24,4,256]{2,1,0:T(4,128)S(1)}, f32[24,4,256]{2,1,0:T(4,128)S(1)}, u32[]{:S(2)}, u32[]{:S(2)}) collective-permute-start(f32[24,4,256]{2,1,0:T(4,128)S(1)} %pad_maximum_fusion.refs_2_), channel_id=1, source_target_pairs={{0,1},{1,0},{2,3},{3,2},{4,5},{5,4},{6,7},{7,6},{8,9},{9,8},{10,11... | collective-permute-start | bytes 294920 | tf_op jit(solution)/shard_map/ppermute | solution.py:344
  32.4 10.0 %collective-permute-start.8 = (bf16[2,64,1024]{2,1,0:T(8,128)(2,1)S(1)}, bf16[2,64,1024]{2,1,0:T(8,128)(2,1)S(1)}, u32[]{:S(2)}, u32[]{:S(2)}) collective-permute-start(bf16[2,64,1024]{2,1,0:T(8,128)(2,1)S(1)} %get-tuple-element.26), channel_id=1, source_target_pairs={{0,6},{2,4},{4,2},{6,0},{8,14},{10,12},{12,10},{14,8},{1,7},{3,5},... | collective-permute-start | bytes 786440 | tf_op jit(solution)/shard_map/ppermute | solution.py:341
  34.7 13.3 %collective-permute-start.10 = (bf16[2,64,1024]{2,1,0:T(8,128)(2,1)}, bf16[2,64,1024]{2,1,0:T(8,128)(2,1)S(1)}, u32[]{:S(2)}, u32[]{:S(2)}) collective-permute-start(bf16[2,64,1024]{2,1,0:T(8,128)(2,1)} %get-tuple-element.28), channel_id=1, source_target_pairs={{0,2},{2,0},{4,6},{6,4},{8,10},{10,8},{12,14},{14,12},{1,3},{3,1},... | collective-permute-start | bytes 786440 | tf_op jit(solution)/shard_map/ppermute | solution.py:341
  35.2 13.0 %collective-permute-start.11 = (bf16[2,64,1024]{2,1,0:T(8,128)(2,1)}, bf16[2,64,1024]{2,1,0:T(8,128)(2,1)S(1)}, u32[]{:S(2)}, u32[]{:S(2)}) collective-permute-start(bf16[2,64,1024]{2,1,0:T(8,128)(2,1)} %get-tuple-element.29), channel_id=1, source_target_pairs={{0,4},{2,6},{4,0},{6,2},{8,12},{10,14},{12,8},{14,10},{1,5},{3,7},... | collective-permute-start | bytes 786440 | tf_op jit(solution)/shard_map/ppermute | solution.py:341
  36.6 17.0 %collective-permute-start.12 = (bf16[2,64,1024]{2,1,0:T(8,128)(2,1)}, bf16[2,64,1024]{2,1,0:T(8,128)(2,1)}, u32[]{:S(2)}, u32[]{:S(2)}) collective-permute-start(bf16[2,64,1024]{2,1,0:T(8,128)(2,1)} %get-tuple-element.30), channel_id=1, source_target_pairs={{0,6},{2,4},{4,2},{6,0},{8,14},{10,12},{12,10},{14,8},{1,7},{3,5},... | collective-permute-start | bytes 786440 | tf_op jit(solution)/shard_map/ppermute | solution.py:341
  53.9 1.0 copy-start.2
  54.8 0.9 copy-start.4
  80.2 8.4 %collective-permute-start.16 = (bf16[2,64,1024]{2,1,0:T(8,128)(2,1)S(1)}, bf16[2,64,1024]{2,1,0:T(8,128)(2,1)S(1)}, u32[]{:S(2)}, u32[]{:S(2)}) collective-permute-start(bf16[2,64,1024]{2,1,0:T(8,128)(2,1)S(1)} %get-tuple-element.36), channel_id=1, source_target_pairs={{0,2},{2,0},{4,6},{6,4},{8,10},{10,8},{12,14},{14,12},{1,3},{3,1},... | collective-permute-start | bytes 786440 | tf_op jit(solution)/shard_map/ppermute | solution.py:341
  81.3 9.2 %collective-permute-start.17 = (bf16[2,64,1024]{2,1,0:T(8,128)(2,1)S(1)}, bf16[2,64,1024]{2,1,0:T(8,128)(2,1)S(1)}, u32[]{:S(2)}, u32[]{:S(2)}) collective-permute-start(bf16[2,64,1024]{2,1,0:T(8,128)(2,1)S(1)} %get-tuple-element.37), channel_id=1, source_target_pairs={{0,4},{2,6},{4,0},{6,2},{8,12},{10,14},{12,8},{14,10},{1,5},{3,7},... | collective-permute-start | bytes 786440 | tf_op jit(solution)/shard_map/ppermute | solution.py:341
  82.5 12.6 %collective-permute-start.18 = (bf16[2,64,1024]{2,1,0:T(8,128)(2,1)S(1)}, bf16[2,64,1024]{2,1,0:T(8,128)(2,1)S(1)}, u32[]{:S(2)}, u32[]{:S(2)}) collective-permute-start(bf16[2,64,1024]{2,1,0:T(8,128)(2,1)S(1)} %get-tuple-element.38), channel_id=1, source_target_pairs={{0,6},{2,4},{4,2},{6,0},{8,14},{10,12},{12,10},{14,8},{1,7},{3,5},... | collective-permute-start | bytes 786440 | tf_op jit(solution)/shard_map/ppermute | solution.py:341
  96.2 26.2 %collective-permute-start.19 = (bf16[2,64,2048]{2,1,0:T(8,128)(2,1)S(1)}, bf16[2,64,2048]{2,1,0:T(8,128)(2,1)S(1)}, u32[]{:S(2)}, u32[]{:S(2)}) collective-permute-start(bf16[2,64,2048]{2,1,0:T(8,128)(2,1)S(1)} %shard_map.103), channel_id=1, source_target_pairs={{0,8},{2,10},{4,12},{6,14},{8,0},{10,2},{12,4},{14,6},{1,9},{3,11}... | collective-permute-start | bytes 1572872 | tf_op jit(solution)/shard_map/ppermute | solution.py:341
  98.7 8.3 %collective-permute-start.13 = (bf16[2,64,1024]{2,1,0:T(8,128)(2,1)S(1)}, bf16[2,64,1024]{2,1,0:T(8,128)(2,1)S(1)}, u32[]{:S(2)}, u32[]{:S(2)}) collective-permute-start(bf16[2,64,1024]{2,1,0:T(8,128)(2,1)S(1)} %get-tuple-element.32), channel_id=1, source_target_pairs={{0,2},{2,0},{4,6},{6,4},{8,10},{10,8},{12,14},{14,12},{1,3},{3,1},... | collective-permute-start | bytes 786440 | tf_op jit(solution)/shard_map/ppermute | solution.py:341
  100.0 16.6 %collective-permute-start.14 = (bf16[2,64,1024]{2,1,0:T(8,128)(2,1)S(1)}, bf16[2,64,1024]{2,1,0:T(8,128)(2,1)S(1)}, u32[]{:S(2)}, u32[]{:S(2)}) collective-permute-start(bf16[2,64,1024]{2,1,0:T(8,128)(2,1)S(1)} %get-tuple-element.33), channel_id=1, source_target_pairs={{0,4},{2,6},{4,0},{6,2},{8,12},{10,14},{12,8},{14,10},{1,5},{3,7},... | collective-permute-start | bytes 786440 | tf_op jit(solution)/shard_map/ppermute | solution.py:341
  101.8 20.7 %collective-permute-start.15 = (bf16[2,64,1024]{2,1,0:T(8,128)(2,1)S(1)}, bf16[2,64,1024]{2,1,0:T(8,128)(2,1)S(1)}, u32[]{:S(2)}, u32[]{:S(2)}) collective-permute-start(bf16[2,64,1024]{2,1,0:T(8,128)(2,1)S(1)} %get-tuple-element.34), channel_id=1, source_target_pairs={{0,6},{2,4},{4,2},{6,0},{8,14},{10,12},{12,10},{14,8},{1,7},{3,5},... | collective-permute-start | bytes 786440 | tf_op jit(solution)/shard_map/ppermute | solution.py:341
  123.6 1.6 %collective-permute-start.20 = (bf16[2,64,1024]{2,1,0:T(8,128)(2,1)S(1)}, bf16[2,64,1024]{2,1,0:T(8,128)(2,1)S(1)}, u32[]{:S(2)}, u32[]{:S(2)}) collective-permute-start(bf16[2,64,1024]{2,1,0:T(8,128)(2,1)S(1)} %get-tuple-element.40), channel_id=1, source_target_pairs={{0,1},{1,0},{2,3},{3,2},{4,5},{5,4},{6,7},{7,6},{8,9},{9,8},{10,11... | collective-permute-start | bytes 786440 | tf_op jit(solution)/shard_map/ppermute | solution.py:344
  (2 other events, 1.3 us)

commit v2 on v1

--- a/solution.py
+++ b/solution.py
@@ -124,7 +124,7 @@
     return summed.astype(jnp.bfloat16)
 
 
-def call(kernel, scalars, arrays, in_specs, out_shapes, out_specs, scratch, grid=(1,), cost=None, vmem=48):
+def call(kernel, scalars, arrays, in_specs, out_shapes, out_specs, scratch, grid=(1,), cost=None, vmem=12):
     return pl.pallas_call(
         kernel,
         grid_spec=pltpu.PrefetchScalarGridSpec(
@@ -196,134 +196,165 @@
 
 
 def finish_kernel(peers, sets, core, *refs):
-    terms, far = refs[:peers], refs[peers]
-    keep, give, total = refs[peers + 1 :]
+    terms, fars = refs[:peers], refs[peers:-3]
+    keep, give, total = refs[-3:]
     add_up(sets, terms, total)
     half = keep.shape[2]
     for out, side in ((keep, core[0]), (give, 1 - core[0])):
         cols = pl.ds(pl.multiple_of(side * half, FB), half)
-        out[...] = (total[:, :, cols] + far[:, :, cols].astype(jnp.float32)).astype(out.dtype)
-
-
-def finish(sets, core, terms, far):
+        for b, far in enumerate(fars):
+            out[b] = (total[b, :, cols] + far[0, :, cols].astype(jnp.float32)).astype(out.dtype)
+
+
+def finish(sets, core, terms, fars):
     nb, sub, wide = terms[0].shape
-    cols = far.shape[2]
+    cols = fars[0].shape[2]
     shape = (nb, sub, cols // 2)
     return call(
         functools.partial(finish_kernel, len(terms)),
         [sets, core],
-        [*terms, far],
-        [whole(t.shape) for t in terms] + [whole(far.shape)],
+        [*terms, *fars],
+        [whole(t.shape) for t in (*terms, *fars)],
         [jax.ShapeDtypeStruct(shape, jnp.bfloat16)] * 2,
         [whole(shape)] * 2,
-        [pltpu.VMEM(far.shape, jnp.float32)],
+        [pltpu.VMEM((nb, sub, cols), jnp.float32)],
         cost=(0, 2 * nb * sub * (2 * cols + 5 * wide)),
     )
 
 
-def batch_kernel(steps, group, pieces, local, kbs, blocks, counts, *refs):
-    xs, quads = refs[0:2], refs[2:4]
-    centre = refs[4]
-    parts = refs[5 : 5 + pieces]
-    outs = refs[5 + pieces : 5 + 2 * pieces]
-    dense, acc, sems = refs[5 + 2 * pieces :]
-    nb, sub = parts[0].shape[:2]
-    step = pl.program_id(0)
-    batches = steps * group
-
-    @pl.when(step == 0)
-    def _():
-        copies = [
-            pltpu.make_async_copy(part, dense.at[pl.ds(nb * k, nb)], sems.at[k])
-            for k, part in enumerate(parts)
-        ]
-        for copy in copies:
-            copy.start()
-        acc[...] = jnp.zeros(acc.shape, acc.dtype)
-        for copy in copies:
-            copy.wait()
-
-    def one(side, g):
-        b = side * batches + step * group + g
-        count = counts[b]
+def batch_kernel(group, pieces, split, order, lives, rows, cols, poss, *refs):
+    xs, quads, centre = refs[0:2], refs[2], refs[3]
+    parts = refs[4 : 4 + pieces]
+    outs = refs[4 + pieces : -5]
+    dense, acc, xbuf, sems, xsems = refs[-5:]
+    nb, sub, wide = parts[0].shape
+    spare = nb * pieces
+    batches, _, pts = xbuf.shape
+    half = batches // 2
+
+    def fetch(j, act):
+        b = order[j]
+        for side in (0, 1):
+
+            @pl.when((b >= half) if side else (b < half))
+            def _():
+                act(pltpu.make_async_copy(xs[side].at[b - half * side], xbuf.at[j], xsems.at[j]))
+
+    copies = [
+        pltpu.make_async_copy(part, dense.at[pl.ds(nb * k, nb), :, pl.ds(0, wide)], sems.at[k])
+        for k, part in enumerate(parts)
+    ]
+    for copy in copies:
+        copy.start()
+
+    @pl.loop(0, batches)
+    def _(j):
+        fetch(j, lambda copy: copy.start())
+
+    acc[...] = jnp.zeros(acc.shape, acc.dtype)
+    dense[:, :, wide:] = jnp.zeros((spare + 1, sub, FB), dense.dtype)
+    dense[spare, :, :wide] = jnp.zeros((sub, wide), dense.dtype)
+    for copy in copies:
+        copy.wait()
+
+    def lanes(col):
+        return jnp.concatenate([col] * (pts // FB), axis=1)
+
+    def one(j, live):
+        b = order[j]
+        row = [rows[b * TMAX + s] for s in range(live)]
+        col = [pl.ds(pl.multiple_of(cols[b * TMAX + s] * FB, FB), FB) for s in range(live)]
+        pos = [poss[b * TMAX + s] for s in range(live)]
+        x = xbuf[j, : live * FB, :]
+        quad = quads[b]
+        d = jnp.concatenate(
+            [
+                jnp.concatenate([dense[row[s], :, col[t]] for t in range(live)], axis=1)
+                for s in range(live)
+            ],
+            axis=0,
+        )
+        gval = jnp.dot(d, x, preferred_element_type=jnp.float32)
+        fval = []
+        for s in range(live):
+            dist = None
+            for axis in range(3):
+                diff = lanes(centre[axis, pos[s]]) - quad[axis : axis + 1, :]
+                dist = diff * diff if dist is None else dist + diff * diff
+            dist = dist + lanes(centre[3, pos[s]])
+            fval.append((gval[s * sub : (s + 1) * sub] * lax.rsqrt(dist)).astype(jnp.bfloat16))
+        fval = jnp.concatenate(fval, axis=0)
+        xw = (x.astype(jnp.float32) * quad[3:4, :]).astype(jnp.bfloat16)
+        part = lax.dot_general(
+            fval, xw, (((1,), (1,)), ((), ())), preferred_element_type=jnp.float32
+        )
+        return row, col, part
+
+    @pl.loop(0, batches // group)
+    def _(h):
+        @pl.loop(0, group)
+        def _(u):
+            fetch(h * group + u, lambda copy: copy.wait())
+
         for live in range(2, TMAX + 1):
 
-            @pl.when(count == live)
+            @pl.when(lives[h] == live)
             def _():
-                pos = [blocks[b * TMAX + s] for s in range(live)]
-                row = [kbs[p] for p in pos]
-                col = [pl.ds(pl.multiple_of(p * FB, FB), FB) for p in pos]
-                x = xs[side][g, : live * FB, :]
-                quad = quads[side]
-                xw = (x.astype(jnp.float32) * quad[g, 3:4, :]).astype(jnp.bfloat16)
-                d = jnp.concatenate(
-                    [
-                        jnp.concatenate([dense[row[s], :, col[t]] for t in range(live)], axis=1)
-                        for s in range(live)
-                    ],
-                    axis=0,
-                )
-                gval = jnp.dot(d, x, preferred_element_type=jnp.float32)
-                fval = []
-                for s in range(live):
-                    dist = None
-                    for axis in range(3):
-                        c = centre[axis, pos[s]]
-                        c = jnp.concatenate([c] * (x.shape[1] // FB), axis=1)
-                        diff = c - quad[g, axis : axis + 1, :]
-                        dist = diff * diff if dist is None else dist + diff * diff
-                    c = centre[3, pos[s]]
-                    dist = dist + jnp.concatenate([c] * (x.shape[1] // FB), axis=1)
-                    fval.append((gval[s * sub : (s + 1) * sub] * lax.rsqrt(dist)).astype(jnp.bfloat16))
-                fval = jnp.concatenate(fval, axis=0)
-                part = lax.dot_general(
-                    fval, xw, (((1,), (1,)), ((), ())), preferred_element_type=jnp.float32
-                )
-                for s in range(live):
-                    for t in range(live):
-                        acc[row[s], :, col[t]] += part[s * sub : (s + 1) * sub, t * FB : (t + 1) * FB]
-
-    for side in (0, 1):
-
-        @pl.loop(0, group)
-        def _(g):
-            one(side, g)
-
-    @pl.when(step == steps - 1)
-    def _():
-        for k, out in enumerate(outs):
-            out[...] = acc[nb * k : nb * (k + 1)].astype(out.dtype)
-
-
-def batch_sums(kbs, blocks, counts, xs, quads, centre, parts, local):
-    batches, width, pts = xs[0].shape
-    group = math.gcd(batches, 4)
-    steps = batches // group
+                for row, col, part in [one(h * group + u, live) for u in range(group)]:
+                    for s in range(live):
+                        for t in range(live):
+                            acc[row[s], :, col[t]] += part[s * sub : (s + 1) * sub, t * FB : (t + 1) * FB]
+
+    for k, out in enumerate(outs):
+        size = out.shape[0]
+        out[...] = acc[size * k : size * (k + 1), :, :wide].astype(out.dtype)
+
+
+def batch_sums(order, lives, rows, cols, poss, xs, quads, centre, parts, split):
+    _, width, pts = xs[0].shape
+    batches = order.shape[0]
+    group = batches // lives.shape[0]
     nb, sub, wide = parts[0].shape
     pieces = len(parts)
+    size = 1 if split else nb
     out_shapes = [
-        jax.ShapeDtypeStruct(parts[0].shape, jnp.float32 if k in local else jnp.bfloat16)
+        jax.ShapeDtypeStruct((size, sub, wide), jnp.bfloat16 if k else jnp.float32)
         for k in range(pieces)
+        for _ in range(nb // size)
     ]
-    flops = 2 * batches * 2 * 2 * width * (width // 2) * pts
+    flops = 2 * batches * 2 * width * (width // 2) * pts
     return call(
-        functools.partial(batch_kernel, steps, group, pieces, local),
-        [kbs, blocks, counts],
-        [*xs, *quads, centre, *parts],
-        [pl.BlockSpec((group, width, pts), lambda i, *_: (i, 0, 0))] * 2
-        + [pl.BlockSpec((group, 4, pts), lambda i, *_: (i, 0, 0))] * 2
-        + [whole(centre.shape)]
+        functools.partial(batch_kernel, group, pieces, split),
+        [order, lives, rows, cols, poss],
+        [*xs, quads, centre, *parts],
+        [pl.BlockSpec(memory_space=pl.ANY)] * 2
+        + [whole(quads.shape), whole(centre.shape)]
         + [pl.BlockSpec(memory_space=pl.ANY)] * pieces,
         out_shapes,
-        [whole(parts[0].shape)] * pieces,
+        [whole((size, sub, wide))] * len(out_shapes),
         [
-            pltpu.VMEM((nb * pieces, sub, wide), jnp.bfloat16),
-            pltpu.VMEM((nb * pieces, sub, wide), jnp.float32),
+            pltpu.VMEM((nb * pieces + 1, sub, wide + FB), jnp.bfloat16),
+            pltpu.VMEM((nb * pieces + 1, sub, wide + FB), jnp.float32),
+            pltpu.VMEM((batches, width, pts), jnp.bfloat16),
             pltpu.SemaphoreType.DMA((pieces,)),
+            pltpu.SemaphoreType.DMA((batches,)),
         ],
-        grid=(steps,),
-        cost=(flops, 2 * batches * width * pts * 2),
-    )
+        cost=(flops, 2 * batches * width * pts),
+        vmem=32,
+    )
+
+
+def sort_by_count(counts, group):
+    n = counts.shape[0]
+    ids = jnp.arange(n, dtype=jnp.int32)
+    ahead = (counts[None, :] > counts[:, None]) | (
+        (counts[None, :] == counts[:, None]) & (ids[None, :] < ids[:, None])
+    )
+    rank = jnp.sum(ahead.astype(jnp.int32), axis=1)
+    place = rank[None, :] == ids[:, None]
+    order = jnp.sum(jnp.where(place, ids[None, :], 0), axis=1)
+    lives = jnp.sum(jnp.where(place[::group], counts[None, :], 0), axis=1)
+    return order, lives
 
 
 def per_device(density, owner, touched, blocks, counts, basis, points, weights, centers, widths):
@@ -344,34 +375,52 @@
         return lax.ppermute(x, "rows", [(a, cores - 1 - a) for a in range(cores)])
 
     own = lax.dynamic_index_in_dim(density.reshape(nb, cores, sub, cols), r, 1, keepdims=False)
+    own, touched, basis, points = lax.optimization_barrier((own, touched, basis, points))
     far = swap(own, near)
     near_sets = jnp.concatenate([touched] + [swap(touched, k) for k in range(1, near)], axis=0).reshape(-1)
 
-    quads = jnp.concatenate([points, weights[:, None, :]], axis=1)
-    tables = jnp.concatenate([blocks, counts[:, None]], axis=1)
-    basis_b, quads_b, tables_b = across(basis), across(quads), across(tables)
-    both = jnp.concatenate([tables, tables_b], axis=0)
-    slots = both[:, :TMAX].reshape(-1)
-    live = both[:, TMAX]
+    pts = points.shape[2]
+    table = jnp.concatenate([blocks, counts[:, None]], axis=1).astype(jnp.float32)
+    table = jnp.pad(table, ((0, 0), (0, pts - table.shape[1])))
+    quads = jnp.concatenate([points, weights[:, None, :], table[:, None, :]], axis=1)
+    quads_b = across(quads)
+    basis_b = across(basis)
+    quads = jnp.concatenate([quads, quads_b], axis=0)
+    table = quads[:, 4, : TMAX + 1].astype(jnp.int32)
+    slots, live = table[:, :TMAX], table[:, TMAX]
+    order, lives = sort_by_count(live, math.gcd(live.shape[0], 4))
 
     own_set = touched[0]
     stored = lookup_owner(owner, own_set)
     kbs = jnp.bitwise_xor(stored // nb, i) * nb + stored % nb
+    active = jnp.arange(TMAX, dtype=jnp.int32)[None, :] < live[:, None]
+    hits = slots[:, :, None] == jnp.arange(UMAX, dtype=jnp.int32)
+    kb = jnp.sum(jnp.where(hits, kbs, 0), axis=2)
+    spare = nb * near
+    col = jnp.where(active, slots, UMAX).reshape(-1)
+    rows_near = jnp.where(active & (kb < spare), kb, spare).reshape(-1)
+    rows_far = jnp.where(active & (kb >= spare), kb - spare, spare).reshape(-1)
+    slots = slots.reshape(-1)
+
     shaped = jnp.concatenate([centers, (widths * widths)[None]], axis=0).reshape(4, block_count, cores, sub)
     shaped = lax.dynamic_index_in_dim(shaped, r, 2, keepdims=False)
     centre = jnp.take(shaped, own_set, axis=1)
     centre = jnp.broadcast_to(centre[..., None], (4, UMAX, sub, FB))
 
+    near_sets, own, order = lax.optimization_barrier((near_sets, own, order))
     picked = pick(near_sets, own, near)
     parts = [picked[0]] + [swap(picked[k], k) for k in range(1, near)]
     picked = pick(near_sets, far, near)
-    parts += [picked[0]] + [swap(picked[k], k) for k in range(1, near)]
-
-    sums = batch_sums(kbs, slots, live, (basis, basis_b), (quads, quads_b), centre, parts, (0, near))
-    terms = [sums[near]] + [swap(sums[near + k], k) for k in range(1, near)]
-    far_sum = swap(merge(near_sets, terms, cols), near)
+    far_parts = [picked[0]] + [swap(picked[k], k) for k in range(1, near)]
+    order, picked = lax.optimization_barrier((order, picked))
+
+    common = (slots, (basis, basis_b), quads, centre)
+    sums = batch_sums(order, lives, rows_near, col, *common, parts, False)
+    far_sums = batch_sums(order, lives, rows_far, col, *common, far_parts, True)
     terms = [sums[0]] + [swap(sums[k], k) for k in range(1, near)]
-    keep, give = finish(near_sets, r.reshape(1), terms, far_sum)
+    chunks = [[far_sums[b]] + [swap(far_sums[nb * k + b], k) for k in range(1, near)] for b in range(nb)]
+    far_terms = [swap(merge(near_sets, chunk, cols), near) for chunk in chunks]
+    keep, give = finish(near_sets, r.reshape(1), terms, far_terms)
     got = across(give)
     pair = jnp.where(r == 0, jnp.stack([keep, got], axis=1), jnp.stack([got, keep], axis=1))
     return pair.reshape(nb * FB, cols // cores)

time: 126 us -> 131 us (1.040); the launches traced: 126 us -> 130 us
  waiting for transfers between devices: 57.1 us -> 46 us
  starting transfers between devices: 25.5 us -> 32.7 us
  local copies, waits for them, and re-layouts: 7.92 us -> 12.2 us
  Pallas kernels: 30 us -> 33.2 us
    ppermute x17 -> x21, waiting for transfers between devices: 55.6 us -> 44.4 us  [swap(): return lax.ppermute(x, 'dom', [(a, a ^ k) for a in range(n)])]
    ppermute x17 -> x21, starting transfers between devices: 24.9 us -> 32.1 us  [swap(): return lax.ppermute(x, 'dom', [(a, a ^ k) for a in range(n)])]
    pallas_call x5 -> x7, Pallas kernels: 30 us -> 33.2 us  [call(): pl.pallas_call(kernel, grid_spec=pltpu.PrefetchScalarGridSpec(num_scalar_...]
    unnamed x11 -> x6, local copies, waits for them, and re-layouts: 4.11 us -> 6.79 us
    concatenate x3 -> x2, other arithmetic: 1.53 us -> 0.15 us  [the longest x1 0.08 us: per_device(): quads = jnp.concatenate([quads, quads_b], axis=0)]
  transfers between devices with their start and end apart: 21 -> 24, of which waited for: 12 -> 8; matrix products, arithmetic and copies ran while one was open for 7% -> 8% of each run, Pallas kernels for 3% -> 25%
where the time goes in v2:
time: 131 us; the launch traced here: 130 us
  waiting for transfers between devices  46 us (35%)
  Pallas kernels  33.2 us (25%)
  starting transfers between devices  32.7 us (25%)
  local copies, waits for them, and re-layouts  12.2 us (9%)
  other arithmetic  5.39 us (4%)
    ppermute x21, waiting for transfers between devices, swap(): return lax.ppermute(x, 'dom', [(a, a ^ k) for a in range(n)])  44.4 us
    pallas_call x7, Pallas kernels, call(): pl.pallas_call(kernel, grid_spec=pltpu.PrefetchScalarGridSpec(num_scalar_...  33.2 us
    ppermute x21, starting transfers between devices, swap(): return lax.ppermute(x, 'dom', [(a, a ^ k) for a in range(n)])  32.1 us
    unnamed x6, local copies, waits for them, and re-layouts  6.79 us
  transfers between devices with their start and end apart: 24, of which 8 were waited for; matrix products, arithmetic and copies ran while one was open for 8% of the time, Pallas kernels for 25%

profile of v2, /device:TPU:0, one launch (start us, length us, event | category | flops | bytes accessed | tf_op | source)
XLA Modules:
  0.0 129.8 jit_solution(16506163044803881023)
XLA Ops:
  0.0 1.2 copy-done
  1.8 2.6 %collective-permute-start = (s32[1,8]{1,0:T(1,128)}, s32[1,8]{1,0:T(1,128)S(1)}, u32[]{:S(2)}, u32[]{:S(2)}) collective-permute-start(s32[1,8]{1,0:T(1,128)} %param.12), channel_id=1, source_target_pairs={{0,2},{2,0},{4,6},{6,4},{8,10},{10,8},{12,14},{14,12},{1,3},{3,1},... | collective-permute-start | bytes 104 | tf_op jit(solution)/shard_map/ppermute | solution.py:372
  4.4 1.6 %collective-permute-start.1 = (s32[1,8]{1,0:T(1,128)}, s32[1,8]{1,0:T(1,128)S(1)}, u32[]{:S(2)}, u32[]{:S(2)}) collective-permute-start(s32[1,8]{1,0:T(1,128)} %param.12), channel_id=1, source_target_pairs={{0,4},{2,6},{4,0},{6,2},{8,12},{10,14},{12,8},{14,10},{1,5},{3,7},... | collective-permute-start | bytes 104 | tf_op jit(solution)/shard_map/ppermute | solution.py:372
  13.3 3.0 %collective-permute-start.4 = (bf16[2,64,2048]{2,1,0:T(8,128)(2,1)S(1)}, bf16[2,64,2048]{2,1,0:T(8,128)(2,1)S(1)}, u32[]{:S(2)}, u32[]{:S(2)}) collective-permute-start(bf16[2,64,2048]{2,1,0:T(8,128)(2,1)S(1)} %dynamic-slice_bitcast_fusion.full), channel_id=1, source_target_pairs={{0,8},{2,10},{4,12},{6,14},{8,0},{10,2},{12,4},{14,6},{1,9},{3,11}... | collective-permute-start | bytes 1572872 | tf_op jit(solution)/shard_map/ppermute | solution.py:372
  18.1 22.1 %collective-permute-done.4.full = bf16[2,64,2048]{2,1,0:T(8,128)(2,1)S(1)} collective-permute-done((bf16[2,64,2048]{2,1,0:T(8,128)(2,1)S(1)}, bf16[2,64,2048]{2,1,0:T(8,128)(2,1)S(1)}, u32[]{:S(2)}, u32[]{:S(2)}) %collective-permute-start.4) | collective-permute-done | bytes 524320 | tf_op jit(solution)/shard_map/ppermute | solution.py:372
  40.2 1.6 %shard_map.100 = (bf16[2,64,1024]{2,1,0:T(8,128)(2,1)S(1)}, bf16[2,64,1024]{2,1,0:T(8,128)(2,1)}, bf16[2,64,1024]{2,1,0:T(8,128)(2,1)}, bf16[2,64,1024]{2,1,0:T(8,128)(2,1)S(1)}) custom-call(s32[32]{0:T(128)S(1)} %reshape.77.sets, bf16[2,64,2048]{2,1,0:T(8,128)(2,1)S(1)} %collective-permute-done.4.full), custom_call_target="tpu_custom_call" | custom-call | bytes 1572864 | tf_op jit(solution)/shard_map/pallas_call | solution.py:128
  41.8 1.6 %collective-permute-start.12 = (bf16[2,64,1024]{2,1,0:T(8,128)(2,1)}, bf16[2,64,1024]{2,1,0:T(8,128)(2,1)S(1)}, u32[]{:S(2)}, u32[]{:S(2)}) collective-permute-start(bf16[2,64,1024]{2,1,0:T(8,128)(2,1)} %get-tuple-element.41), channel_id=1, source_target_pairs={{0,2},{2,0},{4,6},{6,4},{8,10},{10,8},{12,14},{14,12},{1,3},{3,1},... | collective-permute-start | bytes 786440 | tf_op jit(solution)/shard_map/ppermute | solution.py:372
  46.8 1.6 %collective-permute-start.6 = (bf16[2,64,1024]{2,1,0:T(8,128)(2,1)S(1)}, bf16[2,64,1024]{2,1,0:T(8,128)(2,1)S(1)}, u32[]{:S(2)}, u32[]{:S(2)}) collective-permute-start(bf16[2,64,1024]{2,1,0:T(8,128)(2,1)S(1)} %get-tuple-element.48), channel_id=1, source_target_pairs={{0,2},{2,0},{4,6},{6,4},{8,10},{10,8},{12,14},{14,12},{1,3},{3,1},... | collective-permute-start | bytes 786440 | tf_op jit(solution)/shard_map/ppermute | solution.py:372
  48.4 4.0 %collective-permute-done.12.refs_5_ = bf16[2,64,1024]{2,1,0:T(8,128)(2,1)S(1)} collective-permute-done((bf16[2,64,1024]{2,1,0:T(8,128)(2,1)}, bf16[2,64,1024]{2,1,0:T(8,128)(2,1)S(1)}, u32[]{:S(2)}, u32[]{:S(2)}) %collective-permute-start.12) | collective-permute-done | bytes 262176 | tf_op jit(solution)/shard_map/ppermute | solution.py:372
  52.9 5.4 %collective-permute-start.8 = (bf16[2,64,1024]{2,1,0:T(8,128)(2,1)S(1)}, bf16[2,64,1024]{2,1,0:T(8,128)(2,1)S(1)}, u32[]{:S(2)}, u32[]{:S(2)}) collective-permute-start(bf16[2,64,1024]{2,1,0:T(8,128)(2,1)S(1)} %get-tuple-element.50), channel_id=1, source_target_pairs={{0,6},{2,4},{4,2},{6,0},{8,14},{10,12},{12,10},{14,8},{1,7},{3,5},... | collective-permute-start | bytes 786440 | tf_op jit(solution)/shard_map/ppermute | solution.py:372
  58.7 2.8 %copy-done.1 = bf16[24,512,256]{2,1,0:T(8,128)(2,1)S(1)} copy-done((bf16[24,512,256]{2,1,0:T(8,128)(2,1)S(1)}, bf16[24,512,256]{2,1,0:T(8,128)(2,1)}, u32[]{:S(2)}) %copy-start.1) | copy-done | bytes 6291480
  61.5 14.0 %shard_map.103 = (f32[1,64,1024]{2,1,0:T(8,128)S(1)}, f32[1,64,1024]{2,1,0:T(8,128)S(1)}, bf16[1,64,1024]{2,1,0:T(8,128)(2,1)S(1)}, bf16[1,64,1024]{2,1,0:T(8,12...) custom-call(s32[48]{0:T(128)S(1)} %select_reduce_fusion.order, ...), custom_call_target="tpu_custom_call" | custom-call | flops 6442450944 | bytes 12582912 | tf_op jit(solution)/shard_map/pallas_call | solution.py:128
  75.4 1.8 %collective-permute-start.19 = (bf16[1,64,1024]{2,1,0:T(8,128)(2,1)S(1)}, bf16[1,64,1024]{2,1,0:T(8,128)(2,1)S(1)}, u32[]{:S(2)}, u32[]{:S(2)}) collective-permute-start(bf16[1,64,1024]{2,1,0:T(8,128)(2,1)S(1)} %get-tuple-element.60), channel_id=1, source_target_pairs={{0,2},{2,0},{4,6},{6,4},{8,10},{10,8},{12,14},{14,12},{1,3},{3,1},... | collective-permute-start | bytes 393224 | tf_op jit(solution)/shard_map/ppermute | solution.py:372
  77.2 1.8 %collective-permute-start.21 = (bf16[1,64,1024]{2,1,0:T(8,128)(2,1)S(1)}, bf16[1,64,1024]{2,1,0:T(8,128)(2,1)S(1)}, u32[]{:S(2)}, u32[]{:S(2)}) collective-permute-start(bf16[1,64,1024]{2,1,0:T(8,128)(2,1)S(1)} %get-tuple-element.62), channel_id=1, source_target_pairs={{0,6},{2,4},{4,2},{6,0},{8,14},{10,12},{12,10},{14,8},{1,7},{3,5},... | collective-permute-start | bytes 393224 | tf_op jit(solution)/shard_map/ppermute | solution.py:372
  79.0 1.7 %collective-permute-start.15 = (bf16[1,64,1024]{2,1,0:T(8,128)(2,1)S(1)}, bf16[1,64,1024]{2,1,0:T(8,128)(2,1)S(1)}, u32[]{:S(2)}, u32[]{:S(2)}) collective-permute-start(bf16[1,64,1024]{2,1,0:T(8,128)(2,1)S(1)} %get-tuple-element.56), channel_id=1, source_target_pairs={{0,2},{2,0},{4,6},{6,4},{8,10},{10,8},{12,14},{14,12},{1,3},{3,1},... | collective-permute-start | bytes 393224 | tf_op jit(solution)/shard_map/ppermute | solution.py:372
  80.7 2.7 %collective-permute-done.19.refs_1_ = bf16[1,64,1024]{2,1,0:T(8,128)(2,1)S(1)} collective-permute-done((bf16[1,64,1024]{2,1,0:T(8,128)(2,1)S(1)}, bf16[1,64,1024]{2,1,0:T(8,128)(2,1)S(1)}, u32[]{:S(2)}, u32[]{:S(2)}) %collective-permute-start.19) | collective-permute-done | bytes 131104 | tf_op jit(solution)/shard_map/ppermute | solution.py:372
  84.4 2.8 %copy-done.2 = bf16[24,512,256]{2,1,0:T(8,128)(2,1)S(1)} copy-done((bf16[24,512,256]{2,1,0:T(8,128)(2,1)S(1)}, bf16[24,512,256]{2,1,0:T(8,128)(2,1)}, u32[]{:S(2)}) %copy-start.2) | copy-done | bytes 6291480
  87.1 13.9 %shard_map.102 = (f32[2,64,1024]{2,1,0:T(8,128)S(1)}, bf16[2,64,1024]{2,1,0:T(8,128)(2,1)S(1)}, bf16[2,64,1024]{2,1,0:T(8,128)(2,1)S(1)}, bf16[2,64,1024]{2,1,0:T(8,128)(2,1)S(1)}) custom-call(s32[48]{0:T(128)S(1)} %select_reduce_fusion.order, s32[12]{0:T(128)S(1)} %select_reduce_fusion.2.lives, s32[192]{0:T(256)S(1)} %get-tuple-element.68.rows, ...), custom_call_target="tpu_custom_call" | custom-call | flops 6442450944 | bytes 12582912 | tf_op jit(solution)/shard_map/pallas_call | solution.py:128
  101.1 1.8 %collective-permute-start.10 = (bf16[2,64,1024]{2,1,0:T(8,128)(2,1)S(1)}, bf16[2,64,1024]{2,1,0:T(8,128)(2,1)S(1)}, u32[]{:S(2)}, u32[]{:S(2)}) collective-permute-start(bf16[2,64,1024]{2,1,0:T(8,128)(2,1)S(1)} %get-tuple-element.53), channel_id=1, source_target_pairs={{0,4},{2,6},{4,0},{6,2},{8,12},{10,14},{12,8},{14,10},{1,5},{3,7},... | collective-permute-start | bytes 786440 | tf_op jit(solution)/shard_map/ppermute | solution.py:372
  104.2 1.4 %collective-permute-start.9 = (bf16[2,64,1024]{2,1,0:T(8,128)(2,1)S(1)}, bf16[2,64,1024]{2,1,0:T(8,128)(2,1)S(1)}, u32[]{:S(2)}, u32[]{:S(2)}) collective-permute-start(bf16[2,64,1024]{2,1,0:T(8,128)(2,1)S(1)} %get-tuple-element.52), channel_id=1, source_target_pairs={{0,2},{2,0},{4,6},{6,4},{8,10},{10,8},{12,14},{14,12},{1,3},{3,1},... | collective-permute-start | bytes 786440 | tf_op jit(solution)/shard_map/ppermute | solution.py:372
  105.6 4.0 %collective-permute-start.22 = (bf16[1,64,2048]{2,1,0:T(8,128)(2,1)S(1)}, bf16[1,64,2048]{2,1,0:T(8,128)(2,1)S(1)}, u32[]{:S(2)}, u32[]{:S(2)}) collective-permute-start(bf16[1,64,2048]{2,1,0:T(8,128)(2,1)S(1)} %shard_map.105), channel_id=1, source_target_pairs={{0,8},{2,10},{4,12},{6,14},{8,0},{10,2},{12,4},{14,6},{1,9},{3,11}... | collective-permute-start | bytes 786440 | tf_op jit(solution)/shard_map/ppermute | solution.py:372
  110.6 6.0 %collective-permute-done.11.refs_3_ = bf16[2,64,1024]{2,1,0:T(8,128)(2,1)S(1)} collective-permute-done((bf16[2,64,1024]{2,1,0:T(8,128)(2,1)S(1)}, bf16[2,64,1024]{2,1,0:T(8,128)(2,1)S(1)}, u32[]{:S(2)}, u32[]{:S(2)}) %collective-permute-start.11) | collective-permute-done | bytes 262176 | tf_op jit(solution)/shard_map/ppermute | solution.py:372
  117.7 8.4 %collective-permute-done.18.refs_4_ = bf16[1,64,2048]{2,1,0:T(8,128)(2,1)S(1)} collective-permute-done((bf16[1,64,2048]{2,1,0:T(8,128)(2,1)S(1)}, bf16[1,64,2048]{2,1,0:T(8,128)(2,1)S(1)}, u32[]{:S(2)}, u32[]{:S(2)}) %collective-permute-start.18) | collective-permute-done | bytes 262176 | tf_op jit(solution)/shard_map/ppermute | solution.py:372
  127.4 1.5 %collective-permute-done.23 = bf16[2,64,1024]{2,1,0:T(8,128)(2,1)S(1)} collective-permute-done((bf16[2,64,1024]{2,1,0:T(8,128)(2,1)S(1)}, bf16[2,64,1024]{2,1,0:T(8,128)(2,1)S(1)}, u32[]{:S(2)}, u32[]{:S(2)}) %collective-permute-start.23) | collective-permute-done | bytes 262176 | tf_op jit(solution)/shard_map/ppermute | solution.py:375
  (82 shorter events, 20.3 us)
Async XLA Ops:
  1.3 57.1 %collective-permute-start.5 = (bf16[24,512,256]{2,1,0:T(8,128)(2,1)}, bf16[24,512,256]{2,1,0:T(8,128)(2,1)}, u32[]{:S(2)}, u32[]{:S(2)}) collective-permute-start(bf16[24,512,256]{2,1,0:T(8,128)(2,1)} %refs_0_.1), channel_id=1, source_target_pairs={{0,1},{1,0},{2,3},{3,2},{4,5},{5,4},{6,7},{7,6},{8,9},{9,8},{10,11... | collective-permute-start | bytes 18874376 | tf_op jit(solution)/shard_map/ppermute | solution.py:375
  1.8 11.5 %collective-permute-start = (s32[1,8]{1,0:T(1,128)}, s32[1,8]{1,0:T(1,128)S(1)}, u32[]{:S(2)}, u32[]{:S(2)}) collective-permute-start(s32[1,8]{1,0:T(1,128)} %param.12), channel_id=1, source_target_pairs={{0,2},{2,0},{4,6},{6,4},{8,10},{10,8},{12,14},{14,12},{1,3},{3,1},... | collective-permute-start | bytes 104 | tf_op jit(solution)/shard_map/ppermute | solution.py:372
  4.4 12.0 %collective-permute-start.1 = (s32[1,8]{1,0:T(1,128)}, s32[1,8]{1,0:T(1,128)S(1)}, u32[]{:S(2)}, u32[]{:S(2)}) collective-permute-start(s32[1,8]{1,0:T(1,128)} %param.12), channel_id=1, source_target_pairs={{0,4},{2,6},{4,0},{6,2},{8,12},{10,14},{12,8},{14,10},{1,5},{3,7},... | collective-permute-start | bytes 104 | tf_op jit(solution)/shard_map/ppermute | solution.py:372
  6.0 10.4 %collective-permute-start.2 = (s32[1,8]{1,0:T(1,128)}, s32[1,8]{1,0:T(1,128)S(1)}, u32[]{:S(2)}, u32[]{:S(2)}) collective-permute-start(s32[1,8]{1,0:T(1,128)} %param.12), channel_id=1, source_target_pairs={{0,6},{2,4},{4,2},{6,0},{8,14},{10,12},{12,10},{14,8},{1,7},{3,5},... | collective-permute-start | bytes 104 | tf_op jit(solution)/shard_map/ppermute | solution.py:372
  8.6 8.6 %collective-permute-start.3 = (f32[24,5,256]{2,1,0:T(8,128)S(1)}, f32[24,5,256]{2,1,0:T(8,128)S(1)}, u32[]{:S(2)}, u32[]{:S(2)}) collective-permute-start(f32[24,5,256]{2,1,0:T(8,128)S(1)} %pad_maximum_fusion.1), channel_id=1, source_target_pairs={{0,1},{1,0},{2,3},{3,2},{4,5},{5,4},{6,7},{7,6},{8,9},{9,8},{10,11... | collective-permute-start | bytes 368648 | tf_op jit(solution)/shard_map/ppermute | solution.py:375
  13.3 26.9 %collective-permute-start.4 = (bf16[2,64,2048]{2,1,0:T(8,128)(2,1)S(1)}, bf16[2,64,2048]{2,1,0:T(8,128)(2,1)S(1)}, u32[]{:S(2)}, u32[]{:S(2)}) collective-permute-start(bf16[2,64,2048]{2,1,0:T(8,128)(2,1)S(1)} %dynamic-slice_bitcast_fusion.full), channel_id=1, source_target_pairs={{0,8},{2,10},{4,12},{6,14},{8,0},{10,2},{12,4},{14,6},{1,9},{3,11}... | collective-permute-start | bytes 1572872 | tf_op jit(solution)/shard_map/ppermute | solution.py:372
  41.8 10.6 %collective-permute-start.12 = (bf16[2,64,1024]{2,1,0:T(8,128)(2,1)}, bf16[2,64,1024]{2,1,0:T(8,128)(2,1)S(1)}, u32[]{:S(2)}, u32[]{:S(2)}) collective-permute-start(bf16[2,64,1024]{2,1,0:T(8,128)(2,1)} %get-tuple-element.41), channel_id=1, source_target_pairs={{0,2},{2,0},{4,6},{6,4},{8,10},{10,8},{12,14},{14,12},{1,3},{3,1},... | collective-permute-start | bytes 786440 | tf_op jit(solution)/shard_map/ppermute | solution.py:372
  43.4 9.5 %collective-permute-start.13 = (bf16[2,64,1024]{2,1,0:T(8,128)(2,1)}, bf16[2,64,1024]{2,1,0:T(8,128)(2,1)S(1)}, u32[]{:S(2)}, u32[]{:S(2)}) collective-permute-start(bf16[2,64,1024]{2,1,0:T(8,128)(2,1)} %get-tuple-element.42), channel_id=1, source_target_pairs={{0,4},{2,6},{4,0},{6,2},{8,12},{10,14},{12,8},{14,10},{1,5},{3,7},... | collective-permute-start | bytes 786440 | tf_op jit(solution)/shard_map/ppermute | solution.py:372
  44.1 14.3 %collective-permute-start.14 = (bf16[2,64,1024]{2,1,0:T(8,128)(2,1)S(1)}, bf16[2,64,1024]{2,1,0:T(8,128)(2,1)S(1)}, u32[]{:S(2)}, u32[]{:S(2)}) collective-permute-start(bf16[2,64,1024]{2,1,0:T(8,128)(2,1)S(1)} %get-tuple-element.43), channel_id=1, source_target_pairs={{0,6},{2,4},{4,2},{6,0},{8,14},{10,12},{12,10},{14,8},{1,7},{3,5},... | collective-permute-start | bytes 786440 | tf_op jit(solution)/shard_map/ppermute | solution.py:372
  46.8 30.5 %collective-permute-start.6 = (bf16[2,64,1024]{2,1,0:T(8,128)(2,1)S(1)}, bf16[2,64,1024]{2,1,0:T(8,128)(2,1)S(1)}, u32[]{:S(2)}, u32[]{:S(2)}) collective-permute-start(bf16[2,64,1024]{2,1,0:T(8,128)(2,1)S(1)} %get-tuple-element.48), channel_id=1, source_target_pairs={{0,2},{2,0},{4,6},{6,4},{8,10},{10,8},{12,14},{14,12},{1,3},{3,1},... | collective-permute-start | bytes 786440 | tf_op jit(solution)/shard_map/ppermute | solution.py:372
  52.4 26.6 %collective-permute-start.7 = (bf16[2,64,1024]{2,1,0:T(8,128)(2,1)S(1)}, bf16[2,64,1024]{2,1,0:T(8,128)(2,1)S(1)}, u32[]{:S(2)}, u32[]{:S(2)}) collective-permute-start(bf16[2,64,1024]{2,1,0:T(8,128)(2,1)S(1)} %get-tuple-element.49), channel_id=1, source_target_pairs={{0,4},{2,6},{4,0},{6,2},{8,12},{10,14},{12,8},{14,10},{1,5},{3,7},... | collective-permute-start | bytes 786440 | tf_op jit(solution)/shard_map/ppermute | solution.py:372
  52.9 27.8 %collective-permute-start.8 = (bf16[2,64,1024]{2,1,0:T(8,128)(2,1)S(1)}, bf16[2,64,1024]{2,1,0:T(8,128)(2,1)S(1)}, u32[]{:S(2)}, u32[]{:S(2)}) collective-permute-start(bf16[2,64,1024]{2,1,0:T(8,128)(2,1)S(1)} %get-tuple-element.50), channel_id=1, source_target_pairs={{0,6},{2,4},{4,2},{6,0},{8,14},{10,12},{12,10},{14,8},{1,7},{3,5},... | collective-permute-start | bytes 786440 | tf_op jit(solution)/shard_map/ppermute | solution.py:372
  75.4 8.0 %collective-permute-start.19 = (bf16[1,64,1024]{2,1,0:T(8,128)(2,1)S(1)}, bf16[1,64,1024]{2,1,0:T(8,128)(2,1)S(1)}, u32[]{:S(2)}, u32[]{:S(2)}) collective-permute-start(bf16[1,64,1024]{2,1,0:T(8,128)(2,1)S(1)} %get-tuple-element.60), channel_id=1, source_target_pairs={{0,2},{2,0},{4,6},{6,4},{8,10},{10,8},{12,14},{14,12},{1,3},{3,1},... | collective-permute-start | bytes 393224 | tf_op jit(solution)/shard_map/ppermute | solution.py:372
  77.2 23.9 %collective-permute-start.20 = (bf16[1,64,1024]{2,1,0:T(8,128)(2,1)S(1)}, bf16[1,64,1024]{2,1,0:T(8,128)(2,1)S(1)}, u32[]{:S(2)}, u32[]{:S(2)}) collective-permute-start(bf16[1,64,1024]{2,1,0:T(8,128)(2,1)S(1)} %get-tuple-element.61), channel_id=1, source_target_pairs={{0,4},{2,6},{4,0},{6,2},{8,12},{10,14},{12,8},{14,10},{1,5},{3,7},... | collective-permute-start | bytes 393224 | tf_op jit(solution)/shard_map/ppermute | solution.py:372
  77.2 25.7 %collective-permute-start.21 = (bf16[1,64,1024]{2,1,0:T(8,128)(2,1)S(1)}, bf16[1,64,1024]{2,1,0:T(8,128)(2,1)S(1)}, u32[]{:S(2)}, u32[]{:S(2)}) collective-permute-start(bf16[1,64,1024]{2,1,0:T(8,128)(2,1)S(1)} %get-tuple-element.62), channel_id=1, source_target_pairs={{0,6},{2,4},{4,2},{6,0},{8,14},{10,12},{12,10},{14,8},{1,7},{3,5},... | collective-permute-start | bytes 393224 | tf_op jit(solution)/shard_map/ppermute | solution.py:372
  79.0 25.2 %collective-permute-start.15 = (bf16[1,64,1024]{2,1,0:T(8,128)(2,1)S(1)}, bf16[1,64,1024]{2,1,0:T(8,128)(2,1)S(1)}, u32[]{:S(2)}, u32[]{:S(2)}) collective-permute-start(bf16[1,64,1024]{2,1,0:T(8,128)(2,1)S(1)} %get-tuple-element.56), channel_id=1, source_target_pairs={{0,2},{2,0},{4,6},{6,4},{8,10},{10,8},{12,14},{14,12},{1,3},{3,1},... | collective-permute-start | bytes 393224 | tf_op jit(solution)/shard_map/ppermute | solution.py:372
  80.7 24.9 %collective-permute-start.16 = (bf16[1,64,1024]{2,1,0:T(8,128)(2,1)S(1)}, bf16[1,64,1024]{2,1,0:T(8,128)(2,1)S(1)}, u32[]{:S(2)}, u32[]{:S(2)}) collective-permute-start(bf16[1,64,1024]{2,1,0:T(8,128)(2,1)S(1)} %get-tuple-element.57), channel_id=1, source_target_pairs={{0,4},{2,6},{4,0},{6,2},{8,12},{10,14},{12,8},{14,10},{1,5},{3,7},... | collective-permute-start | bytes 393224 | tf_op jit(solution)/shard_map/ppermute | solution.py:372
  83.4 26.2 %collective-permute-start.17 = (bf16[1,64,1024]{2,1,0:T(8,128)(2,1)S(1)}, bf16[1,64,1024]{2,1,0:T(8,128)(2,1)S(1)}, u32[]{:S(2)}, u32[]{:S(2)}) collective-permute-start(bf16[1,64,1024]{2,1,0:T(8,128)(2,1)S(1)} %get-tuple-element.58), channel_id=1, source_target_pairs={{0,6},{2,4},{4,2},{6,0},{8,14},{10,12},{12,10},{14,8},{1,7},{3,5},... | collective-permute-start | bytes 393224 | tf_op jit(solution)/shard_map/ppermute | solution.py:372
  101.1 9.5 %collective-permute-start.10 = (bf16[2,64,1024]{2,1,0:T(8,128)(2,1)S(1)}, bf16[2,64,1024]{2,1,0:T(8,128)(2,1)S(1)}, u32[]{:S(2)}, u32[]{:S(2)}) collective-permute-start(bf16[2,64,1024]{2,1,0:T(8,128)(2,1)S(1)} %get-tuple-element.53), channel_id=1, source_target_pairs={{0,4},{2,6},{4,0},{6,2},{8,12},{10,14},{12,8},{14,10},{1,5},{3,7},... | collective-permute-start | bytes 786440 | tf_op jit(solution)/shard_map/ppermute | solution.py:372
  102.9 13.6 %collective-permute-start.11 = (bf16[2,64,1024]{2,1,0:T(8,128)(2,1)S(1)}, bf16[2,64,1024]{2,1,0:T(8,128)(2,1)S(1)}, u32[]{:S(2)}, u32[]{:S(2)}) collective-permute-start(bf16[2,64,1024]{2,1,0:T(8,128)(2,1)S(1)} %get-tuple-element.54), channel_id=1, source_target_pairs={{0,6},{2,4},{4,2},{6,0},{8,14},{10,12},{12,10},{14,8},{1,7},{3,5},... | collective-permute-start | bytes 786440 | tf_op jit(solution)/shard_map/ppermute | solution.py:372
  104.2 12.3 %collective-permute-start.9 = (bf16[2,64,1024]{2,1,0:T(8,128)(2,1)S(1)}, bf16[2,64,1024]{2,1,0:T(8,128)(2,1)S(1)}, u32[]{:S(2)}, u32[]{:S(2)}) collective-permute-start(bf16[2,64,1024]{2,1,0:T(8,128)(2,1)S(1)} %get-tuple-element.52), channel_id=1, source_target_pairs={{0,2},{2,0},{4,6},{6,4},{8,10},{10,8},{12,14},{14,12},{1,3},{3,1},... | collective-permute-start | bytes 786440 | tf_op jit(solution)/shard_map/ppermute | solution.py:372
  105.6 12.1 %collective-permute-start.22 = (bf16[1,64,2048]{2,1,0:T(8,128)(2,1)S(1)}, bf16[1,64,2048]{2,1,0:T(8,128)(2,1)S(1)}, u32[]{:S(2)}, u32[]{:S(2)}) collective-permute-start(bf16[1,64,2048]{2,1,0:T(8,128)(2,1)S(1)} %shard_map.105), channel_id=1, source_target_pairs={{0,8},{2,10},{4,12},{6,14},{8,0},{10,2},{12,4},{14,6},{1,9},{3,11}... | collective-permute-start | bytes 786440 | tf_op jit(solution)/shard_map/ppermute | solution.py:372
  110.5 15.6 %collective-permute-start.18 = (bf16[1,64,2048]{2,1,0:T(8,128)(2,1)S(1)}, bf16[1,64,2048]{2,1,0:T(8,128)(2,1)S(1)}, u32[]{:S(2)}, u32[]{:S(2)}) collective-permute-start(bf16[1,64,2048]{2,1,0:T(8,128)(2,1)S(1)} %shard_map.104), channel_id=1, source_target_pairs={{0,8},{2,10},{4,12},{6,14},{8,0},{10,2},{12,4},{14,6},{1,9},{3,11}... | collective-permute-start | bytes 786440 | tf_op jit(solution)/shard_map/ppermute | solution.py:372
  127.3 1.6 %collective-permute-start.23 = (bf16[2,64,1024]{2,1,0:T(8,128)(2,1)S(1)}, bf16[2,64,1024]{2,1,0:T(8,128)(2,1)S(1)}, u32[]{:S(2)}, u32[]{:S(2)}) collective-permute-start(bf16[2,64,1024]{2,1,0:T(8,128)(2,1)S(1)} %get-tuple-element.64), channel_id=1, source_target_pairs={{0,1},{1,0},{2,3},{3,2},{4,5},{5,4},{6,7},{7,6},{8,9},{9,8},{10,11... | collective-permute-start | bytes 786440 | tf_op jit(solution)/shard_map/ppermute | solution.py:375
  (3 other events, 6.8 us)

commit v3 on v2

--- a/solution.py
+++ b/solution.py
@@ -144,19 +144,21 @@
     return pl.BlockSpec(shape, lambda *_: (0,) * len(shape))
 
 
-def pick_kernel(sets, full, *outs):
-    for k, out in enumerate(outs):
+def pick_kernel(peers, *refs):
+    sets, full, outs = refs[:peers], refs[peers], refs[peers + 1 :]
+    for k in range(peers):
         for q in range(UMAX):
-            block = sets[k * UMAX + q]
-            out[:, :, q * FB : (q + 1) * FB] = full[:, :, pl.ds(pl.multiple_of(block * FB, FB), FB)]
-
-
-def pick(sets, full, peers):
+            cols = pl.ds(pl.multiple_of(sets[k][0, q] * FB, FB), FB)
+            outs[k][:, :, q * FB : (q + 1) * FB] = full[:, :, cols]
+
+
+def pick(sets, full):
     nb, sub, cols = full.shape
     shape = (nb, sub, UMAX * FB)
+    peers = len(sets)
     return call(
-        pick_kernel,
-        [sets],
+        functools.partial(pick_kernel, peers),
+        sets,
         [full],
         [whole(full.shape)],
         [jax.ShapeDtypeStruct(shape, full.dtype)] * peers,
@@ -166,16 +168,107 @@
     )
 
 
+def centre_kernel(own_set, core, centers, widths, out, turned):
+    sub = out.shape[2]
+    for p in range(UMAX):
+        cols = pl.ds(pl.multiple_of(own_set[0, p] * FB, FB), FB)
+        width = widths[:, cols]
+        rows = jnp.concatenate([centers[:, cols], width * width, jnp.zeros((4, FB), jnp.float32)], axis=0)
+        turned[...] = rows.T
+        start = pl.multiple_of(core[0] * sub, sub)
+        for c in range(4):
+            out[c, p] = jnp.broadcast_to(turned[pl.ds(start, sub), c : c + 1], (sub, FB))
+
+
+def centre_rows(own_set, core, centers, widths, sub):
+    shape = (4, UMAX, sub, FB)
+    return call(
+        centre_kernel,
+        [own_set, core],
+        [centers, widths.reshape(1, -1)],
+        [whole(centers.shape), whole((1, widths.shape[0]))],
+        jax.ShapeDtypeStruct(shape, jnp.float32),
+        whole(shape),
+        [pltpu.VMEM((FB, 8), jnp.float32)],
+        cost=(0, 2 * 4 * UMAX * sub * FB * 4),
+    )
+
+
+def table_kernel(nb, near, group, me, owner, own_set, blocks_a, blocks_b, counts_a, counts_b, *refs):
+    order, lives, rows_near, rows_far, cols, slots, kbs, fill = refs
+    half = counts_a.shape[0]
+    spare = nb * near
+    for p in range(UMAX):
+        stored = owner[own_set[0, p]]
+        kbs[p] = (lax.div(stored, nb) ^ me[0]) * nb + lax.rem(stored, nb)
+    for c in range(TMAX + 1):
+        fill[c] = 0
+
+    def each(todo):
+        for side, (blocks, counts) in enumerate(((blocks_a, counts_a), (blocks_b, counts_b))):
+
+            @pl.loop(0, half)
+            def _(b):
+                todo(side, b, blocks, counts[b])
+
+    def tally(side, b, blocks, count):
+        fill[count] = fill[count] + 1
+
+    each(tally)
+    place = 0
+    for c in range(TMAX, -1, -1):
+        many = fill[c]
+        fill[c] = place
+        place = place + many
+
+    def put(side, b, blocks, count):
+        j = fill[count]
+        fill[count] = j + 1
+        order[j] = side * half + b
+
+        @pl.when(lax.rem(j, group) == 0)
+        def _():
+            lives[lax.div(j, group)] = count
+
+        for s in range(TMAX):
+            pos = blocks[b, s]
+            kb = kbs[pos]
+            on = s < count
+            at = j * TMAX + s
+            slots[at] = pos
+            cols[at] = jnp.where(on, pos, UMAX)
+            rows_near[at] = jnp.where(on & (kb < spare), kb, spare)
+            rows_far[at] = jnp.where(on & (kb >= spare), kb - spare, spare)
+
+    each(put)
+
+
+def batch_tables(me, owner, own_set, blocks, counts, nb, near):
+    batches = 2 * counts[0].shape[0]
+    group = math.gcd(batches, 4)
+    sizes = (batches, batches // group) + (batches * TMAX,) * 4
+    return call(
+        functools.partial(table_kernel, nb, near, group),
+        [me, owner, own_set, *blocks, *counts],
+        [],
+        [],
+        [jax.ShapeDtypeStruct((size,), jnp.int32) for size in sizes],
+        [pl.BlockSpec(memory_space=pltpu.SMEM)] * len(sizes),
+        [pltpu.SMEM((UMAX,), jnp.int32), pltpu.SMEM((TMAX + 1,), jnp.int32)],
+        cost=(0, 8 * batches * TMAX),
+    )
+
+
 def add_up(sets, terms, total):
     total[...] = jnp.zeros(total.shape, total.dtype)
     for k, term in enumerate(terms):
         for q in range(UMAX):
-            cols = pl.ds(pl.multiple_of(sets[k * UMAX + q] * FB, FB), FB)
+            cols = pl.ds(pl.multiple_of(sets[k][0, q] * FB, FB), FB)
             total[:, :, cols] += term[:, :, q * FB : (q + 1) * FB].astype(jnp.float32)
 
 
-def merge_kernel(peers, sets, *refs):
-    terms, out, total = refs[:peers], refs[peers], refs[peers + 1]
+def merge_kernel(peers, *refs):
+    sets, terms, out, total = refs[:peers], refs[peers : 2 * peers], refs[-2], refs[-1]
     add_up(sets, terms, total)
     out[...] = total[...].astype(out.dtype)
 
@@ -185,7 +278,7 @@
     shape = (nb, sub, cols)
     return call(
         functools.partial(merge_kernel, len(terms)),
-        [sets],
+        sets,
         terms,
         [whole(t.shape) for t in terms],
         jax.ShapeDtypeStruct(shape, jnp.bfloat16),
@@ -195,8 +288,9 @@
     )
 
 
-def finish_kernel(peers, sets, core, *refs):
-    terms, fars = refs[:peers], refs[peers:-3]
+def finish_kernel(peers, *refs):
+    sets, core = refs[:peers], refs[peers]
+    terms, fars = refs[peers + 1 : 2 * peers + 1], refs[2 * peers + 1 : -3]
     keep, give, total = refs[-3:]
     add_up(sets, terms, total)
     half = keep.shape[2]
@@ -212,7 +306,7 @@
     shape = (nb, sub, cols // 2)
     return call(
         functools.partial(finish_kernel, len(terms)),
-        [sets, core],
+        [*sets, core],
         [*terms, *fars],
         [whole(t.shape) for t in (*terms, *fars)],
         [jax.ShapeDtypeStruct(shape, jnp.bfloat16)] * 2,
@@ -222,11 +316,11 @@
     )
 
 
-def batch_kernel(group, pieces, split, order, lives, rows, cols, poss, *refs):
-    xs, quads, centre = refs[0:2], refs[2], refs[3]
-    parts = refs[4 : 4 + pieces]
-    outs = refs[4 + pieces : -5]
-    dense, acc, xbuf, sems, xsems = refs[-5:]
+def batch_kernel(group, pieces, order, lives, rows, cols, poss, *refs):
+    xs, coords, weights, centre = refs[0:2], refs[2:4], refs[4:6], refs[6]
+    parts = refs[7 : 7 + pieces]
+    outs = refs[7 + pieces : -8]
+    dense, acc, xbuf, pbuf, wbuf, sems, xsems, qsems = refs[-8:]
     nb, sub, wide = parts[0].shape
     spare = nb * pieces
     batches, _, pts = xbuf.shape
@@ -244,6 +338,10 @@
         pltpu.make_async_copy(part, dense.at[pl.ds(nb * k, nb), :, pl.ds(0, wide)], sems.at[k])
         for k, part in enumerate(parts)
     ]
+    for side in (0, 1):
+        rest = pl.ds(half * side, half)
+        copies.append(pltpu.make_async_copy(coords[side], pbuf.at[rest], qsems.at[side]))
+        copies.append(pltpu.make_async_copy(weights[side], wbuf.at[rest], qsems.at[2 + side]))
     for copy in copies:
         copy.start()
 
@@ -262,11 +360,11 @@
 
     def one(j, live):
         b = order[j]
-        row = [rows[b * TMAX + s] for s in range(live)]
-        col = [pl.ds(pl.multiple_of(cols[b * TMAX + s] * FB, FB), FB) for s in range(live)]
-        pos = [poss[b * TMAX + s] for s in range(live)]
+        row = [rows[j * TMAX + s] for s in range(live)]
+        col = [pl.ds(pl.multiple_of(cols[j * TMAX + s] * FB, FB), FB) for s in range(live)]
+        pos = [poss[j * TMAX + s] for s in range(live)]
         x = xbuf[j, : live * FB, :]
-        quad = quads[b]
+        point = pbuf[b]
         d = jnp.concatenate(
             [
                 jnp.concatenate([dense[row[s], :, col[t]] for t in range(live)], axis=1)
@@ -279,12 +377,12 @@
         for s in range(live):
             dist = None
             for axis in range(3):
-                diff = lanes(centre[axis, pos[s]]) - quad[axis : axis + 1, :]
+                diff = lanes(centre[axis, pos[s]]) - point[axis : axis + 1, :]
                 dist = diff * diff if dist is None else dist + diff * diff
             dist = dist + lanes(centre[3, pos[s]])
             fval.append((gval[s * sub : (s + 1) * sub] * lax.rsqrt(dist)).astype(jnp.bfloat16))
         fval = jnp.concatenate(fval, axis=0)
-        xw = (x.astype(jnp.float32) * quad[3:4, :]).astype(jnp.bfloat16)
+        xw = (x.astype(jnp.float32) * wbuf[pl.ds(b, 1), :]).astype(jnp.bfloat16)
         part = lax.dot_general(
             fval, xw, (((1,), (1,)), ((), ())), preferred_element_type=jnp.float32
         )
@@ -310,7 +408,7 @@
         out[...] = acc[size * k : size * (k + 1), :, :wide].astype(out.dtype)
 
 
-def batch_sums(order, lives, rows, cols, poss, xs, quads, centre, parts, split):
+def batch_sums(order, lives, rows, cols, poss, xs, coords, weights, centre, parts, split):
     _, width, pts = xs[0].shape
     batches = order.shape[0]
     group = batches // lives.shape[0]
@@ -324,11 +422,12 @@
     ]
     flops = 2 * batches * 2 * width * (width // 2) * pts
     return call(
-        functools.partial(batch_kernel, group, pieces, split),
+        functools.partial(batch_kernel, group, pieces),
         [order, lives, rows, cols, poss],
-        [*xs, quads, centre, *parts],
-        [pl.BlockSpec(memory_space=pl.ANY)] * 2
-        + [whole(quads.shape), whole(centre.shape)]
+        [*xs, *coords, *weights, centre, *parts],
+        [pl.BlockSpec(memory_space=pltpu.HBM)] * 2
+        + [pl.BlockSpec(memory_space=pl.ANY)] * 4
+        + [whole(centre.shape)]
         + [pl.BlockSpec(memory_space=pl.ANY)] * pieces,
         out_shapes,
         [whole((size, sub, wide))] * len(out_shapes),
@@ -336,25 +435,15 @@
             pltpu.VMEM((nb * pieces + 1, sub, wide + FB), jnp.bfloat16),
             pltpu.VMEM((nb * pieces + 1, sub, wide + FB), jnp.float32),
             pltpu.VMEM((batches, width, pts), jnp.bfloat16),
+            pltpu.VMEM((batches, 3, pts), jnp.float32),
+            pltpu.VMEM((batches, pts), jnp.float32),
             pltpu.SemaphoreType.DMA((pieces,)),
             pltpu.SemaphoreType.DMA((batches,)),
+            pltpu.SemaphoreType.DMA((4,)),
         ],
         cost=(flops, 2 * batches * width * pts),
         vmem=32,
     )
-
-
-def sort_by_count(counts, group):
-    n = counts.shape[0]
-    ids = jnp.arange(n, dtype=jnp.int32)
-    ahead = (counts[None, :] > counts[:, None]) | (
-        (counts[None, :] == counts[:, None]) & (ids[None, :] < ids[:, None])
-    )
-    rank = jnp.sum(ahead.astype(jnp.int32), axis=1)
-    place = rank[None, :] == ids[:, None]
-    order = jnp.sum(jnp.where(place, ids[None, :], 0), axis=1)
-    lives = jnp.sum(jnp.where(place[::group], counts[None, :], 0), axis=1)
-    return order, lives
 
 
 def per_device(density, owner, touched, blocks, counts, basis, points, weights, centers, widths):
@@ -365,8 +454,8 @@
     nb = density.shape[0] // FB
     sub = FB // cores
     cols = density.shape[1]
-    block_count = owner.shape[0]
     near = n // 2
+    core = r.reshape(1)
 
     def swap(x, k):
         return lax.ppermute(x, "dom", [(a, a ^ k) for a in range(n)])
@@ -375,52 +464,27 @@
         return lax.ppermute(x, "rows", [(a, cores - 1 - a) for a in range(cores)])
 
     own = lax.dynamic_index_in_dim(density.reshape(nb, cores, sub, cols), r, 1, keepdims=False)
-    own, touched, basis, points = lax.optimization_barrier((own, touched, basis, points))
     far = swap(own, near)
-    near_sets = jnp.concatenate([touched] + [swap(touched, k) for k in range(1, near)], axis=0).reshape(-1)
-
-    pts = points.shape[2]
-    table = jnp.concatenate([blocks, counts[:, None]], axis=1).astype(jnp.float32)
-    table = jnp.pad(table, ((0, 0), (0, pts - table.shape[1])))
-    quads = jnp.concatenate([points, weights[:, None, :], table[:, None, :]], axis=1)
-    quads_b = across(quads)
-    basis_b = across(basis)
-    quads = jnp.concatenate([quads, quads_b], axis=0)
-    table = quads[:, 4, : TMAX + 1].astype(jnp.int32)
-    slots, live = table[:, :TMAX], table[:, TMAX]
-    order, lives = sort_by_count(live, math.gcd(live.shape[0], 4))
-
-    own_set = touched[0]
-    stored = lookup_owner(owner, own_set)
-    kbs = jnp.bitwise_xor(stored // nb, i) * nb + stored % nb
-    active = jnp.arange(TMAX, dtype=jnp.int32)[None, :] < live[:, None]
-    hits = slots[:, :, None] == jnp.arange(UMAX, dtype=jnp.int32)
-    kb = jnp.sum(jnp.where(hits, kbs, 0), axis=2)
-    spare = nb * near
-    col = jnp.where(active, slots, UMAX).reshape(-1)
-    rows_near = jnp.where(active & (kb < spare), kb, spare).reshape(-1)
-    rows_far = jnp.where(active & (kb >= spare), kb - spare, spare).reshape(-1)
-    slots = slots.reshape(-1)
-
-    shaped = jnp.concatenate([centers, (widths * widths)[None]], axis=0).reshape(4, block_count, cores, sub)
-    shaped = lax.dynamic_index_in_dim(shaped, r, 2, keepdims=False)
-    centre = jnp.take(shaped, own_set, axis=1)
-    centre = jnp.broadcast_to(centre[..., None], (4, UMAX, sub, FB))
-
-    near_sets, own, order = lax.optimization_barrier((near_sets, own, order))
-    picked = pick(near_sets, own, near)
+    sets = [touched] + [swap(touched, k) for k in range(1, near)]
+    both = [(x, across(x)) for x in (basis, points, weights, blocks, counts)]
+    tables = batch_tables(i.reshape(1), owner, touched, both[3], both[4], nb, near)
+    order, lives, rows_near, rows_far, col, slots = tables
+    centre = centre_rows(touched, core, centers, widths, sub)
+
+    picked = pick(sets, own)
     parts = [picked[0]] + [swap(picked[k], k) for k in range(1, near)]
-    picked = pick(near_sets, far, near)
+    picked = pick(sets, far)
     far_parts = [picked[0]] + [swap(picked[k], k) for k in range(1, near)]
-    order, picked = lax.optimization_barrier((order, picked))
-
-    common = (slots, (basis, basis_b), quads, centre)
+    order, _ = lax.optimization_barrier((order, picked[0]))
+
+    common = (slots, *both[:3], centre)
     sums = batch_sums(order, lives, rows_near, col, *common, parts, False)
+    order, _ = lax.optimization_barrier((order, sums[0]))
     far_sums = batch_sums(order, lives, rows_far, col, *common, far_parts, True)
     terms = [sums[0]] + [swap(sums[k], k) for k in range(1, near)]
     chunks = [[far_sums[b]] + [swap(far_sums[nb * k + b], k) for k in range(1, near)] for b in range(nb)]
-    far_terms = [swap(merge(near_sets, chunk, cols), near) for chunk in chunks]
-    keep, give = finish(near_sets, r.reshape(1), terms, far_terms)
+    far_terms = [swap(merge(sets, chunk, cols), near) for chunk in chunks]
+    keep, give = finish(sets, core, terms, far_terms)
     got = across(give)
     pair = jnp.where(r == 0, jnp.stack([keep, got], axis=1), jnp.stack([got, keep], axis=1))
     return pair.reshape(nb * FB, cols // cores)

time: 131 us -> 125 us (0.954)
  waiting for transfers between devices: 46 us -> 34.5 us
  Pallas kernels: 33.2 us -> 39.9 us
  other arithmetic: 5.39 us -> 0.08 us
  local copies, waits for them, and re-layouts: 12.2 us -> 15.1 us
  starting transfers between devices: 32.7 us -> 35 us
    ppermute x21, waiting for transfers between devices: 44.4 us -> 32.9 us  [swap(): return lax.ppermute(x, 'dom', [(a, a ^ k) for a in range(n)])]
    unnamed x6 -> x42, local copies, waits for them, and re-layouts: 6.79 us -> 14.2 us
    pallas_call x7 -> x9, Pallas kernels: 33.2 us -> 39.9 us  [call(): pl.pallas_call(kernel, grid_spec=pltpu.PrefetchScalarGridSpec(num_scalar_...]
    ppermute x21, starting transfers between devices: 32.1 us -> 34 us  [swap(): return lax.ppermute(x, 'dom', [(a, a ^ k) for a in range(n)])]
    reduce_sum x5 -> x0, other arithmetic: 1.35 us -> none  [the longest x1 0.85 us: lookup_owner(): return jnp.sum(jnp.where(match, owner[None, :], 0), axis=1)]
  transfers between devices with their start and end apart: 24 -> 27, of which waited for: 8 -> 10; matrix products, arithmetic and copies ran while one was open for 8% -> 1% of each run, Pallas kernels for 25% -> 19%
where the time goes in v3:
time: 125 us
  Pallas kernels  39.9 us (32%)
  starting transfers between devices  35 us (28%)
  waiting for transfers between devices  34.5 us (28%)
  local copies, waits for them, and re-layouts  15.1 us (12%)
    pallas_call x9, Pallas kernels, call(): pl.pallas_call(kernel, grid_spec=pltpu.PrefetchScalarGridSpec(num_scalar_...  39.9 us
    ppermute x21, starting transfers between devices, swap(): return lax.ppermute(x, 'dom', [(a, a ^ k) for a in range(n)])  34 us
    ppermute x21, waiting for transfers between devices, swap(): return lax.ppermute(x, 'dom', [(a, a ^ k) for a in range(n)])  32.9 us
    unnamed x42, local copies, waits for them, and re-layouts  14.2 us
  transfers between devices with their start and end apart: 27, of which 10 were waited for; matrix products, arithmetic and copies ran while one was open for 1% of the time, Pallas kernels for 19%

profile of v3, /device:TPU:0, one launch (start us, length us, event | category | flops | bytes accessed | tf_op | source)
XLA Modules:
  0.0 124.8 jit_solution(1859439662267945057)
XLA Ops:
  1.3 4.1 %collective-permute-start.5 = (bf16[2,64,2048]{2,1,0:T(8,128)(2,1)S(1)}, bf16[2,64,2048]{2,1,0:T(8,128)(2,1)S(1)}, u32[]{:S(2)}, u32[]{:S(2)}) collective-permute-start(bf16[2,64,2048]{2,1,0:T(8,128)(2,1)S(1)} %dynamic-slice_bitcast_fusion.refs_4_), channel_id=1, source_target_pairs={{0,8},{2,10},{4,12},{6,14},{8,0},{10,2},{12,4},{14,6},{1,9},{3,11}... | collective-permute-start | bytes 1572872 | tf_op jit(solution)/shard_map/ppermute | solution.py:461
  6.9 1.6 %collective-permute-start.1 = (s32[1,8]{1,0:T(1,128)}, s32[1,8]{1,0:T(1,128)S(1)}, u32[]{:S(2)}, u32[]{:S(2)}) collective-permute-start(s32[1,8]{1,0:T(1,128)} %refs_0_.13), channel_id=1, source_target_pairs={{0,4},{2,6},{4,0},{6,2},{8,12},{10,14},{12,8},{14,10},{1,5},{3,7},... | collective-permute-start | bytes 104 | tf_op jit(solution)/shard_map/ppermute | solution.py:461
  9.2 2.3 %collective-permute-start.2 = (s32[1,8]{1,0:T(1,128)}, s32[1,8]{1,0:T(1,128)S(1)}, u32[]{:S(2)}, u32[]{:S(2)}) collective-permute-start(s32[1,8]{1,0:T(1,128)} %refs_0_.13), channel_id=1, source_target_pairs={{0,6},{2,4},{4,2},{6,0},{8,14},{10,12},{12,10},{14,8},{1,7},{3,5},... | collective-permute-start | bytes 104 | tf_op jit(solution)/shard_map/ppermute | solution.py:461
  11.6 5.1 %collective-permute-done.1.refs_2_ = s32[1,8]{1,0:T(1,128)S(1)} collective-permute-done((s32[1,8]{1,0:T(1,128)}, s32[1,8]{1,0:T(1,128)S(1)}, u32[]{:S(2)}, u32[]{:S(2)}) %collective-permute-start.1) | collective-permute-done | bytes 64 | tf_op jit(solution)/shard_map/ppermute | solution.py:461
  17.8 1.6 %shard_map.103 = (bf16[2,64,1024]{2,1,0:T(8,128)(2,1)S(1)}, bf16[2,64,1024]{2,1,0:T(8,128)(2,1)}, bf16[2,64,1024]{2,1,0:T(8,128)(2,1)}, bf16[2,64,1024]{2,1,0:T(8,128)(2,1)S(1)}) custom-call(s32[1,8]{1,0:T(1,128)S(1)} %copy-done.2, s32[1,8]{1,0:T(1,128)S(1)} %collective-permute-done.refs_1_, s32[1,8]{1,0:T(1,128)S(1)} %collective-permute-done.1.refs_2_, ...), custom_call_target="tpu_custom_call" | custom-call | bytes 1572864 | tf_op jit(solution)/shard_map/pallas_call | solution.py:128
  21.0 2.4 %collective-permute-start.10 = (bf16[2,64,1024]{2,1,0:T(8,128)(2,1)}, bf16[2,64,1024]{2,1,0:T(8,128)(2,1)S(1)}, u32[]{:S(2)}, u32[]{:S(2)}) collective-permute-start(bf16[2,64,1024]{2,1,0:T(8,128)(2,1)} %get-tuple-element.44), channel_id=1, source_target_pairs={{0,4},{2,6},{4,0},{6,2},{8,12},{10,14},{12,8},{14,10},{1,5},{3,7},... | collective-permute-start | bytes 786440 | tf_op jit(solution)/shard_map/ppermute | solution.py:461
  25.3 3.3 %collective-permute-done.5.refs_4_ = bf16[2,64,2048]{2,1,0:T(8,128)(2,1)S(1)} collective-permute-done((bf16[2,64,2048]{2,1,0:T(8,128)(2,1)S(1)}, bf16[2,64,2048]{2,1,0:T(8,128)(2,1)S(1)}, u32[]{:S(2)}, u32[]{:S(2)}) %collective-permute-start.5) | collective-permute-done | bytes 524320 | tf_op jit(solution)/shard_map/ppermute | solution.py:461
  34.0 3.5 %shard_map.100 = (s32[48]{0:T(128)S(1)}, s32[12]{0:T(128)S(1)}, s32[192]{0:T(256)S(1)}, s32[192]{0:T(256)S(1)}, s32[192]{0:T(256)S(1)}, /*index=5*/s32[192]{0:T(256)S(1)}) custom-call(s32[1]{0:T(128)} %bitcast.1.me, s32[16]{0:T(128)S(1)} %copy-done.8, s32[1,8]{1,0:T(1,128)S(1)} %copy-done.4, s32[24,4]{1,0:T(8,128)S(1)} %copy.18.blocks_a, ...), custom_call_target="tpu_custom_call" | custom-call | bytes 1536 | tf_op jit(solution)/shard_map/pallas_call | solution.py:128
  39.6 1.6 %collective-permute-start.15 = (bf16[2,64,1024]{2,1,0:T(8,128)(2,1)S(1)}, bf16[2,64,1024]{2,1,0:T(8,128)(2,1)S(1)}, u32[]{:S(2)}, u32[]{:S(2)}) collective-permute-start(bf16[2,64,1024]{2,1,0:T(8,128)(2,1)S(1)} %get-tuple-element.52), channel_id=1, source_target_pairs={{0,2},{2,0},{4,6},{6,4},{8,10},{10,8},{12,14},{14,12},{1,3},{3,1},... | collective-permute-start | bytes 786440 | tf_op jit(solution)/shard_map/ppermute | solution.py:461
  43.1 2.8 %copy-done.10 = bf16[24,512,256]{2,1,0:T(8,128)(2,1)S(1)} copy-done((bf16[24,512,256]{2,1,0:T(8,128)(2,1)S(1)}, bf16[24,512,256]{2,1,0:T(8,128)(2,1)}, u32[]{:S(2)}) %copy-start.10) | copy-done | bytes 6291480
  48.3 14.9 %shard_map.104 = (f32[2,64,1024]{2,1,0:T(8,128)S(1)}, bf16[2,64,1024]{2,1,0:T(8,128)(2,1)S(1)}, bf16[2,64,1024]{2,1,0:T(8,128)(2,1)S(1)}, bf16[2,64,1024]{2,1,0:T(8,128)(2,1)S(1)}) custom-call(s32[48]{0:T(128)S(1)} %get-tuple-element.50.order, s32[12]{0:T(128)S(1)} %get-tuple-element.38.lives, s32[192]{0:T(256)S(1)} %get-tuple-element.39.rows, ...), custom_call_target="tpu_custom_call" | custom-call | flops 6442450944 | bytes 12582912 | tf_op jit(solution)/shard_map/pallas_call | solution.py:128
  63.2 14.9 %shard_map.105 = (f32[1,64,1024]{2,1,0:T(8,128)S(1)}, f32[1,64,1024]{2,1,0:T(8,128)S(1)}, bf16[1,64,1024]{2,1,0:T(8,128)(2,1)S(1)}, bf16[1,64,1024]{2,1,0:T(8,12...) custom-call(s32[48]{0:T(128)S(1)} %get-tuple-element.50.order, ...), custom_call_target="tpu_custom_call" | custom-call | flops 6442450944 | bytes 12582912 | tf_op jit(solution)/shard_map/pallas_call | solution.py:128
  78.1 2.6 %collective-permute-start.18 = (bf16[1,64,1024]{2,1,0:T(8,128)(2,1)S(1)}, bf16[1,64,1024]{2,1,0:T(8,128)(2,1)S(1)}, u32[]{:S(2)}, u32[]{:S(2)}) collective-permute-start(bf16[1,64,1024]{2,1,0:T(8,128)(2,1)S(1)} %get-tuple-element.56), channel_id=1, source_target_pairs={{0,2},{2,0},{4,6},{6,4},{8,10},{10,8},{12,14},{14,12},{1,3},{3,1},... | collective-permute-start | bytes 393224 | tf_op jit(solution)/shard_map/ppermute | solution.py:461
  80.8 1.5 %collective-permute-start.20 = (bf16[1,64,1024]{2,1,0:T(8,128)(2,1)S(1)}, bf16[1,64,1024]{2,1,0:T(8,128)(2,1)S(1)}, u32[]{:S(2)}, u32[]{:S(2)}) collective-permute-start(bf16[1,64,1024]{2,1,0:T(8,128)(2,1)S(1)} %get-tuple-element.58), channel_id=1, source_target_pairs={{0,6},{2,4},{4,2},{6,0},{8,14},{10,12},{12,10},{14,8},{1,7},{3,5},... | collective-permute-start | bytes 393224 | tf_op jit(solution)/shard_map/ppermute | solution.py:461
  82.3 1.9 %collective-permute-start.22 = (bf16[1,64,1024]{2,1,0:T(8,128)(2,1)S(1)}, bf16[1,64,1024]{2,1,0:T(8,128)(2,1)S(1)}, u32[]{:S(2)}, u32[]{:S(2)}) collective-permute-start(bf16[1,64,1024]{2,1,0:T(8,128)(2,1)S(1)} %get-tuple-element.60), channel_id=1, source_target_pairs={{0,2},{2,0},{4,6},{6,4},{8,10},{10,8},{12,14},{14,12},{1,3},{3,1},... | collective-permute-start | bytes 393224 | tf_op jit(solution)/shard_map/ppermute | solution.py:461
  84.3 1.5 %collective-permute-start.24 = (bf16[1,64,1024]{2,1,0:T(8,128)(2,1)S(1)}, bf16[1,64,1024]{2,1,0:T(8,128)(2,1)S(1)}, u32[]{:S(2)}, u32[]{:S(2)}) collective-permute-start(bf16[1,64,1024]{2,1,0:T(8,128)(2,1)S(1)} %get-tuple-element.62), channel_id=1, source_target_pairs={{0,6},{2,4},{4,2},{6,0},{8,14},{10,12},{12,10},{14,8},{1,7},{3,5},... | collective-permute-start | bytes 393224 | tf_op jit(solution)/shard_map/ppermute | solution.py:461
  87.8 1.7 %collective-permute-done.20.refs_7_ = bf16[1,64,1024]{2,1,0:T(8,128)(2,1)S(1)} collective-permute-done((bf16[1,64,1024]{2,1,0:T(8,128)(2,1)S(1)}, bf16[1,64,1024]{2,1,0:T(8,128)(2,1)S(1)}, u32[]{:S(2)}, u32[]{:S(2)}) %collective-permute-start.20) | collective-permute-done | bytes 131104 | tf_op jit(solution)/shard_map/ppermute | solution.py:461
  91.6 2.3 %collective-permute-start.14 = (bf16[2,64,1024]{2,1,0:T(8,128)(2,1)S(1)}, bf16[2,64,1024]{2,1,0:T(8,128)(2,1)S(1)}, u32[]{:S(2)}, u32[]{:S(2)}) collective-permute-start(bf16[2,64,1024]{2,1,0:T(8,128)(2,1)S(1)} %get-tuple-element.49), channel_id=1, source_target_pairs={{0,6},{2,4},{4,2},{6,0},{8,14},{10,12},{12,10},{14,8},{1,7},{3,5},... | collective-permute-start | bytes 786440 | tf_op jit(solution)/shard_map/ppermute | solution.py:461
  93.9 3.2 %collective-permute-start.21 = (bf16[1,64,2048]{2,1,0:T(8,128)(2,1)S(1)}, bf16[1,64,2048]{2,1,0:T(8,128)(2,1)S(1)}, u32[]{:S(2)}, u32[]{:S(2)}) collective-permute-start(bf16[1,64,2048]{2,1,0:T(8,128)(2,1)S(1)} %shard_map.106), channel_id=1, source_target_pairs={{0,8},{2,10},{4,12},{6,14},{8,0},{10,2},{12,4},{14,6},{1,9},{3,11}... | collective-permute-start | bytes 786440 | tf_op jit(solution)/shard_map/ppermute | solution.py:461
  97.1 6.4 %collective-permute-done.24.refs_7_ = bf16[1,64,1024]{2,1,0:T(8,128)(2,1)S(1)} collective-permute-done((bf16[1,64,1024]{2,1,0:T(8,128)(2,1)S(1)}, bf16[1,64,1024]{2,1,0:T(8,128)(2,1)S(1)}, u32[]{:S(2)}, u32[]{:S(2)}) %collective-permute-start.24) | collective-permute-done | bytes 131104 | tf_op jit(solution)/shard_map/ppermute | solution.py:461
  104.4 2.2 %collective-permute-start.25 = (bf16[1,64,2048]{2,1,0:T(8,128)(2,1)S(1)}, bf16[1,64,2048]{2,1,0:T(8,128)(2,1)S(1)}, u32[]{:S(2)}, u32[]{:S(2)}) collective-permute-start(bf16[1,64,2048]{2,1,0:T(8,128)(2,1)S(1)} %shard_map.107), channel_id=1, source_target_pairs={{0,8},{2,10},{4,12},{6,14},{8,0},{10,2},{12,4},{14,6},{1,9},{3,11}... | collective-permute-start | bytes 786440 | tf_op jit(solution)/shard_map/ppermute | solution.py:461
  106.6 3.1 %collective-permute-done.13.refs_7_ = bf16[2,64,1024]{2,1,0:T(8,128)(2,1)S(1)} collective-permute-done((bf16[2,64,1024]{2,1,0:T(8,128)(2,1)S(1)}, bf16[2,64,1024]{2,1,0:T(8,128)(2,1)S(1)}, u32[]{:S(2)}, u32[]{:S(2)}) %collective-permute-start.13) | collective-permute-done | bytes 262176 | tf_op jit(solution)/shard_map/ppermute | solution.py:461
  109.8 3.8 %collective-permute-done.14.refs_8_ = bf16[2,64,1024]{2,1,0:T(8,128)(2,1)S(1)} collective-permute-done((bf16[2,64,1024]{2,1,0:T(8,128)(2,1)S(1)}, bf16[2,64,1024]{2,1,0:T(8,128)(2,1)S(1)}, u32[]{:S(2)}, u32[]{:S(2)}) %collective-permute-start.14) | collective-permute-done | bytes 262176 | tf_op jit(solution)/shard_map/ppermute | solution.py:461
  113.6 7.5 %collective-permute-done.25.refs_10_ = bf16[1,64,2048]{2,1,0:T(8,128)(2,1)S(1)} collective-permute-done((bf16[1,64,2048]{2,1,0:T(8,128)(2,1)S(1)}, bf16[1,64,2048]{2,1,0:T(8,128)(2,1)S(1)}, u32[]{:S(2)}, u32[]{:S(2)}) %collective-permute-start.25) | collective-permute-done | bytes 262176 | tf_op jit(solution)/shard_map/ppermute | solution.py:461
  (84 shorter events, 28.6 us)
Async XLA Ops:
  0.0 43.1 %collective-permute-start.6 = (bf16[24,512,256]{2,1,0:T(8,128)(2,1)}, bf16[24,512,256]{2,1,0:T(8,128)(2,1)}, u32[]{:S(2)}, u32[]{:S(2)}) collective-permute-start(bf16[24,512,256]{2,1,0:T(8,128)(2,1)} %refs_0_.10), channel_id=1, source_target_pairs={{0,1},{1,0},{2,3},{3,2},{4,5},{5,4},{6,7},{7,6},{8,9},{9,8},{10,11... | collective-permute-start | bytes 18874376 | tf_op jit(solution)/shard_map/ppermute | solution.py:464
  1.3 27.4 %collective-permute-start.5 = (bf16[2,64,2048]{2,1,0:T(8,128)(2,1)S(1)}, bf16[2,64,2048]{2,1,0:T(8,128)(2,1)S(1)}, u32[]{:S(2)}, u32[]{:S(2)}) collective-permute-start(bf16[2,64,2048]{2,1,0:T(8,128)(2,1)S(1)} %dynamic-slice_bitcast_fusion.refs_4_), channel_id=1, source_target_pairs={{0,8},{2,10},{4,12},{6,14},{8,0},{10,2},{12,4},{14,6},{1,9},{3,11}... | collective-permute-start | bytes 1572872 | tf_op jit(solution)/shard_map/ppermute | solution.py:461
  5.4 18.0 %collective-permute-start.8 = (f32[24,256]{1,0:T(8,128)}, f32[24,256]{1,0:T(8,128)S(1)}, u32[]{:S(2)}, u32[]{:S(2)}) collective-permute-start(f32[24,256]{1,0:T(8,128)} %refs_4_.3), channel_id=1, source_target_pairs={{0,1},{1,0},{2,3},{3,2},{4,5},{5,4},{6,7},{7,6},{8,9},{9,8},{10,11... | collective-permute-start | bytes 73736 | tf_op jit(solution)/shard_map/ppermute | solution.py:464
  6.9 9.8 %collective-permute-start.1 = (s32[1,8]{1,0:T(1,128)}, s32[1,8]{1,0:T(1,128)S(1)}, u32[]{:S(2)}, u32[]{:S(2)}) collective-permute-start(s32[1,8]{1,0:T(1,128)} %refs_0_.13), channel_id=1, source_target_pairs={{0,4},{2,6},{4,0},{6,2},{8,12},{10,14},{12,8},{14,10},{1,5},{3,7},... | collective-permute-start | bytes 104 | tf_op jit(solution)/shard_map/ppermute | solution.py:461
  9.2 7.4 %collective-permute-start.2 = (s32[1,8]{1,0:T(1,128)}, s32[1,8]{1,0:T(1,128)S(1)}, u32[]{:S(2)}, u32[]{:S(2)}) collective-permute-start(s32[1,8]{1,0:T(1,128)} %refs_0_.13), channel_id=1, source_target_pairs={{0,6},{2,4},{4,2},{6,0},{8,14},{10,12},{12,10},{14,8},{1,7},{3,5},... | collective-permute-start | bytes 104 | tf_op jit(solution)/shard_map/ppermute | solution.py:461
  16.6 4.3 %collective-permute-start.3 = (s32[24,4]{1,0:T(8,128)S(1)}, s32[24,4]{1,0:T(8,128)S(1)}, u32[]{:S(2)}, u32[]{:S(2)}) collective-permute-start(s32[24,4]{1,0:T(8,128)S(1)} %copy.18.blocks_a), channel_id=1, source_target_pairs={{0,1},{1,0},{2,3},{3,2},{4,5},{5,4},{6,7},{7,6},{8,9},{9,8},{10,11... | collective-permute-start | bytes 1160 | tf_op jit(solution)/shard_map/ppermute | solution.py:464
  19.5 21.7 %collective-permute-start.9 = (bf16[2,64,1024]{2,1,0:T(8,128)(2,1)}, bf16[2,64,1024]{2,1,0:T(8,128)(2,1)S(1)}, u32[]{:S(2)}, u32[]{:S(2)}) collective-permute-start(bf16[2,64,1024]{2,1,0:T(8,128)(2,1)} %get-tuple-element.43), channel_id=1, source_target_pairs={{0,2},{2,0},{4,6},{6,4},{8,10},{10,8},{12,14},{14,12},{1,3},{3,1},... | collective-permute-start | bytes 786440 | tf_op jit(solution)/shard_map/ppermute | solution.py:461
  21.0 20.8 %collective-permute-start.10 = (bf16[2,64,1024]{2,1,0:T(8,128)(2,1)}, bf16[2,64,1024]{2,1,0:T(8,128)(2,1)S(1)}, u32[]{:S(2)}, u32[]{:S(2)}) collective-permute-start(bf16[2,64,1024]{2,1,0:T(8,128)(2,1)} %get-tuple-element.44), channel_id=1, source_target_pairs={{0,4},{2,6},{4,0},{6,2},{8,12},{10,14},{12,8},{14,10},{1,5},{3,7},... | collective-permute-start | bytes 786440 | tf_op jit(solution)/shard_map/ppermute | solution.py:461
  24.0 19.1 %collective-permute-start.11 = (bf16[2,64,1024]{2,1,0:T(8,128)(2,1)S(1)}, bf16[2,64,1024]{2,1,0:T(8,128)(2,1)S(1)}, u32[]{:S(2)}, u32[]{:S(2)}) collective-permute-start(bf16[2,64,1024]{2,1,0:T(8,128)(2,1)S(1)} %get-tuple-element.45), channel_id=1, source_target_pairs={{0,6},{2,4},{4,2},{6,0},{8,14},{10,12},{12,10},{14,8},{1,7},{3,5},... | collective-permute-start | bytes 786440 | tf_op jit(solution)/shard_map/ppermute | solution.py:461
  28.6 10.3 %collective-permute-start.7 = (f32[24,3,256]{2,1,0:T(4,128)S(1)}, f32[24,3,256]{2,1,0:T(4,128)S(1)}, u32[]{:S(2)}, u32[]{:S(2)}) collective-permute-start(f32[24,3,256]{2,1,0:T(4,128)S(1)} %copy.21.refs_2_), channel_id=1, source_target_pairs={{0,1},{1,0},{2,3},{3,2},{4,5},{5,4},{6,7},{7,6},{8,9},{9,8},{10,11... | collective-permute-start | bytes 221192 | tf_op jit(solution)/shard_map/ppermute | solution.py:464
  39.6 23.5 %collective-permute-start.15 = (bf16[2,64,1024]{2,1,0:T(8,128)(2,1)S(1)}, bf16[2,64,1024]{2,1,0:T(8,128)(2,1)S(1)}, u32[]{:S(2)}, u32[]{:S(2)}) collective-permute-start(bf16[2,64,1024]{2,1,0:T(8,128)(2,1)S(1)} %get-tuple-element.52), channel_id=1, source_target_pairs={{0,2},{2,0},{4,6},{6,4},{8,10},{10,8},{12,14},{14,12},{1,3},{3,1},... | collective-permute-start | bytes 786440 | tf_op jit(solution)/shard_map/ppermute | solution.py:461
  41.2 22.0 %collective-permute-start.16 = (bf16[2,64,1024]{2,1,0:T(8,128)(2,1)S(1)}, bf16[2,64,1024]{2,1,0:T(8,128)(2,1)S(1)}, u32[]{:S(2)}, u32[]{:S(2)}) collective-permute-start(bf16[2,64,1024]{2,1,0:T(8,128)(2,1)S(1)} %get-tuple-element.53), channel_id=1, source_target_pairs={{0,4},{2,6},{4,0},{6,2},{8,12},{10,14},{12,8},{14,10},{1,5},{3,7},... | collective-permute-start | bytes 786440 | tf_op jit(solution)/shard_map/ppermute | solution.py:461
  41.8 21.4 %collective-permute-start.17 = (bf16[2,64,1024]{2,1,0:T(8,128)(2,1)S(1)}, bf16[2,64,1024]{2,1,0:T(8,128)(2,1)S(1)}, u32[]{:S(2)}, u32[]{:S(2)}) collective-permute-start(bf16[2,64,1024]{2,1,0:T(8,128)(2,1)S(1)} %get-tuple-element.54), channel_id=1, source_target_pairs={{0,6},{2,4},{4,2},{6,0},{8,14},{10,12},{12,10},{14,8},{1,7},{3,5},... | collective-permute-start | bytes 786440 | tf_op jit(solution)/shard_map/ppermute | solution.py:461
  78.1 6.1 %collective-permute-start.18 = (bf16[1,64,1024]{2,1,0:T(8,128)(2,1)S(1)}, bf16[1,64,1024]{2,1,0:T(8,128)(2,1)S(1)}, u32[]{:S(2)}, u32[]{:S(2)}) collective-permute-start(bf16[1,64,1024]{2,1,0:T(8,128)(2,1)S(1)} %get-tuple-element.56), channel_id=1, source_target_pairs={{0,2},{2,0},{4,6},{6,4},{8,10},{10,8},{12,14},{14,12},{1,3},{3,1},... | collective-permute-start | bytes 393224 | tf_op jit(solution)/shard_map/ppermute | solution.py:461
  80.8 6.4 %collective-permute-start.19 = (bf16[1,64,1024]{2,1,0:T(8,128)(2,1)S(1)}, bf16[1,64,1024]{2,1,0:T(8,128)(2,1)S(1)}, u32[]{:S(2)}, u32[]{:S(2)}) collective-permute-start(bf16[1,64,1024]{2,1,0:T(8,128)(2,1)S(1)} %get-tuple-element.57), channel_id=1, source_target_pairs={{0,4},{2,6},{4,0},{6,2},{8,12},{10,14},{12,8},{14,10},{1,5},{3,7},... | collective-permute-start | bytes 393224 | tf_op jit(solution)/shard_map/ppermute | solution.py:461
  80.8 8.7 %collective-permute-start.20 = (bf16[1,64,1024]{2,1,0:T(8,128)(2,1)S(1)}, bf16[1,64,1024]{2,1,0:T(8,128)(2,1)S(1)}, u32[]{:S(2)}, u32[]{:S(2)}) collective-permute-start(bf16[1,64,1024]{2,1,0:T(8,128)(2,1)S(1)} %get-tuple-element.58), channel_id=1, source_target_pairs={{0,6},{2,4},{4,2},{6,0},{8,14},{10,12},{12,10},{14,8},{1,7},{3,5},... | collective-permute-start | bytes 393224 | tf_op jit(solution)/shard_map/ppermute | solution.py:461
  82.3 9.3 %collective-permute-start.22 = (bf16[1,64,1024]{2,1,0:T(8,128)(2,1)S(1)}, bf16[1,64,1024]{2,1,0:T(8,128)(2,1)S(1)}, u32[]{:S(2)}, u32[]{:S(2)}) collective-permute-start(bf16[1,64,1024]{2,1,0:T(8,128)(2,1)S(1)} %get-tuple-element.60), channel_id=1, source_target_pairs={{0,2},{2,0},{4,6},{6,4},{8,10},{10,8},{12,14},{14,12},{1,3},{3,1},... | collective-permute-start | bytes 393224 | tf_op jit(solution)/shard_map/ppermute | solution.py:461
  84.3 9.7 %collective-permute-start.23 = (bf16[1,64,1024]{2,1,0:T(8,128)(2,1)S(1)}, bf16[1,64,1024]{2,1,0:T(8,128)(2,1)S(1)}, u32[]{:S(2)}, u32[]{:S(2)}) collective-permute-start(bf16[1,64,1024]{2,1,0:T(8,128)(2,1)S(1)} %get-tuple-element.61), channel_id=1, source_target_pairs={{0,4},{2,6},{4,0},{6,2},{8,12},{10,14},{12,8},{14,10},{1,5},{3,7},... | collective-permute-start | bytes 393224 | tf_op jit(solution)/shard_map/ppermute | solution.py:461
  84.3 19.3 %collective-permute-start.24 = (bf16[1,64,1024]{2,1,0:T(8,128)(2,1)S(1)}, bf16[1,64,1024]{2,1,0:T(8,128)(2,1)S(1)}, u32[]{:S(2)}, u32[]{:S(2)}) collective-permute-start(bf16[1,64,1024]{2,1,0:T(8,128)(2,1)S(1)} %get-tuple-element.62), channel_id=1, source_target_pairs={{0,6},{2,4},{4,2},{6,0},{8,14},{10,12},{12,10},{14,8},{1,7},{3,5},... | collective-permute-start | bytes 393224 | tf_op jit(solution)/shard_map/ppermute | solution.py:461
  87.2 19.4 %collective-permute-start.12 = (bf16[2,64,1024]{2,1,0:T(8,128)(2,1)S(1)}, bf16[2,64,1024]{2,1,0:T(8,128)(2,1)S(1)}, u32[]{:S(2)}, u32[]{:S(2)}) collective-permute-start(bf16[2,64,1024]{2,1,0:T(8,128)(2,1)S(1)} %get-tuple-element.47), channel_id=1, source_target_pairs={{0,2},{2,0},{4,6},{6,4},{8,10},{10,8},{12,14},{14,12},{1,3},{3,1},... | collective-permute-start | bytes 786440 | tf_op jit(solution)/shard_map/ppermute | solution.py:461
  89.5 20.3 %collective-permute-start.13 = (bf16[2,64,1024]{2,1,0:T(8,128)(2,1)S(1)}, bf16[2,64,1024]{2,1,0:T(8,128)(2,1)S(1)}, u32[]{:S(2)}, u32[]{:S(2)}) collective-permute-start(bf16[2,64,1024]{2,1,0:T(8,128)(2,1)S(1)} %get-tuple-element.48), channel_id=1, source_target_pairs={{0,4},{2,6},{4,0},{6,2},{8,12},{10,14},{12,8},{14,10},{1,5},{3,7},... | collective-permute-start | bytes 786440 | tf_op jit(solution)/shard_map/ppermute | solution.py:461
  91.6 22.0 %collective-permute-start.14 = (bf16[2,64,1024]{2,1,0:T(8,128)(2,1)S(1)}, bf16[2,64,1024]{2,1,0:T(8,128)(2,1)S(1)}, u32[]{:S(2)}, u32[]{:S(2)}) collective-permute-start(bf16[2,64,1024]{2,1,0:T(8,128)(2,1)S(1)} %get-tuple-element.49), channel_id=1, source_target_pairs={{0,6},{2,4},{4,2},{6,0},{8,14},{10,12},{12,10},{14,8},{1,7},{3,5},... | collective-permute-start | bytes 786440 | tf_op jit(solution)/shard_map/ppermute | solution.py:461
  93.9 19.7 %collective-permute-start.21 = (bf16[1,64,2048]{2,1,0:T(8,128)(2,1)S(1)}, bf16[1,64,2048]{2,1,0:T(8,128)(2,1)S(1)}, u32[]{:S(2)}, u32[]{:S(2)}) collective-permute-start(bf16[1,64,2048]{2,1,0:T(8,128)(2,1)S(1)} %shard_map.106), channel_id=1, source_target_pairs={{0,8},{2,10},{4,12},{6,14},{8,0},{10,2},{12,4},{14,6},{1,9},{3,11}... | collective-permute-start | bytes 786440 | tf_op jit(solution)/shard_map/ppermute | solution.py:461
  104.4 16.6 %collective-permute-start.25 = (bf16[1,64,2048]{2,1,0:T(8,128)(2,1)S(1)}, bf16[1,64,2048]{2,1,0:T(8,128)(2,1)S(1)}, u32[]{:S(2)}, u32[]{:S(2)}) collective-permute-start(bf16[1,64,2048]{2,1,0:T(8,128)(2,1)S(1)} %shard_map.107), channel_id=1, source_target_pairs={{0,8},{2,10},{4,12},{6,14},{8,0},{10,2},{12,4},{14,6},{1,9},{3,11}... | collective-permute-start | bytes 786440 | tf_op jit(solution)/shard_map/ppermute | solution.py:461
  (23 other events, 107.9 us)

commit v4 on v3

--- a/solution.py
+++ b/solution.py
@@ -124,7 +124,7 @@
     return summed.astype(jnp.bfloat16)
 
 
-def call(kernel, scalars, arrays, in_specs, out_shapes, out_specs, scratch, grid=(1,), cost=None, vmem=12):
+def call(kernel, scalars, arrays, in_specs, out_shapes, out_specs, scratch, grid=(1,), cost=None, vmem=44):
     return pl.pallas_call(
         kernel,
         grid_spec=pltpu.PrefetchScalarGridSpec(
@@ -185,8 +185,8 @@
     return call(
         centre_kernel,
         [own_set, core],
-        [centers, widths.reshape(1, -1)],
-        [whole(centers.shape), whole((1, widths.shape[0]))],
+        [centers, widths],
+        [whole(centers.shape), whole(widths.shape)],
         jax.ShapeDtypeStruct(shape, jnp.float32),
         whole(shape),
         [pltpu.VMEM((FB, 8), jnp.float32)],
@@ -194,9 +194,9 @@
     )
 
 
-def table_kernel(nb, near, group, me, owner, own_set, blocks_a, blocks_b, counts_a, counts_b, *refs):
-    order, lives, rows_near, rows_far, cols, slots, kbs, fill = refs
+def table_kernel(nb, near, group, me, owner, own_set, blocks_a, blocks_b, counts_a, counts_b, out, kbs, fill):
     half = counts_a.shape[0]
+    at_lives, at_near, at_far, at_col, at_pos = table_places(2 * half, group)
     spare = nb * near
     for p in range(UMAX):
         stored = owner[own_set[0, p]]
@@ -224,36 +224,42 @@
     def put(side, b, blocks, count):
         j = fill[count]
         fill[count] = j + 1
-        order[j] = side * half + b
+        out[j] = side * half + b
 
         @pl.when(lax.rem(j, group) == 0)
         def _():
-            lives[lax.div(j, group)] = count
+            out[at_lives + lax.div(j, group)] = count
 
         for s in range(TMAX):
             pos = blocks[b, s]
             kb = kbs[pos]
             on = s < count
             at = j * TMAX + s
-            slots[at] = pos
-            cols[at] = jnp.where(on, pos, UMAX)
-            rows_near[at] = jnp.where(on & (kb < spare), kb, spare)
-            rows_far[at] = jnp.where(on & (kb >= spare), kb - spare, spare)
+            out[at_pos + at] = pos
+            out[at_col + at] = jnp.where(on, pos, UMAX)
+            out[at_near + at] = jnp.where(on & (kb < spare), kb, spare)
+            out[at_far + at] = jnp.where(on & (kb >= spare), kb - spare, spare)
 
     each(put)
+
+
+def table_places(batches, group):
+    lives = batches
+    near = lives + batches // group
+    return lives, near, near + batches * TMAX, near + 2 * batches * TMAX, near + 3 * batches * TMAX
 
 
 def batch_tables(me, owner, own_set, blocks, counts, nb, near):
     batches = 2 * counts[0].shape[0]
     group = math.gcd(batches, 4)
-    sizes = (batches, batches // group) + (batches * TMAX,) * 4
+    size = table_places(batches, group)[-1] + batches * TMAX
     return call(
         functools.partial(table_kernel, nb, near, group),
         [me, owner, own_set, *blocks, *counts],
         [],
         [],
-        [jax.ShapeDtypeStruct((size,), jnp.int32) for size in sizes],
-        [pl.BlockSpec(memory_space=pltpu.SMEM)] * len(sizes),
+        jax.ShapeDtypeStruct((size,), jnp.int32),
+        pl.BlockSpec(memory_space=pltpu.SMEM),
         [pltpu.SMEM((UMAX,), jnp.int32), pltpu.SMEM((TMAX + 1,), jnp.int32)],
         cost=(0, 8 * batches * TMAX),
     )
@@ -316,7 +322,7 @@
     )
 
 
-def batch_kernel(group, pieces, order, lives, rows, cols, poss, *refs):
+def batch_kernel(group, pieces, split, table, *refs):
     xs, coords, weights, centre = refs[0:2], refs[2:4], refs[4:6], refs[6]
     parts = refs[7 : 7 + pieces]
     outs = refs[7 + pieces : -8]
@@ -325,9 +331,11 @@
     spare = nb * pieces
     batches, _, pts = xbuf.shape
     half = batches // 2
+    at_lives, at_near, at_far, at_col, at_pos = table_places(batches, group)
+    at_row = at_far if split else at_near
 
     def fetch(j, act):
-        b = order[j]
+        b = table[j]
         for side in (0, 1):
 
             @pl.when((b >= half) if side else (b < half))
@@ -340,7 +348,7 @@
     ]
     for side in (0, 1):
         rest = pl.ds(half * side, half)
-        copies.append(pltpu.make_async_copy(coords[side], pbuf.at[rest], qsems.at[side]))
+        copies.append(pltpu.make_async_copy(coords[side], pbuf.at[:, rest], qsems.at[side]))
         copies.append(pltpu.make_async_copy(weights[side], wbuf.at[rest], qsems.at[2 + side]))
     for copy in copies:
         copy.start()
@@ -359,12 +367,11 @@
         return jnp.concatenate([col] * (pts // FB), axis=1)
 
     def one(j, live):
-        b = order[j]
-        row = [rows[j * TMAX + s] for s in range(live)]
-        col = [pl.ds(pl.multiple_of(cols[j * TMAX + s] * FB, FB), FB) for s in range(live)]
-        pos = [poss[j * TMAX + s] for s in range(live)]
+        b = table[j]
+        row = [table[at_row + j * TMAX + s] for s in range(live)]
+        col = [pl.ds(pl.multiple_of(table[at_col + j * TMAX + s] * FB, FB), FB) for s in range(live)]
+        pos = [table[at_pos + j * TMAX + s] for s in range(live)]
         x = xbuf[j, : live * FB, :]
-        point = pbuf[b]
         d = jnp.concatenate(
             [
                 jnp.concatenate([dense[row[s], :, col[t]] for t in range(live)], axis=1)
@@ -377,7 +384,7 @@
         for s in range(live):
             dist = None
             for axis in range(3):
-                diff = lanes(centre[axis, pos[s]]) - point[axis : axis + 1, :]
+                diff = lanes(centre[axis, pos[s]]) - pbuf[axis, pl.ds(b, 1), :]
                 dist = diff * diff if dist is None else dist + diff * diff
             dist = dist + lanes(centre[3, pos[s]])
             fval.append((gval[s * sub : (s + 1) * sub] * lax.rsqrt(dist)).astype(jnp.bfloat16))
@@ -396,7 +403,7 @@
 
         for live in range(2, TMAX + 1):
 
-            @pl.when(lives[h] == live)
+            @pl.when(table[at_lives + h] == live)
             def _():
                 for row, col, part in [one(h * group + u, live) for u in range(group)]:
                     for s in range(live):
@@ -408,10 +415,10 @@
         out[...] = acc[size * k : size * (k + 1), :, :wide].astype(out.dtype)
 
 
-def batch_sums(order, lives, rows, cols, poss, xs, coords, weights, centre, parts, split):
+def batch_sums(table, xs, coords, weights, centre, parts, split):
     _, width, pts = xs[0].shape
-    batches = order.shape[0]
-    group = batches // lives.shape[0]
+    batches = 2 * xs[0].shape[0]
+    group = math.gcd(batches, 4)
     nb, sub, wide = parts[0].shape
     pieces = len(parts)
     size = 1 if split else nb
@@ -422,8 +429,8 @@
     ]
     flops = 2 * batches * 2 * width * (width // 2) * pts
     return call(
-        functools.partial(batch_kernel, group, pieces),
-        [order, lives, rows, cols, poss],
+        functools.partial(batch_kernel, group, pieces, split),
+        [table],
         [*xs, *coords, *weights, centre, *parts],
         [pl.BlockSpec(memory_space=pltpu.HBM)] * 2
         + [pl.BlockSpec(memory_space=pl.ANY)] * 4
@@ -435,14 +442,13 @@
             pltpu.VMEM((nb * pieces + 1, sub, wide + FB), jnp.bfloat16),
             pltpu.VMEM((nb * pieces + 1, sub, wide + FB), jnp.float32),
             pltpu.VMEM((batches, width, pts), jnp.bfloat16),
-            pltpu.VMEM((batches, 3, pts), jnp.float32),
+            pltpu.VMEM((3, batches, pts), jnp.float32),
             pltpu.VMEM((batches, pts), jnp.float32),
             pltpu.SemaphoreType.DMA((pieces,)),
             pltpu.SemaphoreType.DMA((batches,)),
             pltpu.SemaphoreType.DMA((4,)),
         ],
         cost=(flops, 2 * batches * width * pts),
-        vmem=32,
     )
 
 
@@ -463,25 +469,31 @@
     def across(x):
         return lax.ppermute(x, "rows", [(a, cores - 1 - a) for a in range(cores)])
 
+    def stay(x):
+        return pltpu.with_memory_space_constraint(x, pltpu.HBM)
+
     own = lax.dynamic_index_in_dim(density.reshape(nb, cores, sub, cols), r, 1, keepdims=False)
     far = swap(own, near)
     sets = [touched] + [swap(touched, k) for k in range(1, near)]
-    both = [(x, across(x)) for x in (basis, points, weights, blocks, counts)]
-    tables = batch_tables(i.reshape(1), owner, touched, both[3], both[4], nb, near)
-    order, lives, rows_near, rows_far, col, slots = tables
-    centre = centre_rows(touched, core, centers, widths, sub)
+    points = points.transpose(1, 0, 2)
+    both = [(stay(x), across(x)) for x in (basis, points, weights, counts)] + [(blocks, across(blocks))]
+    sets[0] = stay(touched)
+    table = batch_tables(i.reshape(1), stay(owner), sets[0], both[4], both[3], nb, near)
+    centre = centre_rows(sets[0], core, stay(centers), stay(widths.reshape(1, -1)), sub)
 
     picked = pick(sets, own)
     parts = [picked[0]] + [swap(picked[k], k) for k in range(1, near)]
+    far, table, centre, own_part = lax.optimization_barrier((far, table, centre, picked[0]))
     picked = pick(sets, far)
     far_parts = [picked[0]] + [swap(picked[k], k) for k in range(1, near)]
-    order, _ = lax.optimization_barrier((order, picked[0]))
-
-    common = (slots, *both[:3], centre)
-    sums = batch_sums(order, lives, rows_near, col, *common, parts, False)
-    order, _ = lax.optimization_barrier((order, sums[0]))
-    far_sums = batch_sums(order, lives, rows_far, col, *common, far_parts, True)
+    table, _ = lax.optimization_barrier((table, picked[0]))
+
+    common = (*both[:3], centre)
+    sums = batch_sums(table, *common, parts, False)
+    table, _ = lax.optimization_barrier((table, sums[0]))
+    far_sums = batch_sums(table, *common, far_parts, True)
     terms = [sums[0]] + [swap(sums[k], k) for k in range(1, near)]
+    far_sums, terms = lax.optimization_barrier((far_sums, terms))
     chunks = [[far_sums[b]] + [swap(far_sums[nb * k + b], k) for k in range(1, near)] for b in range(nb)]
     far_terms = [swap(merge(sets, chunk, cols), near) for chunk in chunks]
     keep, give = finish(sets, core, terms, far_terms)

time: 125 us -> 113 us (0.904)
  local copies, waits for them, and re-layouts: 15.1 us -> 2.4 us
  waiting for transfers between devices: 34.5 us -> 32.7 us
  starting transfers between devices: 35 us -> 36.5 us
    unnamed x42 -> x3, local copies, waits for them, and re-layouts: 14.2 us -> 1.53 us
    ppermute x21, waiting for transfers between devices: 32.9 us -> 31.2 us  [swap(): return lax.ppermute(x, 'dom', [(a, a ^ k) for a in range(n)])]
    ppermute x21, starting transfers between devices: 34 us -> 35.4 us  [swap(): return lax.ppermute(x, 'dom', [(a, a ^ k) for a in range(n)])]
  transfers between devices with their start and end apart: 27 -> 27, of which waited for: 10 -> 9; matrix products, arithmetic and copies ran while one was open for 1% -> 1% of each run, Pallas kernels for 19% -> 35%
where the time goes in v4:
time: 113 us; the launch traced here: 112 us
  Pallas kernels  39.9 us (35%)
  starting transfers between devices  36.5 us (32%)
  waiting for transfers between devices  32.7 us (29%)
  local copies, waits for them, and re-layouts  2.4 us (2%)
    pallas_call x9, Pallas kernels, call(): pl.pallas_call(kernel, grid_spec=pltpu.PrefetchScalarGridSpec(num_scalar_...  39.9 us
    ppermute x21, starting transfers between devices, swap(): return lax.ppermute(x, 'dom', [(a, a ^ k) for a in range(n)])  35.4 us
    ppermute x21, waiting for transfers between devices, swap(): return lax.ppermute(x, 'dom', [(a, a ^ k) for a in range(n)])  31.2 us
  transfers between devices with their start and end apart: 27, of which 9 were waited for; matrix products, arithmetic and copies ran while one was open for 1% of the time, Pallas kernels for 35%

profile of v4, /device:TPU:0, one launch (start us, length us, event | category | flops | bytes accessed | tf_op | source)
XLA Modules:
  0.0 111.8 jit_solution(4714140530221479439)
XLA Ops:
  1.3 4.1 %collective-permute-start.3 = (bf16[2,64,2048]{2,1,0:T(8,128)(2,1)S(1)}, bf16[2,64,2048]{2,1,0:T(8,128)(2,1)S(1)}, u32[]{:S(2)}, u32[]{:S(2)}) collective-permute-start(bf16[2,64,2048]{2,1,0:T(8,128)(2,1)S(1)} %dynamic-slice_bitcast_fusion.refs_4_), channel_id=1, source_target_pairs={{0,8},{2,10},{4,12},{6,14},{8,0},{10,2},{12,4},{14,6},{1,9},{3,11}... | collective-permute-start | bytes 1572872 | tf_op jit(solution)/shard_map/ppermute | solution.py:467
  5.4 1.5 %collective-permute-start = (s32[1,8]{1,0:T(1,128)}, s32[1,8]{1,0:T(1,128)S(1)}, u32[]{:S(2)}, u32[]{:S(2)}) collective-permute-start(s32[1,8]{1,0:T(1,128)} %refs_0_.13), channel_id=1, source_target_pairs={{0,2},{2,0},{4,6},{6,4},{8,10},{10,8},{12,14},{14,12},{1,3},{3,1},... | collective-permute-start | bytes 104 | tf_op jit(solution)/shard_map/ppermute | solution.py:467
  6.9 1.6 %collective-permute-start.1 = (s32[1,8]{1,0:T(1,128)}, s32[1,8]{1,0:T(1,128)S(1)}, u32[]{:S(2)}, u32[]{:S(2)}) collective-permute-start(s32[1,8]{1,0:T(1,128)} %refs_0_.13), channel_id=1, source_target_pairs={{0,4},{2,6},{4,0},{6,2},{8,12},{10,14},{12,8},{14,10},{1,5},{3,7},... | collective-permute-start | bytes 104 | tf_op jit(solution)/shard_map/ppermute | solution.py:467
  9.2 2.3 %collective-permute-start.2 = (s32[1,8]{1,0:T(1,128)}, s32[1,8]{1,0:T(1,128)S(1)}, u32[]{:S(2)}, u32[]{:S(2)}) collective-permute-start(s32[1,8]{1,0:T(1,128)} %refs_0_.13), channel_id=1, source_target_pairs={{0,6},{2,4},{4,2},{6,0},{8,14},{10,12},{12,10},{14,8},{1,7},{3,5},... | collective-permute-start | bytes 104 | tf_op jit(solution)/shard_map/ppermute | solution.py:467
  11.6 5.1 %collective-permute-done.1.refs_2_ = s32[1,8]{1,0:T(1,128)S(1)} collective-permute-done((s32[1,8]{1,0:T(1,128)}, s32[1,8]{1,0:T(1,128)S(1)}, u32[]{:S(2)}, u32[]{:S(2)}) %collective-permute-start.1) | collective-permute-done | bytes 64 | tf_op jit(solution)/shard_map/ppermute | solution.py:467
  17.2 1.8 %shard_map.102 = (bf16[2,64,1024]{2,1,0:T(8,128)(2,1)S(1)}, bf16[2,64,1024]{2,1,0:T(8,128)(2,1)S(1)}, bf16[2,64,1024]{2,1,0:T(8,128)(2,1)}, bf16[2,64,1024]{2,1,0:T(8,128)(2,1)}) custom-call(s32[1,8]{1,0:T(1,128)} %refs_0_.13, s32[1,8]{1,0:T(1,128)S(1)} %collective-permute-done.refs_1_, s32[1,8]{1,0:T(1,128)S(1)} %collective-permute-done.1.refs_2_, ...), custom_call_target="tpu_custom_call" | custom-call | bytes 1572864 | tf_op jit(solution)/shard_map/pallas_call | solution.py:128
  18.9 2.9 %collective-permute-start.10 = (bf16[2,64,1024]{2,1,0:T(8,128)(2,1)}, bf16[2,64,1024]{2,1,0:T(8,128)(2,1)S(1)}, u32[]{:S(2)}, u32[]{:S(2)}) collective-permute-start(bf16[2,64,1024]{2,1,0:T(8,128)(2,1)} %get-tuple-element.51), channel_id=1, source_target_pairs={{0,4},{2,6},{4,0},{6,2},{8,12},{10,14},{12,8},{14,10},{1,5},{3,7},... | collective-permute-start | bytes 786440 | tf_op jit(solution)/shard_map/ppermute | solution.py:467
  23.3 5.3 %collective-permute-done.3.refs_4_ = bf16[2,64,2048]{2,1,0:T(8,128)(2,1)S(1)} collective-permute-done((bf16[2,64,2048]{2,1,0:T(8,128)(2,1)S(1)}, bf16[2,64,2048]{2,1,0:T(8,128)(2,1)S(1)}, u32[]{:S(2)}, u32[]{:S(2)}) %collective-permute-start.3) | collective-permute-done | bytes 524320 | tf_op jit(solution)/shard_map/ppermute | solution.py:467
  28.6 2.1 %shard_map.101.refs_6_ = f32[4,8,64,128]{3,2,1,0:T(8,128)S(1)} custom-call(s32[1,8]{1,0:T(1,128)} %refs_0_.13, s32[1]{0:T(128)} %bitcast.core.refs_4_, f32[3,2048]{1,0:T(4,128)} %centers.1, f32[1,2048]{1,0:T(1,128)} %bitcast.15), custom_call_target="tpu_custom_call" | custom-call | bytes 2097152 | tf_op jit(solution)/shard_map/pallas_call | solution.py:128
  30.8 3.6 %shard_map.100.table = s32[828]{0:T(1024)S(1)} custom-call(s32[1]{0:T(128)} %bitcast.3.me, s32[16]{0:T(128)} %owner.1, s32[1,8]{1,0:T(1,128)} %refs_0_.13, s32[24,4]{1,0:T(8,128)S(1)} %copy.16.blocks_a, s32[24,4]{1,0:T(8,128)S(1)} %collective-permute-done.4.blocks_b, s32[24]{0:T(128)} %counts_a.1, s32[24]{0:T(128)S(1)} %collective-permute-done.5.counts_b), custom_call_target="tpu_custom_call" | custom-call | bytes 1536 | tf_op jit(solution)/shard_map/pallas_call | solution.py:128
  35.3 1.6 %collective-permute-start.12 = (bf16[2,64,1024]{2,1,0:T(8,128)(2,1)S(1)}, bf16[2,64,1024]{2,1,0:T(8,128)(2,1)S(1)}, u32[]{:S(2)}, u32[]{:S(2)}) collective-permute-start(bf16[2,64,1024]{2,1,0:T(8,128)(2,1)S(1)} %get-tuple-element.55), channel_id=1, source_target_pairs={{0,2},{2,0},{4,6},{6,4},{8,10},{10,8},{12,14},{14,12},{1,3},{3,1},... | collective-permute-start | bytes 786440 | tf_op jit(solution)/shard_map/ppermute | solution.py:467
  37.6 3.3 %collective-permute-done.11.refs_10_ = bf16[2,64,1024]{2,1,0:T(8,128)(2,1)S(1)} collective-permute-done((bf16[2,64,1024]{2,1,0:T(8,128)(2,1)}, bf16[2,64,1024]{2,1,0:T(8,128)(2,1)S(1)}, u32[]{:S(2)}, u32[]{:S(2)}) %collective-permute-start.11) | collective-permute-done | bytes 262176 | tf_op jit(solution)/shard_map/ppermute | solution.py:467
  40.9 14.1 %shard_map.104 = (f32[2,64,1024]{2,1,0:T(8,128)S(1)}, bf16[2,64,1024]{2,1,0:T(8,128)(2,1)S(1)}, bf16[2,64,1024]{2,1,0:T(8,128)(2,1)S(1)}, bf16[2,64,1024]{2,1,0:T(8,128)(2,1)S(1)}) custom-call(s32[828]{0:T(1024)S(1)} %shard_map.100.table, bf16[24,512,256]{2,1,0:T(8,128)(2,1)} %refs_0_.10, bf16[24,512,256]{2,1,0:T(8,128)(2,1)} %collective-permute-done.6.refs_1_, ...), custom_call_target="tpu_custom_call" | custom-call | flops 6442450944 | bytes 12582912 | tf_op jit(solution)/shard_map/pallas_call | solution.py:128
  56.2 2.5 %collective-permute-start.16 = (bf16[2,64,1024]{2,1,0:T(8,128)(2,1)S(1)}, bf16[2,64,1024]{2,1,0:T(8,128)(2,1)S(1)}, u32[]{:S(2)}, u32[]{:S(2)}) collective-permute-start(bf16[2,64,1024]{2,1,0:T(8,128)(2,1)S(1)} %get-tuple-element.67), channel_id=1, source_target_pairs={{0,4},{2,6},{4,0},{6,2},{8,12},{10,14},{12,8},{14,10},{1,5},{3,7},... | collective-permute-start | bytes 786440 | tf_op jit(solution)/shard_map/ppermute | solution.py:467
  58.7 14.1 %shard_map.105 = (f32[1,64,1024]{2,1,0:T(8,128)S(1)}, f32[1,64,1024]{2,1,0:T(8,128)S(1)}, bf16[1,64,1024]{2,1,0:T(8,128)(2,1)S(1)}, bf16[1,64,1024]{2,1,0:T(8,12...) custom-call(s32[828]{0:T(1024)S(1)} %shard_map.100.table, ...), custom_call_target="tpu_custom_call" | custom-call | flops 6442450944 | bytes 12582912 | tf_op jit(solution)/shard_map/pallas_call | solution.py:128
  72.9 2.2 %collective-permute-start.22 = (bf16[1,64,1024]{2,1,0:T(8,128)(2,1)S(1)}, bf16[1,64,1024]{2,1,0:T(8,128)(2,1)S(1)}, u32[]{:S(2)}, u32[]{:S(2)}) collective-permute-start(bf16[1,64,1024]{2,1,0:T(8,128)(2,1)S(1)} %get-tuple-element.78), channel_id=1, source_target_pairs={{0,2},{2,0},{4,6},{6,4},{8,10},{10,8},{12,14},{14,12},{1,3},{3,1},... | collective-permute-start | bytes 393224 | tf_op jit(solution)/shard_map/ppermute | solution.py:467
  76.7 1.9 %collective-permute-start.18 = (bf16[1,64,1024]{2,1,0:T(8,128)(2,1)S(1)}, bf16[1,64,1024]{2,1,0:T(8,128)(2,1)S(1)}, u32[]{:S(2)}, u32[]{:S(2)}) collective-permute-start(bf16[1,64,1024]{2,1,0:T(8,128)(2,1)S(1)} %get-tuple-element.74), channel_id=1, source_target_pairs={{0,2},{2,0},{4,6},{6,4},{8,10},{10,8},{12,14},{14,12},{1,3},{3,1},... | collective-permute-start | bytes 393224 | tf_op jit(solution)/shard_map/ppermute | solution.py:467
  80.1 3.2 %collective-permute-start.20 = (bf16[1,64,1024]{2,1,0:T(8,128)(2,1)S(1)}, bf16[1,64,1024]{2,1,0:T(8,128)(2,1)S(1)}, u32[]{:S(2)}, u32[]{:S(2)}) collective-permute-start(bf16[1,64,1024]{2,1,0:T(8,128)(2,1)S(1)} %get-tuple-element.76), channel_id=1, source_target_pairs={{0,6},{2,4},{4,2},{6,0},{8,14},{10,12},{12,10},{14,8},{1,7},{3,5},... | collective-permute-start | bytes 393224 | tf_op jit(solution)/shard_map/ppermute | solution.py:467
  84.9 3.2 %collective-permute-start.25 = (bf16[1,64,2048]{2,1,0:T(8,128)(2,1)S(1)}, bf16[1,64,2048]{2,1,0:T(8,128)(2,1)S(1)}, u32[]{:S(2)}, u32[]{:S(2)}) collective-permute-start(bf16[1,64,2048]{2,1,0:T(8,128)(2,1)S(1)} %shard_map.107), channel_id=1, source_target_pairs={{0,8},{2,10},{4,12},{6,14},{8,0},{10,2},{12,4},{14,6},{1,9},{3,11}... | collective-permute-start | bytes 786440 | tf_op jit(solution)/shard_map/ppermute | solution.py:467
  88.4 2.4 %collective-permute-done.20.refs_7_ = bf16[1,64,1024]{2,1,0:T(8,128)(2,1)S(1)} collective-permute-done((bf16[1,64,1024]{2,1,0:T(8,128)(2,1)S(1)}, bf16[1,64,1024]{2,1,0:T(8,128)(2,1)S(1)}, u32[]{:S(2)}, u32[]{:S(2)}) %collective-permute-start.20) | collective-permute-done | bytes 131104 | tf_op jit(solution)/shard_map/ppermute | solution.py:467
  91.8 1.9 %collective-permute-start.21 = (bf16[1,64,2048]{2,1,0:T(8,128)(2,1)S(1)}, bf16[1,64,2048]{2,1,0:T(8,128)(2,1)S(1)}, u32[]{:S(2)}, u32[]{:S(2)}) collective-permute-start(bf16[1,64,2048]{2,1,0:T(8,128)(2,1)S(1)} %shard_map.106), channel_id=1, source_target_pairs={{0,8},{2,10},{4,12},{6,14},{8,0},{10,2},{12,4},{14,6},{1,9},{3,11}... | collective-permute-start | bytes 786440 | tf_op jit(solution)/shard_map/ppermute | solution.py:467
  93.7 10.8 %collective-permute-done.25.refs_10_ = bf16[1,64,2048]{2,1,0:T(8,128)(2,1)S(1)} collective-permute-done((bf16[1,64,2048]{2,1,0:T(8,128)(2,1)S(1)}, bf16[1,64,2048]{2,1,0:T(8,128)(2,1)S(1)}, u32[]{:S(2)}, u32[]{:S(2)}) %collective-permute-start.25) | collective-permute-done | bytes 262176 | tf_op jit(solution)/shard_map/ppermute | solution.py:467
  104.5 3.4 %collective-permute-done.21.refs_9_ = bf16[1,64,2048]{2,1,0:T(8,128)(2,1)S(1)} collective-permute-done((bf16[1,64,2048]{2,1,0:T(8,128)(2,1)S(1)}, bf16[1,64,2048]{2,1,0:T(8,128)(2,1)S(1)}, u32[]{:S(2)}, u32[]{:S(2)}) %collective-permute-start.21) | collective-permute-done | bytes 262176 | tf_op jit(solution)/shard_map/ppermute | solution.py:467
  109.4 1.5 %collective-permute-done.26 = bf16[2,64,1024]{2,1,0:T(8,128)(2,1)S(1)} collective-permute-done((bf16[2,64,1024]{2,1,0:T(8,128)(2,1)S(1)}, bf16[2,64,1024]{2,1,0:T(8,128)(2,1)S(1)}, u32[]{:S(2)}, u32[]{:S(2)}) %collective-permute-start.26) | collective-permute-done | bytes 262176 | tf_op jit(solution)/shard_map/ppermute | solution.py:470
  (45 shorter events, 15.1 us)
Async XLA Ops:
  0.0 40.9 %collective-permute-start.6 = (bf16[24,512,256]{2,1,0:T(8,128)(2,1)}, bf16[24,512,256]{2,1,0:T(8,128)(2,1)}, u32[]{:S(2)}, u32[]{:S(2)}) collective-permute-start(bf16[24,512,256]{2,1,0:T(8,128)(2,1)} %refs_0_.10), channel_id=1, source_target_pairs={{0,1},{1,0},{2,3},{3,2},{4,5},{5,4},{6,7},{7,6},{8,9},{9,8},{10,11... | collective-permute-start | bytes 18874376 | tf_op jit(solution)/shard_map/ppermute | solution.py:470
  1.3 27.4 %collective-permute-start.3 = (bf16[2,64,2048]{2,1,0:T(8,128)(2,1)S(1)}, bf16[2,64,2048]{2,1,0:T(8,128)(2,1)S(1)}, u32[]{:S(2)}, u32[]{:S(2)}) collective-permute-start(bf16[2,64,2048]{2,1,0:T(8,128)(2,1)S(1)} %dynamic-slice_bitcast_fusion.refs_4_), channel_id=1, source_target_pairs={{0,8},{2,10},{4,12},{6,14},{8,0},{10,2},{12,4},{14,6},{1,9},{3,11}... | collective-permute-start | bytes 1572872 | tf_op jit(solution)/shard_map/ppermute | solution.py:467
  5.4 17.0 %collective-permute-start.8 = (f32[24,256]{1,0:T(8,128)}, f32[24,256]{1,0:T(8,128)S(1)}, u32[]{:S(2)}, u32[]{:S(2)}) collective-permute-start(f32[24,256]{1,0:T(8,128)} %refs_4_.3), channel_id=1, source_target_pairs={{0,1},{1,0},{2,3},{3,2},{4,5},{5,4},{6,7},{7,6},{8,9},{9,8},{10,11... | collective-permute-start | bytes 73736 | tf_op jit(solution)/shard_map/ppermute | solution.py:470
  6.9 9.8 %collective-permute-start.1 = (s32[1,8]{1,0:T(1,128)}, s32[1,8]{1,0:T(1,128)S(1)}, u32[]{:S(2)}, u32[]{:S(2)}) collective-permute-start(s32[1,8]{1,0:T(1,128)} %refs_0_.13), channel_id=1, source_target_pairs={{0,4},{2,6},{4,0},{6,2},{8,12},{10,14},{12,8},{14,10},{1,5},{3,7},... | collective-permute-start | bytes 104 | tf_op jit(solution)/shard_map/ppermute | solution.py:467
  9.2 7.4 %collective-permute-start.2 = (s32[1,8]{1,0:T(1,128)}, s32[1,8]{1,0:T(1,128)S(1)}, u32[]{:S(2)}, u32[]{:S(2)}) collective-permute-start(s32[1,8]{1,0:T(1,128)} %refs_0_.13), channel_id=1, source_target_pairs={{0,6},{2,4},{4,2},{6,0},{8,14},{10,12},{12,10},{14,8},{1,7},{3,5},... | collective-permute-start | bytes 104 | tf_op jit(solution)/shard_map/ppermute | solution.py:467
  16.7 5.2 %collective-permute-start.4 = (s32[24,4]{1,0:T(8,128)S(1)}, s32[24,4]{1,0:T(8,128)S(1)}, u32[]{:S(2)}, u32[]{:S(2)}) collective-permute-start(s32[24,4]{1,0:T(8,128)S(1)} %copy.16.blocks_a), channel_id=1, source_target_pairs={{0,1},{1,0},{2,3},{3,2},{4,5},{5,4},{6,7},{7,6},{8,9},{9,8},{10,11... | collective-permute-start | bytes 1160 | tf_op jit(solution)/shard_map/ppermute | solution.py:470
  18.9 18.0 %collective-permute-start.10 = (bf16[2,64,1024]{2,1,0:T(8,128)(2,1)}, bf16[2,64,1024]{2,1,0:T(8,128)(2,1)S(1)}, u32[]{:S(2)}, u32[]{:S(2)}) collective-permute-start(bf16[2,64,1024]{2,1,0:T(8,128)(2,1)} %get-tuple-element.51), channel_id=1, source_target_pairs={{0,4},{2,6},{4,0},{6,2},{8,12},{10,14},{12,8},{14,10},{1,5},{3,7},... | collective-permute-start | bytes 786440 | tf_op jit(solution)/shard_map/ppermute | solution.py:467
  21.8 19.1 %collective-permute-start.11 = (bf16[2,64,1024]{2,1,0:T(8,128)(2,1)}, bf16[2,64,1024]{2,1,0:T(8,128)(2,1)S(1)}, u32[]{:S(2)}, u32[]{:S(2)}) collective-permute-start(bf16[2,64,1024]{2,1,0:T(8,128)(2,1)} %get-tuple-element.52), channel_id=1, source_target_pairs={{0,6},{2,4},{4,2},{6,0},{8,14},{10,12},{12,10},{14,8},{1,7},{3,5},... | collective-permute-start | bytes 786440 | tf_op jit(solution)/shard_map/ppermute | solution.py:467
  22.4 18.5 %collective-permute-start.9 = (bf16[2,64,1024]{2,1,0:T(8,128)(2,1)S(1)}, bf16[2,64,1024]{2,1,0:T(8,128)(2,1)S(1)}, u32[]{:S(2)}, u32[]{:S(2)}) collective-permute-start(bf16[2,64,1024]{2,1,0:T(8,128)(2,1)S(1)} %get-tuple-element.50), channel_id=1, source_target_pairs={{0,2},{2,0},{4,6},{6,4},{8,10},{10,8},{12,14},{14,12},{1,3},{3,1},... | collective-permute-start | bytes 786440 | tf_op jit(solution)/shard_map/ppermute | solution.py:467
  28.6 6.7 %collective-permute-start.7 = (f32[3,24,256]{2,1,0:T(8,128)}, f32[3,24,256]{2,1,0:T(8,128)S(1)}, u32[]{:S(2)}, u32[]{:S(2)}) collective-permute-start(f32[3,24,256]{2,1,0:T(8,128)} %bitcast.16), channel_id=1, source_target_pairs={{0,1},{1,0},{2,3},{3,2},{4,5},{5,4},{6,7},{7,6},{8,9},{9,8},{10,11... | collective-permute-start | bytes 221192 | tf_op jit(solution)/shard_map/ppermute | solution.py:470
  35.3 23.4 %collective-permute-start.12 = (bf16[2,64,1024]{2,1,0:T(8,128)(2,1)S(1)}, bf16[2,64,1024]{2,1,0:T(8,128)(2,1)S(1)}, u32[]{:S(2)}, u32[]{:S(2)}) collective-permute-start(bf16[2,64,1024]{2,1,0:T(8,128)(2,1)S(1)} %get-tuple-element.55), channel_id=1, source_target_pairs={{0,2},{2,0},{4,6},{6,4},{8,10},{10,8},{12,14},{14,12},{1,3},{3,1},... | collective-permute-start | bytes 786440 | tf_op jit(solution)/shard_map/ppermute | solution.py:467
  37.0 21.8 %collective-permute-start.13 = (bf16[2,64,1024]{2,1,0:T(8,128)(2,1)S(1)}, bf16[2,64,1024]{2,1,0:T(8,128)(2,1)S(1)}, u32[]{:S(2)}, u32[]{:S(2)}) collective-permute-start(bf16[2,64,1024]{2,1,0:T(8,128)(2,1)S(1)} %get-tuple-element.56), channel_id=1, source_target_pairs={{0,4},{2,6},{4,0},{6,2},{8,12},{10,14},{12,8},{14,10},{1,5},{3,7},... | collective-permute-start | bytes 786440 | tf_op jit(solution)/shard_map/ppermute | solution.py:467
  40.9 17.9 %collective-permute-start.14 = (bf16[2,64,1024]{2,1,0:T(8,128)(2,1)S(1)}, bf16[2,64,1024]{2,1,0:T(8,128)(2,1)S(1)}, u32[]{:S(2)}, u32[]{:S(2)}) collective-permute-start(bf16[2,64,1024]{2,1,0:T(8,128)(2,1)S(1)} %get-tuple-element.57), channel_id=1, source_target_pairs={{0,6},{2,4},{4,2},{6,0},{8,14},{10,12},{12,10},{14,8},{1,7},{3,5},... | collective-permute-start | bytes 786440 | tf_op jit(solution)/shard_map/ppermute | solution.py:467
  55.0 17.9 %collective-permute-start.15 = (bf16[2,64,1024]{2,1,0:T(8,128)(2,1)S(1)}, bf16[2,64,1024]{2,1,0:T(8,128)(2,1)S(1)}, u32[]{:S(2)}, u32[]{:S(2)}) collective-permute-start(bf16[2,64,1024]{2,1,0:T(8,128)(2,1)S(1)} %get-tuple-element.66), channel_id=1, source_target_pairs={{0,2},{2,0},{4,6},{6,4},{8,10},{10,8},{12,14},{14,12},{1,3},{3,1},... | collective-permute-start | bytes 786440 | tf_op jit(solution)/shard_map/ppermute | solution.py:467
  56.2 16.7 %collective-permute-start.16 = (bf16[2,64,1024]{2,1,0:T(8,128)(2,1)S(1)}, bf16[2,64,1024]{2,1,0:T(8,128)(2,1)S(1)}, u32[]{:S(2)}, u32[]{:S(2)}) collective-permute-start(bf16[2,64,1024]{2,1,0:T(8,128)(2,1)S(1)} %get-tuple-element.67), channel_id=1, source_target_pairs={{0,4},{2,6},{4,0},{6,2},{8,12},{10,14},{12,8},{14,10},{1,5},{3,7},... | collective-permute-start | bytes 786440 | tf_op jit(solution)/shard_map/ppermute | solution.py:467
  58.7 14.2 %collective-permute-start.17 = (bf16[2,64,1024]{2,1,0:T(8,128)(2,1)S(1)}, bf16[2,64,1024]{2,1,0:T(8,128)(2,1)S(1)}, u32[]{:S(2)}, u32[]{:S(2)}) collective-permute-start(bf16[2,64,1024]{2,1,0:T(8,128)(2,1)S(1)} %get-tuple-element.68), channel_id=1, source_target_pairs={{0,6},{2,4},{4,2},{6,0},{8,14},{10,12},{12,10},{14,8},{1,7},{3,5},... | collective-permute-start | bytes 786440 | tf_op jit(solution)/shard_map/ppermute | solution.py:467
  72.9 7.2 %collective-permute-start.22 = (bf16[1,64,1024]{2,1,0:T(8,128)(2,1)S(1)}, bf16[1,64,1024]{2,1,0:T(8,128)(2,1)S(1)}, u32[]{:S(2)}, u32[]{:S(2)}) collective-permute-start(bf16[1,64,1024]{2,1,0:T(8,128)(2,1)S(1)} %get-tuple-element.78), channel_id=1, source_target_pairs={{0,2},{2,0},{4,6},{6,4},{8,10},{10,8},{12,14},{14,12},{1,3},{3,1},... | collective-permute-start | bytes 393224 | tf_op jit(solution)/shard_map/ppermute | solution.py:467
  75.1 8.2 %collective-permute-start.23 = (bf16[1,64,1024]{2,1,0:T(8,128)(2,1)S(1)}, bf16[1,64,1024]{2,1,0:T(8,128)(2,1)S(1)}, u32[]{:S(2)}, u32[]{:S(2)}) collective-permute-start(bf16[1,64,1024]{2,1,0:T(8,128)(2,1)S(1)} %get-tuple-element.79), channel_id=1, source_target_pairs={{0,4},{2,6},{4,0},{6,2},{8,12},{10,14},{12,8},{14,10},{1,5},{3,7},... | collective-permute-start | bytes 393224 | tf_op jit(solution)/shard_map/ppermute | solution.py:467
  76.6 7.3 %collective-permute-start.24 = (bf16[1,64,1024]{2,1,0:T(8,128)(2,1)S(1)}, bf16[1,64,1024]{2,1,0:T(8,128)(2,1)S(1)}, u32[]{:S(2)}, u32[]{:S(2)}) collective-permute-start(bf16[1,64,1024]{2,1,0:T(8,128)(2,1)S(1)} %get-tuple-element.80), channel_id=1, source_target_pairs={{0,6},{2,4},{4,2},{6,0},{8,14},{10,12},{12,10},{14,8},{1,7},{3,5},... | collective-permute-start | bytes 393224 | tf_op jit(solution)/shard_map/ppermute | solution.py:467
  76.7 11.5 %collective-permute-start.18 = (bf16[1,64,1024]{2,1,0:T(8,128)(2,1)S(1)}, bf16[1,64,1024]{2,1,0:T(8,128)(2,1)S(1)}, u32[]{:S(2)}, u32[]{:S(2)}) collective-permute-start(bf16[1,64,1024]{2,1,0:T(8,128)(2,1)S(1)} %get-tuple-element.74), channel_id=1, source_target_pairs={{0,2},{2,0},{4,6},{6,4},{8,10},{10,8},{12,14},{14,12},{1,3},{3,1},... | collective-permute-start | bytes 393224 | tf_op jit(solution)/shard_map/ppermute | solution.py:467
  78.6 9.8 %collective-permute-start.19 = (bf16[1,64,1024]{2,1,0:T(8,128)(2,1)S(1)}, bf16[1,64,1024]{2,1,0:T(8,128)(2,1)S(1)}, u32[]{:S(2)}, u32[]{:S(2)}) collective-permute-start(bf16[1,64,1024]{2,1,0:T(8,128)(2,1)S(1)} %get-tuple-element.75), channel_id=1, source_target_pairs={{0,4},{2,6},{4,0},{6,2},{8,12},{10,14},{12,8},{14,10},{1,5},{3,7},... | collective-permute-start | bytes 393224 | tf_op jit(solution)/shard_map/ppermute | solution.py:467
  80.1 10.7 %collective-permute-start.20 = (bf16[1,64,1024]{2,1,0:T(8,128)(2,1)S(1)}, bf16[1,64,1024]{2,1,0:T(8,128)(2,1)S(1)}, u32[]{:S(2)}, u32[]{:S(2)}) collective-permute-start(bf16[1,64,1024]{2,1,0:T(8,128)(2,1)S(1)} %get-tuple-element.76), channel_id=1, source_target_pairs={{0,6},{2,4},{4,2},{6,0},{8,14},{10,12},{12,10},{14,8},{1,7},{3,5},... | collective-permute-start | bytes 393224 | tf_op jit(solution)/shard_map/ppermute | solution.py:467
  84.9 19.6 %collective-permute-start.25 = (bf16[1,64,2048]{2,1,0:T(8,128)(2,1)S(1)}, bf16[1,64,2048]{2,1,0:T(8,128)(2,1)S(1)}, u32[]{:S(2)}, u32[]{:S(2)}) collective-permute-start(bf16[1,64,2048]{2,1,0:T(8,128)(2,1)S(1)} %shard_map.107), channel_id=1, source_target_pairs={{0,8},{2,10},{4,12},{6,14},{8,0},{10,2},{12,4},{14,6},{1,9},{3,11}... | collective-permute-start | bytes 786440 | tf_op jit(solution)/shard_map/ppermute | solution.py:467
  91.8 16.2 %collective-permute-start.21 = (bf16[1,64,2048]{2,1,0:T(8,128)(2,1)S(1)}, bf16[1,64,2048]{2,1,0:T(8,128)(2,1)S(1)}, u32[]{:S(2)}, u32[]{:S(2)}) collective-permute-start(bf16[1,64,2048]{2,1,0:T(8,128)(2,1)S(1)} %shard_map.106), channel_id=1, source_target_pairs={{0,8},{2,10},{4,12},{6,14},{8,0},{10,2},{12,4},{14,6},{1,9},{3,11}... | collective-permute-start | bytes 786440 | tf_op jit(solution)/shard_map/ppermute | solution.py:467
  (4 other events, 9.0 us)

commit v5 on v4

--- a/solution.py
+++ b/solution.py
@@ -481,9 +481,10 @@
     table = batch_tables(i.reshape(1), stay(owner), sets[0], both[4], both[3], nb, near)
     centre = centre_rows(sets[0], core, stay(centers), stay(widths.reshape(1, -1)), sub)
 
+    own, table, centre, both = lax.optimization_barrier((own, table, centre, both))
     picked = pick(sets, own)
     parts = [picked[0]] + [swap(picked[k], k) for k in range(1, near)]
-    far, table, centre, own_part = lax.optimization_barrier((far, table, centre, picked[0]))
+    far, _ = lax.optimization_barrier((far, picked[0]))
     picked = pick(sets, far)
     far_parts = [picked[0]] + [swap(picked[k], k) for k in range(1, near)]
     table, _ = lax.optimization_barrier((table, picked[0]))
@@ -494,8 +495,12 @@
     far_sums = batch_sums(table, *common, far_parts, True)
     terms = [sums[0]] + [swap(sums[k], k) for k in range(1, near)]
     far_sums, terms = lax.optimization_barrier((far_sums, terms))
-    chunks = [[far_sums[b]] + [swap(far_sums[nb * k + b], k) for k in range(1, near)] for b in range(nb)]
-    far_terms = [swap(merge(sets, chunk, cols), near) for chunk in chunks]
+    far_terms = []
+    for b in range(nb):
+        chunk = [far_sums[b]] + [swap(far_sums[nb * k + b], k) for k in range(1, near)]
+        merged = merge(sets, chunk, cols)
+        far_sums, merged = lax.optimization_barrier((far_sums, merged))
+        far_terms.append(swap(merged, near))
     keep, give = finish(sets, core, terms, far_terms)
     got = across(give)
     pair = jnp.where(r == 0, jnp.stack([keep, got], axis=1), jnp.stack([got, keep], axis=1))

time: 113 us -> 114 us (level)
  waiting for transfers between devices: 32.7 us -> 43.5 us
  starting transfers between devices: 36.5 us -> 27.5 us
    ppermute x21, starting transfers between devices: 35.4 us -> 26.1 us  [swap(): return lax.ppermute(x, 'dom', [(a, a ^ k) for a in range(n)])]
    ppermute x21, waiting for transfers between devices: 31.2 us -> 38.1 us  [swap(): return lax.ppermute(x, 'dom', [(a, a ^ k) for a in range(n)])]
    ppermute x6, waiting for transfers between devices: 1.53 us -> 5.47 us  [across(): return lax.ppermute(x, 'rows', [(a, cores - 1 - a) for a in range(cores)])]
  transfers between devices with their start and end apart: 27 -> 27, of which waited for: 9 -> 15; matrix products, arithmetic and copies ran while one was open for 1% -> 1% of each run, Pallas kernels for 35% -> 33%
where the time goes in v5:
time: 114 us; the launch traced here: 113 us
  waiting for transfers between devices  43.5 us (38%)
  Pallas kernels  39.7 us (35%)
  starting transfers between devices  27.5 us (24%)
  local copies, waits for them, and re-layouts  2.4 us (2%)
    pallas_call x9, Pallas kernels, call(): pl.pallas_call(kernel, grid_spec=pltpu.PrefetchScalarGridSpec(num_scalar_...  39.7 us
    ppermute x21, waiting for transfers between devices, swap(): return lax.ppermute(x, 'dom', [(a, a ^ k) for a in range(n)])  38.1 us
    ppermute x21, starting transfers between devices, swap(): return lax.ppermute(x, 'dom', [(a, a ^ k) for a in range(n)])  26.1 us
    ppermute x6, waiting for transfers between devices, across(): return lax.ppermute(x, 'rows', [(a, cores - 1 - a) for a in range(cores)])  5.47 us
  transfers between devices with their start and end apart: 27, of which 15 were waited for; matrix products, arithmetic and copies ran while one was open for 1% of the time, Pallas kernels for 33%

profile of v5, /device:TPU:0, one launch (start us, length us, event | category | flops | bytes accessed | tf_op | source)
XLA Modules:
  0.0 113.3 jit_solution(6841796324109744399)
XLA Ops:
  1.3 4.1 %collective-permute-start.8 = (bf16[2,64,2048]{2,1,0:T(8,128)(2,1)S(1)}, bf16[2,64,2048]{2,1,0:T(8,128)(2,1)S(1)}, u32[]{:S(2)}, u32[]{:S(2)}) collective-permute-start(bf16[2,64,2048]{2,1,0:T(8,128)(2,1)S(1)} %dynamic-slice_bitcast_fusion.refs_4_), channel_id=1, source_target_pairs={{0,8},{2,10},{4,12},{6,14},{8,0},{10,2},{12,4},{14,6},{1,9},{3,11}... | collective-permute-start | bytes 1572872 | tf_op jit(solution)/shard_map/ppermute | solution.py:467
  6.7 3.9 %collective-permute-done.4.counts_b = s32[24]{0:T(128)S(1)} collective-permute-done((s32[24]{0:T(128)}, s32[24]{0:T(128)S(1)}, u32[]{:S(2)}, u32[]{:S(2)}) %collective-permute-start.4) | collective-permute-done | bytes 128 | tf_op jit(solution)/shard_map/ppermute | solution.py:470
  11.0 2.1 %shard_map.101.refs_6_ = f32[4,8,64,128]{3,2,1,0:T(8,128)S(1)} custom-call(s32[1,8]{1,0:T(1,128)} %refs_0_.11, s32[1]{0:T(128)} %bitcast.core.refs_4_, f32[3,2048]{1,0:T(4,128)} %centers.1, f32[1,2048]{1,0:T(1,128)} %bitcast.15), custom_call_target="tpu_custom_call" | custom-call | bytes 2097152 | tf_op jit(solution)/shard_map/pallas_call | solution.py:128
  13.1 2.7 %collective-permute-start = (s32[1,8]{1,0:T(1,128)}, s32[1,8]{1,0:T(1,128)S(1)}, u32[]{:S(2)}, u32[]{:S(2)}) collective-permute-start(s32[1,8]{1,0:T(1,128)} %refs_0_.11), channel_id=1, source_target_pairs={{0,2},{2,0},{4,6},{6,4},{8,10},{10,8},{12,14},{14,12},{1,3},{3,1},... | collective-permute-start | bytes 104 | tf_op jit(solution)/shard_map/ppermute | solution.py:467
  15.8 3.6 %shard_map.100.table = s32[828]{0:T(1024)S(1)} custom-call(s32[1]{0:T(128)} %bitcast.3.me, s32[16]{0:T(128)} %owner.1, s32[1,8]{1,0:T(1,128)} %refs_0_.11, s32[24,4]{1,0:T(8,128)S(1)} %copy.16.blocks_a, s32[24,4]{1,0:T(8,128)S(1)} %collective-permute-done.3.blocks_b, s32[24]{0:T(128)} %counts_a.1, s32[24]{0:T(128)S(1)} %collective-permute-done.4.counts_b), custom_call_target="tpu_custom_call" | custom-call | bytes 1536 | tf_op jit(solution)/shard_map/pallas_call | solution.py:128
  19.4 1.6 %collective-permute-start.1 = (s32[1,8]{1,0:T(1,128)}, s32[1,8]{1,0:T(1,128)S(1)}, u32[]{:S(2)}, u32[]{:S(2)}) collective-permute-start(s32[1,8]{1,0:T(1,128)} %refs_0_.11), channel_id=1, source_target_pairs={{0,4},{2,6},{4,0},{6,2},{8,12},{10,14},{12,8},{14,10},{1,5},{3,7},... | collective-permute-start | bytes 104 | tf_op jit(solution)/shard_map/ppermute | solution.py:467
  21.1 2.1 %collective-permute-done.1.refs_2_ = s32[1,8]{1,0:T(1,128)S(1)} collective-permute-done((s32[1,8]{1,0:T(1,128)}, s32[1,8]{1,0:T(1,128)S(1)}, u32[]{:S(2)}, u32[]{:S(2)}) %collective-permute-start.1) | collective-permute-done | bytes 64 | tf_op jit(solution)/shard_map/ppermute | solution.py:467
  23.2 2.5 %collective-permute-done.2.refs_3_ = s32[1,8]{1,0:T(1,128)S(1)} collective-permute-done((s32[1,8]{1,0:T(1,128)}, s32[1,8]{1,0:T(1,128)S(1)}, u32[]{:S(2)}, u32[]{:S(2)}) %collective-permute-start.2) | collective-permute-done | bytes 64 | tf_op jit(solution)/shard_map/ppermute | solution.py:467
  27.1 1.5 %collective-permute-start.11 = (bf16[2,64,1024]{2,1,0:T(8,128)(2,1)S(1)}, bf16[2,64,1024]{2,1,0:T(8,128)(2,1)S(1)}, u32[]{:S(2)}, u32[]{:S(2)}) collective-permute-start(bf16[2,64,1024]{2,1,0:T(8,128)(2,1)S(1)} %get-tuple-element.72), channel_id=1, source_target_pairs={{0,6},{2,4},{4,2},{6,0},{8,14},{10,12},{12,10},{14,8},{1,7},{3,5},... | collective-permute-start | bytes 786440 | tf_op jit(solution)/shard_map/ppermute | solution.py:467
  28.7 1.5 %collective-permute-start.9 = (bf16[2,64,1024]{2,1,0:T(8,128)(2,1)S(1)}, bf16[2,64,1024]{2,1,0:T(8,128)(2,1)S(1)}, u32[]{:S(2)}, u32[]{:S(2)}) collective-permute-start(bf16[2,64,1024]{2,1,0:T(8,128)(2,1)S(1)} %get-tuple-element.70), channel_id=1, source_target_pairs={{0,2},{2,0},{4,6},{6,4},{8,10},{10,8},{12,14},{14,12},{1,3},{3,1},... | collective-permute-start | bytes 786440 | tf_op jit(solution)/shard_map/ppermute | solution.py:467
  31.8 4.1 %collective-permute-done.10.refs_9_ = bf16[2,64,1024]{2,1,0:T(8,128)(2,1)S(1)} collective-permute-done((bf16[2,64,1024]{2,1,0:T(8,128)(2,1)S(1)}, bf16[2,64,1024]{2,1,0:T(8,128)(2,1)S(1)}, u32[]{:S(2)}, u32[]{:S(2)}) %collective-permute-start.10) | collective-permute-done | bytes 262176 | tf_op jit(solution)/shard_map/ppermute | solution.py:467
  36.0 5.6 %collective-permute-done.11.refs_10_ = bf16[2,64,1024]{2,1,0:T(8,128)(2,1)S(1)} collective-permute-done((bf16[2,64,1024]{2,1,0:T(8,128)(2,1)S(1)}, bf16[2,64,1024]{2,1,0:T(8,128)(2,1)S(1)}, u32[]{:S(2)}, u32[]{:S(2)}) %collective-permute-start.11) | collective-permute-done | bytes 262176 | tf_op jit(solution)/shard_map/ppermute | solution.py:467
  41.5 2.0 %collective-permute-done.9.refs_8_ = bf16[2,64,1024]{2,1,0:T(8,128)(2,1)S(1)} collective-permute-done((bf16[2,64,1024]{2,1,0:T(8,128)(2,1)S(1)}, bf16[2,64,1024]{2,1,0:T(8,128)(2,1)S(1)}, u32[]{:S(2)}, u32[]{:S(2)}) %collective-permute-start.9) | collective-permute-done | bytes 262176 | tf_op jit(solution)/shard_map/ppermute | solution.py:467
  43.5 14.4 %shard_map.104 = (f32[2,64,1024]{2,1,0:T(8,128)S(1)}, bf16[2,64,1024]{2,1,0:T(8,128)(2,1)S(1)}, bf16[2,64,1024]{2,1,0:T(8,128)(2,1)S(1)}, bf16[2,64,1024]{2,1,0:T(8,128)(2,1)S(1)}) custom-call(s32[828]{0:T(1024)S(1)} %shard_map.100.table, bf16[24,512,256]{2,1,0:T(8,128)(2,1)} %refs_0_.8, bf16[24,512,256]{2,1,0:T(8,128)(2,1)} %collective-permute-done.5.refs_1_, ...), custom_call_target="tpu_custom_call" | custom-call | flops 6442450944 | bytes 12582912 | tf_op jit(solution)/shard_map/pallas_call | solution.py:128
  59.6 1.9 %collective-permute-start.17 = (bf16[2,64,1024]{2,1,0:T(8,128)(2,1)S(1)}, bf16[2,64,1024]{2,1,0:T(8,128)(2,1)S(1)}, u32[]{:S(2)}, u32[]{:S(2)}) collective-permute-start(bf16[2,64,1024]{2,1,0:T(8,128)(2,1)S(1)} %get-tuple-element.88), channel_id=1, source_target_pairs={{0,6},{2,4},{4,2},{6,0},{8,14},{10,12},{12,10},{14,8},{1,7},{3,5},... | collective-permute-start | bytes 786440 | tf_op jit(solution)/shard_map/ppermute | solution.py:467
  61.5 14.4 %shard_map.105 = (f32[1,64,1024]{2,1,0:T(8,128)S(1)}, f32[1,64,1024]{2,1,0:T(8,128)S(1)}, bf16[1,64,1024]{2,1,0:T(8,128)(2,1)S(1)}, bf16[1,64,1024]{2,1,0:T(8,12...) custom-call(s32[828]{0:T(1024)S(1)} %shard_map.100.table, ...), custom_call_target="tpu_custom_call" | custom-call | flops 6442450944 | bytes 12582912 | tf_op jit(solution)/shard_map/pallas_call | solution.py:128
  77.1 2.3 %collective-permute-start.20 = (bf16[1,64,1024]{2,1,0:T(8,128)(2,1)S(1)}, bf16[1,64,1024]{2,1,0:T(8,128)(2,1)S(1)}, u32[]{:S(2)}, u32[]{:S(2)}) collective-permute-start(bf16[1,64,1024]{2,1,0:T(8,128)(2,1)S(1)} %get-tuple-element.99), channel_id=1, source_target_pairs={{0,6},{2,4},{4,2},{6,0},{8,14},{10,12},{12,10},{14,8},{1,7},{3,5},... | collective-permute-start | bytes 393224 | tf_op jit(solution)/shard_map/ppermute | solution.py:467
  82.0 2.5 %collective-permute-done.20.refs_7_ = bf16[1,64,1024]{2,1,0:T(8,128)(2,1)S(1)} collective-permute-done((bf16[1,64,1024]{2,1,0:T(8,128)(2,1)S(1)}, bf16[1,64,1024]{2,1,0:T(8,128)(2,1)S(1)}, u32[]{:S(2)}, u32[]{:S(2)}) %collective-permute-start.20) | collective-permute-done | bytes 131104 | tf_op jit(solution)/shard_map/ppermute | solution.py:467
  85.5 1.7 %collective-permute-start.22 = (bf16[1,64,1024]{2,1,0:T(8,128)(2,1)S(1)}, bf16[1,64,1024]{2,1,0:T(8,128)(2,1)S(1)}, u32[]{:S(2)}, u32[]{:S(2)}) collective-permute-start(bf16[1,64,1024]{2,1,0:T(8,128)(2,1)S(1)} %get-tuple-element.103), channel_id=1, source_target_pairs={{0,2},{2,0},{4,6},{6,4},{8,10},{10,8},{12,14},{14,12},{1,3},{3,1},... | collective-permute-start | bytes 393224 | tf_op jit(solution)/shard_map/ppermute | solution.py:467
  90.5 1.9 %collective-permute-done.23.refs_6_ = bf16[1,64,1024]{2,1,0:T(8,128)(2,1)S(1)} collective-permute-done((bf16[1,64,1024]{2,1,0:T(8,128)(2,1)S(1)}, bf16[1,64,1024]{2,1,0:T(8,128)(2,1)S(1)}, u32[]{:S(2)}, u32[]{:S(2)}) %collective-permute-start.23) | collective-permute-done | bytes 131104 | tf_op jit(solution)/shard_map/ppermute | solution.py:467
  92.3 2.5 %collective-permute-done.24.refs_7_ = bf16[1,64,1024]{2,1,0:T(8,128)(2,1)S(1)} collective-permute-done((bf16[1,64,1024]{2,1,0:T(8,128)(2,1)S(1)}, bf16[1,64,1024]{2,1,0:T(8,128)(2,1)S(1)}, u32[]{:S(2)}, u32[]{:S(2)}) %collective-permute-start.24) | collective-permute-done | bytes 131104 | tf_op jit(solution)/shard_map/ppermute | solution.py:467
  95.8 1.7 %collective-permute-start.25 = (bf16[1,64,2048]{2,1,0:T(8,128)(2,1)S(1)}, bf16[1,64,2048]{2,1,0:T(8,128)(2,1)S(1)}, u32[]{:S(2)}, u32[]{:S(2)}) collective-permute-start(bf16[1,64,2048]{2,1,0:T(8,128)(2,1)S(1)} %shard_map.107), channel_id=1, source_target_pairs={{0,8},{2,10},{4,12},{6,14},{8,0},{10,2},{12,4},{14,6},{1,9},{3,11}... | collective-permute-start | bytes 786440 | tf_op jit(solution)/shard_map/ppermute | solution.py:467
  97.4 9.2 %collective-permute-done.21.refs_9_ = bf16[1,64,2048]{2,1,0:T(8,128)(2,1)S(1)} collective-permute-done((bf16[1,64,2048]{2,1,0:T(8,128)(2,1)S(1)}, bf16[1,64,2048]{2,1,0:T(8,128)(2,1)S(1)}, u32[]{:S(2)}, u32[]{:S(2)}) %collective-permute-start.21) | collective-permute-done | bytes 262176 | tf_op jit(solution)/shard_map/ppermute | solution.py:467
  106.7 2.8 %collective-permute-done.25.refs_10_ = bf16[1,64,2048]{2,1,0:T(8,128)(2,1)S(1)} collective-permute-done((bf16[1,64,2048]{2,1,0:T(8,128)(2,1)S(1)}, bf16[1,64,2048]{2,1,0:T(8,128)(2,1)S(1)}, u32[]{:S(2)}, u32[]{:S(2)}) %collective-permute-start.25) | collective-permute-done | bytes 262176 | tf_op jit(solution)/shard_map/ppermute | solution.py:467
  (45 shorter events, 20.5 us)
Async XLA Ops:
  0.0 21.1 %collective-permute-start.5 = (bf16[24,512,256]{2,1,0:T(8,128)(2,1)}, bf16[24,512,256]{2,1,0:T(8,128)(2,1)}, u32[]{:S(2)}, u32[]{:S(2)}) collective-permute-start(bf16[24,512,256]{2,1,0:T(8,128)(2,1)} %refs_0_.8), channel_id=1, source_target_pairs={{0,1},{1,0},{2,3},{3,2},{4,5},{5,4},{6,7},{7,6},{8,9},{9,8},{10,11... | collective-permute-start | bytes 18874376 | tf_op jit(solution)/shard_map/ppermute | solution.py:470
  1.3 28.9 %collective-permute-start.8 = (bf16[2,64,2048]{2,1,0:T(8,128)(2,1)S(1)}, bf16[2,64,2048]{2,1,0:T(8,128)(2,1)S(1)}, u32[]{:S(2)}, u32[]{:S(2)}) collective-permute-start(bf16[2,64,2048]{2,1,0:T(8,128)(2,1)S(1)} %dynamic-slice_bitcast_fusion.refs_4_), channel_id=1, source_target_pairs={{0,8},{2,10},{4,12},{6,14},{8,0},{10,2},{12,4},{14,6},{1,9},{3,11}... | collective-permute-start | bytes 1572872 | tf_op jit(solution)/shard_map/ppermute | solution.py:467
  5.4 15.7 %collective-permute-start.6 = (f32[3,24,256]{2,1,0:T(8,128)}, f32[3,24,256]{2,1,0:T(8,128)S(1)}, u32[]{:S(2)}, u32[]{:S(2)}) collective-permute-start(f32[3,24,256]{2,1,0:T(8,128)} %bitcast.16), channel_id=1, source_target_pairs={{0,1},{1,0},{2,3},{3,2},{4,5},{5,4},{6,7},{7,6},{8,9},{9,8},{10,11... | collective-permute-start | bytes 221192 | tf_op jit(solution)/shard_map/ppermute | solution.py:470
  5.4 14.1 %collective-permute-start.7 = (f32[24,256]{1,0:T(8,128)}, f32[24,256]{1,0:T(8,128)S(1)}, u32[]{:S(2)}, u32[]{:S(2)}) collective-permute-start(f32[24,256]{1,0:T(8,128)} %refs_4_.1), channel_id=1, source_target_pairs={{0,1},{1,0},{2,3},{3,2},{4,5},{5,4},{6,7},{7,6},{8,9},{9,8},{10,11... | collective-permute-start | bytes 73736 | tf_op jit(solution)/shard_map/ppermute | solution.py:470
  5.9 4.7 %collective-permute-start.4 = (s32[24]{0:T(128)}, s32[24]{0:T(128)S(1)}, u32[]{:S(2)}, u32[]{:S(2)}) collective-permute-start(s32[24]{0:T(128)} %counts_a.1), channel_id=1, source_target_pairs={{0,1},{1,0},{2,3},{3,2},{4,5},{5,4},{6,7},{7,6},{8,9},{9,8},{10,11... | collective-permute-start | bytes 296 | tf_op jit(solution)/shard_map/ppermute | solution.py:470
  13.1 8.0 %collective-permute-start = (s32[1,8]{1,0:T(1,128)}, s32[1,8]{1,0:T(1,128)S(1)}, u32[]{:S(2)}, u32[]{:S(2)}) collective-permute-start(s32[1,8]{1,0:T(1,128)} %refs_0_.11), channel_id=1, source_target_pairs={{0,2},{2,0},{4,6},{6,4},{8,10},{10,8},{12,14},{14,12},{1,3},{3,1},... | collective-permute-start | bytes 104 | tf_op jit(solution)/shard_map/ppermute | solution.py:467
  21.1 4.6 %collective-permute-start.2 = (s32[1,8]{1,0:T(1,128)}, s32[1,8]{1,0:T(1,128)S(1)}, u32[]{:S(2)}, u32[]{:S(2)}) collective-permute-start(s32[1,8]{1,0:T(1,128)} %refs_0_.11), channel_id=1, source_target_pairs={{0,6},{2,4},{4,2},{6,0},{8,14},{10,12},{12,10},{14,8},{1,7},{3,5},... | collective-permute-start | bytes 104 | tf_op jit(solution)/shard_map/ppermute | solution.py:467
  26.6 9.3 %collective-permute-start.10 = (bf16[2,64,1024]{2,1,0:T(8,128)(2,1)S(1)}, bf16[2,64,1024]{2,1,0:T(8,128)(2,1)S(1)}, u32[]{:S(2)}, u32[]{:S(2)}) collective-permute-start(bf16[2,64,1024]{2,1,0:T(8,128)(2,1)S(1)} %get-tuple-element.71), channel_id=1, source_target_pairs={{0,4},{2,6},{4,0},{6,2},{8,12},{10,14},{12,8},{14,10},{1,5},{3,7},... | collective-permute-start | bytes 786440 | tf_op jit(solution)/shard_map/ppermute | solution.py:467
  27.1 14.4 %collective-permute-start.11 = (bf16[2,64,1024]{2,1,0:T(8,128)(2,1)S(1)}, bf16[2,64,1024]{2,1,0:T(8,128)(2,1)S(1)}, u32[]{:S(2)}, u32[]{:S(2)}) collective-permute-start(bf16[2,64,1024]{2,1,0:T(8,128)(2,1)S(1)} %get-tuple-element.72), channel_id=1, source_target_pairs={{0,6},{2,4},{4,2},{6,0},{8,14},{10,12},{12,10},{14,8},{1,7},{3,5},... | collective-permute-start | bytes 786440 | tf_op jit(solution)/shard_map/ppermute | solution.py:467
  28.7 14.9 %collective-permute-start.9 = (bf16[2,64,1024]{2,1,0:T(8,128)(2,1)S(1)}, bf16[2,64,1024]{2,1,0:T(8,128)(2,1)S(1)}, u32[]{:S(2)}, u32[]{:S(2)}) collective-permute-start(bf16[2,64,1024]{2,1,0:T(8,128)(2,1)S(1)} %get-tuple-element.70), channel_id=1, source_target_pairs={{0,2},{2,0},{4,6},{6,4},{8,10},{10,8},{12,14},{14,12},{1,3},{3,1},... | collective-permute-start | bytes 786440 | tf_op jit(solution)/shard_map/ppermute | solution.py:467
  31.1 28.4 %collective-permute-start.12 = (bf16[2,64,1024]{2,1,0:T(8,128)(2,1)S(1)}, bf16[2,64,1024]{2,1,0:T(8,128)(2,1)S(1)}, u32[]{:S(2)}, u32[]{:S(2)}) collective-permute-start(bf16[2,64,1024]{2,1,0:T(8,128)(2,1)S(1)} %get-tuple-element.75), channel_id=1, source_target_pairs={{0,2},{2,0},{4,6},{6,4},{8,10},{10,8},{12,14},{14,12},{1,3},{3,1},... | collective-permute-start | bytes 786440 | tf_op jit(solution)/shard_map/ppermute | solution.py:467
  31.7 29.8 %collective-permute-start.13 = (bf16[2,64,1024]{2,1,0:T(8,128)(2,1)S(1)}, bf16[2,64,1024]{2,1,0:T(8,128)(2,1)S(1)}, u32[]{:S(2)}, u32[]{:S(2)}) collective-permute-start(bf16[2,64,1024]{2,1,0:T(8,128)(2,1)S(1)} %get-tuple-element.76), channel_id=1, source_target_pairs={{0,4},{2,6},{4,0},{6,2},{8,12},{10,14},{12,8},{14,10},{1,5},{3,7},... | collective-permute-start | bytes 786440 | tf_op jit(solution)/shard_map/ppermute | solution.py:467
  35.9 25.6 %collective-permute-start.14 = (bf16[2,64,1024]{2,1,0:T(8,128)(2,1)S(1)}, bf16[2,64,1024]{2,1,0:T(8,128)(2,1)S(1)}, u32[]{:S(2)}, u32[]{:S(2)}) collective-permute-start(bf16[2,64,1024]{2,1,0:T(8,128)(2,1)S(1)} %get-tuple-element.77), channel_id=1, source_target_pairs={{0,6},{2,4},{4,2},{6,0},{8,14},{10,12},{12,10},{14,8},{1,7},{3,5},... | collective-permute-start | bytes 786440 | tf_op jit(solution)/shard_map/ppermute | solution.py:467
  57.9 18.0 %collective-permute-start.15 = (bf16[2,64,1024]{2,1,0:T(8,128)(2,1)S(1)}, bf16[2,64,1024]{2,1,0:T(8,128)(2,1)S(1)}, u32[]{:S(2)}, u32[]{:S(2)}) collective-permute-start(bf16[2,64,1024]{2,1,0:T(8,128)(2,1)S(1)} %get-tuple-element.86), channel_id=1, source_target_pairs={{0,2},{2,0},{4,6},{6,4},{8,10},{10,8},{12,14},{14,12},{1,3},{3,1},... | collective-permute-start | bytes 786440 | tf_op jit(solution)/shard_map/ppermute | solution.py:467
  59.3 16.7 %collective-permute-start.16 = (bf16[2,64,1024]{2,1,0:T(8,128)(2,1)S(1)}, bf16[2,64,1024]{2,1,0:T(8,128)(2,1)S(1)}, u32[]{:S(2)}, u32[]{:S(2)}) collective-permute-start(bf16[2,64,1024]{2,1,0:T(8,128)(2,1)S(1)} %get-tuple-element.87), channel_id=1, source_target_pairs={{0,4},{2,6},{4,0},{6,2},{8,12},{10,14},{12,8},{14,10},{1,5},{3,7},... | collective-permute-start | bytes 786440 | tf_op jit(solution)/shard_map/ppermute | solution.py:467
  59.6 16.4 %collective-permute-start.17 = (bf16[2,64,1024]{2,1,0:T(8,128)(2,1)S(1)}, bf16[2,64,1024]{2,1,0:T(8,128)(2,1)S(1)}, u32[]{:S(2)}, u32[]{:S(2)}) collective-permute-start(bf16[2,64,1024]{2,1,0:T(8,128)(2,1)S(1)} %get-tuple-element.88), channel_id=1, source_target_pairs={{0,6},{2,4},{4,2},{6,0},{8,14},{10,12},{12,10},{14,8},{1,7},{3,5},... | collective-permute-start | bytes 786440 | tf_op jit(solution)/shard_map/ppermute | solution.py:467
  75.9 5.0 %collective-permute-start.18 = (bf16[1,64,1024]{2,1,0:T(8,128)(2,1)S(1)}, bf16[1,64,1024]{2,1,0:T(8,128)(2,1)S(1)}, u32[]{:S(2)}, u32[]{:S(2)}) collective-permute-start(bf16[1,64,1024]{2,1,0:T(8,128)(2,1)S(1)} %get-tuple-element.95), channel_id=1, source_target_pairs={{0,2},{2,0},{4,6},{6,4},{8,10},{10,8},{12,14},{14,12},{1,3},{3,1},... | collective-permute-start | bytes 393224 | tf_op jit(solution)/shard_map/ppermute | solution.py:467
  77.0 5.0 %collective-permute-start.19 = (bf16[1,64,1024]{2,1,0:T(8,128)(2,1)S(1)}, bf16[1,64,1024]{2,1,0:T(8,128)(2,1)S(1)}, u32[]{:S(2)}, u32[]{:S(2)}) collective-permute-start(bf16[1,64,1024]{2,1,0:T(8,128)(2,1)S(1)} %get-tuple-element.97), channel_id=1, source_target_pairs={{0,4},{2,6},{4,0},{6,2},{8,12},{10,14},{12,8},{14,10},{1,5},{3,7},... | collective-permute-start | bytes 393224 | tf_op jit(solution)/shard_map/ppermute | solution.py:467
  77.1 7.3 %collective-permute-start.20 = (bf16[1,64,1024]{2,1,0:T(8,128)(2,1)S(1)}, bf16[1,64,1024]{2,1,0:T(8,128)(2,1)S(1)}, u32[]{:S(2)}, u32[]{:S(2)}) collective-permute-start(bf16[1,64,1024]{2,1,0:T(8,128)(2,1)S(1)} %get-tuple-element.99), channel_id=1, source_target_pairs={{0,6},{2,4},{4,2},{6,0},{8,14},{10,12},{12,10},{14,8},{1,7},{3,5},... | collective-permute-start | bytes 393224 | tf_op jit(solution)/shard_map/ppermute | solution.py:467
  85.5 5.0 %collective-permute-start.22 = (bf16[1,64,1024]{2,1,0:T(8,128)(2,1)S(1)}, bf16[1,64,1024]{2,1,0:T(8,128)(2,1)S(1)}, u32[]{:S(2)}, u32[]{:S(2)}) collective-permute-start(bf16[1,64,1024]{2,1,0:T(8,128)(2,1)S(1)} %get-tuple-element.103), channel_id=1, source_target_pairs={{0,2},{2,0},{4,6},{6,4},{8,10},{10,8},{12,14},{14,12},{1,3},{3,1},... | collective-permute-start | bytes 393224 | tf_op jit(solution)/shard_map/ppermute | solution.py:467
  87.2 5.1 %collective-permute-start.23 = (bf16[1,64,1024]{2,1,0:T(8,128)(2,1)S(1)}, bf16[1,64,1024]{2,1,0:T(8,128)(2,1)S(1)}, u32[]{:S(2)}, u32[]{:S(2)}) collective-permute-start(bf16[1,64,1024]{2,1,0:T(8,128)(2,1)S(1)} %get-tuple-element.104), channel_id=1, source_target_pairs={{0,4},{2,6},{4,0},{6,2},{8,12},{10,14},{12,8},{14,10},{1,5},{3,7},... | collective-permute-start | bytes 393224 | tf_op jit(solution)/shard_map/ppermute | solution.py:467
  88.0 6.8 %collective-permute-start.24 = (bf16[1,64,1024]{2,1,0:T(8,128)(2,1)S(1)}, bf16[1,64,1024]{2,1,0:T(8,128)(2,1)S(1)}, u32[]{:S(2)}, u32[]{:S(2)}) collective-permute-start(bf16[1,64,1024]{2,1,0:T(8,128)(2,1)S(1)} %get-tuple-element.105), channel_id=1, source_target_pairs={{0,6},{2,4},{4,2},{6,0},{8,14},{10,12},{12,10},{14,8},{1,7},{3,5},... | collective-permute-start | bytes 393224 | tf_op jit(solution)/shard_map/ppermute | solution.py:467
  89.0 17.7 %collective-permute-start.21 = (bf16[1,64,2048]{2,1,0:T(8,128)(2,1)S(1)}, bf16[1,64,2048]{2,1,0:T(8,128)(2,1)S(1)}, u32[]{:S(2)}, u32[]{:S(2)}) collective-permute-start(bf16[1,64,2048]{2,1,0:T(8,128)(2,1)S(1)} %shard_map.106), channel_id=1, source_target_pairs={{0,8},{2,10},{4,12},{6,14},{8,0},{10,2},{12,4},{14,6},{1,9},{3,11}... | collective-permute-start | bytes 786440 | tf_op jit(solution)/shard_map/ppermute | solution.py:467
  95.8 13.7 %collective-permute-start.25 = (bf16[1,64,2048]{2,1,0:T(8,128)(2,1)S(1)}, bf16[1,64,2048]{2,1,0:T(8,128)(2,1)S(1)}, u32[]{:S(2)}, u32[]{:S(2)}) collective-permute-start(bf16[1,64,2048]{2,1,0:T(8,128)(2,1)S(1)} %shard_map.107), channel_id=1, source_target_pairs={{0,8},{2,10},{4,12},{6,14},{8,0},{10,2},{12,4},{14,6},{1,9},{3,11}... | collective-permute-start | bytes 786440 | tf_op jit(solution)/shard_map/ppermute | solution.py:467
  (4 other events, 9.1 us)

commit v6 on v4

--- a/solution.py
+++ b/solution.py
@@ -274,51 +274,52 @@
 
 
 def merge_kernel(peers, *refs):
-    sets, terms, out, total = refs[:peers], refs[peers : 2 * peers], refs[-2], refs[-1]
-    add_up(sets, terms, total)
-    out[...] = total[...].astype(out.dtype)
-
-
-def merge(sets, terms, cols):
-    nb, sub, wide = terms[0].shape
-    shape = (nb, sub, cols)
-    return call(
-        functools.partial(merge_kernel, len(terms)),
-        sets,
-        terms,
-        [whole(t.shape) for t in terms],
-        jax.ShapeDtypeStruct(shape, jnp.bfloat16),
-        whole(shape),
-        [pltpu.VMEM(shape, jnp.float32)],
-        cost=(0, 2 * nb * sub * (cols + 5 * wide)),
-    )
-
-
-def finish_kernel(peers, *refs):
     sets, core = refs[:peers], refs[peers]
-    terms, fars = refs[peers + 1 : 2 * peers + 1], refs[2 * peers + 1 : -3]
+    terms = refs[peers + 1 : 2 * peers + 1]
     keep, give, total = refs[-3:]
     add_up(sets, terms, total)
     half = keep.shape[2]
     for out, side in ((keep, core[0]), (give, 1 - core[0])):
-        cols = pl.ds(pl.multiple_of(side * half, FB), half)
-        for b, far in enumerate(fars):
-            out[b] = (total[b, :, cols] + far[0, :, cols].astype(jnp.float32)).astype(out.dtype)
-
-
-def finish(sets, core, terms, fars):
+        out[...] = total[:, :, pl.ds(pl.multiple_of(side * half, FB), half)].astype(out.dtype)
+
+
+def merge(sets, core, terms, cols, dtype):
     nb, sub, wide = terms[0].shape
-    cols = fars[0].shape[2]
     shape = (nb, sub, cols // 2)
     return call(
-        functools.partial(finish_kernel, len(terms)),
+        functools.partial(merge_kernel, len(terms)),
         [*sets, core],
-        [*terms, *fars],
-        [whole(t.shape) for t in (*terms, *fars)],
-        [jax.ShapeDtypeStruct(shape, jnp.bfloat16)] * 2,
+        terms,
+        [whole(t.shape) for t in terms],
+        [jax.ShapeDtypeStruct(shape, dtype)] * 2,
         [whole(shape)] * 2,
         [pltpu.VMEM((nb, sub, cols), jnp.float32)],
-        cost=(0, 2 * nb * sub * (2 * cols + 5 * wide)),
+        cost=(0, 2 * nb * sub * (cols + 5 * wide)),
+    )
+
+
+def finish_kernel(nb, core, *refs):
+    out = refs[-1]
+    for other in (0, 1):
+        near, fars = refs[other], refs[2 + other * nb : 2 + (other + 1) * nb]
+        side = (1 - core[0]) if other else core[0]
+        for b in range(nb):
+            out[b, side] = (near[b] + fars[b][0].astype(jnp.float32)).astype(out.dtype)
+
+
+def finish(core, nears, fars):
+    nb, sub, wide = nears[0].shape
+    shape = (nb, 2, sub, wide)
+    arrays = [*nears, *(far[0] for far in fars), *(far[1] for far in fars)]
+    return call(
+        functools.partial(finish_kernel, nb),
+        [core],
+        arrays,
+        [whole(t.shape) for t in arrays],
+        jax.ShapeDtypeStruct(shape, jnp.bfloat16),
+        whole(shape),
+        [],
+        cost=(0, 16 * nb * sub * wide),
     )
 
 
@@ -469,21 +470,27 @@
     def across(x):
         return lax.ppermute(x, "rows", [(a, cores - 1 - a) for a in range(cores)])
 
+    def swap_both(x):
+        pairs = [(a, (a // cores ^ near) * cores + cores - 1 - a % cores) for a in range(n * cores)]
+        return lax.ppermute(x, ("dom", "rows"), pairs)
+
     def stay(x):
         return pltpu.with_memory_space_constraint(x, pltpu.HBM)
 
     own = lax.dynamic_index_in_dim(density.reshape(nb, cores, sub, cols), r, 1, keepdims=False)
+    sets = [touched] + [swap(touched, k) for k in range(1, near)]
+    small = (points.transpose(1, 0, 2), weights, counts, blocks)
+    small_b = [across(x) for x in small]
+    own, sets, basis, small_b = lax.optimization_barrier((own, sets, basis, small_b))
     far = swap(own, near)
-    sets = [touched] + [swap(touched, k) for k in range(1, near)]
-    points = points.transpose(1, 0, 2)
-    both = [(stay(x), across(x)) for x in (basis, points, weights, counts)] + [(blocks, across(blocks))]
     sets[0] = stay(touched)
-    table = batch_tables(i.reshape(1), stay(owner), sets[0], both[4], both[3], nb, near)
-    centre = centre_rows(sets[0], core, stay(centers), stay(widths.reshape(1, -1)), sub)
-
     picked = pick(sets, own)
     parts = [picked[0]] + [swap(picked[k], k) for k in range(1, near)]
-    far, table, centre, own_part = lax.optimization_barrier((far, table, centre, picked[0]))
+    both = [(stay(basis), across(basis))] + [(stay(x), y) for x, y in zip(small[:3], small_b)]
+    table = batch_tables(i.reshape(1), stay(owner), sets[0], (small[3], small_b[3]), both[3], nb, near)
+    centre = centre_rows(sets[0], core, stay(centers), stay(widths.reshape(1, -1)), sub)
+
+    far, table, centre = lax.optimization_barrier((far, table, centre))
     picked = pick(sets, far)
     far_parts = [picked[0]] + [swap(picked[k], k) for k in range(1, near)]
     table, _ = lax.optimization_barrier((table, picked[0]))
@@ -494,12 +501,19 @@
     far_sums = batch_sums(table, *common, far_parts, True)
     terms = [sums[0]] + [swap(sums[k], k) for k in range(1, near)]
     far_sums, terms = lax.optimization_barrier((far_sums, terms))
-    chunks = [[far_sums[b]] + [swap(far_sums[nb * k + b], k) for k in range(1, near)] for b in range(nb)]
-    far_terms = [swap(merge(sets, chunk, cols), near) for chunk in chunks]
-    keep, give = finish(sets, core, terms, far_terms)
-    got = across(give)
-    pair = jnp.where(r == 0, jnp.stack([keep, got], axis=1), jnp.stack([got, keep], axis=1))
-    return pair.reshape(nb * FB, cols // cores)
+    nears = merge(sets, core, terms, cols, jnp.float32)
+    fars = []
+    for b in range(nb):
+        chunk = [far_sums[b]] + [swap(far_sums[nb * k + b], k) for k in range(1, near)]
+        if b == 0:
+            chunk, nears = lax.optimization_barrier((chunk, nears))
+        else:
+            chunk, fars[-1] = lax.optimization_barrier((chunk, fars[-1]))
+        halves = merge(sets, core, chunk, cols, jnp.bfloat16)
+        far_sums, halves, nears = lax.optimization_barrier((far_sums, halves, nears))
+        fars.append((swap(halves[0], near), swap_both(halves[1])))
+    nears = (nears[0], across(nears[1]))
+    return finish(core, nears, fars).reshape(nb * FB, cols // cores)
 
 
 def solution(mesh):

time: 113 us -> 116 us (1.027)
  waiting for transfers between devices: 32.7 us -> 40.7 us
  starting transfers between devices: 36.5 us -> 33.7 us
  local copies, waits for them, and re-layouts: 2.4 us -> 0.8 us
    ppermute x21, waiting for transfers between devices: 31.2 us -> 37.8 us  [swap(): return lax.ppermute(x, 'dom', [(a, a ^ k) for a in range(n)])]
    ppermute x21, starting transfers between devices: 35.4 us -> 30.5 us  [swap(): return lax.ppermute(x, 'dom', [(a, a ^ k) for a in range(n)])]
    ppermute x0 -> x2, waiting for transfers between devices: none -> 2.91 us  [swap_both(): return lax.ppermute(x, ('dom', 'rows'), pairs)]
    ppermute x0 -> x2, starting transfers between devices: none -> 2.53 us  [swap_both(): return lax.ppermute(x, ('dom', 'rows'), pairs)]
    ppermute x6, waiting for transfers between devices: 1.53 us -> 0.02 us  [across(): return lax.ppermute(x, 'rows', [(a, cores - 1 - a) for a in range(cores)])]
    pallas_call x9 -> x10, Pallas kernels: 39.9 us -> 39.9 us  [call(): pl.pallas_call(kernel, grid_spec=pltpu.PrefetchScalarGridSpec(num_scalar_...]
  transfers between devices with their start and end apart: 27 -> 29, of which waited for: 9 -> 12; matrix products, arithmetic and copies ran while one was open for 1% -> 1% of each run, Pallas kernels for 35% -> 32%
where the time goes in v6:
time: 116 us; the launch traced here: 115 us
  waiting for transfers between devices  40.7 us (35%)
  Pallas kernels  39.9 us (34%)
  starting transfers between devices  33.7 us (29%)
    pallas_call x10, Pallas kernels, call(): pl.pallas_call(kernel, grid_spec=pltpu.PrefetchScalarGridSpec(num_scalar_...  39.9 us
    ppermute x21, waiting for transfers between devices, swap(): return lax.ppermute(x, 'dom', [(a, a ^ k) for a in range(n)])  37.8 us
    ppermute x21, starting transfers between devices, swap(): return lax.ppermute(x, 'dom', [(a, a ^ k) for a in range(n)])  30.5 us
    ppermute x2, waiting for transfers between devices, swap_both(): return lax.ppermute(x, ('dom', 'rows'), pairs)  2.91 us
    ppermute x2, starting transfers between devices, swap_both(): return lax.ppermute(x, ('dom', 'rows'), pairs)  2.53 us
  transfers between devices with their start and end apart: 29, of which 12 were waited for; matrix products, arithmetic and copies ran while one was open for 1% of the time, Pallas kernels for 32%

profile of v6, /device:TPU:0, one launch (start us, length us, event | category | flops | bytes accessed | tf_op | source)
XLA Modules:
  0.0 115.3 jit_solution(63948383920247294)
XLA Ops:
  0.0 4.0 %collective-permute-start.2 = (s32[1,8]{1,0:T(1,128)}, s32[1,8]{1,0:T(1,128)S(1)}, u32[]{:S(2)}, u32[]{:S(2)}) collective-permute-start(s32[1,8]{1,0:T(1,128)} %refs_0_.11), channel_id=1, source_target_pairs={{0,6},{2,4},{4,2},{6,0},{8,14},{10,12},{12,10},{14,8},{1,7},{3,5},... | collective-permute-start | bytes 104 | tf_op jit(solution)/shard_map/ppermute | solution.py:468
  5.8 1.8 %collective-permute-start = (s32[1,8]{1,0:T(1,128)}, s32[1,8]{1,0:T(1,128)S(1)}, u32[]{:S(2)}, u32[]{:S(2)}) collective-permute-start(s32[1,8]{1,0:T(1,128)} %refs_0_.11), channel_id=1, source_target_pairs={{0,2},{2,0},{4,6},{6,4},{8,10},{10,8},{12,14},{14,12},{1,3},{3,1},... | collective-permute-start | bytes 104 | tf_op jit(solution)/shard_map/ppermute | solution.py:468
  7.7 1.8 %collective-permute-done.refs_1_ = s32[1,8]{1,0:T(1,128)S(1)} collective-permute-done((s32[1,8]{1,0:T(1,128)}, s32[1,8]{1,0:T(1,128)S(1)}, u32[]{:S(2)}, u32[]{:S(2)}) %collective-permute-start) | collective-permute-done | bytes 64 | tf_op jit(solution)/shard_map/ppermute | solution.py:468
  9.6 2.9 %collective-permute-start.7 = (bf16[2,64,2048]{2,1,0:T(8,128)(2,1)S(1)}, bf16[2,64,2048]{2,1,0:T(8,128)(2,1)S(1)}, u32[]{:S(2)}, u32[]{:S(2)}) collective-permute-start(bf16[2,64,2048]{2,1,0:T(8,128)(2,1)S(1)} %dynamic-slice_bitcast_fusion.refs_4_), channel_id=1, source_target_pairs={{0,8},{2,10},{4,12},{6,14},{8,0},{10,2},{12,4},{14,6},{1,9},{3,11}... | collective-permute-start | bytes 1572872 | tf_op jit(solution)/shard_map/ppermute | solution.py:468
  12.5 1.7 %shard_map.103 = (bf16[2,64,1024]{2,1,0:T(8,128)(2,1)S(1)}, bf16[2,64,1024]{2,1,0:T(8,128)(2,1)}, bf16[2,64,1024]{2,1,0:T(8,128)(2,1)}, bf16[2,64,1024]{2,1,0:T(8,128)(2,1)S(1)}) custom-call(s32[1,8]{1,0:T(1,128)} %refs_0_.11, s32[1,8]{1,0:T(1,128)S(1)} %collective-permute-done.refs_1_, s32[1,8]{1,0:T(1,128)S(1)} %collective-permute-done.1.refs_2_, ...), custom_call_target="tpu_custom_call" | custom-call | bytes 1572864 | tf_op jit(solution)/shard_map/pallas_call | solution.py:128
  17.7 2.1 %shard_map.101.refs_6_ = f32[4,8,64,128]{3,2,1,0:T(8,128)S(1)} custom-call(s32[1,8]{1,0:T(1,128)} %refs_0_.11, s32[1]{0:T(128)} %bitcast.core.refs_4_, f32[3,2048]{1,0:T(4,128)} %centers.1, f32[1,2048]{1,0:T(1,128)} %bitcast.11), custom_call_target="tpu_custom_call" | custom-call | bytes 2097152 | tf_op jit(solution)/shard_map/pallas_call | solution.py:128
  19.8 3.6 %shard_map.100.table = s32[828]{0:T(1024)S(1)} custom-call(s32[1]{0:T(128)} %bitcast.4.me, s32[16]{0:T(128)} %owner.1, s32[1,8]{1,0:T(1,128)} %refs_0_.11, s32[24,4]{1,0:T(8,128)S(1)} %copy.12.blocks_a, s32[24,4]{1,0:T(8,128)S(1)} %collective-permute-done.6.blocks_b, s32[24]{0:T(128)} %counts_a.1, s32[24]{0:T(128)S(1)} %collective-permute-done.5.counts_b), custom_call_target="tpu_custom_call" | custom-call | bytes 1536 | tf_op jit(solution)/shard_map/pallas_call | solution.py:128
  23.4 12.9 %collective-permute-done.7.refs_4_ = bf16[2,64,2048]{2,1,0:T(8,128)(2,1)S(1)} collective-permute-done((bf16[2,64,2048]{2,1,0:T(8,128)(2,1)S(1)}, bf16[2,64,2048]{2,1,0:T(8,128)(2,1)S(1)}, u32[]{:S(2)}, u32[]{:S(2)}) %collective-permute-start.7) | collective-permute-done | bytes 524320 | tf_op jit(solution)/shard_map/ppermute | solution.py:468
  37.3 1.6 %collective-permute-start.12 = (bf16[2,64,1024]{2,1,0:T(8,128)(2,1)S(1)}, bf16[2,64,1024]{2,1,0:T(8,128)(2,1)S(1)}, u32[]{:S(2)}, u32[]{:S(2)}) collective-permute-start(bf16[2,64,1024]{2,1,0:T(8,128)(2,1)S(1)} %get-tuple-element.101), channel_id=1, source_target_pairs={{0,2},{2,0},{4,6},{6,4},{8,10},{10,8},{12,14},{14,12},{1,3},{3,1},... | collective-permute-start | bytes 786440 | tf_op jit(solution)/shard_map/ppermute | solution.py:468
  40.8 13.7 %shard_map.104 = (f32[2,64,1024]{2,1,0:T(8,128)S(1)}, bf16[2,64,1024]{2,1,0:T(8,128)(2,1)S(1)}, bf16[2,64,1024]{2,1,0:T(8,128)(2,1)S(1)}, bf16[2,64,1024]{2,1,0:T(8,128)(2,1)S(1)}) custom-call(s32[828]{0:T(1024)S(1)} %shard_map.100.table, bf16[24,512,256]{2,1,0:T(8,128)(2,1)} %refs_0_.8, bf16[24,512,256]{2,1,0:T(8,128)(2,1)} %collective-permute-done.8.refs_1_, ...), custom_call_target="tpu_custom_call" | custom-call | flops 6442450944 | bytes 12582912 | tf_op jit(solution)/shard_map/pallas_call | solution.py:128
  54.6 1.9 %collective-permute-start.15 = (bf16[2,64,1024]{2,1,0:T(8,128)(2,1)S(1)}, bf16[2,64,1024]{2,1,0:T(8,128)(2,1)S(1)}, u32[]{:S(2)}, u32[]{:S(2)}) collective-permute-start(bf16[2,64,1024]{2,1,0:T(8,128)(2,1)S(1)} %get-tuple-element.112), channel_id=1, source_target_pairs={{0,2},{2,0},{4,6},{6,4},{8,10},{10,8},{12,14},{14,12},{1,3},{3,1},... | collective-permute-start | bytes 786440 | tf_op jit(solution)/shard_map/ppermute | solution.py:468
  58.1 13.7 %shard_map.105 = (f32[1,64,1024]{2,1,0:T(8,128)S(1)}, f32[1,64,1024]{2,1,0:T(8,128)S(1)}, bf16[1,64,1024]{2,1,0:T(8,128)(2,1)S(1)}, bf16[1,64,1024]{2,1,0:T(8,12...) custom-call(s32[828]{0:T(1024)S(1)} %shard_map.100.table, ...), custom_call_target="tpu_custom_call" | custom-call | flops 6442450944 | bytes 12582912 | tf_op jit(solution)/shard_map/pallas_call | solution.py:128
  71.9 2.1 %collective-permute-start.18 = (bf16[1,64,1024]{2,1,0:T(8,128)(2,1)S(1)}, bf16[1,64,1024]{2,1,0:T(8,128)(2,1)S(1)}, u32[]{:S(2)}, u32[]{:S(2)}) collective-permute-start(bf16[1,64,1024]{2,1,0:T(8,128)(2,1)S(1)} %get-tuple-element.117), channel_id=1, source_target_pairs={{0,2},{2,0},{4,6},{6,4},{8,10},{10,8},{12,14},{14,12},{1,3},{3,1},... | collective-permute-start | bytes 393224 | tf_op jit(solution)/shard_map/ppermute | solution.py:468
  74.0 2.4 %collective-permute-start.19 = (bf16[1,64,1024]{2,1,0:T(8,128)(2,1)S(1)}, bf16[1,64,1024]{2,1,0:T(8,128)(2,1)S(1)}, u32[]{:S(2)}, u32[]{:S(2)}) collective-permute-start(bf16[1,64,1024]{2,1,0:T(8,128)(2,1)S(1)} %get-tuple-element.119), channel_id=1, source_target_pairs={{0,4},{2,6},{4,0},{6,2},{8,12},{10,14},{12,8},{14,10},{1,5},{3,7},... | collective-permute-start | bytes 393224 | tf_op jit(solution)/shard_map/ppermute | solution.py:468
  77.9 1.6 %collective-permute-done.19.refs_7_ = bf16[1,64,1024]{2,1,0:T(8,128)(2,1)S(1)} collective-permute-done((bf16[1,64,1024]{2,1,0:T(8,128)(2,1)S(1)}, bf16[1,64,1024]{2,1,0:T(8,128)(2,1)S(1)}, u32[]{:S(2)}, u32[]{:S(2)}) %collective-permute-start.19) | collective-permute-done | bytes 131104 | tf_op jit(solution)/shard_map/ppermute | solution.py:468
  79.6 2.7 %collective-permute-done.20.refs_8_ = bf16[1,64,1024]{2,1,0:T(8,128)(2,1)S(1)} collective-permute-done((bf16[1,64,1024]{2,1,0:T(8,128)(2,1)S(1)}, bf16[1,64,1024]{2,1,0:T(8,128)(2,1)S(1)}, u32[]{:S(2)}, u32[]{:S(2)}) %collective-permute-start.20) | collective-permute-done | bytes 131104 | tf_op jit(solution)/shard_map/ppermute | solution.py:468
  83.2 2.7 %collective-permute-start.24 = (bf16[1,64,1024]{2,1,0:T(8,128)(2,1)S(1)}, bf16[1,64,1024]{2,1,0:T(8,128)(2,1)S(1)}, u32[]{:S(2)}, u32[]{:S(2)}) collective-permute-start(bf16[1,64,1024]{2,1,0:T(8,128)(2,1)S(1)} %get-tuple-element.141), channel_id=1, source_target_pairs={{0,8},{2,10},{4,12},{6,14},{8,0},{10,2},{12,4},{14,6},{1,9},{3,11}... | collective-permute-start | bytes 393224 | tf_op jit(solution)/shard_map/ppermute | solution.py:468
  86.1 1.8 %collective-permute-start.22 = (bf16[1,64,1024]{2,1,0:T(8,128)(2,1)S(1)}, bf16[1,64,1024]{2,1,0:T(8,128)(2,1)S(1)}, u32[]{:S(2)}, u32[]{:S(2)}) collective-permute-start(bf16[1,64,1024]{2,1,0:T(8,128)(2,1)S(1)} %get-tuple-element.139), channel_id=1, source_target_pairs={{0,4},{2,6},{4,0},{6,2},{8,12},{10,14},{12,8},{14,10},{1,5},{3,7},... | collective-permute-start | bytes 393224 | tf_op jit(solution)/shard_map/ppermute | solution.py:468
  89.4 5.1 %collective-permute-done.24.refs_2_ = bf16[1,64,1024]{2,1,0:T(8,128)(2,1)S(1)} collective-permute-done((bf16[1,64,1024]{2,1,0:T(8,128)(2,1)S(1)}, bf16[1,64,1024]{2,1,0:T(8,128)(2,1)S(1)}, u32[]{:S(2)}, u32[]{:S(2)}) %collective-permute-start.24) | collective-permute-done | bytes 131104 | tf_op jit(solution)/shard_map/ppermute | solution.py:468
  94.7 1.9 %collective-permute-done.22.refs_7_ = bf16[1,64,1024]{2,1,0:T(8,128)(2,1)S(1)} collective-permute-done((bf16[1,64,1024]{2,1,0:T(8,128)(2,1)S(1)}, bf16[1,64,1024]{2,1,0:T(8,128)(2,1)S(1)}, u32[]{:S(2)}, u32[]{:S(2)}) %collective-permute-start.22) | collective-permute-done | bytes 131104 | tf_op jit(solution)/shard_map/ppermute | solution.py:468
  96.5 2.1 %collective-permute-done.23.refs_8_ = bf16[1,64,1024]{2,1,0:T(8,128)(2,1)S(1)} collective-permute-done((bf16[1,64,1024]{2,1,0:T(8,128)(2,1)S(1)}, bf16[1,64,1024]{2,1,0:T(8,128)(2,1)S(1)}, u32[]{:S(2)}, u32[]{:S(2)}) %collective-permute-start.23) | collective-permute-done | bytes 131104 | tf_op jit(solution)/shard_map/ppermute | solution.py:468
  99.9 2.5 %collective-permute-start.28 = (bf16[1,64,1024]{2,1,0:T(8,128)(2,1)S(1)}, bf16[1,64,1024]{2,1,0:T(8,128)(2,1)S(1)}, u32[]{:S(2)}, u32[]{:S(2)}) collective-permute-start(bf16[1,64,1024]{2,1,0:T(8,128)(2,1)S(1)} %get-tuple-element.156), channel_id=1, source_target_pairs={{0,9},{1,8},{2,11},{3,10},{4,13},{5,12},{6,15},{7,14},{8,1},{9,0},... | collective-permute-start | bytes 393224 | tf_op jit(solution)/shard_map/ppermute | solution.py:475
  102.4 9.2 %collective-permute-done.27.refs_3_ = bf16[1,64,1024]{2,1,0:T(8,128)(2,1)S(1)} collective-permute-done((bf16[1,64,1024]{2,1,0:T(8,128)(2,1)S(1)}, bf16[1,64,1024]{2,1,0:T(8,128)(2,1)S(1)}, u32[]{:S(2)}, u32[]{:S(2)}) %collective-permute-start.27) | collective-permute-done | bytes 131104 | tf_op jit(solution)/shard_map/ppermute | solution.py:468
  111.7 2.7 %collective-permute-done.28.refs_5_ = bf16[1,64,1024]{2,1,0:T(8,128)(2,1)S(1)} collective-permute-done((bf16[1,64,1024]{2,1,0:T(8,128)(2,1)S(1)}, bf16[1,64,1024]{2,1,0:T(8,128)(2,1)S(1)}, u32[]{:S(2)}, u32[]{:S(2)}) %collective-permute-start.28) | collective-permute-done | bytes 131104 | tf_op jit(solution)/shard_map/ppermute | solution.py:475
  (48 shorter events, 16.6 us)
Async XLA Ops:
  0.0 5.7 %collective-permute-start.2 = (s32[1,8]{1,0:T(1,128)}, s32[1,8]{1,0:T(1,128)S(1)}, u32[]{:S(2)}, u32[]{:S(2)}) collective-permute-start(s32[1,8]{1,0:T(1,128)} %refs_0_.11), channel_id=1, source_target_pairs={{0,6},{2,4},{4,2},{6,0},{8,14},{10,12},{12,10},{14,8},{1,7},{3,5},... | collective-permute-start | bytes 104 | tf_op jit(solution)/shard_map/ppermute | solution.py:468
  5.2 4.3 %collective-permute-start.6 = (s32[24,4]{1,0:T(8,128)S(1)}, s32[24,4]{1,0:T(8,128)S(1)}, u32[]{:S(2)}, u32[]{:S(2)}) collective-permute-start(s32[24,4]{1,0:T(8,128)S(1)} %copy.12.blocks_a), channel_id=1, source_target_pairs={{0,1},{1,0},{2,3},{3,2},{4,5},{5,4},{6,7},{7,6},{8,9},{9,8},{10,11... | collective-permute-start | bytes 1160 | tf_op jit(solution)/shard_map/ppermute | solution.py:471
  9.5 31.3 %collective-permute-start.8 = (bf16[24,512,256]{2,1,0:T(8,128)(2,1)}, bf16[24,512,256]{2,1,0:T(8,128)(2,1)}, u32[]{:S(2)}, u32[]{:S(2)}) collective-permute-start(bf16[24,512,256]{2,1,0:T(8,128)(2,1)} %refs_0_.8), channel_id=1, source_target_pairs={{0,1},{1,0},{2,3},{3,2},{4,5},{5,4},{6,7},{7,6},{8,9},{9,8},{10,11... | collective-permute-start | bytes 18874376 | tf_op jit(solution)/shard_map/ppermute | solution.py:471
  9.6 26.7 %collective-permute-start.7 = (bf16[2,64,2048]{2,1,0:T(8,128)(2,1)S(1)}, bf16[2,64,2048]{2,1,0:T(8,128)(2,1)S(1)}, u32[]{:S(2)}, u32[]{:S(2)}) collective-permute-start(bf16[2,64,2048]{2,1,0:T(8,128)(2,1)S(1)} %dynamic-slice_bitcast_fusion.refs_4_), channel_id=1, source_target_pairs={{0,8},{2,10},{4,12},{6,14},{8,0},{10,2},{12,4},{14,6},{1,9},{3,11}... | collective-permute-start | bytes 1572872 | tf_op jit(solution)/shard_map/ppermute | solution.py:468
  14.2 24.7 %collective-permute-start.9 = (bf16[2,64,1024]{2,1,0:T(8,128)(2,1)}, bf16[2,64,1024]{2,1,0:T(8,128)(2,1)S(1)}, u32[]{:S(2)}, u32[]{:S(2)}) collective-permute-start(bf16[2,64,1024]{2,1,0:T(8,128)(2,1)} %get-tuple-element.96), channel_id=1, source_target_pairs={{0,2},{2,0},{4,6},{6,4},{8,10},{10,8},{12,14},{14,12},{1,3},{3,1},... | collective-permute-start | bytes 786440 | tf_op jit(solution)/shard_map/ppermute | solution.py:468
  15.7 23.8 %collective-permute-start.10 = (bf16[2,64,1024]{2,1,0:T(8,128)(2,1)}, bf16[2,64,1024]{2,1,0:T(8,128)(2,1)S(1)}, u32[]{:S(2)}, u32[]{:S(2)}) collective-permute-start(bf16[2,64,1024]{2,1,0:T(8,128)(2,1)} %get-tuple-element.97), channel_id=1, source_target_pairs={{0,4},{2,6},{4,0},{6,2},{8,12},{10,14},{12,8},{14,10},{1,5},{3,7},... | collective-permute-start | bytes 786440 | tf_op jit(solution)/shard_map/ppermute | solution.py:468
  17.3 23.5 %collective-permute-start.11 = (bf16[2,64,1024]{2,1,0:T(8,128)(2,1)S(1)}, bf16[2,64,1024]{2,1,0:T(8,128)(2,1)S(1)}, u32[]{:S(2)}, u32[]{:S(2)}) collective-permute-start(bf16[2,64,1024]{2,1,0:T(8,128)(2,1)S(1)} %get-tuple-element.98), channel_id=1, source_target_pairs={{0,6},{2,4},{4,2},{6,0},{8,14},{10,12},{12,10},{14,8},{1,7},{3,5},... | collective-permute-start | bytes 786440 | tf_op jit(solution)/shard_map/ppermute | solution.py:468
  37.3 20.7 %collective-permute-start.12 = (bf16[2,64,1024]{2,1,0:T(8,128)(2,1)S(1)}, bf16[2,64,1024]{2,1,0:T(8,128)(2,1)S(1)}, u32[]{:S(2)}, u32[]{:S(2)}) collective-permute-start(bf16[2,64,1024]{2,1,0:T(8,128)(2,1)S(1)} %get-tuple-element.101), channel_id=1, source_target_pairs={{0,2},{2,0},{4,6},{6,4},{8,10},{10,8},{12,14},{14,12},{1,3},{3,1},... | collective-permute-start | bytes 786440 | tf_op jit(solution)/shard_map/ppermute | solution.py:468
  38.9 19.2 %collective-permute-start.13 = (bf16[2,64,1024]{2,1,0:T(8,128)(2,1)S(1)}, bf16[2,64,1024]{2,1,0:T(8,128)(2,1)S(1)}, u32[]{:S(2)}, u32[]{:S(2)}) collective-permute-start(bf16[2,64,1024]{2,1,0:T(8,128)(2,1)S(1)} %get-tuple-element.102), channel_id=1, source_target_pairs={{0,4},{2,6},{4,0},{6,2},{8,12},{10,14},{12,8},{14,10},{1,5},{3,7},... | collective-permute-start | bytes 786440 | tf_op jit(solution)/shard_map/ppermute | solution.py:468
  39.6 18.6 %collective-permute-start.14 = (bf16[2,64,1024]{2,1,0:T(8,128)(2,1)S(1)}, bf16[2,64,1024]{2,1,0:T(8,128)(2,1)S(1)}, u32[]{:S(2)}, u32[]{:S(2)}) collective-permute-start(bf16[2,64,1024]{2,1,0:T(8,128)(2,1)S(1)} %get-tuple-element.103), channel_id=1, source_target_pairs={{0,6},{2,4},{4,2},{6,0},{8,14},{10,12},{12,10},{14,8},{1,7},{3,5},... | collective-permute-start | bytes 786440 | tf_op jit(solution)/shard_map/ppermute | solution.py:468
  54.6 17.3 %collective-permute-start.15 = (bf16[2,64,1024]{2,1,0:T(8,128)(2,1)S(1)}, bf16[2,64,1024]{2,1,0:T(8,128)(2,1)S(1)}, u32[]{:S(2)}, u32[]{:S(2)}) collective-permute-start(bf16[2,64,1024]{2,1,0:T(8,128)(2,1)S(1)} %get-tuple-element.112), channel_id=1, source_target_pairs={{0,2},{2,0},{4,6},{6,4},{8,10},{10,8},{12,14},{14,12},{1,3},{3,1},... | collective-permute-start | bytes 786440 | tf_op jit(solution)/shard_map/ppermute | solution.py:468
  56.5 15.4 %collective-permute-start.16 = (bf16[2,64,1024]{2,1,0:T(8,128)(2,1)S(1)}, bf16[2,64,1024]{2,1,0:T(8,128)(2,1)S(1)}, u32[]{:S(2)}, u32[]{:S(2)}) collective-permute-start(bf16[2,64,1024]{2,1,0:T(8,128)(2,1)S(1)} %get-tuple-element.113), channel_id=1, source_target_pairs={{0,4},{2,6},{4,0},{6,2},{8,12},{10,14},{12,8},{14,10},{1,5},{3,7},... | collective-permute-start | bytes 786440 | tf_op jit(solution)/shard_map/ppermute | solution.py:468
  58.0 13.9 %collective-permute-start.17 = (bf16[2,64,1024]{2,1,0:T(8,128)(2,1)S(1)}, bf16[2,64,1024]{2,1,0:T(8,128)(2,1)S(1)}, u32[]{:S(2)}, u32[]{:S(2)}) collective-permute-start(bf16[2,64,1024]{2,1,0:T(8,128)(2,1)S(1)} %get-tuple-element.114), channel_id=1, source_target_pairs={{0,6},{2,4},{4,2},{6,0},{8,14},{10,12},{12,10},{14,8},{1,7},{3,5},... | collective-permute-start | bytes 786440 | tf_op jit(solution)/shard_map/ppermute | solution.py:468
  71.9 6.0 %collective-permute-start.18 = (bf16[1,64,1024]{2,1,0:T(8,128)(2,1)S(1)}, bf16[1,64,1024]{2,1,0:T(8,128)(2,1)S(1)}, u32[]{:S(2)}, u32[]{:S(2)}) collective-permute-start(bf16[1,64,1024]{2,1,0:T(8,128)(2,1)S(1)} %get-tuple-element.117), channel_id=1, source_target_pairs={{0,2},{2,0},{4,6},{6,4},{8,10},{10,8},{12,14},{14,12},{1,3},{3,1},... | collective-permute-start | bytes 393224 | tf_op jit(solution)/shard_map/ppermute | solution.py:468
  74.0 5.5 %collective-permute-start.19 = (bf16[1,64,1024]{2,1,0:T(8,128)(2,1)S(1)}, bf16[1,64,1024]{2,1,0:T(8,128)(2,1)S(1)}, u32[]{:S(2)}, u32[]{:S(2)}) collective-permute-start(bf16[1,64,1024]{2,1,0:T(8,128)(2,1)S(1)} %get-tuple-element.119), channel_id=1, source_target_pairs={{0,4},{2,6},{4,0},{6,2},{8,12},{10,14},{12,8},{14,10},{1,5},{3,7},... | collective-permute-start | bytes 393224 | tf_op jit(solution)/shard_map/ppermute | solution.py:468
  76.4 5.9 %collective-permute-start.20 = (bf16[1,64,1024]{2,1,0:T(8,128)(2,1)S(1)}, bf16[1,64,1024]{2,1,0:T(8,128)(2,1)S(1)}, u32[]{:S(2)}, u32[]{:S(2)}) collective-permute-start(bf16[1,64,1024]{2,1,0:T(8,128)(2,1)S(1)} %get-tuple-element.121), channel_id=1, source_target_pairs={{0,6},{2,4},{4,2},{6,0},{8,14},{10,12},{12,10},{14,8},{1,7},{3,5},... | collective-permute-start | bytes 393224 | tf_op jit(solution)/shard_map/ppermute | solution.py:468
  83.2 11.2 %collective-permute-start.24 = (bf16[1,64,1024]{2,1,0:T(8,128)(2,1)S(1)}, bf16[1,64,1024]{2,1,0:T(8,128)(2,1)S(1)}, u32[]{:S(2)}, u32[]{:S(2)}) collective-permute-start(bf16[1,64,1024]{2,1,0:T(8,128)(2,1)S(1)} %get-tuple-element.141), channel_id=1, source_target_pairs={{0,8},{2,10},{4,12},{6,14},{8,0},{10,2},{12,4},{14,6},{1,9},{3,11}... | collective-permute-start | bytes 393224 | tf_op jit(solution)/shard_map/ppermute | solution.py:468
  85.9 8.8 %collective-permute-start.25 = (bf16[1,64,1024]{2,1,0:T(8,128)(2,1)S(1)}, bf16[1,64,1024]{2,1,0:T(8,128)(2,1)S(1)}, u32[]{:S(2)}, u32[]{:S(2)}) collective-permute-start(bf16[1,64,1024]{2,1,0:T(8,128)(2,1)S(1)} %get-tuple-element.142), channel_id=1, source_target_pairs={{0,9},{1,8},{2,11},{3,10},{4,13},{5,12},{6,15},{7,14},{8,1},{9,0},... | collective-permute-start | bytes 393224 | tf_op jit(solution)/shard_map/ppermute | solution.py:475
  85.9 8.8 %collective-permute-start.21 = (bf16[1,64,1024]{2,1,0:T(8,128)(2,1)S(1)}, bf16[1,64,1024]{2,1,0:T(8,128)(2,1)S(1)}, u32[]{:S(2)}, u32[]{:S(2)}) collective-permute-start(bf16[1,64,1024]{2,1,0:T(8,128)(2,1)S(1)} %get-tuple-element.138), channel_id=1, source_target_pairs={{0,2},{2,0},{4,6},{6,4},{8,10},{10,8},{12,14},{14,12},{1,3},{3,1},... | collective-permute-start | bytes 393224 | tf_op jit(solution)/shard_map/ppermute | solution.py:468
  86.1 10.4 %collective-permute-start.22 = (bf16[1,64,1024]{2,1,0:T(8,128)(2,1)S(1)}, bf16[1,64,1024]{2,1,0:T(8,128)(2,1)S(1)}, u32[]{:S(2)}, u32[]{:S(2)}) collective-permute-start(bf16[1,64,1024]{2,1,0:T(8,128)(2,1)S(1)} %get-tuple-element.139), channel_id=1, source_target_pairs={{0,4},{2,6},{4,0},{6,2},{8,12},{10,14},{12,8},{14,10},{1,5},{3,7},... | collective-permute-start | bytes 393224 | tf_op jit(solution)/shard_map/ppermute | solution.py:468
  87.9 10.8 %collective-permute-start.23 = (bf16[1,64,1024]{2,1,0:T(8,128)(2,1)S(1)}, bf16[1,64,1024]{2,1,0:T(8,128)(2,1)S(1)}, u32[]{:S(2)}, u32[]{:S(2)}) collective-permute-start(bf16[1,64,1024]{2,1,0:T(8,128)(2,1)S(1)} %get-tuple-element.140), channel_id=1, source_target_pairs={{0,6},{2,4},{4,2},{6,0},{8,14},{10,12},{12,10},{14,8},{1,7},{3,5},... | collective-permute-start | bytes 393224 | tf_op jit(solution)/shard_map/ppermute | solution.py:468
  99.6 14.8 %collective-permute-start.26 = (f32[2,64,1024]{2,1,0:T(8,128)S(1)}, f32[2,64,1024]{2,1,0:T(8,128)S(1)}, u32[]{:S(2)}, u32[]{:S(2)}) collective-permute-start(f32[2,64,1024]{2,1,0:T(8,128)S(1)} %get-tuple-element.152), channel_id=1, source_target_pairs={{0,1},{1,0},{2,3},{3,2},{4,5},{5,4},{6,7},{7,6},{8,9},{9,8},{10,11... | collective-permute-start | bytes 1572872 | tf_op jit(solution)/shard_map/ppermute | solution.py:471
  99.7 12.0 %collective-permute-start.27 = (bf16[1,64,1024]{2,1,0:T(8,128)(2,1)S(1)}, bf16[1,64,1024]{2,1,0:T(8,128)(2,1)S(1)}, u32[]{:S(2)}, u32[]{:S(2)}) collective-permute-start(bf16[1,64,1024]{2,1,0:T(8,128)(2,1)S(1)} %get-tuple-element.154), channel_id=1, source_target_pairs={{0,8},{2,10},{4,12},{6,14},{8,0},{10,2},{12,4},{14,6},{1,9},{3,11}... | collective-permute-start | bytes 393224 | tf_op jit(solution)/shard_map/ppermute | solution.py:468
  99.9 14.5 %collective-permute-start.28 = (bf16[1,64,1024]{2,1,0:T(8,128)(2,1)S(1)}, bf16[1,64,1024]{2,1,0:T(8,128)(2,1)S(1)}, u32[]{:S(2)}, u32[]{:S(2)}) collective-permute-start(bf16[1,64,1024]{2,1,0:T(8,128)(2,1)S(1)} %get-tuple-element.156), channel_id=1, source_target_pairs={{0,9},{1,8},{2,11},{3,10},{4,13},{5,12},{6,15},{7,14},{8,1},{9,0},... | collective-permute-start | bytes 393224 | tf_op jit(solution)/shard_map/ppermute | solution.py:475
  (6 other events, 23.1 us)

commit v7 on v5

--- a/solution.py
+++ b/solution.py
@@ -11,6 +11,7 @@
 FB = 128
 TMAX = 4
 UMAX = 8
+GROUP = 6
 MIB = 1024 * 1024
 
 
@@ -124,7 +125,7 @@
     return summed.astype(jnp.bfloat16)
 
 
-def call(kernel, scalars, arrays, in_specs, out_shapes, out_specs, scratch, grid=(1,), cost=None, vmem=44):
+def call(kernel, scalars, arrays, in_specs, out_shapes, out_specs, scratch, grid=(1,), cost=None, vmem=36):
     return pl.pallas_call(
         kernel,
         grid_spec=pltpu.PrefetchScalarGridSpec(
@@ -194,74 +195,110 @@
     )
 
 
-def table_kernel(nb, near, group, me, owner, own_set, blocks_a, blocks_b, counts_a, counts_b, out, kbs, fill):
-    half = counts_a.shape[0]
-    at_lives, at_near, at_far, at_col, at_pos = table_places(2 * half, group)
-    spare = nb * near
+def table_places(batches, group):
+    lives = batches
+    rows = lives + batches // group
+    slots = batches * TMAX
+    return lives, rows, rows + slots, rows + 2 * slots, rows + 3 * slots
+
+
+def table_kernel(nb, group, me, owner, own_set, blocks, packed, counts, out, kbs, fill, bundle, sem):
+    copy = pltpu.make_async_copy(packed.at[TMAX], bundle, sem)
+    copy.start()
+    half = counts.shape[0]
+    at_lives, at_row, at_pos, at_col, _ = table_places(2 * half, group)
+    spare = owner.shape[0]
     for p in range(UMAX):
         stored = owner[own_set[0, p]]
         kbs[p] = (lax.div(stored, nb) ^ me[0]) * nb + lax.rem(stored, nb)
     for c in range(TMAX + 1):
         fill[c] = 0
-
-    def each(todo):
-        for side, (blocks, counts) in enumerate(((blocks_a, counts_a), (blocks_b, counts_b))):
-
-            @pl.loop(0, half)
-            def _(b):
-                todo(side, b, blocks, counts[b])
-
-    def tally(side, b, blocks, count):
-        fill[count] = fill[count] + 1
-
-    each(tally)
+    copy.wait()
+
+    def count_of(side, b):
+        return bundle[b, TMAX].astype(jnp.int32) if side else counts[b]
+
+    for side in (0, 1):
+
+        @pl.loop(0, half)
+        def _(b):
+            count = count_of(side, b)
+            fill[count] = fill[count] + 1
+
     place = 0
     for c in range(TMAX, -1, -1):
         many = fill[c]
         fill[c] = place
         place = place + many
 
-    def put(side, b, blocks, count):
-        j = fill[count]
-        fill[count] = j + 1
-        out[j] = side * half + b
-
-        @pl.when(lax.rem(j, group) == 0)
-        def _():
-            out[at_lives + lax.div(j, group)] = count
-
-        for s in range(TMAX):
-            pos = blocks[b, s]
-            kb = kbs[pos]
-            on = s < count
-            at = j * TMAX + s
-            out[at_pos + at] = pos
-            out[at_col + at] = jnp.where(on, pos, UMAX)
-            out[at_near + at] = jnp.where(on & (kb < spare), kb, spare)
-            out[at_far + at] = jnp.where(on & (kb >= spare), kb - spare, spare)
-
-    each(put)
-
-
-def table_places(batches, group):
-    lives = batches
-    near = lives + batches // group
-    return lives, near, near + batches * TMAX, near + 2 * batches * TMAX, near + 3 * batches * TMAX
-
-
-def batch_tables(me, owner, own_set, blocks, counts, nb, near):
-    batches = 2 * counts[0].shape[0]
-    group = math.gcd(batches, 4)
-    size = table_places(batches, group)[-1] + batches * TMAX
-    return call(
-        functools.partial(table_kernel, nb, near, group),
-        [me, owner, own_set, *blocks, *counts],
-        [],
-        [],
+    for side in (0, 1):
+
+        @pl.loop(0, half)
+        def _(b):
+            count = count_of(side, b)
+            j = fill[count]
+            fill[count] = j + 1
+            out[j] = side * half + b
+
+            @pl.when(lax.rem(j, group) == 0)
+            def _():
+                out[at_lives + lax.div(j, group)] = count
+
+            for s in range(TMAX):
+                pos = bundle[b, s].astype(jnp.int32) if side else blocks[s, b]
+                on = s < count
+                at = j * TMAX + s
+                out[at_pos + at] = pos
+                out[at_col + at] = jnp.where(on, pos, UMAX)
+                out[at_row + at] = jnp.where(on, kbs[pos], spare)
+
+
+def batch_tables(me, owner, own_set, blocks, packed, counts, nb):
+    batches = 2 * counts.shape[0]
+    group = math.gcd(batches, GROUP)
+    size = table_places(batches, group)[-1]
+    return call(
+        functools.partial(table_kernel, nb, group),
+        [me, owner, own_set, blocks],
+        [packed, counts],
+        [pl.BlockSpec(memory_space=pl.ANY), pl.BlockSpec(memory_space=pltpu.SMEM)],
         jax.ShapeDtypeStruct((size,), jnp.int32),
         pl.BlockSpec(memory_space=pltpu.SMEM),
-        [pltpu.SMEM((UMAX,), jnp.int32), pltpu.SMEM((TMAX + 1,), jnp.int32)],
+        [
+            pltpu.SMEM((UMAX,), jnp.int32),
+            pltpu.SMEM((TMAX + 1,), jnp.int32),
+            pltpu.SMEM(packed.shape[1:], packed.dtype),
+            pltpu.SemaphoreType.DMA,
+        ],
         cost=(0, 8 * batches * TMAX),
+    )
+
+
+def pack_kernel(points, weights, blocks, counts, out):
+    batches, pts = weights.shape
+    out[0:3] = points[...]
+    out[3] = weights[...]
+    lane = lax.broadcasted_iota(jnp.int32, (1, pts), 1)
+
+    @pl.loop(0, batches)
+    def _(b):
+        row = jnp.where(lane == TMAX, counts[b], 0)
+        for s in range(TMAX):
+            row = jnp.where(lane == s, blocks[s, b], row)
+        out[4, pl.ds(b, 1), :] = row.astype(jnp.float32)
+
+
+def pack(points, weights, blocks, counts):
+    shape = (5, *weights.shape)
+    return call(
+        pack_kernel,
+        [],
+        [points, weights, blocks, counts],
+        [whole(points.shape), whole(weights.shape)] + [pl.BlockSpec(memory_space=pltpu.SMEM)] * 2,
+        jax.ShapeDtypeStruct(shape, jnp.float32),
+        whole(shape),
+        [],
+        cost=(0, 10 * 4 * weights.size),
     )
 
 
@@ -322,17 +359,16 @@
     )
 
 
-def batch_kernel(group, pieces, split, table, *refs):
-    xs, coords, weights, centre = refs[0:2], refs[2:4], refs[4:6], refs[6]
-    parts = refs[7 : 7 + pieces]
-    outs = refs[7 + pieces : -8]
-    dense, acc, xbuf, pbuf, wbuf, sems, xsems, qsems = refs[-8:]
+def batch_kernel(group, pieces, table, *refs):
+    xs, quads, centre_in = refs[0:2], refs[2:4], refs[4]
+    parts = refs[5 : 5 + pieces]
+    outs = refs[5 + pieces : -7]
+    dense, acc, xbuf, qbuf, centre, sems, xsems = refs[-7:]
     nb, sub, wide = parts[0].shape
     spare = nb * pieces
     batches, _, pts = xbuf.shape
     half = batches // 2
-    at_lives, at_near, at_far, at_col, at_pos = table_places(batches, group)
-    at_row = at_far if split else at_near
+    at_lives, at_row, at_pos, at_col, _ = table_places(batches, group)
 
     def fetch(j, act):
         b = table[j]
@@ -346,10 +382,10 @@
         pltpu.make_async_copy(part, dense.at[pl.ds(nb * k, nb), :, pl.ds(0, wide)], sems.at[k])
         for k, part in enumerate(parts)
     ]
+    copies.append(pltpu.make_async_copy(centre_in, centre, sems.at[pieces]))
     for side in (0, 1):
-        rest = pl.ds(half * side, half)
-        copies.append(pltpu.make_async_copy(coords[side], pbuf.at[:, rest], qsems.at[side]))
-        copies.append(pltpu.make_async_copy(weights[side], wbuf.at[rest], qsems.at[2 + side]))
+        quad = qbuf.at[:, pl.ds(half * side, half)]
+        copies.append(pltpu.make_async_copy(quads[side].at[pl.ds(0, 4)], quad, sems.at[pieces + 1 + side]))
     for copy in copies:
         copy.start()
 
@@ -369,27 +405,23 @@
     def one(j, live):
         b = table[j]
         row = [table[at_row + j * TMAX + s] for s in range(live)]
+        pos = [table[at_pos + j * TMAX + s] for s in range(live)]
         col = [pl.ds(pl.multiple_of(table[at_col + j * TMAX + s] * FB, FB), FB) for s in range(live)]
-        pos = [table[at_pos + j * TMAX + s] for s in range(live)]
         x = xbuf[j, : live * FB, :]
         d = jnp.concatenate(
-            [
-                jnp.concatenate([dense[row[s], :, col[t]] for t in range(live)], axis=1)
-                for s in range(live)
-            ],
-            axis=0,
+            [jnp.concatenate([dense[r, :, c] for c in col], axis=1) for r in row], axis=0
         )
         gval = jnp.dot(d, x, preferred_element_type=jnp.float32)
         fval = []
         for s in range(live):
             dist = None
             for axis in range(3):
-                diff = lanes(centre[axis, pos[s]]) - pbuf[axis, pl.ds(b, 1), :]
+                diff = lanes(centre[axis, pos[s]]) - qbuf[axis, pl.ds(b, 1), :]
                 dist = diff * diff if dist is None else dist + diff * diff
             dist = dist + lanes(centre[3, pos[s]])
             fval.append((gval[s * sub : (s + 1) * sub] * lax.rsqrt(dist)).astype(jnp.bfloat16))
         fval = jnp.concatenate(fval, axis=0)
-        xw = (x.astype(jnp.float32) * wbuf[pl.ds(b, 1), :]).astype(jnp.bfloat16)
+        xw = (x.astype(jnp.float32) * qbuf[3, pl.ds(b, 1), :]).astype(jnp.bfloat16)
         part = lax.dot_general(
             fval, xw, (((1,), (1,)), ((), ())), preferred_element_type=jnp.float32
         )
@@ -410,43 +442,41 @@
                         for t in range(live):
                             acc[row[s], :, col[t]] += part[s * sub : (s + 1) * sub, t * FB : (t + 1) * FB]
 
-    for k, out in enumerate(outs):
-        size = out.shape[0]
-        out[...] = acc[size * k : size * (k + 1), :, :wide].astype(out.dtype)
-
-
-def batch_sums(table, xs, coords, weights, centre, parts, split):
+    start = 0
+    for out in outs:
+        rows = out.shape[0]
+        out[...] = acc[start : start + rows, :, :wide].astype(out.dtype)
+        start += rows
+
+
+def batch_sums(table, xs, quads, centre, parts):
     _, width, pts = xs[0].shape
     batches = 2 * xs[0].shape[0]
-    group = math.gcd(batches, 4)
+    group = math.gcd(batches, GROUP)
     nb, sub, wide = parts[0].shape
     pieces = len(parts)
-    size = 1 if split else nb
+    near = pieces // 2
     out_shapes = [
-        jax.ShapeDtypeStruct((size, sub, wide), jnp.bfloat16 if k else jnp.float32)
+        jax.ShapeDtypeStruct((nb if k < near else 1, sub, wide), jnp.bfloat16 if k % near else jnp.float32)
         for k in range(pieces)
-        for _ in range(nb // size)
+        for _ in range(1 if k < near else nb)
     ]
     flops = 2 * batches * 2 * width * (width // 2) * pts
     return call(
-        functools.partial(batch_kernel, group, pieces, split),
+        functools.partial(batch_kernel, group, pieces),
         [table],
-        [*xs, *coords, *weights, centre, *parts],
-        [pl.BlockSpec(memory_space=pltpu.HBM)] * 2
-        + [pl.BlockSpec(memory_space=pl.ANY)] * 4
-        + [whole(centre.shape)]
-        + [pl.BlockSpec(memory_space=pl.ANY)] * pieces,
+        [*xs, *quads, centre, *parts],
+        [pl.BlockSpec(memory_space=pl.ANY)] * (5 + pieces),
         out_shapes,
-        [whole((size, sub, wide))] * len(out_shapes),
+        [whole(out.shape) for out in out_shapes],
         [
             pltpu.VMEM((nb * pieces + 1, sub, wide + FB), jnp.bfloat16),
             pltpu.VMEM((nb * pieces + 1, sub, wide + FB), jnp.float32),
             pltpu.VMEM((batches, width, pts), jnp.bfloat16),
-            pltpu.VMEM((3, batches, pts), jnp.float32),
-            pltpu.VMEM((batches, pts), jnp.float32),
-            pltpu.SemaphoreType.DMA((pieces,)),
+            pltpu.VMEM((4, batches, pts), jnp.float32),
+            pltpu.VMEM(centre.shape, jnp.float32),
+            pltpu.SemaphoreType.DMA((pieces + 3,)),
             pltpu.SemaphoreType.DMA((batches,)),
-            pltpu.SemaphoreType.DMA((4,)),
         ],
         cost=(flops, 2 * batches * width * pts),
     )
@@ -473,34 +503,36 @@
         return pltpu.with_memory_space_constraint(x, pltpu.HBM)
 
     own = lax.dynamic_index_in_dim(density.reshape(nb, cores, sub, cols), r, 1, keepdims=False)
+    sets = [touched] + [swap(touched, k) for k in range(1, near)]
+    own, sets = lax.optimization_barrier((own, sets))
     far = swap(own, near)
-    sets = [touched] + [swap(touched, k) for k in range(1, near)]
-    points = points.transpose(1, 0, 2)
-    both = [(stay(x), across(x)) for x in (basis, points, weights, counts)] + [(blocks, across(blocks))]
     sets[0] = stay(touched)
-    table = batch_tables(i.reshape(1), stay(owner), sets[0], both[4], both[3], nb, near)
-    centre = centre_rows(sets[0], core, stay(centers), stay(widths.reshape(1, -1)), sub)
-
-    own, table, centre, both = lax.optimization_barrier((own, table, centre, both))
     picked = pick(sets, own)
     parts = [picked[0]] + [swap(picked[k], k) for k in range(1, near)]
-    far, _ = lax.optimization_barrier((far, picked[0]))
+    xs = (stay(basis), across(basis))
+    far, parts = lax.optimization_barrier((far, parts))
     picked = pick(sets, far)
-    far_parts = [picked[0]] + [swap(picked[k], k) for k in range(1, near)]
-    table, _ = lax.optimization_barrier((table, picked[0]))
-
-    common = (*both[:3], centre)
-    sums = batch_sums(table, *common, parts, False)
-    table, _ = lax.optimization_barrier((table, sums[0]))
-    far_sums = batch_sums(table, *common, far_parts, True)
-    terms = [sums[0]] + [swap(sums[k], k) for k in range(1, near)]
-    far_sums, terms = lax.optimization_barrier((far_sums, terms))
+    small = (points.transpose(1, 0, 2), weights, blocks.T, counts)
+    small, centers, widths, picked = lax.optimization_barrier((small, centers, widths, picked))
+    parts += [picked[0]] + [swap(picked[k], k) for k in range(1, near)]
+
+    small = [stay(x) for x in small]
+    packed = pack(*small)
+    packed_b = across(packed)
+    table = batch_tables(i.reshape(1), stay(owner), sets[0], small[2], packed_b, small[3], nb)
+    centre = centre_rows(sets[0], core, stay(centers), stay(widths.reshape(1, -1)), sub)
+    parts, table, centre = lax.optimization_barrier((parts, table, centre))
+
+    sums = batch_sums(table, xs, (packed, packed_b), centre, parts)
+    sums, far_sums = sums[:near], sums[near:]
     far_terms = []
     for b in range(nb):
         chunk = [far_sums[b]] + [swap(far_sums[nb * k + b], k) for k in range(1, near)]
         merged = merge(sets, chunk, cols)
-        far_sums, merged = lax.optimization_barrier((far_sums, merged))
+        sums, far_sums, merged = lax.optimization_barrier((sums, far_sums, merged))
         far_terms.append(swap(merged, near))
+    sums, far_terms[0] = lax.optimization_barrier((sums, far_terms[0]))
+    terms = [sums[0]] + [swap(sums[k], k) for k in range(1, near)]
     keep, give = finish(sets, core, terms, far_terms)
     got = across(give)
     pair = jnp.where(r == 0, jnp.stack([keep, got], axis=1), jnp.stack([got, keep], axis=1))

time: 114 us -> 113 us (level); the launches traced: 113 us -> 111 us
  Pallas kernels: 39.7 us -> 27.3 us
  waiting for transfers between devices: 43.5 us -> 53.5 us
  starting transfers between devices: 27.5 us -> 29.2 us
  local copies, waits for them, and re-layouts: 2.4 us -> 0.87 us
    ppermute x21, waiting for transfers between devices: 38.1 us -> 52 us  [swap(): return lax.ppermute(x, 'dom', [(a, a ^ k) for a in range(n)])]
    pallas_call x9, Pallas kernels: 39.7 us -> 27.3 us  [call(): pl.pallas_call(kernel, grid_spec=pltpu.PrefetchScalarGridSpec(num_scalar_...]
    ppermute x6 -> x3, waiting for transfers between devices: 5.47 us -> 1.52 us  [across(): return lax.ppermute(x, 'rows', [(a, cores - 1 - a) for a in range(cores)])]
    ppermute x21, starting transfers between devices: 26.1 us -> 28.6 us  [swap(): return lax.ppermute(x, 'dom', [(a, a ^ k) for a in range(n)])]
    unnamed x3 -> x2, local copies, waits for them, and re-layouts: 1.53 us -> 0.01 us
  transfers between devices with their start and end apart: 27 -> 24, of which waited for: 15 -> 16; matrix products, arithmetic and copies ran while one was open for 1% -> 0% of each run, Pallas kernels for 33% -> 11%
where the time goes in v7:
time: 113 us; the launch traced here: 111 us
  waiting for transfers between devices  53.5 us (47%)
  starting transfers between devices  29.2 us (26%)
  Pallas kernels  27.3 us (24%)
    ppermute x21, waiting for transfers between devices, swap(): return lax.ppermute(x, 'dom', [(a, a ^ k) for a in range(n)])  52 us
    ppermute x21, starting transfers between devices, swap(): return lax.ppermute(x, 'dom', [(a, a ^ k) for a in range(n)])  28.6 us
    pallas_call x9, Pallas kernels, call(): pl.pallas_call(kernel, grid_spec=pltpu.PrefetchScalarGridSpec(num_scalar_...  27.3 us
  transfers between devices with their start and end apart: 24, of which 16 were waited for; matrix products, arithmetic and copies ran while one was open for 0% of the time, Pallas kernels for 11%

profile of v7, /device:TPU:0, one launch (start us, length us, event | category | flops | bytes accessed | tf_op | source)
XLA Modules:
  0.0 111.1 jit_solution(8603717703881005800)
XLA Ops:
  0.5 2.6 %collective-permute-start = (s32[1,8]{1,0:T(1,128)}, s32[1,8]{1,0:T(1,128)S(1)}, u32[]{:S(2)}, u32[]{:S(2)}) collective-permute-start(s32[1,8]{1,0:T(1,128)} %refs_0_.11), channel_id=1, source_target_pairs={{0,2},{2,0},{4,6},{6,4},{8,10},{10,8},{12,14},{14,12},{1,3},{3,1},... | collective-permute-start | bytes 104 | tf_op jit(solution)/shard_map/ppermute | solution.py:497
  4.7 2.0 %collective-permute-done.1.refs_2_ = s32[1,8]{1,0:T(1,128)S(1)} collective-permute-done((s32[1,8]{1,0:T(1,128)}, s32[1,8]{1,0:T(1,128)S(1)}, u32[]{:S(2)}, u32[]{:S(2)}) %collective-permute-start.1) | collective-permute-done | bytes 64 | tf_op jit(solution)/shard_map/ppermute | solution.py:497
  6.7 2.5 %collective-permute-done.2.refs_3_ = s32[1,8]{1,0:T(1,128)S(1)} collective-permute-done((s32[1,8]{1,0:T(1,128)}, s32[1,8]{1,0:T(1,128)S(1)}, u32[]{:S(2)}, u32[]{:S(2)}) %collective-permute-start.2) | collective-permute-done | bytes 64 | tf_op jit(solution)/shard_map/ppermute | solution.py:497
  9.2 2.6 %collective-permute-start.3 = (bf16[2,64,2048]{2,1,0:T(8,128)(2,1)S(1)}, bf16[2,64,2048]{2,1,0:T(8,128)(2,1)S(1)}, u32[]{:S(2)}, u32[]{:S(2)}) collective-permute-start(bf16[2,64,2048]{2,1,0:T(8,128)(2,1)S(1)} %dynamic-slice_bitcast_fusion.refs_4_), channel_id=1, source_target_pairs={{0,8},{2,10},{4,12},{6,14},{8,0},{10,2},{12,4},{14,6},{1,9},{3,11}... | collective-permute-start | bytes 1572872 | tf_op jit(solution)/shard_map/ppermute | solution.py:497
  13.7 2.5 %collective-permute-start.6 = (bf16[2,64,1024]{2,1,0:T(8,128)(2,1)S(1)}, bf16[2,64,1024]{2,1,0:T(8,128)(2,1)S(1)}, u32[]{:S(2)}, u32[]{:S(2)}) collective-permute-start(bf16[2,64,1024]{2,1,0:T(8,128)(2,1)S(1)} %get-tuple-element.82), channel_id=1, source_target_pairs={{0,6},{2,4},{4,2},{6,0},{8,14},{10,12},{12,10},{14,8},{1,7},{3,5},... | collective-permute-start | bytes 786440 | tf_op jit(solution)/shard_map/ppermute | solution.py:497
  16.3 4.7 %collective-permute-done.4.refs_6_ = bf16[2,64,1024]{2,1,0:T(8,128)(2,1)S(1)} collective-permute-done((bf16[2,64,1024]{2,1,0:T(8,128)(2,1)S(1)}, bf16[2,64,1024]{2,1,0:T(8,128)(2,1)S(1)}, u32[]{:S(2)}, u32[]{:S(2)}) %collective-permute-start.4) | collective-permute-done | bytes 262176 | tf_op jit(solution)/shard_map/ppermute | solution.py:497
  21.0 8.8 %collective-permute-done.5.refs_7_ = bf16[2,64,1024]{2,1,0:T(8,128)(2,1)S(1)} collective-permute-done((bf16[2,64,1024]{2,1,0:T(8,128)(2,1)S(1)}, bf16[2,64,1024]{2,1,0:T(8,128)(2,1)S(1)}, u32[]{:S(2)}, u32[]{:S(2)}) %collective-permute-start.5) | collective-permute-done | bytes 262176 | tf_op jit(solution)/shard_map/ppermute | solution.py:497
  29.8 7.6 %collective-permute-done.6.refs_8_ = bf16[2,64,1024]{2,1,0:T(8,128)(2,1)S(1)} collective-permute-done((bf16[2,64,1024]{2,1,0:T(8,128)(2,1)S(1)}, bf16[2,64,1024]{2,1,0:T(8,128)(2,1)S(1)}, u32[]{:S(2)}, u32[]{:S(2)}) %collective-permute-start.6) | collective-permute-done | bytes 262176 | tf_op jit(solution)/shard_map/ppermute | solution.py:497
  37.4 1.8 %shard_map.101 = (bf16[2,64,1024]{2,1,0:T(8,128)(2,1)S(1)}, bf16[2,64,1024]{2,1,0:T(8,128)(2,1)}, bf16[2,64,1024]{2,1,0:T(8,128)(2,1)}, bf16[2,64,1024]{2,1,0:T(8,128)(2,1)}) custom-call(s32[1,8]{1,0:T(1,128)} %refs_0_.11, s32[1,8]{1,0:T(1,128)S(1)} %collective-permute-done.refs_1_, s32[1,8]{1,0:T(1,128)S(1)} %collective-permute-done.1.refs_2_, ...), custom_call_target="tpu_custom_call" | custom-call | bytes 1572864 | tf_op jit(solution)/shard_map/pallas_call | solution.py:129
  39.7 3.0 %collective-permute-start.9 = (bf16[2,64,1024]{2,1,0:T(8,128)(2,1)}, bf16[2,64,1024]{2,1,0:T(8,128)(2,1)S(1)}, u32[]{:S(2)}, u32[]{:S(2)}) collective-permute-start(bf16[2,64,1024]{2,1,0:T(8,128)(2,1)} %get-tuple-element.95), channel_id=1, source_target_pairs={{0,6},{2,4},{4,2},{6,0},{8,14},{10,12},{12,10},{14,8},{1,7},{3,5},... | collective-permute-start | bytes 786440 | tf_op jit(solution)/shard_map/ppermute | solution.py:497
  43.9 2.1 %shard_map.104.refs_4_ = f32[4,8,64,128]{3,2,1,0:T(8,128)S(1)} custom-call(s32[1,8]{1,0:T(1,128)} %refs_0_.11, s32[1]{0:T(128)} %bitcast.2.core.refs_4_, f32[3,2048]{1,0:T(4,128)} %centers, f32[1,2048]{1,0:T(1,128)} %bitcast.17), custom_call_target="tpu_custom_call" | custom-call | bytes 2097152 | tf_op jit(solution)/shard_map/pallas_call | solution.py:129
  46.1 4.8 %shard_map.103.table = s32[632]{0:T(1024)S(1)} custom-call(s32[1]{0:T(128)} %bitcast.5.me, s32[16]{0:T(128)} %owner.1, s32[1,8]{1,0:T(1,128)} %refs_0_.11, s32[4,24]{1,0:T(4,128)} %bitcast.19, f32[5,24,256]{2,1,0:T(8,128)S(1)} %collective-permute-done.10.packed.refs_3_, s32[24]{0:T(128)} %counts.1), custom_call_target="tpu_custom_call" | custom-call | bytes 1536 | tf_op jit(solution)/shard_map/pallas_call | solution.py:129
  51.3 13.2 %shard_map.105 = (f32[2,64,1024]{2,1,0:T(8,128)S(1)}, bf16[2,64,1024]{2,1,0:T(8,128)(2,1)S(1)}, bf16[2,64,1024]{2,1,0:T(8,128)(2,1)S(1)}, bf16[2,64,1024]{2,1,0:...) custom-call(s32[632]{0:T(1024)S(1)} %shard_map.103.table, ...), custom_call_target="tpu_custom_call" | custom-call | flops 6442450944 | bytes 12582912 | tf_op jit(solution)/shard_map/pallas_call | solution.py:129
  65.8 2.3 %collective-permute-start.14 = (bf16[1,64,1024]{2,1,0:T(8,128)(2,1)S(1)}, bf16[1,64,1024]{2,1,0:T(8,128)(2,1)S(1)}, u32[]{:S(2)}, u32[]{:S(2)}) collective-permute-start(bf16[1,64,1024]{2,1,0:T(8,128)(2,1)S(1)} %get-tuple-element.122), channel_id=1, source_target_pairs={{0,6},{2,4},{4,2},{6,0},{8,14},{10,12},{12,10},{14,8},{1,7},{3,5},... | collective-permute-start | bytes 393224 | tf_op jit(solution)/shard_map/ppermute | solution.py:497
  68.1 2.0 %collective-permute-done.12.refs_5_ = bf16[1,64,1024]{2,1,0:T(8,128)(2,1)S(1)} collective-permute-done((bf16[1,64,1024]{2,1,0:T(8,128)(2,1)S(1)}, bf16[1,64,1024]{2,1,0:T(8,128)(2,1)S(1)}, u32[]{:S(2)}, u32[]{:S(2)}) %collective-permute-start.12) | collective-permute-done | bytes 131104 | tf_op jit(solution)/shard_map/ppermute | solution.py:497
  71.2 2.9 %collective-permute-done.14.refs_7_ = bf16[1,64,1024]{2,1,0:T(8,128)(2,1)S(1)} collective-permute-done((bf16[1,64,1024]{2,1,0:T(8,128)(2,1)S(1)}, bf16[1,64,1024]{2,1,0:T(8,128)(2,1)S(1)}, u32[]{:S(2)}, u32[]{:S(2)}) %collective-permute-start.14) | collective-permute-done | bytes 131104 | tf_op jit(solution)/shard_map/ppermute | solution.py:497
  76.4 2.4 %collective-permute-start.17 = (bf16[1,64,1024]{2,1,0:T(8,128)(2,1)S(1)}, bf16[1,64,1024]{2,1,0:T(8,128)(2,1)S(1)}, u32[]{:S(2)}, u32[]{:S(2)}) collective-permute-start(bf16[1,64,1024]{2,1,0:T(8,128)(2,1)S(1)} %get-tuple-element.131), channel_id=1, source_target_pairs={{0,6},{2,4},{4,2},{6,0},{8,14},{10,12},{12,10},{14,8},{1,7},{3,5},... | collective-permute-start | bytes 393224 | tf_op jit(solution)/shard_map/ppermute | solution.py:497
  78.7 2.9 %collective-permute-done.15.refs_5_ = bf16[1,64,1024]{2,1,0:T(8,128)(2,1)S(1)} collective-permute-done((bf16[1,64,1024]{2,1,0:T(8,128)(2,1)S(1)}, bf16[1,64,1024]{2,1,0:T(8,128)(2,1)S(1)}, u32[]{:S(2)}, u32[]{:S(2)}) %collective-permute-start.15) | collective-permute-done | bytes 131104 | tf_op jit(solution)/shard_map/ppermute | solution.py:497
  81.6 2.8 %collective-permute-done.16.refs_6_ = bf16[1,64,1024]{2,1,0:T(8,128)(2,1)S(1)} collective-permute-done((bf16[1,64,1024]{2,1,0:T(8,128)(2,1)S(1)}, bf16[1,64,1024]{2,1,0:T(8,128)(2,1)S(1)}, u32[]{:S(2)}, u32[]{:S(2)}) %collective-permute-start.16) | collective-permute-done | bytes 131104 | tf_op jit(solution)/shard_map/ppermute | solution.py:497
  86.8 4.1 %collective-permute-start.22 = (bf16[1,64,2048]{2,1,0:T(8,128)(2,1)S(1)}, bf16[1,64,2048]{2,1,0:T(8,128)(2,1)S(1)}, u32[]{:S(2)}, u32[]{:S(2)}) collective-permute-start(bf16[1,64,2048]{2,1,0:T(8,128)(2,1)S(1)} %shard_map.107), channel_id=1, source_target_pairs={{0,8},{2,10},{4,12},{6,14},{8,0},{10,2},{12,4},{14,6},{1,9},{3,11}... | collective-permute-start | bytes 786440 | tf_op jit(solution)/shard_map/ppermute | solution.py:497
  91.5 1.7 %collective-permute-start.20 = (bf16[2,64,1024]{2,1,0:T(8,128)(2,1)S(1)}, bf16[2,64,1024]{2,1,0:T(8,128)(2,1)S(1)}, u32[]{:S(2)}, u32[]{:S(2)}) collective-permute-start(bf16[2,64,1024]{2,1,0:T(8,128)(2,1)S(1)} %get-tuple-element.139), channel_id=1, source_target_pairs={{0,4},{2,6},{4,0},{6,2},{8,12},{10,14},{12,8},{14,10},{1,5},{3,7},... | collective-permute-start | bytes 786440 | tf_op jit(solution)/shard_map/ppermute | solution.py:497
  94.4 6.8 %collective-permute-done.22.refs_10_ = bf16[1,64,2048]{2,1,0:T(8,128)(2,1)S(1)} collective-permute-done((bf16[1,64,2048]{2,1,0:T(8,128)(2,1)S(1)}, bf16[1,64,2048]{2,1,0:T(8,128)(2,1)S(1)}, u32[]{:S(2)}, u32[]{:S(2)}) %collective-permute-start.22) | collective-permute-done | bytes 262176 | tf_op jit(solution)/shard_map/ppermute | solution.py:497
  101.2 3.5 %collective-permute-done.20.refs_7_ = bf16[2,64,1024]{2,1,0:T(8,128)(2,1)S(1)} collective-permute-done((bf16[2,64,1024]{2,1,0:T(8,128)(2,1)S(1)}, bf16[2,64,1024]{2,1,0:T(8,128)(2,1)S(1)}, u32[]{:S(2)}, u32[]{:S(2)}) %collective-permute-start.20) | collective-permute-done | bytes 262176 | tf_op jit(solution)/shard_map/ppermute | solution.py:497
  104.8 2.5 %collective-permute-done.21.refs_8_ = bf16[2,64,1024]{2,1,0:T(8,128)(2,1)S(1)} collective-permute-done((bf16[2,64,1024]{2,1,0:T(8,128)(2,1)S(1)}, bf16[2,64,1024]{2,1,0:T(8,128)(2,1)S(1)}, u32[]{:S(2)}, u32[]{:S(2)}) %collective-permute-start.21) | collective-permute-done | bytes 262176 | tf_op jit(solution)/shard_map/ppermute | solution.py:497
  (38 shorter events, 18.8 us)
Async XLA Ops:
  0.0 51.3 %collective-permute-start.11 = (bf16[24,512,256]{2,1,0:T(8,128)(2,1)}, bf16[24,512,256]{2,1,0:T(8,128)(2,1)}, u32[]{:S(2)}, u32[]{:S(2)}) collective-permute-start(bf16[24,512,256]{2,1,0:T(8,128)(2,1)} %refs_0_.8), channel_id=1, source_target_pairs={{0,1},{1,0},{2,3},{3,2},{4,5},{5,4},{6,7},{7,6},{8,9},{9,8},{10,11... | collective-permute-start | bytes 18874376 | tf_op jit(solution)/shard_map/ppermute | solution.py:500
  0.5 4.2 %collective-permute-start = (s32[1,8]{1,0:T(1,128)}, s32[1,8]{1,0:T(1,128)S(1)}, u32[]{:S(2)}, u32[]{:S(2)}) collective-permute-start(s32[1,8]{1,0:T(1,128)} %refs_0_.11), channel_id=1, source_target_pairs={{0,2},{2,0},{4,6},{6,4},{8,10},{10,8},{12,14},{14,12},{1,3},{3,1},... | collective-permute-start | bytes 104 | tf_op jit(solution)/shard_map/ppermute | solution.py:497
  3.0 3.7 %collective-permute-start.1 = (s32[1,8]{1,0:T(1,128)}, s32[1,8]{1,0:T(1,128)S(1)}, u32[]{:S(2)}, u32[]{:S(2)}) collective-permute-start(s32[1,8]{1,0:T(1,128)} %refs_0_.11), channel_id=1, source_target_pairs={{0,4},{2,6},{4,0},{6,2},{8,12},{10,14},{12,8},{14,10},{1,5},{3,7},... | collective-permute-start | bytes 104 | tf_op jit(solution)/shard_map/ppermute | solution.py:497
  4.6 4.6 %collective-permute-start.2 = (s32[1,8]{1,0:T(1,128)}, s32[1,8]{1,0:T(1,128)S(1)}, u32[]{:S(2)}, u32[]{:S(2)}) collective-permute-start(s32[1,8]{1,0:T(1,128)} %refs_0_.11), channel_id=1, source_target_pairs={{0,6},{2,4},{4,2},{6,0},{8,14},{10,12},{12,10},{14,8},{1,7},{3,5},... | collective-permute-start | bytes 104 | tf_op jit(solution)/shard_map/ppermute | solution.py:497
  9.2 28.2 %collective-permute-start.3 = (bf16[2,64,2048]{2,1,0:T(8,128)(2,1)S(1)}, bf16[2,64,2048]{2,1,0:T(8,128)(2,1)S(1)}, u32[]{:S(2)}, u32[]{:S(2)}) collective-permute-start(bf16[2,64,2048]{2,1,0:T(8,128)(2,1)S(1)} %dynamic-slice_bitcast_fusion.refs_4_), channel_id=1, source_target_pairs={{0,8},{2,10},{4,12},{6,14},{8,0},{10,2},{12,4},{14,6},{1,9},{3,11}... | collective-permute-start | bytes 1572872 | tf_op jit(solution)/shard_map/ppermute | solution.py:497
  12.7 8.2 %collective-permute-start.4 = (bf16[2,64,1024]{2,1,0:T(8,128)(2,1)S(1)}, bf16[2,64,1024]{2,1,0:T(8,128)(2,1)S(1)}, u32[]{:S(2)}, u32[]{:S(2)}) collective-permute-start(bf16[2,64,1024]{2,1,0:T(8,128)(2,1)S(1)} %get-tuple-element.80), channel_id=1, source_target_pairs={{0,2},{2,0},{4,6},{6,4},{8,10},{10,8},{12,14},{14,12},{1,3},{3,1},... | collective-permute-start | bytes 786440 | tf_op jit(solution)/shard_map/ppermute | solution.py:497
  13.3 16.5 %collective-permute-start.5 = (bf16[2,64,1024]{2,1,0:T(8,128)(2,1)S(1)}, bf16[2,64,1024]{2,1,0:T(8,128)(2,1)S(1)}, u32[]{:S(2)}, u32[]{:S(2)}) collective-permute-start(bf16[2,64,1024]{2,1,0:T(8,128)(2,1)S(1)} %get-tuple-element.81), channel_id=1, source_target_pairs={{0,4},{2,6},{4,0},{6,2},{8,12},{10,14},{12,8},{14,10},{1,5},{3,7},... | collective-permute-start | bytes 786440 | tf_op jit(solution)/shard_map/ppermute | solution.py:497
  13.7 23.6 %collective-permute-start.6 = (bf16[2,64,1024]{2,1,0:T(8,128)(2,1)S(1)}, bf16[2,64,1024]{2,1,0:T(8,128)(2,1)S(1)}, u32[]{:S(2)}, u32[]{:S(2)}) collective-permute-start(bf16[2,64,1024]{2,1,0:T(8,128)(2,1)S(1)} %get-tuple-element.82), channel_id=1, source_target_pairs={{0,6},{2,4},{4,2},{6,0},{8,14},{10,12},{12,10},{14,8},{1,7},{3,5},... | collective-permute-start | bytes 786440 | tf_op jit(solution)/shard_map/ppermute | solution.py:497
  39.2 11.7 %collective-permute-start.7 = (bf16[2,64,1024]{2,1,0:T(8,128)(2,1)}, bf16[2,64,1024]{2,1,0:T(8,128)(2,1)S(1)}, u32[]{:S(2)}, u32[]{:S(2)}) collective-permute-start(bf16[2,64,1024]{2,1,0:T(8,128)(2,1)} %get-tuple-element.93), channel_id=1, source_target_pairs={{0,2},{2,0},{4,6},{6,4},{8,10},{10,8},{12,14},{14,12},{1,3},{3,1},... | collective-permute-start | bytes 786440 | tf_op jit(solution)/shard_map/ppermute | solution.py:497
  39.7 11.2 %collective-permute-start.8 = (bf16[2,64,1024]{2,1,0:T(8,128)(2,1)}, bf16[2,64,1024]{2,1,0:T(8,128)(2,1)S(1)}, u32[]{:S(2)}, u32[]{:S(2)}) collective-permute-start(bf16[2,64,1024]{2,1,0:T(8,128)(2,1)} %get-tuple-element.94), channel_id=1, source_target_pairs={{0,4},{2,6},{4,0},{6,2},{8,12},{10,14},{12,8},{14,10},{1,5},{3,7},... | collective-permute-start | bytes 786440 | tf_op jit(solution)/shard_map/ppermute | solution.py:497
  39.7 11.7 %collective-permute-start.9 = (bf16[2,64,1024]{2,1,0:T(8,128)(2,1)}, bf16[2,64,1024]{2,1,0:T(8,128)(2,1)S(1)}, u32[]{:S(2)}, u32[]{:S(2)}) collective-permute-start(bf16[2,64,1024]{2,1,0:T(8,128)(2,1)} %get-tuple-element.95), channel_id=1, source_target_pairs={{0,6},{2,4},{4,2},{6,0},{8,14},{10,12},{12,10},{14,8},{1,7},{3,5},... | collective-permute-start | bytes 786440 | tf_op jit(solution)/shard_map/ppermute | solution.py:497
  43.9 2.2 %collective-permute-start.10 = (f32[5,24,256]{2,1,0:T(8,128)S(1)}, f32[5,24,256]{2,1,0:T(8,128)S(1)}, u32[]{:S(2)}, u32[]{:S(2)}) collective-permute-start(f32[5,24,256]{2,1,0:T(8,128)S(1)} %shard_map.102.refs_2_), channel_id=1, source_target_pairs={{0,1},{1,0},{2,3},{3,2},{4,5},{5,4},{6,7},{7,6},{8,9},{9,8},{10,11... | collective-permute-start | bytes 368648 | tf_op jit(solution)/shard_map/ppermute | solution.py:500
  64.6 5.6 %collective-permute-start.12 = (bf16[1,64,1024]{2,1,0:T(8,128)(2,1)S(1)}, bf16[1,64,1024]{2,1,0:T(8,128)(2,1)S(1)}, u32[]{:S(2)}, u32[]{:S(2)}) collective-permute-start(bf16[1,64,1024]{2,1,0:T(8,128)(2,1)S(1)} %get-tuple-element.118), channel_id=1, source_target_pairs={{0,2},{2,0},{4,6},{6,4},{8,10},{10,8},{12,14},{14,12},{1,3},{3,1},... | collective-permute-start | bytes 393224 | tf_op jit(solution)/shard_map/ppermute | solution.py:497
  64.9 6.4 %collective-permute-start.13 = (bf16[1,64,1024]{2,1,0:T(8,128)(2,1)S(1)}, bf16[1,64,1024]{2,1,0:T(8,128)(2,1)S(1)}, u32[]{:S(2)}, u32[]{:S(2)}) collective-permute-start(bf16[1,64,1024]{2,1,0:T(8,128)(2,1)S(1)} %get-tuple-element.120), channel_id=1, source_target_pairs={{0,4},{2,6},{4,0},{6,2},{8,12},{10,14},{12,8},{14,10},{1,5},{3,7},... | collective-permute-start | bytes 393224 | tf_op jit(solution)/shard_map/ppermute | solution.py:497
  65.8 8.3 %collective-permute-start.14 = (bf16[1,64,1024]{2,1,0:T(8,128)(2,1)S(1)}, bf16[1,64,1024]{2,1,0:T(8,128)(2,1)S(1)}, u32[]{:S(2)}, u32[]{:S(2)}) collective-permute-start(bf16[1,64,1024]{2,1,0:T(8,128)(2,1)S(1)} %get-tuple-element.122), channel_id=1, source_target_pairs={{0,6},{2,4},{4,2},{6,0},{8,14},{10,12},{12,10},{14,8},{1,7},{3,5},... | collective-permute-start | bytes 393224 | tf_op jit(solution)/shard_map/ppermute | solution.py:497
  75.1 15.8 %collective-permute-start.18 = (bf16[1,64,2048]{2,1,0:T(8,128)(2,1)S(1)}, bf16[1,64,2048]{2,1,0:T(8,128)(2,1)S(1)}, u32[]{:S(2)}, u32[]{:S(2)}) collective-permute-start(bf16[1,64,2048]{2,1,0:T(8,128)(2,1)S(1)} %shard_map.106), channel_id=1, source_target_pairs={{0,8},{2,10},{4,12},{6,14},{8,0},{10,2},{12,4},{14,6},{1,9},{3,11}... | collective-permute-start | bytes 786440 | tf_op jit(solution)/shard_map/ppermute | solution.py:497
  75.2 6.4 %collective-permute-start.15 = (bf16[1,64,1024]{2,1,0:T(8,128)(2,1)S(1)}, bf16[1,64,1024]{2,1,0:T(8,128)(2,1)S(1)}, u32[]{:S(2)}, u32[]{:S(2)}) collective-permute-start(bf16[1,64,1024]{2,1,0:T(8,128)(2,1)S(1)} %get-tuple-element.129), channel_id=1, source_target_pairs={{0,2},{2,0},{4,6},{6,4},{8,10},{10,8},{12,14},{14,12},{1,3},{3,1},... | collective-permute-start | bytes 393224 | tf_op jit(solution)/shard_map/ppermute | solution.py:497
  75.7 8.7 %collective-permute-start.16 = (bf16[1,64,1024]{2,1,0:T(8,128)(2,1)S(1)}, bf16[1,64,1024]{2,1,0:T(8,128)(2,1)S(1)}, u32[]{:S(2)}, u32[]{:S(2)}) collective-permute-start(bf16[1,64,1024]{2,1,0:T(8,128)(2,1)S(1)} %get-tuple-element.130), channel_id=1, source_target_pairs={{0,4},{2,6},{4,0},{6,2},{8,12},{10,14},{12,8},{14,10},{1,5},{3,7},... | collective-permute-start | bytes 393224 | tf_op jit(solution)/shard_map/ppermute | solution.py:497
  76.4 9.4 %collective-permute-start.17 = (bf16[1,64,1024]{2,1,0:T(8,128)(2,1)S(1)}, bf16[1,64,1024]{2,1,0:T(8,128)(2,1)S(1)}, u32[]{:S(2)}, u32[]{:S(2)}) collective-permute-start(bf16[1,64,1024]{2,1,0:T(8,128)(2,1)S(1)} %get-tuple-element.131), channel_id=1, source_target_pairs={{0,6},{2,4},{4,2},{6,0},{8,14},{10,12},{12,10},{14,8},{1,7},{3,5},... | collective-permute-start | bytes 393224 | tf_op jit(solution)/shard_map/ppermute | solution.py:497
  86.8 14.4 %collective-permute-start.22 = (bf16[1,64,2048]{2,1,0:T(8,128)(2,1)S(1)}, bf16[1,64,2048]{2,1,0:T(8,128)(2,1)S(1)}, u32[]{:S(2)}, u32[]{:S(2)}) collective-permute-start(bf16[1,64,2048]{2,1,0:T(8,128)(2,1)S(1)} %shard_map.107), channel_id=1, source_target_pairs={{0,8},{2,10},{4,12},{6,14},{8,0},{10,2},{12,4},{14,6},{1,9},{3,11}... | collective-permute-start | bytes 786440 | tf_op jit(solution)/shard_map/ppermute | solution.py:497
  90.9 10.3 %collective-permute-start.19 = (bf16[2,64,1024]{2,1,0:T(8,128)(2,1)S(1)}, bf16[2,64,1024]{2,1,0:T(8,128)(2,1)S(1)}, u32[]{:S(2)}, u32[]{:S(2)}) collective-permute-start(bf16[2,64,1024]{2,1,0:T(8,128)(2,1)S(1)} %get-tuple-element.138), channel_id=1, source_target_pairs={{0,2},{2,0},{4,6},{6,4},{8,10},{10,8},{12,14},{14,12},{1,3},{3,1},... | collective-permute-start | bytes 786440 | tf_op jit(solution)/shard_map/ppermute | solution.py:497
  91.5 13.2 %collective-permute-start.20 = (bf16[2,64,1024]{2,1,0:T(8,128)(2,1)S(1)}, bf16[2,64,1024]{2,1,0:T(8,128)(2,1)S(1)}, u32[]{:S(2)}, u32[]{:S(2)}) collective-permute-start(bf16[2,64,1024]{2,1,0:T(8,128)(2,1)S(1)} %get-tuple-element.139), channel_id=1, source_target_pairs={{0,4},{2,6},{4,0},{6,2},{8,12},{10,14},{12,8},{14,10},{1,5},{3,7},... | collective-permute-start | bytes 786440 | tf_op jit(solution)/shard_map/ppermute | solution.py:497
  93.2 14.1 %collective-permute-start.21 = (bf16[2,64,1024]{2,1,0:T(8,128)(2,1)S(1)}, bf16[2,64,1024]{2,1,0:T(8,128)(2,1)S(1)}, u32[]{:S(2)}, u32[]{:S(2)}) collective-permute-start(bf16[2,64,1024]{2,1,0:T(8,128)(2,1)S(1)} %get-tuple-element.140), channel_id=1, source_target_pairs={{0,6},{2,4},{4,2},{6,0},{8,14},{10,12},{12,10},{14,8},{1,7},{3,5},... | collective-permute-start | bytes 786440 | tf_op jit(solution)/shard_map/ppermute | solution.py:497
  108.6 1.6 %collective-permute-start.23 = (bf16[2,64,1024]{2,1,0:T(8,128)(2,1)S(1)}, bf16[2,64,1024]{2,1,0:T(8,128)(2,1)S(1)}, u32[]{:S(2)}, u32[]{:S(2)}) collective-permute-start(bf16[2,64,1024]{2,1,0:T(8,128)(2,1)S(1)} %get-tuple-element.144), channel_id=1, source_target_pairs={{0,1},{1,0},{2,3},{3,2},{4,5},{5,4},{6,7},{7,6},{8,9},{9,8},{10,11... | collective-permute-start | bytes 786440 | tf_op jit(solution)/shard_map/ppermute | solution.py:500
  (1 other events, 4.6 us)

commit v8 on v7

--- a/solution.py
+++ b/solution.py
@@ -146,26 +146,29 @@
 
 
 def pick_kernel(peers, *refs):
-    sets, full, outs = refs[:peers], refs[peers], refs[peers + 1 :]
+    sets, fulls, outs = refs[:peers], refs[peers:-peers], refs[-peers:]
     for k in range(peers):
         for q in range(UMAX):
             cols = pl.ds(pl.multiple_of(sets[k][0, q] * FB, FB), FB)
-            outs[k][:, :, q * FB : (q + 1) * FB] = full[:, :, cols]
-
-
-def pick(sets, full):
-    nb, sub, cols = full.shape
+            picked = fulls[0][:, :, cols]
+            for full in fulls[1:]:
+                picked = picked + full[:, :, cols]
+            outs[k][:, :, q * FB : (q + 1) * FB] = picked
+
+
+def pick(sets, fulls):
+    nb, sub, cols = fulls[0].shape
     shape = (nb, sub, UMAX * FB)
     peers = len(sets)
     return call(
         functools.partial(pick_kernel, peers),
         sets,
-        [full],
-        [whole(full.shape)],
-        [jax.ShapeDtypeStruct(shape, full.dtype)] * peers,
+        fulls,
+        [whole(full.shape) for full in fulls],
+        [jax.ShapeDtypeStruct(shape, fulls[0].dtype)] * peers,
         [whole(shape)] * peers,
         [],
-        cost=(0, 2 * nb * sub * (cols + peers * UMAX * FB)),
+        cost=(0, 2 * nb * sub * (cols * len(fulls) + peers * UMAX * FB)),
     )
 
 
@@ -339,8 +342,10 @@
     half = keep.shape[2]
     for out, side in ((keep, core[0]), (give, 1 - core[0])):
         cols = pl.ds(pl.multiple_of(side * half, FB), half)
-        for b, far in enumerate(fars):
-            out[b] = (total[b, :, cols] + far[0, :, cols].astype(jnp.float32)).astype(out.dtype)
+        here = total[:, :, cols]
+        for far in fars:
+            here = here + far[:, :, cols].astype(jnp.float32)
+        out[...] = here.astype(out.dtype)
 
 
 def finish(sets, core, terms, fars):
@@ -457,9 +462,7 @@
     pieces = len(parts)
     near = pieces // 2
     out_shapes = [
-        jax.ShapeDtypeStruct((nb if k < near else 1, sub, wide), jnp.bfloat16 if k % near else jnp.float32)
-        for k in range(pieces)
-        for _ in range(1 if k < near else nb)
+        jax.ShapeDtypeStruct((nb, sub, wide), jnp.bfloat16 if k % near else jnp.float32) for k in range(pieces)
     ]
     flops = 2 * batches * 2 * width * (width // 2) * pts
     return call(
@@ -503,15 +506,23 @@
         return pltpu.with_memory_space_constraint(x, pltpu.HBM)
 
     own = lax.dynamic_index_in_dim(density.reshape(nb, cores, sub, cols), r, 1, keepdims=False)
+    def mirror(x, meanwhile):
+        goes = ([], [])
+        for a in range(n):
+            inner = (a & (near // 2) != 0) != (a & near != 0)
+            goes[inner].append((a, a ^ near))
+        first = lax.ppermute(x, "dom", goes[0])
+        x, first, meanwhile = lax.optimization_barrier((x, first, meanwhile))
+        return [first, lax.ppermute(x, "dom", goes[1])], meanwhile
+
     sets = [touched] + [swap(touched, k) for k in range(1, near)]
     own, sets = lax.optimization_barrier((own, sets))
-    far = swap(own, near)
     sets[0] = stay(touched)
-    picked = pick(sets, own)
+    fars, picked = mirror(own, pick(sets, [own]))
     parts = [picked[0]] + [swap(picked[k], k) for k in range(1, near)]
     xs = (stay(basis), across(basis))
-    far, parts = lax.optimization_barrier((far, parts))
-    picked = pick(sets, far)
+    fars, parts = lax.optimization_barrier((fars, parts))
+    picked = pick(sets, fars)
     small = (points.transpose(1, 0, 2), weights, blocks.T, counts)
     small, centers, widths, picked = lax.optimization_barrier((small, centers, widths, picked))
     parts += [picked[0]] + [swap(picked[k], k) for k in range(1, near)]
@@ -524,16 +535,12 @@
     parts, table, centre = lax.optimization_barrier((parts, table, centre))
 
     sums = batch_sums(table, xs, (packed, packed_b), centre, parts)
-    sums, far_sums = sums[:near], sums[near:]
-    far_terms = []
-    for b in range(nb):
-        chunk = [far_sums[b]] + [swap(far_sums[nb * k + b], k) for k in range(1, near)]
-        merged = merge(sets, chunk, cols)
-        sums, far_sums, merged = lax.optimization_barrier((sums, far_sums, merged))
-        far_terms.append(swap(merged, near))
-    sums, far_terms[0] = lax.optimization_barrier((sums, far_terms[0]))
+    far_terms = [sums[near]] + [swap(sums[near + k], k) for k in range(1, near)]
+    merged = merge(sets, far_terms, cols)
+    sums, merged = lax.optimization_barrier((sums, merged))
+    fars, sums = mirror(merged, sums)
     terms = [sums[0]] + [swap(sums[k], k) for k in range(1, near)]
-    keep, give = finish(sets, core, terms, far_terms)
+    keep, give = finish(sets, core, terms, fars)
     got = across(give)
     pair = jnp.where(r == 0, jnp.stack([keep, got], axis=1), jnp.stack([got, keep], axis=1))
     return pair.reshape(nb * FB, cols // cores)

time: 113 us -> 139 us (1.23); the launches traced: 111 us -> 139 us
  waiting for transfers between devices: 53.5 us -> 79.7 us
  starting transfers between devices: 29.2 us -> 31.4 us
    ppermute x0 -> x4, waiting for transfers between devices: none -> 19.2 us  [the longest x2 19.2 us: mirror(): first = lax.ppermute(x, 'dom', goes[0])]
    ppermute x0 -> x4, starting transfers between devices: none -> 12.1 us  [the longest x2 9.55 us: mirror(): first = lax.ppermute(x, 'dom', goes[0])]
    ppermute x21 -> x15, starting transfers between devices: 28.6 us -> 18.7 us  [swap(): return lax.ppermute(x, 'dom', [(a, a ^ k) for a in range(n)])]
    ppermute x21 -> x15, waiting for transfers between devices: 52 us -> 59 us  [swap(): return lax.ppermute(x, 'dom', [(a, a ^ k) for a in range(n)])]
    pallas_call x9 -> x8, Pallas kernels: 27.3 us -> 27 us  [call(): pl.pallas_call(kernel, grid_spec=pltpu.PrefetchScalarGridSpec(num_scalar_...]
  transfers between devices with their start and end apart: 24 -> 22, of which waited for: 16 -> 15; matrix products, arithmetic and copies ran while one was open for 0% -> 0% of each run, Pallas kernels for 11% -> 8%
where the time goes in v8:
time: 139 us
  waiting for transfers between devices  79.7 us (57%)
  starting transfers between devices  31.4 us (23%)
  Pallas kernels  27 us (19%)
    ppermute x15, waiting for transfers between devices, swap(): return lax.ppermute(x, 'dom', [(a, a ^ k) for a in range(n)])  59 us
    pallas_call x8, Pallas kernels, call(): pl.pallas_call(kernel, grid_spec=pltpu.PrefetchScalarGridSpec(num_scalar_...  27 us
    ppermute x2, waiting for transfers between devices, mirror(): first = lax.ppermute(x, 'dom', goes[0])  19.2 us
    ppermute x15, starting transfers between devices, swap(): return lax.ppermute(x, 'dom', [(a, a ^ k) for a in range(n)])  18.7 us
    ppermute x2, starting transfers between devices, mirror(): first = lax.ppermute(x, 'dom', goes[0])  9.55 us
  transfers between devices with their start and end apart: 22, of which 15 were waited for; matrix products, arithmetic and copies ran while one was open for 0% of the time, Pallas kernels for 8%

profile of v8, /device:TPU:0, one launch (start us, length us, event | category | flops | bytes accessed | tf_op | source)
XLA Modules:
  0.0 139.2 jit_solution(14278676818969246757)
XLA Ops:
  0.5 2.6 %collective-permute-start = (s32[1,8]{1,0:T(1,128)}, s32[1,8]{1,0:T(1,128)S(1)}, u32[]{:S(2)}, u32[]{:S(2)}) collective-permute-start(s32[1,8]{1,0:T(1,128)} %refs_0_.9), channel_id=1, source_target_pairs={{0,2},{2,0},{4,6},{6,4},{8,10},{10,8},{12,14},{14,12},{1,3},{3,1},... | collective-permute-start | bytes 104 | tf_op jit(solution)/shard_map/ppermute | solution.py:500
  4.7 2.0 %collective-permute-done.1.refs_2_ = s32[1,8]{1,0:T(1,128)S(1)} collective-permute-done((s32[1,8]{1,0:T(1,128)}, s32[1,8]{1,0:T(1,128)S(1)}, u32[]{:S(2)}, u32[]{:S(2)}) %collective-permute-start.1) | collective-permute-done | bytes 64 | tf_op jit(solution)/shard_map/ppermute | solution.py:500
  6.7 2.5 %collective-permute-done.2.refs_3_ = s32[1,8]{1,0:T(1,128)S(1)} collective-permute-done((s32[1,8]{1,0:T(1,128)}, s32[1,8]{1,0:T(1,128)S(1)}, u32[]{:S(2)}, u32[]{:S(2)}) %collective-permute-start.2) | collective-permute-done | bytes 64 | tf_op jit(solution)/shard_map/ppermute | solution.py:500
  9.2 4.5 %collective-permute-start.3 = (bf16[2,64,2048]{2,1,0:T(8,128)(2,1)S(1)}, bf16[2,64,2048]{2,1,0:T(8,128)(2,1)S(1)}, u32[]{:S(2)}, u32[]{:S(2)}) collective-permute-start(bf16[2,64,2048]{2,1,0:T(8,128)(2,1)S(1)} %dynamic-slice_bitcast_fusion.refs_4_), channel_id=1, source_target_pairs={{0,8},{2,10},{12,4},{14,6},{1,9},{3,11},{13,5},{15,7},{16,24},{18,... | collective-permute-start | bytes 1572872 | tf_op jit(solution)/shard_map/ppermute | solution.py:514
  14.7 9.1 %collective-permute-done.3.refs_4_ = bf16[2,64,2048]{2,1,0:T(8,128)(2,1)S(1)} collective-permute-done((bf16[2,64,2048]{2,1,0:T(8,128)(2,1)S(1)}, bf16[2,64,2048]{2,1,0:T(8,128)(2,1)S(1)}, u32[]{:S(2)}, u32[]{:S(2)}) %collective-permute-start.3) | collective-permute-done | bytes 524320 | tf_op jit(solution)/shard_map/ppermute | solution.py:514
  28.6 2.9 %collective-permute-done.5.refs_6_ = bf16[2,64,1024]{2,1,0:T(8,128)(2,1)S(1)} collective-permute-done((bf16[2,64,1024]{2,1,0:T(8,128)(2,1)S(1)}, bf16[2,64,1024]{2,1,0:T(8,128)(2,1)S(1)}, u32[]{:S(2)}, u32[]{:S(2)}) %collective-permute-start.5) | collective-permute-done | bytes 262176 | tf_op jit(solution)/shard_map/ppermute | solution.py:500
  31.5 12.6 %collective-permute-done.6.refs_7_ = bf16[2,64,1024]{2,1,0:T(8,128)(2,1)S(1)} collective-permute-done((bf16[2,64,1024]{2,1,0:T(8,128)(2,1)S(1)}, bf16[2,64,1024]{2,1,0:T(8,128)(2,1)S(1)}, u32[]{:S(2)}, u32[]{:S(2)}) %collective-permute-start.6) | collective-permute-done | bytes 262176 | tf_op jit(solution)/shard_map/ppermute | solution.py:500
  44.1 5.1 %collective-permute-done.7.refs_8_ = bf16[2,64,1024]{2,1,0:T(8,128)(2,1)S(1)} collective-permute-done((bf16[2,64,1024]{2,1,0:T(8,128)(2,1)S(1)}, bf16[2,64,1024]{2,1,0:T(8,128)(2,1)S(1)}, u32[]{:S(2)}, u32[]{:S(2)}) %collective-permute-start.7) | collective-permute-done | bytes 262176 | tf_op jit(solution)/shard_map/ppermute | solution.py:500
  49.2 2.0 %shard_map.101 = (bf16[2,64,1024]{2,1,0:T(8,128)(2,1)S(1)}, bf16[2,64,1024]{2,1,0:T(8,128)(2,1)}, bf16[2,64,1024]{2,1,0:T(8,128)(2,1)}, bf16[2,64,1024]{2,1,0:T(8,128)(2,1)}) custom-call(s32[1,8]{1,0:T(1,128)} %refs_0_.9, s32[1,8]{1,0:T(1,128)S(1)} %collective-permute-done.refs_1_, s32[1,8]{1,0:T(1,128)S(1)} %collective-permute-done.1.refs_2_, ...), custom_call_target="tpu_custom_call" | custom-call | bytes 2097152 | tf_op jit(solution)/shard_map/pallas_call | solution.py:129
  51.7 3.0 %collective-permute-start.9 = (bf16[2,64,1024]{2,1,0:T(8,128)(2,1)}, bf16[2,64,1024]{2,1,0:T(8,128)(2,1)S(1)}, u32[]{:S(2)}, u32[]{:S(2)}) collective-permute-start(bf16[2,64,1024]{2,1,0:T(8,128)(2,1)} %get-tuple-element.96), channel_id=1, source_target_pairs={{0,4},{2,6},{4,0},{6,2},{8,12},{10,14},{12,8},{14,10},{1,5},{3,7},... | collective-permute-start | bytes 786440 | tf_op jit(solution)/shard_map/ppermute | solution.py:500
  55.9 2.1 %shard_map.104.refs_4_ = f32[4,8,64,128]{3,2,1,0:T(8,128)S(1)} custom-call(s32[1,8]{1,0:T(1,128)} %refs_0_.9, s32[1]{0:T(128)} %bitcast.2.core.refs_4_, f32[3,2048]{1,0:T(4,128)} %centers, f32[1,2048]{1,0:T(1,128)} %bitcast.17), custom_call_target="tpu_custom_call" | custom-call | bytes 2097152 | tf_op jit(solution)/shard_map/pallas_call | solution.py:129
  58.1 4.8 %shard_map.103.table = s32[632]{0:T(1024)S(1)} custom-call(s32[1]{0:T(128)} %bitcast.5.me, s32[16]{0:T(128)} %owner.1, s32[1,8]{1,0:T(1,128)} %refs_0_.9, s32[4,24]{1,0:T(4,128)} %bitcast.19, f32[5,24,256]{2,1,0:T(8,128)S(1)} %collective-permute-done.11.packed.refs_3_, s32[24]{0:T(128)} %counts.1), custom_call_target="tpu_custom_call" | custom-call | bytes 1536 | tf_op jit(solution)/shard_map/pallas_call | solution.py:129
  62.9 1.9 %collective-permute-done.8.refs_10_ = bf16[2,64,1024]{2,1,0:T(8,128)(2,1)S(1)} collective-permute-done((bf16[2,64,1024]{2,1,0:T(8,128)(2,1)}, bf16[2,64,1024]{2,1,0:T(8,128)(2,1)S(1)}, u32[]{:S(2)}, u32[]{:S(2)}) %collective-permute-start.8) | collective-permute-done | bytes 262176 | tf_op jit(solution)/shard_map/ppermute | solution.py:500
  64.8 13.2 %shard_map.105 = (f32[2,64,1024]{2,1,0:T(8,128)S(1)}, bf16[2,64,1024]{2,1,0:T(8,128)(2,1)S(1)}, bf16[2,64,1024]{2,1,0:T(8,128)(2,1)S(1)}, bf16[2,64,1024]{2,1,0:...) custom-call(s32[632]{0:T(1024)S(1)} %shard_map.103.table, ...), custom_call_target="tpu_custom_call" | custom-call | flops 6442450944 | bytes 12582912 | tf_op jit(solution)/shard_map/pallas_call | solution.py:129
  79.7 1.7 %collective-permute-start.14 = (bf16[2,64,1024]{2,1,0:T(8,128)(2,1)S(1)}, bf16[2,64,1024]{2,1,0:T(8,128)(2,1)S(1)}, u32[]{:S(2)}, u32[]{:S(2)}) collective-permute-start(bf16[2,64,1024]{2,1,0:T(8,128)(2,1)S(1)} %get-tuple-element.120), channel_id=1, source_target_pairs={{0,4},{2,6},{4,0},{6,2},{8,12},{10,14},{12,8},{14,10},{1,5},{3,7},... | collective-permute-start | bytes 786440 | tf_op jit(solution)/shard_map/ppermute | solution.py:500
  81.6 3.8 %collective-permute-done.13.refs_5_ = bf16[2,64,1024]{2,1,0:T(8,128)(2,1)S(1)} collective-permute-done((bf16[2,64,1024]{2,1,0:T(8,128)(2,1)S(1)}, bf16[2,64,1024]{2,1,0:T(8,128)(2,1)S(1)}, u32[]{:S(2)}, u32[]{:S(2)}) %collective-permute-start.13) | collective-permute-done | bytes 262176 | tf_op jit(solution)/shard_map/ppermute | solution.py:500
  85.4 3.5 %collective-permute-done.14.refs_6_ = bf16[2,64,1024]{2,1,0:T(8,128)(2,1)S(1)} collective-permute-done((bf16[2,64,1024]{2,1,0:T(8,128)(2,1)S(1)}, bf16[2,64,1024]{2,1,0:T(8,128)(2,1)S(1)}, u32[]{:S(2)}, u32[]{:S(2)}) %collective-permute-start.14) | collective-permute-done | bytes 262176 | tf_op jit(solution)/shard_map/ppermute | solution.py:500
  88.9 4.1 %collective-permute-done.15.refs_7_ = bf16[2,64,1024]{2,1,0:T(8,128)(2,1)S(1)} collective-permute-done((bf16[2,64,1024]{2,1,0:T(8,128)(2,1)S(1)}, bf16[2,64,1024]{2,1,0:T(8,128)(2,1)S(1)}, u32[]{:S(2)}, u32[]{:S(2)}) %collective-permute-start.15) | collective-permute-done | bytes 262176 | tf_op jit(solution)/shard_map/ppermute | solution.py:500
  94.3 5.0 %collective-permute-start.16 = (bf16[2,64,2048]{2,1,0:T(8,128)(2,1)S(1)}, bf16[2,64,2048]{2,1,0:T(8,128)(2,1)S(1)}, u32[]{:S(2)}, u32[]{:S(2)}) collective-permute-start(bf16[2,64,2048]{2,1,0:T(8,128)(2,1)S(1)} %shard_map.106), channel_id=1, source_target_pairs={{0,8},{2,10},{12,4},{14,6},{1,9},{3,11},{13,5},{15,7},{16,24},{18,... | collective-permute-start | bytes 1572872 | tf_op jit(solution)/shard_map/ppermute | solution.py:514
  99.3 10.1 %collective-permute-done.16.refs_9_ = bf16[2,64,2048]{2,1,0:T(8,128)(2,1)S(1)} collective-permute-done((bf16[2,64,2048]{2,1,0:T(8,128)(2,1)S(1)}, bf16[2,64,2048]{2,1,0:T(8,128)(2,1)S(1)}, u32[]{:S(2)}, u32[]{:S(2)}) %collective-permute-start.16) | collective-permute-done | bytes 524320 | tf_op jit(solution)/shard_map/ppermute | solution.py:514
  111.5 3.2 %collective-permute-start.18 = (bf16[2,64,1024]{2,1,0:T(8,128)(2,1)S(1)}, bf16[2,64,1024]{2,1,0:T(8,128)(2,1)S(1)}, u32[]{:S(2)}, u32[]{:S(2)}) collective-permute-start(bf16[2,64,1024]{2,1,0:T(8,128)(2,1)S(1)} %get-tuple-element.129), channel_id=1, source_target_pairs={{0,4},{2,6},{4,0},{6,2},{8,12},{10,14},{12,8},{14,10},{1,5},{3,7},... | collective-permute-start | bytes 786440 | tf_op jit(solution)/shard_map/ppermute | solution.py:500
  114.6 2.5 %collective-permute-done.17.refs_6_ = bf16[2,64,1024]{2,1,0:T(8,128)(2,1)S(1)} collective-permute-done((bf16[2,64,1024]{2,1,0:T(8,128)(2,1)S(1)}, bf16[2,64,1024]{2,1,0:T(8,128)(2,1)S(1)}, u32[]{:S(2)}, u32[]{:S(2)}) %collective-permute-start.17) | collective-permute-done | bytes 262176 | tf_op jit(solution)/shard_map/ppermute | solution.py:500
  117.2 12.6 %collective-permute-done.18.refs_7_ = bf16[2,64,1024]{2,1,0:T(8,128)(2,1)S(1)} collective-permute-done((bf16[2,64,1024]{2,1,0:T(8,128)(2,1)S(1)}, bf16[2,64,1024]{2,1,0:T(8,128)(2,1)S(1)}, u32[]{:S(2)}, u32[]{:S(2)}) %collective-permute-start.18) | collective-permute-done | bytes 262176 | tf_op jit(solution)/shard_map/ppermute | solution.py:500
  129.8 5.5 %collective-permute-done.19.refs_8_ = bf16[2,64,1024]{2,1,0:T(8,128)(2,1)S(1)} collective-permute-done((bf16[2,64,1024]{2,1,0:T(8,128)(2,1)S(1)}, bf16[2,64,1024]{2,1,0:T(8,128)(2,1)S(1)}, u32[]{:S(2)}, u32[]{:S(2)}) %collective-permute-start.19) | collective-permute-done | bytes 262176 | tf_op jit(solution)/shard_map/ppermute | solution.py:500
  (33 shorter events, 18.7 us)
Async XLA Ops:
  0.0 4.6 %copy-start = (bf16[256,2048]{1,0:T(8,128)(2,1)S(1)}, bf16[256,2048]{1,0:T(8,128)(2,1)}, u32[]{:S(2)}) copy-start(bf16[256,2048]{1,0:T(8,128)(2,1)} %param.10) | copy-start | bytes 3145732
  0.0 64.8 %collective-permute-start.12 = (bf16[24,512,256]{2,1,0:T(8,128)(2,1)}, bf16[24,512,256]{2,1,0:T(8,128)(2,1)}, u32[]{:S(2)}, u32[]{:S(2)}) collective-permute-start(bf16[24,512,256]{2,1,0:T(8,128)(2,1)} %refs_0_.7), channel_id=1, source_target_pairs={{0,1},{1,0},{2,3},{3,2},{4,5},{5,4},{6,7},{7,6},{8,9},{9,8},{10,11... | collective-permute-start | bytes 18874376 | tf_op jit(solution)/shard_map/ppermute | solution.py:503
  0.5 4.2 %collective-permute-start = (s32[1,8]{1,0:T(1,128)}, s32[1,8]{1,0:T(1,128)S(1)}, u32[]{:S(2)}, u32[]{:S(2)}) collective-permute-start(s32[1,8]{1,0:T(1,128)} %refs_0_.9), channel_id=1, source_target_pairs={{0,2},{2,0},{4,6},{6,4},{8,10},{10,8},{12,14},{14,12},{1,3},{3,1},... | collective-permute-start | bytes 104 | tf_op jit(solution)/shard_map/ppermute | solution.py:500
  3.0 3.7 %collective-permute-start.1 = (s32[1,8]{1,0:T(1,128)}, s32[1,8]{1,0:T(1,128)S(1)}, u32[]{:S(2)}, u32[]{:S(2)}) collective-permute-start(s32[1,8]{1,0:T(1,128)} %refs_0_.9), channel_id=1, source_target_pairs={{0,4},{2,6},{4,0},{6,2},{8,12},{10,14},{12,8},{14,10},{1,5},{3,7},... | collective-permute-start | bytes 104 | tf_op jit(solution)/shard_map/ppermute | solution.py:500
  4.6 4.6 %collective-permute-start.2 = (s32[1,8]{1,0:T(1,128)}, s32[1,8]{1,0:T(1,128)S(1)}, u32[]{:S(2)}, u32[]{:S(2)}) collective-permute-start(s32[1,8]{1,0:T(1,128)} %refs_0_.9), channel_id=1, source_target_pairs={{0,6},{2,4},{4,2},{6,0},{8,14},{10,12},{12,10},{14,8},{1,7},{3,5},... | collective-permute-start | bytes 104 | tf_op jit(solution)/shard_map/ppermute | solution.py:500
  9.2 14.5 %collective-permute-start.3 = (bf16[2,64,2048]{2,1,0:T(8,128)(2,1)S(1)}, bf16[2,64,2048]{2,1,0:T(8,128)(2,1)S(1)}, u32[]{:S(2)}, u32[]{:S(2)}) collective-permute-start(bf16[2,64,2048]{2,1,0:T(8,128)(2,1)S(1)} %dynamic-slice_bitcast_fusion.refs_4_), channel_id=1, source_target_pairs={{0,8},{2,10},{12,4},{14,6},{1,9},{3,11},{13,5},{15,7},{16,24},{18,... | collective-permute-start | bytes 1572872 | tf_op jit(solution)/shard_map/ppermute | solution.py:514
  23.7 25.4 %collective-permute-start.4 = (bf16[2,64,2048]{2,1,0:T(8,128)(2,1)S(1)}, bf16[2,64,2048]{2,1,0:T(8,128)(2,1)S(1)}, u32[]{:S(2)}, u32[]{:S(2)}) collective-permute-start(bf16[2,64,2048]{2,1,0:T(8,128)(2,1)S(1)} %dynamic-slice_bitcast_fusion.refs_4_), channel_id=1, source_target_pairs={{4,12},{6,14},{8,0},{10,2},{5,13},{7,15},{9,1},{11,3},{20,28},{22,... | collective-permute-start | bytes 1572872 | tf_op jit(solution)/shard_map/ppermute | solution.py:516
  25.0 6.4 %collective-permute-start.5 = (bf16[2,64,1024]{2,1,0:T(8,128)(2,1)S(1)}, bf16[2,64,1024]{2,1,0:T(8,128)(2,1)S(1)}, u32[]{:S(2)}, u32[]{:S(2)}) collective-permute-start(bf16[2,64,1024]{2,1,0:T(8,128)(2,1)S(1)} %get-tuple-element.81), channel_id=1, source_target_pairs={{0,2},{2,0},{4,6},{6,4},{8,10},{10,8},{12,14},{14,12},{1,3},{3,1},... | collective-permute-start | bytes 786440 | tf_op jit(solution)/shard_map/ppermute | solution.py:500
  25.6 18.5 %collective-permute-start.6 = (bf16[2,64,1024]{2,1,0:T(8,128)(2,1)S(1)}, bf16[2,64,1024]{2,1,0:T(8,128)(2,1)S(1)}, u32[]{:S(2)}, u32[]{:S(2)}) collective-permute-start(bf16[2,64,1024]{2,1,0:T(8,128)(2,1)S(1)} %get-tuple-element.82), channel_id=1, source_target_pairs={{0,4},{2,6},{4,0},{6,2},{8,12},{10,14},{12,8},{14,10},{1,5},{3,7},... | collective-permute-start | bytes 786440 | tf_op jit(solution)/shard_map/ppermute | solution.py:500
  27.0 22.2 %collective-permute-start.7 = (bf16[2,64,1024]{2,1,0:T(8,128)(2,1)S(1)}, bf16[2,64,1024]{2,1,0:T(8,128)(2,1)S(1)}, u32[]{:S(2)}, u32[]{:S(2)}) collective-permute-start(bf16[2,64,1024]{2,1,0:T(8,128)(2,1)S(1)} %get-tuple-element.83), channel_id=1, source_target_pairs={{0,6},{2,4},{4,2},{6,0},{8,14},{10,12},{12,10},{14,8},{1,7},{3,5},... | collective-permute-start | bytes 786440 | tf_op jit(solution)/shard_map/ppermute | solution.py:500
  51.2 11.7 %collective-permute-start.10 = (bf16[2,64,1024]{2,1,0:T(8,128)(2,1)}, bf16[2,64,1024]{2,1,0:T(8,128)(2,1)S(1)}, u32[]{:S(2)}, u32[]{:S(2)}) collective-permute-start(bf16[2,64,1024]{2,1,0:T(8,128)(2,1)} %get-tuple-element.97), channel_id=1, source_target_pairs={{0,6},{2,4},{4,2},{6,0},{8,14},{10,12},{12,10},{14,8},{1,7},{3,5},... | collective-permute-start | bytes 786440 | tf_op jit(solution)/shard_map/ppermute | solution.py:500
  51.2 13.7 %collective-permute-start.8 = (bf16[2,64,1024]{2,1,0:T(8,128)(2,1)}, bf16[2,64,1024]{2,1,0:T(8,128)(2,1)S(1)}, u32[]{:S(2)}, u32[]{:S(2)}) collective-permute-start(bf16[2,64,1024]{2,1,0:T(8,128)(2,1)} %get-tuple-element.95), channel_id=1, source_target_pairs={{0,2},{2,0},{4,6},{6,4},{8,10},{10,8},{12,14},{14,12},{1,3},{3,1},... | collective-permute-start | bytes 786440 | tf_op jit(solution)/shard_map/ppermute | solution.py:500
  51.7 13.2 %collective-permute-start.9 = (bf16[2,64,1024]{2,1,0:T(8,128)(2,1)}, bf16[2,64,1024]{2,1,0:T(8,128)(2,1)S(1)}, u32[]{:S(2)}, u32[]{:S(2)}) collective-permute-start(bf16[2,64,1024]{2,1,0:T(8,128)(2,1)} %get-tuple-element.96), channel_id=1, source_target_pairs={{0,4},{2,6},{4,0},{6,2},{8,12},{10,14},{12,8},{14,10},{1,5},{3,7},... | collective-permute-start | bytes 786440 | tf_op jit(solution)/shard_map/ppermute | solution.py:500
  55.8 2.2 %collective-permute-start.11 = (f32[5,24,256]{2,1,0:T(8,128)S(1)}, f32[5,24,256]{2,1,0:T(8,128)S(1)}, u32[]{:S(2)}, u32[]{:S(2)}) collective-permute-start(f32[5,24,256]{2,1,0:T(8,128)S(1)} %shard_map.102.refs_2_), channel_id=1, source_target_pairs={{0,1},{1,0},{2,3},{3,2},{4,5},{5,4},{6,7},{7,6},{8,9},{9,8},{10,11... | collective-permute-start | bytes 368648 | tf_op jit(solution)/shard_map/ppermute | solution.py:503
  78.1 7.3 %collective-permute-start.13 = (bf16[2,64,1024]{2,1,0:T(8,128)(2,1)S(1)}, bf16[2,64,1024]{2,1,0:T(8,128)(2,1)S(1)}, u32[]{:S(2)}, u32[]{:S(2)}) collective-permute-start(bf16[2,64,1024]{2,1,0:T(8,128)(2,1)S(1)} %get-tuple-element.119), channel_id=1, source_target_pairs={{0,2},{2,0},{4,6},{6,4},{8,10},{10,8},{12,14},{14,12},{1,3},{3,1},... | collective-permute-start | bytes 786440 | tf_op jit(solution)/shard_map/ppermute | solution.py:500
  79.7 9.2 %collective-permute-start.14 = (bf16[2,64,1024]{2,1,0:T(8,128)(2,1)S(1)}, bf16[2,64,1024]{2,1,0:T(8,128)(2,1)S(1)}, u32[]{:S(2)}, u32[]{:S(2)}) collective-permute-start(bf16[2,64,1024]{2,1,0:T(8,128)(2,1)S(1)} %get-tuple-element.120), channel_id=1, source_target_pairs={{0,4},{2,6},{4,0},{6,2},{8,12},{10,14},{12,8},{14,10},{1,5},{3,7},... | collective-permute-start | bytes 786440 | tf_op jit(solution)/shard_map/ppermute | solution.py:500
  81.4 11.6 %collective-permute-start.15 = (bf16[2,64,1024]{2,1,0:T(8,128)(2,1)S(1)}, bf16[2,64,1024]{2,1,0:T(8,128)(2,1)S(1)}, u32[]{:S(2)}, u32[]{:S(2)}) collective-permute-start(bf16[2,64,1024]{2,1,0:T(8,128)(2,1)S(1)} %get-tuple-element.121), channel_id=1, source_target_pairs={{0,6},{2,4},{4,2},{6,0},{8,14},{10,12},{12,10},{14,8},{1,7},{3,5},... | collective-permute-start | bytes 786440 | tf_op jit(solution)/shard_map/ppermute | solution.py:500
  94.3 15.2 %collective-permute-start.16 = (bf16[2,64,2048]{2,1,0:T(8,128)(2,1)S(1)}, bf16[2,64,2048]{2,1,0:T(8,128)(2,1)S(1)}, u32[]{:S(2)}, u32[]{:S(2)}) collective-permute-start(bf16[2,64,2048]{2,1,0:T(8,128)(2,1)S(1)} %shard_map.106), channel_id=1, source_target_pairs={{0,8},{2,10},{12,4},{14,6},{1,9},{3,11},{13,5},{15,7},{16,24},{18,... | collective-permute-start | bytes 1572872 | tf_op jit(solution)/shard_map/ppermute | solution.py:514
  109.4 25.8 %collective-permute-start.20 = (bf16[2,64,2048]{2,1,0:T(8,128)(2,1)S(1)}, bf16[2,64,2048]{2,1,0:T(8,128)(2,1)S(1)}, u32[]{:S(2)}, u32[]{:S(2)}) collective-permute-start(bf16[2,64,2048]{2,1,0:T(8,128)(2,1)S(1)} %shard_map.106), channel_id=1, source_target_pairs={{4,12},{6,14},{8,0},{10,2},{5,13},{7,15},{9,1},{11,3},{20,28},{22,... | collective-permute-start | bytes 1572872 | tf_op jit(solution)/shard_map/ppermute | solution.py:516
  110.7 6.4 %collective-permute-start.17 = (bf16[2,64,1024]{2,1,0:T(8,128)(2,1)S(1)}, bf16[2,64,1024]{2,1,0:T(8,128)(2,1)S(1)}, u32[]{:S(2)}, u32[]{:S(2)}) collective-permute-start(bf16[2,64,1024]{2,1,0:T(8,128)(2,1)S(1)} %get-tuple-element.128), channel_id=1, source_target_pairs={{0,2},{2,0},{4,6},{6,4},{8,10},{10,8},{12,14},{14,12},{1,3},{3,1},... | collective-permute-start | bytes 786440 | tf_op jit(solution)/shard_map/ppermute | solution.py:500
  111.5 18.3 %collective-permute-start.18 = (bf16[2,64,1024]{2,1,0:T(8,128)(2,1)S(1)}, bf16[2,64,1024]{2,1,0:T(8,128)(2,1)S(1)}, u32[]{:S(2)}, u32[]{:S(2)}) collective-permute-start(bf16[2,64,1024]{2,1,0:T(8,128)(2,1)S(1)} %get-tuple-element.129), channel_id=1, source_target_pairs={{0,4},{2,6},{4,0},{6,2},{8,12},{10,14},{12,8},{14,10},{1,5},{3,7},... | collective-permute-start | bytes 786440 | tf_op jit(solution)/shard_map/ppermute | solution.py:500
  114.6 20.6 %collective-permute-start.19 = (bf16[2,64,1024]{2,1,0:T(8,128)(2,1)S(1)}, bf16[2,64,1024]{2,1,0:T(8,128)(2,1)S(1)}, u32[]{:S(2)}, u32[]{:S(2)}) collective-permute-start(bf16[2,64,1024]{2,1,0:T(8,128)(2,1)S(1)} %get-tuple-element.130), channel_id=1, source_target_pairs={{0,6},{2,4},{4,2},{6,0},{8,14},{10,12},{12,10},{14,8},{1,7},{3,5},... | collective-permute-start | bytes 786440 | tf_op jit(solution)/shard_map/ppermute | solution.py:500
  136.7 1.6 %collective-permute-start.21 = (bf16[2,64,1024]{2,1,0:T(8,128)(2,1)S(1)}, bf16[2,64,1024]{2,1,0:T(8,128)(2,1)S(1)}, u32[]{:S(2)}, u32[]{:S(2)}) collective-permute-start(bf16[2,64,1024]{2,1,0:T(8,128)(2,1)S(1)} %get-tuple-element.134), channel_id=1, source_target_pairs={{0,1},{1,0},{2,3},{3,2},{4,5},{5,4},{6,7},{7,6},{8,9},{9,8},{10,11... | collective-permute-start | bytes 786440 | tf_op jit(solution)/shard_map/ppermute | solution.py:503

commit v9 on v7

--- a/solution.py
+++ b/solution.py
@@ -146,26 +146,31 @@
 
 
 def pick_kernel(peers, *refs):
-    sets, full, outs = refs[:peers], refs[peers], refs[peers + 1 :]
+    sets, fulls, outs = refs[:peers], refs[peers:-peers], refs[-peers:]
     for k in range(peers):
         for q in range(UMAX):
             cols = pl.ds(pl.multiple_of(sets[k][0, q] * FB, FB), FB)
-            outs[k][:, :, q * FB : (q + 1) * FB] = full[:, :, cols]
-
-
-def pick(sets, full):
-    nb, sub, cols = full.shape
-    shape = (nb, sub, UMAX * FB)
+            row = 0
+            for full in fulls:
+                rows = full.shape[0]
+                outs[k][row : row + rows, :, q * FB : (q + 1) * FB] = full[:, :, cols]
+                row += rows
+
+
+def pick(sets, fulls):
+    rows = sum(full.shape[0] for full in fulls)
+    _, sub, cols = fulls[0].shape
+    shape = (rows, sub, UMAX * FB)
     peers = len(sets)
     return call(
         functools.partial(pick_kernel, peers),
         sets,
-        [full],
-        [whole(full.shape)],
-        [jax.ShapeDtypeStruct(shape, full.dtype)] * peers,
+        fulls,
+        [whole(full.shape) for full in fulls],
+        [jax.ShapeDtypeStruct(shape, fulls[0].dtype)] * peers,
         [whole(shape)] * peers,
         [],
-        cost=(0, 2 * nb * sub * (cols + peers * UMAX * FB)),
+        cost=(0, 2 * rows * sub * (cols + peers * UMAX * FB)),
     )
 
 
@@ -199,15 +204,15 @@
     lives = batches
     rows = lives + batches // group
     slots = batches * TMAX
-    return lives, rows, rows + slots, rows + 2 * slots, rows + 3 * slots
-
-
-def table_kernel(nb, group, me, owner, own_set, blocks, packed, counts, out, kbs, fill, bundle, sem):
+    return lives, rows, rows + slots, rows + 2 * slots, rows + 3 * slots, rows + 4 * slots
+
+
+def table_kernel(nb, near, group, me, owner, own_set, blocks, packed, counts, out, kbs, fill, bundle, sem):
     copy = pltpu.make_async_copy(packed.at[TMAX], bundle, sem)
     copy.start()
     half = counts.shape[0]
-    at_lives, at_row, at_pos, at_col, _ = table_places(2 * half, group)
-    spare = owner.shape[0]
+    at_lives, at_near, at_far, at_pos, at_col, _ = table_places(2 * half, group)
+    spare = nb * near
     for p in range(UMAX):
         stored = owner[own_set[0, p]]
         kbs[p] = (lax.div(stored, nb) ^ me[0]) * nb + lax.rem(stored, nb)
@@ -250,15 +255,17 @@
                 at = j * TMAX + s
                 out[at_pos + at] = pos
                 out[at_col + at] = jnp.where(on, pos, UMAX)
-                out[at_row + at] = jnp.where(on, kbs[pos], spare)
-
-
-def batch_tables(me, owner, own_set, blocks, packed, counts, nb):
+                kb = kbs[pos]
+                out[at_near + at] = jnp.where(on & (kb < spare), kb, spare)
+                out[at_far + at] = jnp.where(on & (kb >= spare), kb - spare, spare)
+
+
+def batch_tables(me, owner, own_set, blocks, packed, counts, nb, near):
     batches = 2 * counts.shape[0]
     group = math.gcd(batches, GROUP)
     size = table_places(batches, group)[-1]
     return call(
-        functools.partial(table_kernel, nb, group),
+        functools.partial(table_kernel, nb, near, group),
         [me, owner, own_set, blocks],
         [packed, counts],
         [pl.BlockSpec(memory_space=pl.ANY), pl.BlockSpec(memory_space=pltpu.SMEM)],
@@ -359,16 +366,18 @@
     )
 
 
-def batch_kernel(group, pieces, table, *refs):
+def batch_kernel(group, nb, places, split, table, *refs):
     xs, quads, centre_in = refs[0:2], refs[2:4], refs[4]
-    parts = refs[5 : 5 + pieces]
-    outs = refs[5 + pieces : -7]
+    parts = refs[5 : 5 + len(places)]
+    outs = refs[5 + len(places) : -7]
     dense, acc, xbuf, qbuf, centre, sems, xsems = refs[-7:]
-    nb, sub, wide = parts[0].shape
+    _, sub, wide = parts[0].shape
+    pieces = sum(len(where) for where in places)
     spare = nb * pieces
     batches, _, pts = xbuf.shape
     half = batches // 2
-    at_lives, at_row, at_pos, at_col, _ = table_places(batches, group)
+    at_lives, at_near, at_far, at_pos, at_col, _ = table_places(batches, group)
+    at_row = at_far if split else at_near
 
     def fetch(j, act):
         b = table[j]
@@ -378,10 +387,11 @@
             def _():
                 act(pltpu.make_async_copy(xs[side].at[b - half * side], xbuf.at[j], xsems.at[j]))
 
-    copies = [
-        pltpu.make_async_copy(part, dense.at[pl.ds(nb * k, nb), :, pl.ds(0, wide)], sems.at[k])
-        for k, part in enumerate(parts)
-    ]
+    copies = []
+    for part, where in zip(parts, places):
+        for j, piece in enumerate(where):
+            block = dense.at[pl.ds(nb * piece, nb), :, pl.ds(0, wide)]
+            copies.append(pltpu.make_async_copy(part.at[pl.ds(nb * j, nb)], block, sems.at[piece]))
     copies.append(pltpu.make_async_copy(centre_in, centre, sems.at[pieces]))
     for side in (0, 1):
         quad = qbuf.at[:, pl.ds(half * side, half)]
@@ -449,24 +459,24 @@
         start += rows
 
 
-def batch_sums(table, xs, quads, centre, parts):
+def batch_sums(table, xs, quads, centre, parts, places, nb, split):
     _, width, pts = xs[0].shape
     batches = 2 * xs[0].shape[0]
     group = math.gcd(batches, GROUP)
-    nb, sub, wide = parts[0].shape
-    pieces = len(parts)
-    near = pieces // 2
+    _, sub, wide = parts[0].shape
+    pieces = sum(len(where) for where in places)
+    size = 1 if split else nb
     out_shapes = [
-        jax.ShapeDtypeStruct((nb if k < near else 1, sub, wide), jnp.bfloat16 if k % near else jnp.float32)
-        for k in range(pieces)
-        for _ in range(1 if k < near else nb)
+        jax.ShapeDtypeStruct((size, sub, wide), jnp.bfloat16 if piece else jnp.float32)
+        for piece in range(pieces)
+        for _ in range(nb // size)
     ]
     flops = 2 * batches * 2 * width * (width // 2) * pts
     return call(
-        functools.partial(batch_kernel, group, pieces),
+        functools.partial(batch_kernel, group, nb, places, split),
         [table],
         [*xs, *quads, centre, *parts],
-        [pl.BlockSpec(memory_space=pl.ANY)] * (5 + pieces),
+        [pl.BlockSpec(memory_space=pl.ANY)] * (5 + len(parts)),
         out_shapes,
         [whole(out.shape) for out in out_shapes],
         [
@@ -503,36 +513,43 @@
         return pltpu.with_memory_space_constraint(x, pltpu.HBM)
 
     own = lax.dynamic_index_in_dim(density.reshape(nb, cores, sub, cols), r, 1, keepdims=False)
+    side = near // 2
     sets = [touched] + [swap(touched, k) for k in range(1, near)]
-    own, sets = lax.optimization_barrier((own, sets))
-    far = swap(own, near)
+    packed = pack(stay(points.transpose(1, 0, 2)), stay(weights), stay(blocks.T), stay(counts))
+    packed_b = across(packed)
     sets[0] = stay(touched)
-    picked = pick(sets, own)
-    parts = [picked[0]] + [swap(picked[k], k) for k in range(1, near)]
+    table = batch_tables(i.reshape(1), stay(owner), sets[0], stay(blocks.T), packed_b, stay(counts), nb, near)
+    centre = centre_rows(sets[0], core, stay(centers), stay(widths.reshape(1, -1)), sub)
+    beside = swap(own, side)
+    fars = []
+    for b in range(nb):
+        if fars:
+            own, beside, sets, table, centre, fars[-1] = lax.optimization_barrier(
+                (own, beside, sets, table, centre, fars[-1])
+            )
+        fars.append(swap(own[b : b + 1], near))
+    peers = range(1, side)
+    picked = pick([sets[0]] + [sets[k] for k in peers], [own, beside])
+    parts = [picked[0]] + [swap(picked[1 + j], k) for j, k in enumerate(peers)]
+    places = [(0, side)] + [(k, k + side) for k in peers]
+    basis, fars[0] = lax.optimization_barrier((basis, fars[0]))
     xs = (stay(basis), across(basis))
-    far, parts = lax.optimization_barrier((far, parts))
-    picked = pick(sets, far)
-    small = (points.transpose(1, 0, 2), weights, blocks.T, counts)
-    small, centers, widths, picked = lax.optimization_barrier((small, centers, widths, picked))
-    parts += [picked[0]] + [swap(picked[k], k) for k in range(1, near)]
-
-    small = [stay(x) for x in small]
-    packed = pack(*small)
-    packed_b = across(packed)
-    table = batch_tables(i.reshape(1), stay(owner), sets[0], small[2], packed_b, small[3], nb)
-    centre = centre_rows(sets[0], core, stay(centers), stay(widths.reshape(1, -1)), sub)
-    parts, table, centre = lax.optimization_barrier((parts, table, centre))
-
-    sums = batch_sums(table, xs, (packed, packed_b), centre, parts)
-    sums, far_sums = sums[:near], sums[near:]
+    picked = pick(sets, fars)
+    table, picked = lax.optimization_barrier((table, picked))
+    far_parts = [picked[0]] + [swap(picked[k], k) for k in range(1, near)]
+
+    common = (xs, (packed, packed_b), centre)
+    sums = batch_sums(table, *common, parts, places, nb, False)
+    table, sums = lax.optimization_barrier((table, sums))
+    far_sums = batch_sums(table, *common, far_parts, [(k,) for k in range(near)], nb, True)
+    terms = [sums[0]] + [swap(sums[k], k) for k in range(1, near)]
+    far_sums, terms = lax.optimization_barrier((far_sums, terms))
     far_terms = []
     for b in range(nb):
         chunk = [far_sums[b]] + [swap(far_sums[nb * k + b], k) for k in range(1, near)]
         merged = merge(sets, chunk, cols)
-        sums, far_sums, merged = lax.optimization_barrier((sums, far_sums, merged))
+        far_sums, merged = lax.optimization_barrier((far_sums, merged))
         far_terms.append(swap(merged, near))
-    sums, far_terms[0] = lax.optimization_barrier((sums, far_terms[0]))
-    terms = [sums[0]] + [swap(sums[k], k) for k in range(1, near)]
     keep, give = finish(sets, core, terms, far_terms)
     got = across(give)
     pair = jnp.where(r == 0, jnp.stack([keep, got], axis=1), jnp.stack([got, keep], axis=1))

time: 113 us -> 116 us (1.027)
  waiting for transfers between devices: 53.5 us -> 38.6 us
  Pallas kernels: 27.3 us -> 42 us
  starting transfers between devices: 29.2 us -> 32.1 us
  local copies, waits for them, and re-layouts: 0.87 us -> 2.12 us
    ppermute x21, waiting for transfers between devices: 52 us -> 37.1 us  [swap(): return lax.ppermute(x, 'dom', [(a, a ^ k) for a in range(n)])]
    pallas_call x9 -> x10, Pallas kernels: 27.3 us -> 42 us  [call(): pl.pallas_call(kernel, grid_spec=pltpu.PrefetchScalarGridSpec(num_scalar_...]
    ppermute x21, starting transfers between devices: 28.6 us -> 31.9 us  [swap(): return lax.ppermute(x, 'dom', [(a, a ^ k) for a in range(n)])]
    unnamed x2, local copies, waits for them, and re-layouts: 0.01 us -> 1.22 us
  transfers between devices with their start and end apart: 24 -> 24, of which waited for: 16 -> 10; matrix products, arithmetic and copies ran while one was open for 0% -> 0% of each run, Pallas kernels for 11% -> 35%
where the time goes in v9:
time: 116 us; the launch traced here: 115 us
  Pallas kernels  42 us (36%)
  waiting for transfers between devices  38.6 us (33%)
  starting transfers between devices  32.1 us (28%)
  local copies, waits for them, and re-layouts  2.12 us (2%)
    pallas_call x10, Pallas kernels, call(): pl.pallas_call(kernel, grid_spec=pltpu.PrefetchScalarGridSpec(num_scalar_...  42 us
    ppermute x21, waiting for transfers between devices, swap(): return lax.ppermute(x, 'dom', [(a, a ^ k) for a in range(n)])  37.1 us
    ppermute x21, starting transfers between devices, swap(): return lax.ppermute(x, 'dom', [(a, a ^ k) for a in range(n)])  31.9 us
  transfers between devices with their start and end apart: 24, of which 10 were waited for; matrix products, arithmetic and copies ran while one was open for 0% of the time, Pallas kernels for 35%

profile of v9, /device:TPU:0, one launch (start us, length us, event | category | flops | bytes accessed | tf_op | source)
XLA Modules:
  0.0 115.1 jit_solution(16111704561976642628)
XLA Ops:
  1.3 3.1 %collective-permute-start = (bf16[2,64,2048]{2,1,0:T(8,128)(2,1)S(1)}, bf16[2,64,2048]{2,1,0:T(8,128)(2,1)S(1)}, u32[]{:S(2)}, u32[]{:S(2)}) collective-permute-start(bf16[2,64,2048]{2,1,0:T(8,128)(2,1)S(1)} %dynamic-slice_bitcast_fusion.refs_2_), channel_id=1, source_target_pairs={{0,4},{2,6},{4,0},{6,2},{8,12},{10,14},{12,8},{14,10},{1,5},{3,7},... | collective-permute-start | bytes 1572872 | tf_op jit(solution)/shard_map/ppermute | solution.py:507
  4.4 2.7 %collective-permute-start.5 = (bf16[1,64,2048]{2,1,0:T(8,128)(2,1)S(1)}, bf16[1,64,2048]{2,1,0:T(8,128)(2,1)S(1)}, u32[]{:S(2)}, u32[]{:S(2)}) collective-permute-start(bf16[1,64,2048]{2,1,0:T(8,128)(2,1)S(1)} %dynamic-slice_bitcast_fusion.1), channel_id=1, source_target_pairs={{0,8},{2,10},{4,12},{6,14},{8,0},{10,2},{12,4},{14,6},{1,9},{3,11}... | collective-permute-start | bytes 786440 | tf_op jit(solution)/shard_map/ppermute | solution.py:507
  8.3 1.6 %collective-permute-start.1 = (s32[1,8]{1,0:T(1,128)}, s32[1,8]{1,0:T(1,128)S(1)}, u32[]{:S(2)}, u32[]{:S(2)}) collective-permute-start(s32[1,8]{1,0:T(1,128)} %refs_0_.6), channel_id=1, source_target_pairs={{0,2},{2,0},{4,6},{6,4},{8,10},{10,8},{12,14},{14,12},{1,3},{3,1},... | collective-permute-start | bytes 104 | tf_op jit(solution)/shard_map/ppermute | solution.py:507
  10.3 2.1 %shard_map.102.refs_4_ = f32[4,8,64,128]{3,2,1,0:T(8,128)S(1)} custom-call(s32[1,8]{1,0:T(1,128)} %refs_0_.6, s32[1]{0:T(128)} %bitcast.5.core.refs_4_, f32[3,2048]{1,0:T(4,128)} %centers.1, f32[1,2048]{1,0:T(1,128)} %bitcast.18), custom_call_target="tpu_custom_call" | custom-call | bytes 2097152 | tf_op jit(solution)/shard_map/pallas_call | solution.py:129
  12.5 1.6 %collective-permute-start.3 = (s32[1,8]{1,0:T(1,128)}, s32[1,8]{1,0:T(1,128)S(1)}, u32[]{:S(2)}, u32[]{:S(2)}) collective-permute-start(s32[1,8]{1,0:T(1,128)} %refs_0_.6), channel_id=1, source_target_pairs={{0,6},{2,4},{4,2},{6,0},{8,14},{10,12},{12,10},{14,8},{1,7},{3,5},... | collective-permute-start | bytes 104 | tf_op jit(solution)/shard_map/ppermute | solution.py:507
  14.1 5.4 %shard_map.101.table = s32[824]{0:T(1024)S(1)} custom-call(s32[1]{0:T(128)} %bitcast.2.me, s32[16]{0:T(128)} %owner.1, s32[1,8]{1,0:T(1,128)} %refs_0_.6, s32[4,24]{1,0:T(4,128)} %bitcast.20, f32[5,24,256]{2,1,0:T(8,128)S(1)} %collective-permute-done.4.packed.refs_3_, s32[24]{0:T(128)} %counts.3), custom_call_target="tpu_custom_call" | custom-call | bytes 1536 | tf_op jit(solution)/shard_map/pallas_call | solution.py:129
  19.5 2.5 %collective-permute-done.2.refs_2_ = s32[1,8]{1,0:T(1,128)S(1)} collective-permute-done((s32[1,8]{1,0:T(1,128)}, s32[1,8]{1,0:T(1,128)S(1)}, u32[]{:S(2)}, u32[]{:S(2)}) %collective-permute-start.2) | collective-permute-done | bytes 64 | tf_op jit(solution)/shard_map/ppermute | solution.py:507
  24.8 2.6 %collective-permute-start.6 = (bf16[1,64,2048]{2,1,0:T(8,128)(2,1)S(1)}, bf16[1,64,2048]{2,1,0:T(8,128)(2,1)S(1)}, u32[]{:S(2)}, u32[]{:S(2)}) collective-permute-start(bf16[1,64,2048]{2,1,0:T(8,128)(2,1)S(1)} %slice.11), channel_id=1, source_target_pairs={{0,8},{2,10},{4,12},{6,14},{8,0},{10,2},{12,4},{14,6},{1,9},{3,11}... | collective-permute-start | bytes 786440 | tf_op jit(solution)/shard_map/ppermute | solution.py:507
  27.4 12.4 %collective-permute-done.6.refs_5_ = bf16[1,64,2048]{2,1,0:T(8,128)(2,1)S(1)} collective-permute-done((bf16[1,64,2048]{2,1,0:T(8,128)(2,1)S(1)}, bf16[1,64,2048]{2,1,0:T(8,128)(2,1)S(1)}, u32[]{:S(2)}, u32[]{:S(2)}) %collective-permute-start.6) | collective-permute-done | bytes 262176 | tf_op jit(solution)/shard_map/ppermute | solution.py:507
  41.4 2.2 %collective-permute-start.11 = (bf16[2,64,1024]{2,1,0:T(8,128)(2,1)S(1)}, bf16[2,64,1024]{2,1,0:T(8,128)(2,1)S(1)}, u32[]{:S(2)}, u32[]{:S(2)}) collective-permute-start(bf16[2,64,1024]{2,1,0:T(8,128)(2,1)S(1)} %get-tuple-element.90), channel_id=1, source_target_pairs={{0,6},{2,4},{4,2},{6,0},{8,14},{10,12},{12,10},{14,8},{1,7},{3,5},... | collective-permute-start | bytes 786440 | tf_op jit(solution)/shard_map/ppermute | solution.py:507
  44.3 14.1 %shard_map.105 = (f32[2,64,1024]{2,1,0:T(8,128)S(1)}, bf16[2,64,1024]{2,1,0:T(8,128)(2,1)S(1)}, bf16[2,64,1024]{2,1,0:T(8,128)(2,1)S(1)}, bf16[2,64,1024]{2,1,0:T(8,128)(2,1)S(1)}) custom-call(s32[824]{0:T(1024)S(1)} %shard_map.101.table, bf16[24,512,256]{2,1,0:T(8,128)(2,1)} %refs_0_.3, bf16[24,512,256]{2,1,0:T(8,128)(2,1)S(1)} %collective-permute-done.7.refs_1_, ...), custom_call_target="tpu_custom_call" | custom-call | flops 6442450944 | bytes 12582912 | tf_op jit(solution)/shard_map/pallas_call | solution.py:129
  58.9 1.7 %collective-permute-start.13 = (bf16[2,64,1024]{2,1,0:T(8,128)(2,1)S(1)}, bf16[2,64,1024]{2,1,0:T(8,128)(2,1)S(1)}, u32[]{:S(2)}, u32[]{:S(2)}) collective-permute-start(bf16[2,64,1024]{2,1,0:T(8,128)(2,1)S(1)} %get-tuple-element.101), channel_id=1, source_target_pairs={{0,4},{2,6},{4,0},{6,2},{8,12},{10,14},{12,8},{14,10},{1,5},{3,7},... | collective-permute-start | bytes 786440 | tf_op jit(solution)/shard_map/ppermute | solution.py:507
  62.0 14.1 %shard_map.106 = (f32[1,64,1024]{2,1,0:T(8,128)S(1)}, f32[1,64,1024]{2,1,0:T(8,128)S(1)}, bf16[1,64,1024]{2,1,0:T(8,128)(2,1)S(1)}, bf16[1,64,1024]{2,1,0:T(8,12...) custom-call(s32[824]{0:T(1024)S(1)} %shard_map.101.table, ...), custom_call_target="tpu_custom_call" | custom-call | flops 6442450944 | bytes 12582912 | tf_op jit(solution)/shard_map/pallas_call | solution.py:129
  76.1 2.2 %collective-permute-start.16 = (bf16[1,64,1024]{2,1,0:T(8,128)(2,1)S(1)}, bf16[1,64,1024]{2,1,0:T(8,128)(2,1)S(1)}, u32[]{:S(2)}, u32[]{:S(2)}) collective-permute-start(bf16[1,64,1024]{2,1,0:T(8,128)(2,1)S(1)} %get-tuple-element.111), channel_id=1, source_target_pairs={{0,4},{2,6},{4,0},{6,2},{8,12},{10,14},{12,8},{14,10},{1,5},{3,7},... | collective-permute-start | bytes 393224 | tf_op jit(solution)/shard_map/ppermute | solution.py:507
  79.6 2.8 %collective-permute-done.15.refs_5_ = bf16[1,64,1024]{2,1,0:T(8,128)(2,1)S(1)} collective-permute-done((bf16[1,64,1024]{2,1,0:T(8,128)(2,1)S(1)}, bf16[1,64,1024]{2,1,0:T(8,128)(2,1)S(1)}, u32[]{:S(2)}, u32[]{:S(2)}) %collective-permute-start.15) | collective-permute-done | bytes 131104 | tf_op jit(solution)/shard_map/ppermute | solution.py:507
  82.4 1.8 %collective-permute-done.17.refs_7_ = bf16[1,64,1024]{2,1,0:T(8,128)(2,1)S(1)} collective-permute-done((bf16[1,64,1024]{2,1,0:T(8,128)(2,1)S(1)}, bf16[1,64,1024]{2,1,0:T(8,128)(2,1)S(1)}, u32[]{:S(2)}, u32[]{:S(2)}) %collective-permute-start.17) | collective-permute-done | bytes 131104 | tf_op jit(solution)/shard_map/ppermute | solution.py:507
  85.4 1.8 %collective-permute-start.20 = (bf16[1,64,1024]{2,1,0:T(8,128)(2,1)S(1)}, bf16[1,64,1024]{2,1,0:T(8,128)(2,1)S(1)}, u32[]{:S(2)}, u32[]{:S(2)}) collective-permute-start(bf16[1,64,1024]{2,1,0:T(8,128)(2,1)S(1)} %get-tuple-element.118), channel_id=1, source_target_pairs={{0,4},{2,6},{4,0},{6,2},{8,12},{10,14},{12,8},{14,10},{1,5},{3,7},... | collective-permute-start | bytes 393224 | tf_op jit(solution)/shard_map/ppermute | solution.py:507
  87.2 1.5 %collective-permute-start.21 = (bf16[1,64,1024]{2,1,0:T(8,128)(2,1)S(1)}, bf16[1,64,1024]{2,1,0:T(8,128)(2,1)S(1)}, u32[]{:S(2)}, u32[]{:S(2)}) collective-permute-start(bf16[1,64,1024]{2,1,0:T(8,128)(2,1)S(1)} %get-tuple-element.119), channel_id=1, source_target_pairs={{0,6},{2,4},{4,2},{6,0},{8,14},{10,12},{12,10},{14,8},{1,7},{3,5},... | collective-permute-start | bytes 393224 | tf_op jit(solution)/shard_map/ppermute | solution.py:507
  88.8 2.2 %collective-permute-start.18 = (bf16[1,64,2048]{2,1,0:T(8,128)(2,1)S(1)}, bf16[1,64,2048]{2,1,0:T(8,128)(2,1)S(1)}, u32[]{:S(2)}, u32[]{:S(2)}) collective-permute-start(bf16[1,64,2048]{2,1,0:T(8,128)(2,1)S(1)} %shard_map.107), channel_id=1, source_target_pairs={{0,8},{2,10},{4,12},{6,14},{8,0},{10,2},{12,4},{14,6},{1,9},{3,11}... | collective-permute-start | bytes 786440 | tf_op jit(solution)/shard_map/ppermute | solution.py:507
  91.0 1.6 %collective-permute-done.20.refs_6_ = bf16[1,64,1024]{2,1,0:T(8,128)(2,1)S(1)} collective-permute-done((bf16[1,64,1024]{2,1,0:T(8,128)(2,1)S(1)}, bf16[1,64,1024]{2,1,0:T(8,128)(2,1)S(1)}, u32[]{:S(2)}, u32[]{:S(2)}) %collective-permute-start.20) | collective-permute-done | bytes 131104 | tf_op jit(solution)/shard_map/ppermute | solution.py:507
  92.6 2.9 %collective-permute-done.21.refs_7_ = bf16[1,64,1024]{2,1,0:T(8,128)(2,1)S(1)} collective-permute-done((bf16[1,64,1024]{2,1,0:T(8,128)(2,1)S(1)}, bf16[1,64,1024]{2,1,0:T(8,128)(2,1)S(1)}, u32[]{:S(2)}, u32[]{:S(2)}) %collective-permute-start.21) | collective-permute-done | bytes 131104 | tf_op jit(solution)/shard_map/ppermute | solution.py:507
  96.5 2.8 %collective-permute-start.22 = (bf16[1,64,2048]{2,1,0:T(8,128)(2,1)S(1)}, bf16[1,64,2048]{2,1,0:T(8,128)(2,1)S(1)}, u32[]{:S(2)}, u32[]{:S(2)}) collective-permute-start(bf16[1,64,2048]{2,1,0:T(8,128)(2,1)S(1)} %shard_map.108), channel_id=1, source_target_pairs={{0,8},{2,10},{4,12},{6,14},{8,0},{10,2},{12,4},{14,6},{1,9},{3,11}... | collective-permute-start | bytes 786440 | tf_op jit(solution)/shard_map/ppermute | solution.py:507
  99.2 9.2 %collective-permute-done.18.refs_9_ = bf16[1,64,2048]{2,1,0:T(8,128)(2,1)S(1)} collective-permute-done((bf16[1,64,2048]{2,1,0:T(8,128)(2,1)S(1)}, bf16[1,64,2048]{2,1,0:T(8,128)(2,1)S(1)}, u32[]{:S(2)}, u32[]{:S(2)}) %collective-permute-start.18) | collective-permute-done | bytes 262176 | tf_op jit(solution)/shard_map/ppermute | solution.py:507
  108.4 2.8 %collective-permute-done.22.refs_10_ = bf16[1,64,2048]{2,1,0:T(8,128)(2,1)S(1)} collective-permute-done((bf16[1,64,2048]{2,1,0:T(8,128)(2,1)S(1)}, bf16[1,64,2048]{2,1,0:T(8,128)(2,1)S(1)}, u32[]{:S(2)}, u32[]{:S(2)}) %collective-permute-start.22) | collective-permute-done | bytes 262176 | tf_op jit(solution)/shard_map/ppermute | solution.py:507
  (41 shorter events, 17.4 us)
Async XLA Ops:
  1.3 21.7 %collective-permute-start = (bf16[2,64,2048]{2,1,0:T(8,128)(2,1)S(1)}, bf16[2,64,2048]{2,1,0:T(8,128)(2,1)S(1)}, u32[]{:S(2)}, u32[]{:S(2)}) collective-permute-start(bf16[2,64,2048]{2,1,0:T(8,128)(2,1)S(1)} %dynamic-slice_bitcast_fusion.refs_2_), channel_id=1, source_target_pairs={{0,4},{2,6},{4,0},{6,2},{8,12},{10,14},{12,8},{14,10},{1,5},{3,7},... | collective-permute-start | bytes 1572872 | tf_op jit(solution)/shard_map/ppermute | solution.py:507
  4.4 18.6 %collective-permute-start.5 = (bf16[1,64,2048]{2,1,0:T(8,128)(2,1)S(1)}, bf16[1,64,2048]{2,1,0:T(8,128)(2,1)S(1)}, u32[]{:S(2)}, u32[]{:S(2)}) collective-permute-start(bf16[1,64,2048]{2,1,0:T(8,128)(2,1)S(1)} %dynamic-slice_bitcast_fusion.1), channel_id=1, source_target_pairs={{0,8},{2,10},{4,12},{6,14},{8,0},{10,2},{12,4},{14,6},{1,9},{3,11}... | collective-permute-start | bytes 786440 | tf_op jit(solution)/shard_map/ppermute | solution.py:507
  8.2 4.3 %collective-permute-start.4 = (f32[5,24,256]{2,1,0:T(8,128)S(1)}, f32[5,24,256]{2,1,0:T(8,128)S(1)}, u32[]{:S(2)}, u32[]{:S(2)}) collective-permute-start(f32[5,24,256]{2,1,0:T(8,128)S(1)} %shard_map.100.refs_2_), channel_id=1, source_target_pairs={{0,1},{1,0},{2,3},{3,2},{4,5},{5,4},{6,7},{7,6},{8,9},{9,8},{10,11... | collective-permute-start | bytes 368648 | tf_op jit(solution)/shard_map/ppermute | solution.py:510
  8.3 11.2 %collective-permute-start.1 = (s32[1,8]{1,0:T(1,128)}, s32[1,8]{1,0:T(1,128)S(1)}, u32[]{:S(2)}, u32[]{:S(2)}) collective-permute-start(s32[1,8]{1,0:T(1,128)} %refs_0_.6), channel_id=1, source_target_pairs={{0,2},{2,0},{4,6},{6,4},{8,10},{10,8},{12,14},{14,12},{1,3},{3,1},... | collective-permute-start | bytes 104 | tf_op jit(solution)/shard_map/ppermute | solution.py:507
  9.9 12.1 %collective-permute-start.2 = (s32[1,8]{1,0:T(1,128)}, s32[1,8]{1,0:T(1,128)S(1)}, u32[]{:S(2)}, u32[]{:S(2)}) collective-permute-start(s32[1,8]{1,0:T(1,128)} %refs_0_.6), channel_id=1, source_target_pairs={{0,4},{2,6},{4,0},{6,2},{8,12},{10,14},{12,8},{14,10},{1,5},{3,7},... | collective-permute-start | bytes 104 | tf_op jit(solution)/shard_map/ppermute | solution.py:507
  12.5 10.5 %collective-permute-start.3 = (s32[1,8]{1,0:T(1,128)}, s32[1,8]{1,0:T(1,128)S(1)}, u32[]{:S(2)}, u32[]{:S(2)}) collective-permute-start(s32[1,8]{1,0:T(1,128)} %refs_0_.6), channel_id=1, source_target_pairs={{0,6},{2,4},{4,2},{6,0},{8,14},{10,12},{12,10},{14,8},{1,7},{3,5},... | collective-permute-start | bytes 104 | tf_op jit(solution)/shard_map/ppermute | solution.py:507
  23.0 21.3 %collective-permute-start.7 = (bf16[24,512,256]{2,1,0:T(8,128)(2,1)}, bf16[24,512,256]{2,1,0:T(8,128)(2,1)S(1)}, u32[]{:S(2)}, u32[]{:S(2)}) collective-permute-start(bf16[24,512,256]{2,1,0:T(8,128)(2,1)} %refs_0_.3), channel_id=1, source_target_pairs={{0,1},{1,0},{2,3},{3,2},{4,5},{5,4},{6,7},{7,6},{8,9},{9,8},{10,11... | collective-permute-start | bytes 18874376 | tf_op jit(solution)/shard_map/ppermute | solution.py:510
  24.0 20.3 %collective-permute-start.8 = (bf16[4,64,1024]{2,1,0:T(8,128)(2,1)S(1)}, bf16[4,64,1024]{2,1,0:T(8,128)(2,1)S(1)}, u32[]{:S(2)}, u32[]{:S(2)}) collective-permute-start(bf16[4,64,1024]{2,1,0:T(8,128)(2,1)S(1)} %get-tuple-element.81), channel_id=1, source_target_pairs={{0,2},{2,0},{4,6},{6,4},{8,10},{10,8},{12,14},{14,12},{1,3},{3,1},... | collective-permute-start | bytes 1572872 | tf_op jit(solution)/shard_map/ppermute | solution.py:507
  24.8 15.0 %collective-permute-start.6 = (bf16[1,64,2048]{2,1,0:T(8,128)(2,1)S(1)}, bf16[1,64,2048]{2,1,0:T(8,128)(2,1)S(1)}, u32[]{:S(2)}, u32[]{:S(2)}) collective-permute-start(bf16[1,64,2048]{2,1,0:T(8,128)(2,1)S(1)} %slice.11), channel_id=1, source_target_pairs={{0,8},{2,10},{4,12},{6,14},{8,0},{10,2},{12,4},{14,6},{1,9},{3,11}... | collective-permute-start | bytes 786440 | tf_op jit(solution)/shard_map/ppermute | solution.py:507
  40.8 19.8 %collective-permute-start.10 = (bf16[2,64,1024]{2,1,0:T(8,128)(2,1)S(1)}, bf16[2,64,1024]{2,1,0:T(8,128)(2,1)S(1)}, u32[]{:S(2)}, u32[]{:S(2)}) collective-permute-start(bf16[2,64,1024]{2,1,0:T(8,128)(2,1)S(1)} %get-tuple-element.89), channel_id=1, source_target_pairs={{0,4},{2,6},{4,0},{6,2},{8,12},{10,14},{12,8},{14,10},{1,5},{3,7},... | collective-permute-start | bytes 786440 | tf_op jit(solution)/shard_map/ppermute | solution.py:507
  41.4 20.5 %collective-permute-start.11 = (bf16[2,64,1024]{2,1,0:T(8,128)(2,1)S(1)}, bf16[2,64,1024]{2,1,0:T(8,128)(2,1)S(1)}, u32[]{:S(2)}, u32[]{:S(2)}) collective-permute-start(bf16[2,64,1024]{2,1,0:T(8,128)(2,1)S(1)} %get-tuple-element.90), channel_id=1, source_target_pairs={{0,6},{2,4},{4,2},{6,0},{8,14},{10,12},{12,10},{14,8},{1,7},{3,5},... | collective-permute-start | bytes 786440 | tf_op jit(solution)/shard_map/ppermute | solution.py:507
  43.6 18.4 %collective-permute-start.9 = (bf16[2,64,1024]{2,1,0:T(8,128)(2,1)S(1)}, bf16[2,64,1024]{2,1,0:T(8,128)(2,1)S(1)}, u32[]{:S(2)}, u32[]{:S(2)}) collective-permute-start(bf16[2,64,1024]{2,1,0:T(8,128)(2,1)S(1)} %get-tuple-element.88), channel_id=1, source_target_pairs={{0,2},{2,0},{4,6},{6,4},{8,10},{10,8},{12,14},{14,12},{1,3},{3,1},... | collective-permute-start | bytes 786440 | tf_op jit(solution)/shard_map/ppermute | solution.py:507
  58.4 17.6 %collective-permute-start.12 = (bf16[2,64,1024]{2,1,0:T(8,128)(2,1)S(1)}, bf16[2,64,1024]{2,1,0:T(8,128)(2,1)S(1)}, u32[]{:S(2)}, u32[]{:S(2)}) collective-permute-start(bf16[2,64,1024]{2,1,0:T(8,128)(2,1)S(1)} %get-tuple-element.100), channel_id=1, source_target_pairs={{0,2},{2,0},{4,6},{6,4},{8,10},{10,8},{12,14},{14,12},{1,3},{3,1},... | collective-permute-start | bytes 786440 | tf_op jit(solution)/shard_map/ppermute | solution.py:507
  58.9 17.1 %collective-permute-start.13 = (bf16[2,64,1024]{2,1,0:T(8,128)(2,1)S(1)}, bf16[2,64,1024]{2,1,0:T(8,128)(2,1)S(1)}, u32[]{:S(2)}, u32[]{:S(2)}) collective-permute-start(bf16[2,64,1024]{2,1,0:T(8,128)(2,1)S(1)} %get-tuple-element.101), channel_id=1, source_target_pairs={{0,4},{2,6},{4,0},{6,2},{8,12},{10,14},{12,8},{14,10},{1,5},{3,7},... | collective-permute-start | bytes 786440 | tf_op jit(solution)/shard_map/ppermute | solution.py:507
  60.6 15.5 %collective-permute-start.14 = (bf16[2,64,1024]{2,1,0:T(8,128)(2,1)S(1)}, bf16[2,64,1024]{2,1,0:T(8,128)(2,1)S(1)}, u32[]{:S(2)}, u32[]{:S(2)}) collective-permute-start(bf16[2,64,1024]{2,1,0:T(8,128)(2,1)S(1)} %get-tuple-element.102), channel_id=1, source_target_pairs={{0,6},{2,4},{4,2},{6,0},{8,14},{10,12},{12,10},{14,8},{1,7},{3,5},... | collective-permute-start | bytes 786440 | tf_op jit(solution)/shard_map/ppermute | solution.py:507
  76.1 6.4 %collective-permute-start.15 = (bf16[1,64,1024]{2,1,0:T(8,128)(2,1)S(1)}, bf16[1,64,1024]{2,1,0:T(8,128)(2,1)S(1)}, u32[]{:S(2)}, u32[]{:S(2)}) collective-permute-start(bf16[1,64,1024]{2,1,0:T(8,128)(2,1)S(1)} %get-tuple-element.109), channel_id=1, source_target_pairs={{0,2},{2,0},{4,6},{6,4},{8,10},{10,8},{12,14},{14,12},{1,3},{3,1},... | collective-permute-start | bytes 393224 | tf_op jit(solution)/shard_map/ppermute | solution.py:507
  76.1 6.3 %collective-permute-start.16 = (bf16[1,64,1024]{2,1,0:T(8,128)(2,1)S(1)}, bf16[1,64,1024]{2,1,0:T(8,128)(2,1)S(1)}, u32[]{:S(2)}, u32[]{:S(2)}) collective-permute-start(bf16[1,64,1024]{2,1,0:T(8,128)(2,1)S(1)} %get-tuple-element.111), channel_id=1, source_target_pairs={{0,4},{2,6},{4,0},{6,2},{8,12},{10,14},{12,8},{14,10},{1,5},{3,7},... | collective-permute-start | bytes 393224 | tf_op jit(solution)/shard_map/ppermute | solution.py:507
  78.4 5.9 %collective-permute-start.17 = (bf16[1,64,1024]{2,1,0:T(8,128)(2,1)S(1)}, bf16[1,64,1024]{2,1,0:T(8,128)(2,1)S(1)}, u32[]{:S(2)}, u32[]{:S(2)}) collective-permute-start(bf16[1,64,1024]{2,1,0:T(8,128)(2,1)S(1)} %get-tuple-element.113), channel_id=1, source_target_pairs={{0,6},{2,4},{4,2},{6,0},{8,14},{10,12},{12,10},{14,8},{1,7},{3,5},... | collective-permute-start | bytes 393224 | tf_op jit(solution)/shard_map/ppermute | solution.py:507
  85.2 5.8 %collective-permute-start.19 = (bf16[1,64,1024]{2,1,0:T(8,128)(2,1)S(1)}, bf16[1,64,1024]{2,1,0:T(8,128)(2,1)S(1)}, u32[]{:S(2)}, u32[]{:S(2)}) collective-permute-start(bf16[1,64,1024]{2,1,0:T(8,128)(2,1)S(1)} %get-tuple-element.117), channel_id=1, source_target_pairs={{0,2},{2,0},{4,6},{6,4},{8,10},{10,8},{12,14},{14,12},{1,3},{3,1},... | collective-permute-start | bytes 393224 | tf_op jit(solution)/shard_map/ppermute | solution.py:507
  85.4 7.1 %collective-permute-start.20 = (bf16[1,64,1024]{2,1,0:T(8,128)(2,1)S(1)}, bf16[1,64,1024]{2,1,0:T(8,128)(2,1)S(1)}, u32[]{:S(2)}, u32[]{:S(2)}) collective-permute-start(bf16[1,64,1024]{2,1,0:T(8,128)(2,1)S(1)} %get-tuple-element.118), channel_id=1, source_target_pairs={{0,4},{2,6},{4,0},{6,2},{8,12},{10,14},{12,8},{14,10},{1,5},{3,7},... | collective-permute-start | bytes 393224 | tf_op jit(solution)/shard_map/ppermute | solution.py:507
  87.2 8.2 %collective-permute-start.21 = (bf16[1,64,1024]{2,1,0:T(8,128)(2,1)S(1)}, bf16[1,64,1024]{2,1,0:T(8,128)(2,1)S(1)}, u32[]{:S(2)}, u32[]{:S(2)}) collective-permute-start(bf16[1,64,1024]{2,1,0:T(8,128)(2,1)S(1)} %get-tuple-element.119), channel_id=1, source_target_pairs={{0,6},{2,4},{4,2},{6,0},{8,14},{10,12},{12,10},{14,8},{1,7},{3,5},... | collective-permute-start | bytes 393224 | tf_op jit(solution)/shard_map/ppermute | solution.py:507
  88.8 19.7 %collective-permute-start.18 = (bf16[1,64,2048]{2,1,0:T(8,128)(2,1)S(1)}, bf16[1,64,2048]{2,1,0:T(8,128)(2,1)S(1)}, u32[]{:S(2)}, u32[]{:S(2)}) collective-permute-start(bf16[1,64,2048]{2,1,0:T(8,128)(2,1)S(1)} %shard_map.107), channel_id=1, source_target_pairs={{0,8},{2,10},{4,12},{6,14},{8,0},{10,2},{12,4},{14,6},{1,9},{3,11}... | collective-permute-start | bytes 786440 | tf_op jit(solution)/shard_map/ppermute | solution.py:507
  96.5 14.8 %collective-permute-start.22 = (bf16[1,64,2048]{2,1,0:T(8,128)(2,1)S(1)}, bf16[1,64,2048]{2,1,0:T(8,128)(2,1)S(1)}, u32[]{:S(2)}, u32[]{:S(2)}) collective-permute-start(bf16[1,64,2048]{2,1,0:T(8,128)(2,1)S(1)} %shard_map.108), channel_id=1, source_target_pairs={{0,8},{2,10},{4,12},{6,14},{8,0},{10,2},{12,4},{14,6},{1,9},{3,11}... | collective-permute-start | bytes 786440 | tf_op jit(solution)/shard_map/ppermute | solution.py:507
  112.6 1.6 %collective-permute-start.23 = (bf16[2,64,1024]{2,1,0:T(8,128)(2,1)S(1)}, bf16[2,64,1024]{2,1,0:T(8,128)(2,1)S(1)}, u32[]{:S(2)}, u32[]{:S(2)}) collective-permute-start(bf16[2,64,1024]{2,1,0:T(8,128)(2,1)S(1)} %get-tuple-element.122), channel_id=1, source_target_pairs={{0,1},{1,0},{2,3},{3,2},{4,5},{5,4},{6,7},{7,6},{8,9},{9,8},{10,11... | collective-permute-start | bytes 786440 | tf_op jit(solution)/shard_map/ppermute | solution.py:510
  (1 other events, 1.2 us)

commit v10 on v7

--- a/solution.py
+++ b/solution.py
@@ -125,7 +125,7 @@
     return summed.astype(jnp.bfloat16)
 
 
-def call(kernel, scalars, arrays, in_specs, out_shapes, out_specs, scratch, grid=(1,), cost=None, vmem=36):
+def call(kernel, scalars, arrays, in_specs, out_shapes, out_specs, scratch, grid=(1,), cost=None, vmem=44):
     return pl.pallas_call(
         kernel,
         grid_spec=pltpu.PrefetchScalarGridSpec(
@@ -199,15 +199,15 @@
     lives = batches
     rows = lives + batches // group
     slots = batches * TMAX
-    return lives, rows, rows + slots, rows + 2 * slots, rows + 3 * slots
-
-
-def table_kernel(nb, group, me, owner, own_set, blocks, packed, counts, out, kbs, fill, bundle, sem):
+    return lives, rows, rows + slots, rows + 2 * slots, rows + 3 * slots, rows + 4 * slots
+
+
+def table_kernel(nb, near, group, me, owner, own_set, blocks, packed, counts, out, kbs, fill, bundle, sem):
     copy = pltpu.make_async_copy(packed.at[TMAX], bundle, sem)
     copy.start()
     half = counts.shape[0]
-    at_lives, at_row, at_pos, at_col, _ = table_places(2 * half, group)
-    spare = owner.shape[0]
+    at_lives, at_near, at_far, at_pos, at_col, _ = table_places(2 * half, group)
+    spare = nb * near
     for p in range(UMAX):
         stored = owner[own_set[0, p]]
         kbs[p] = (lax.div(stored, nb) ^ me[0]) * nb + lax.rem(stored, nb)
@@ -250,15 +250,17 @@
                 at = j * TMAX + s
                 out[at_pos + at] = pos
                 out[at_col + at] = jnp.where(on, pos, UMAX)
-                out[at_row + at] = jnp.where(on, kbs[pos], spare)
-
-
-def batch_tables(me, owner, own_set, blocks, packed, counts, nb):
+                kb = kbs[pos]
+                out[at_near + at] = jnp.where(on & (kb < spare), kb, spare)
+                out[at_far + at] = jnp.where(on & (kb >= spare), kb - spare, spare)
+
+
+def batch_tables(me, owner, own_set, blocks, packed, counts, nb, near):
     batches = 2 * counts.shape[0]
     group = math.gcd(batches, GROUP)
     size = table_places(batches, group)[-1]
     return call(
-        functools.partial(table_kernel, nb, group),
+        functools.partial(table_kernel, nb, near, group),
         [me, owner, own_set, blocks],
         [packed, counts],
         [pl.BlockSpec(memory_space=pl.ANY), pl.BlockSpec(memory_space=pltpu.SMEM)],
@@ -359,7 +361,7 @@
     )
 
 
-def batch_kernel(group, pieces, table, *refs):
+def batch_kernel(group, pieces, split, table, *refs):
     xs, quads, centre_in = refs[0:2], refs[2:4], refs[4]
     parts = refs[5 : 5 + pieces]
     outs = refs[5 + pieces : -7]
@@ -368,7 +370,8 @@
     spare = nb * pieces
     batches, _, pts = xbuf.shape
     half = batches // 2
-    at_lives, at_row, at_pos, at_col, _ = table_places(batches, group)
+    at_lives, at_near, at_far, at_pos, at_col, _ = table_places(batches, group)
+    at_row = at_far if split else at_near
 
     def fetch(j, act):
         b = table[j]
@@ -449,21 +452,21 @@
         start += rows
 
 
-def batch_sums(table, xs, quads, centre, parts):
+def batch_sums(table, xs, quads, centre, parts, split):
     _, width, pts = xs[0].shape
     batches = 2 * xs[0].shape[0]
     group = math.gcd(batches, GROUP)
     nb, sub, wide = parts[0].shape
     pieces = len(parts)
-    near = pieces // 2
+    size = 1 if split else nb
     out_shapes = [
-        jax.ShapeDtypeStruct((nb if k < near else 1, sub, wide), jnp.bfloat16 if k % near else jnp.float32)
+        jax.ShapeDtypeStruct((size, sub, wide), jnp.bfloat16 if k else jnp.float32)
         for k in range(pieces)
-        for _ in range(1 if k < near else nb)
+        for _ in range(nb // size)
     ]
     flops = 2 * batches * 2 * width * (width // 2) * pts
     return call(
-        functools.partial(batch_kernel, group, pieces),
+        functools.partial(batch_kernel, group, pieces, split),
         [table],
         [*xs, *quads, centre, *parts],
         [pl.BlockSpec(memory_space=pl.ANY)] * (5 + pieces),
@@ -504,35 +507,35 @@
 
     own = lax.dynamic_index_in_dim(density.reshape(nb, cores, sub, cols), r, 1, keepdims=False)
     sets = [touched] + [swap(touched, k) for k in range(1, near)]
-    own, sets = lax.optimization_barrier((own, sets))
+    packed = pack(stay(points.transpose(1, 0, 2)), stay(weights), stay(blocks.T), stay(counts))
+    packed_b = across(packed)
+    own, sets, basis, packed_b = lax.optimization_barrier((own, sets, basis, packed_b))
     far = swap(own, near)
     sets[0] = stay(touched)
     picked = pick(sets, own)
     parts = [picked[0]] + [swap(picked[k], k) for k in range(1, near)]
     xs = (stay(basis), across(basis))
-    far, parts = lax.optimization_barrier((far, parts))
+    quads = (packed, packed_b)
+    table = batch_tables(i.reshape(1), stay(owner), sets[0], stay(blocks.T), packed_b, stay(counts), nb, near)
+    centre = centre_rows(sets[0], core, stay(centers), stay(widths.reshape(1, -1)), sub)
+
+    far, table, centre = lax.optimization_barrier((far, table, centre))
     picked = pick(sets, far)
-    small = (points.transpose(1, 0, 2), weights, blocks.T, counts)
-    small, centers, widths, picked = lax.optimization_barrier((small, centers, widths, picked))
-    parts += [picked[0]] + [swap(picked[k], k) for k in range(1, near)]
-
-    small = [stay(x) for x in small]
-    packed = pack(*small)
-    packed_b = across(packed)
-    table = batch_tables(i.reshape(1), stay(owner), sets[0], small[2], packed_b, small[3], nb)
-    centre = centre_rows(sets[0], core, stay(centers), stay(widths.reshape(1, -1)), sub)
-    parts, table, centre = lax.optimization_barrier((parts, table, centre))
-
-    sums = batch_sums(table, xs, (packed, packed_b), centre, parts)
-    sums, far_sums = sums[:near], sums[near:]
+    far_parts = [picked[0]] + [swap(picked[k], k) for k in range(1, near)]
+    table, _ = lax.optimization_barrier((table, picked[0]))
+
+    common = (xs, quads, centre)
+    sums = batch_sums(table, *common, parts, False)
+    table, _ = lax.optimization_barrier((table, sums[0]))
+    far_sums = batch_sums(table, *common, far_parts, True)
+    terms = [sums[0]] + [swap(sums[k], k) for k in range(1, near)]
+    far_sums, terms = lax.optimization_barrier((far_sums, terms))
     far_terms = []
     for b in range(nb):
         chunk = [far_sums[b]] + [swap(far_sums[nb * k + b], k) for k in range(1, near)]
         merged = merge(sets, chunk, cols)
-        sums, far_sums, merged = lax.optimization_barrier((sums, far_sums, merged))
+        far_sums, merged = lax.optimization_barrier((far_sums, merged))
         far_terms.append(swap(merged, near))
-    sums, far_terms[0] = lax.optimization_barrier((sums, far_terms[0]))
-    terms = [sums[0]] + [swap(sums[k], k) for k in range(1, near)]
     keep, give = finish(sets, core, terms, far_terms)
     got = across(give)
     pair = jnp.where(r == 0, jnp.stack([keep, got], axis=1), jnp.stack([got, keep], axis=1))

time: 113 us -> 111 us (0.982); the launches traced: 111 us -> 110 us
  Pallas kernels: 27.3 us -> 42.9 us
  waiting for transfers between devices: 53.5 us -> 38.4 us
  starting transfers between devices: 29.2 us -> 28 us
    pallas_call x9 -> x10, Pallas kernels: 27.3 us -> 42.9 us  [call(): pl.pallas_call(kernel, grid_spec=pltpu.PrefetchScalarGridSpec(num_scalar_...]
    ppermute x21, waiting for transfers between devices: 52 us -> 36.9 us  [swap(): return lax.ppermute(x, 'dom', [(a, a ^ k) for a in range(n)])]
  transfers between devices with their start and end apart: 24 -> 24, of which waited for: 16 -> 12; matrix products, arithmetic and copies ran while one was open for 0% -> 0% of each run, Pallas kernels for 11% -> 37%
where the time goes in v10:
time: 111 us; the launch traced here: 110 us
  Pallas kernels  42.9 us (39%)
  waiting for transfers between devices  38.4 us (35%)
  starting transfers between devices  28 us (25%)
    pallas_call x10, Pallas kernels, call(): pl.pallas_call(kernel, grid_spec=pltpu.PrefetchScalarGridSpec(num_scalar_...  42.9 us
    ppermute x21, waiting for transfers between devices, swap(): return lax.ppermute(x, 'dom', [(a, a ^ k) for a in range(n)])  36.9 us
    ppermute x21, starting transfers between devices, swap(): return lax.ppermute(x, 'dom', [(a, a ^ k) for a in range(n)])  27.9 us
  transfers between devices with their start and end apart: 24, of which 12 were waited for; matrix products, arithmetic and copies ran while one was open for 0% of the time, Pallas kernels for 37%

profile of v10, /device:TPU:0, one launch (start us, length us, event | category | flops | bytes accessed | tf_op | source)
XLA Modules:
  0.0 110.5 jit_solution(17898917524594785016)
XLA Ops:
  0.0 3.0 %collective-permute-start = (s32[1,8]{1,0:T(1,128)}, s32[1,8]{1,0:T(1,128)S(1)}, u32[]{:S(2)}, u32[]{:S(2)}) collective-permute-start(s32[1,8]{1,0:T(1,128)} %refs_0_.11), channel_id=1, source_target_pairs={{0,2},{2,0},{4,6},{6,4},{8,10},{10,8},{12,14},{14,12},{1,3},{3,1},... | collective-permute-start | bytes 104 | tf_op jit(solution)/shard_map/ppermute | solution.py:500
  3.0 1.6 %collective-permute-start.1 = (s32[1,8]{1,0:T(1,128)}, s32[1,8]{1,0:T(1,128)S(1)}, u32[]{:S(2)}, u32[]{:S(2)}) collective-permute-start(s32[1,8]{1,0:T(1,128)} %refs_0_.11), channel_id=1, source_target_pairs={{0,4},{2,6},{4,0},{6,2},{8,12},{10,14},{12,8},{14,10},{1,5},{3,7},... | collective-permute-start | bytes 104 | tf_op jit(solution)/shard_map/ppermute | solution.py:500
  6.6 2.5 %collective-permute-done.2.refs_3_ = s32[1,8]{1,0:T(1,128)S(1)} collective-permute-done((s32[1,8]{1,0:T(1,128)}, s32[1,8]{1,0:T(1,128)S(1)}, u32[]{:S(2)}, u32[]{:S(2)}) %collective-permute-start.2) | collective-permute-done | bytes 64 | tf_op jit(solution)/shard_map/ppermute | solution.py:500
  9.1 2.6 %collective-permute-start.4 = (bf16[2,64,2048]{2,1,0:T(8,128)(2,1)S(1)}, bf16[2,64,2048]{2,1,0:T(8,128)(2,1)S(1)}, u32[]{:S(2)}, u32[]{:S(2)}) collective-permute-start(bf16[2,64,2048]{2,1,0:T(8,128)(2,1)S(1)} %dynamic-slice_bitcast_fusion.refs_4_), channel_id=1, source_target_pairs={{0,8},{2,10},{4,12},{6,14},{8,0},{10,2},{12,4},{14,6},{1,9},{3,11}... | collective-permute-start | bytes 1572872 | tf_op jit(solution)/shard_map/ppermute | solution.py:500
  11.7 1.7 %shard_map.104 = (bf16[2,64,1024]{2,1,0:T(8,128)(2,1)S(1)}, bf16[2,64,1024]{2,1,0:T(8,128)(2,1)}, bf16[2,64,1024]{2,1,0:T(8,128)(2,1)}, bf16[2,64,1024]{2,1,0:T(8,128)(2,1)}) custom-call(s32[1,8]{1,0:T(1,128)} %refs_0_.11, s32[1,8]{1,0:T(1,128)S(1)} %collective-permute-done.refs_1_, s32[1,8]{1,0:T(1,128)S(1)} %collective-permute-done.1.refs_2_, ...), custom_call_target="tpu_custom_call" | custom-call | bytes 1572864 | tf_op jit(solution)/shard_map/pallas_call | solution.py:129
  15.1 1.8 %collective-permute-start.8 = (bf16[2,64,1024]{2,1,0:T(8,128)(2,1)}, bf16[2,64,1024]{2,1,0:T(8,128)(2,1)S(1)}, u32[]{:S(2)}, u32[]{:S(2)}) collective-permute-start(bf16[2,64,1024]{2,1,0:T(8,128)(2,1)} %get-tuple-element.70), channel_id=1, source_target_pairs={{0,6},{2,4},{4,2},{6,0},{8,14},{10,12},{12,10},{14,8},{1,7},{3,5},... | collective-permute-start | bytes 786440 | tf_op jit(solution)/shard_map/ppermute | solution.py:500
  17.0 2.1 %shard_map.102.refs_4_ = f32[4,8,64,128]{3,2,1,0:T(8,128)S(1)} custom-call(s32[1,8]{1,0:T(1,128)} %refs_0_.11, s32[1]{0:T(128)} %bitcast.4.core.refs_4_, f32[3,2048]{1,0:T(4,128)} %centers.1, f32[1,2048]{1,0:T(1,128)} %bitcast.17), custom_call_target="tpu_custom_call" | custom-call | bytes 2097152 | tf_op jit(solution)/shard_map/pallas_call | solution.py:129
  19.1 5.4 %shard_map.101.table = s32[824]{0:T(1024)S(1)} custom-call(s32[1]{0:T(128)} %bitcast.5.me, s32[16]{0:T(128)} %owner.1, s32[1,8]{1,0:T(1,128)} %refs_0_.11, s32[4,24]{1,0:T(4,128)} %bitcast.19, f32[5,24,256]{2,1,0:T(8,128)S(1)} %collective-permute-done.3.packed.refs_3_, s32[24]{0:T(128)} %counts.3), custom_call_target="tpu_custom_call" | custom-call | bytes 1536 | tf_op jit(solution)/shard_map/pallas_call | solution.py:129
  24.5 11.1 %collective-permute-done.4.refs_4_ = bf16[2,64,2048]{2,1,0:T(8,128)(2,1)S(1)} collective-permute-done((bf16[2,64,2048]{2,1,0:T(8,128)(2,1)S(1)}, bf16[2,64,2048]{2,1,0:T(8,128)(2,1)S(1)}, u32[]{:S(2)}, u32[]{:S(2)}) %collective-permute-start.4) | collective-permute-done | bytes 524320 | tf_op jit(solution)/shard_map/ppermute | solution.py:500
  36.6 2.1 %collective-permute-start.11 = (bf16[2,64,1024]{2,1,0:T(8,128)(2,1)S(1)}, bf16[2,64,1024]{2,1,0:T(8,128)(2,1)S(1)}, u32[]{:S(2)}, u32[]{:S(2)}) collective-permute-start(bf16[2,64,1024]{2,1,0:T(8,128)(2,1)S(1)} %get-tuple-element.75), channel_id=1, source_target_pairs={{0,6},{2,4},{4,2},{6,0},{8,14},{10,12},{12,10},{14,8},{1,7},{3,5},... | collective-permute-start | bytes 786440 | tf_op jit(solution)/shard_map/ppermute | solution.py:500
  38.7 1.4 %collective-permute-start.9 = (bf16[2,64,1024]{2,1,0:T(8,128)(2,1)S(1)}, bf16[2,64,1024]{2,1,0:T(8,128)(2,1)S(1)}, u32[]{:S(2)}, u32[]{:S(2)}) collective-permute-start(bf16[2,64,1024]{2,1,0:T(8,128)(2,1)S(1)} %get-tuple-element.73), channel_id=1, source_target_pairs={{0,2},{2,0},{4,6},{6,4},{8,10},{10,8},{12,14},{14,12},{1,3},{3,1},... | collective-permute-start | bytes 786440 | tf_op jit(solution)/shard_map/ppermute | solution.py:500
  40.2 14.1 %shard_map.105 = (f32[2,64,1024]{2,1,0:T(8,128)S(1)}, bf16[2,64,1024]{2,1,0:T(8,128)(2,1)S(1)}, bf16[2,64,1024]{2,1,0:T(8,128)(2,1)S(1)}, bf16[2,64,1024]{2,1,0:T(8,128)(2,1)S(1)}) custom-call(s32[824]{0:T(1024)S(1)} %shard_map.101.table, bf16[24,512,256]{2,1,0:T(8,128)(2,1)} %refs_0_.8, bf16[24,512,256]{2,1,0:T(8,128)(2,1)} %collective-permute-done.5.refs_1_, ...), custom_call_target="tpu_custom_call" | custom-call | flops 6442450944 | bytes 12582912 | tf_op jit(solution)/shard_map/pallas_call | solution.py:129
  54.8 3.1 %collective-permute-start.14 = (bf16[2,64,1024]{2,1,0:T(8,128)(2,1)S(1)}, bf16[2,64,1024]{2,1,0:T(8,128)(2,1)S(1)}, u32[]{:S(2)}, u32[]{:S(2)}) collective-permute-start(bf16[2,64,1024]{2,1,0:T(8,128)(2,1)S(1)} %get-tuple-element.86), channel_id=1, source_target_pairs={{0,6},{2,4},{4,2},{6,0},{8,14},{10,12},{12,10},{14,8},{1,7},{3,5},... | collective-permute-start | bytes 786440 | tf_op jit(solution)/shard_map/ppermute | solution.py:500
  57.9 14.1 %shard_map.106 = (f32[1,64,1024]{2,1,0:T(8,128)S(1)}, f32[1,64,1024]{2,1,0:T(8,128)S(1)}, bf16[1,64,1024]{2,1,0:T(8,128)(2,1)S(1)}, bf16[1,64,1024]{2,1,0:T(8,12...) custom-call(s32[824]{0:T(1024)S(1)} %shard_map.101.table, ...), custom_call_target="tpu_custom_call" | custom-call | flops 6442450944 | bytes 12582912 | tf_op jit(solution)/shard_map/pallas_call | solution.py:129
  72.5 3.2 %collective-permute-start.17 = (bf16[1,64,1024]{2,1,0:T(8,128)(2,1)S(1)}, bf16[1,64,1024]{2,1,0:T(8,128)(2,1)S(1)}, u32[]{:S(2)}, u32[]{:S(2)}) collective-permute-start(bf16[1,64,1024]{2,1,0:T(8,128)(2,1)S(1)} %get-tuple-element.97), channel_id=1, source_target_pairs={{0,6},{2,4},{4,2},{6,0},{8,14},{10,12},{12,10},{14,8},{1,7},{3,5},... | collective-permute-start | bytes 393224 | tf_op jit(solution)/shard_map/ppermute | solution.py:500
  75.7 2.7 %collective-permute-done.15.refs_5_ = bf16[1,64,1024]{2,1,0:T(8,128)(2,1)S(1)} collective-permute-done((bf16[1,64,1024]{2,1,0:T(8,128)(2,1)S(1)}, bf16[1,64,1024]{2,1,0:T(8,128)(2,1)S(1)}, u32[]{:S(2)}, u32[]{:S(2)}) %collective-permute-start.15) | collective-permute-done | bytes 131104 | tf_op jit(solution)/shard_map/ppermute | solution.py:500
  78.4 1.6 %collective-permute-done.17.refs_7_ = bf16[1,64,1024]{2,1,0:T(8,128)(2,1)S(1)} collective-permute-done((bf16[1,64,1024]{2,1,0:T(8,128)(2,1)S(1)}, bf16[1,64,1024]{2,1,0:T(8,128)(2,1)S(1)}, u32[]{:S(2)}, u32[]{:S(2)}) %collective-permute-start.17) | collective-permute-done | bytes 131104 | tf_op jit(solution)/shard_map/ppermute | solution.py:500
  81.3 1.8 %collective-permute-start.20 = (bf16[1,64,1024]{2,1,0:T(8,128)(2,1)S(1)}, bf16[1,64,1024]{2,1,0:T(8,128)(2,1)S(1)}, u32[]{:S(2)}, u32[]{:S(2)}) collective-permute-start(bf16[1,64,1024]{2,1,0:T(8,128)(2,1)S(1)} %get-tuple-element.102), channel_id=1, source_target_pairs={{0,4},{2,6},{4,0},{6,2},{8,12},{10,14},{12,8},{14,10},{1,5},{3,7},... | collective-permute-start | bytes 393224 | tf_op jit(solution)/shard_map/ppermute | solution.py:500
  83.1 1.4 %collective-permute-start.21 = (bf16[1,64,1024]{2,1,0:T(8,128)(2,1)S(1)}, bf16[1,64,1024]{2,1,0:T(8,128)(2,1)S(1)}, u32[]{:S(2)}, u32[]{:S(2)}) collective-permute-start(bf16[1,64,1024]{2,1,0:T(8,128)(2,1)S(1)} %get-tuple-element.103), channel_id=1, source_target_pairs={{0,6},{2,4},{4,2},{6,0},{8,14},{10,12},{12,10},{14,8},{1,7},{3,5},... | collective-permute-start | bytes 393224 | tf_op jit(solution)/shard_map/ppermute | solution.py:500
  84.5 1.9 %collective-permute-start.18 = (bf16[1,64,2048]{2,1,0:T(8,128)(2,1)S(1)}, bf16[1,64,2048]{2,1,0:T(8,128)(2,1)S(1)}, u32[]{:S(2)}, u32[]{:S(2)}) collective-permute-start(bf16[1,64,2048]{2,1,0:T(8,128)(2,1)S(1)} %shard_map.107), channel_id=1, source_target_pairs={{0,8},{2,10},{4,12},{6,14},{8,0},{10,2},{12,4},{14,6},{1,9},{3,11}... | collective-permute-start | bytes 786440 | tf_op jit(solution)/shard_map/ppermute | solution.py:500
  87.1 4.7 %collective-permute-done.21.refs_7_ = bf16[1,64,1024]{2,1,0:T(8,128)(2,1)S(1)} collective-permute-done((bf16[1,64,1024]{2,1,0:T(8,128)(2,1)S(1)}, bf16[1,64,1024]{2,1,0:T(8,128)(2,1)S(1)}, u32[]{:S(2)}, u32[]{:S(2)}) %collective-permute-start.21) | collective-permute-done | bytes 131104 | tf_op jit(solution)/shard_map/ppermute | solution.py:500
  94.0 9.0 %collective-permute-done.18.refs_9_ = bf16[1,64,2048]{2,1,0:T(8,128)(2,1)S(1)} collective-permute-done((bf16[1,64,2048]{2,1,0:T(8,128)(2,1)S(1)}, bf16[1,64,2048]{2,1,0:T(8,128)(2,1)S(1)}, u32[]{:S(2)}, u32[]{:S(2)}) %collective-permute-start.18) | collective-permute-done | bytes 262176 | tf_op jit(solution)/shard_map/ppermute | solution.py:500
  103.0 3.7 %collective-permute-done.22.refs_10_ = bf16[1,64,2048]{2,1,0:T(8,128)(2,1)S(1)} collective-permute-done((bf16[1,64,2048]{2,1,0:T(8,128)(2,1)S(1)}, bf16[1,64,2048]{2,1,0:T(8,128)(2,1)S(1)}, u32[]{:S(2)}, u32[]{:S(2)}) %collective-permute-start.22) | collective-permute-done | bytes 262176 | tf_op jit(solution)/shard_map/ppermute | solution.py:500
  108.0 1.5 %collective-permute-done.23 = bf16[2,64,1024]{2,1,0:T(8,128)(2,1)S(1)} collective-permute-done((bf16[2,64,1024]{2,1,0:T(8,128)(2,1)S(1)}, bf16[2,64,1024]{2,1,0:T(8,128)(2,1)S(1)}, u32[]{:S(2)}, u32[]{:S(2)}) %collective-permute-start.23) | collective-permute-done | bytes 262176 | tf_op jit(solution)/shard_map/ppermute | solution.py:503
  (39 shorter events, 12.1 us)
Async XLA Ops:
  0.0 5.9 %collective-permute-start = (s32[1,8]{1,0:T(1,128)}, s32[1,8]{1,0:T(1,128)S(1)}, u32[]{:S(2)}, u32[]{:S(2)}) collective-permute-start(s32[1,8]{1,0:T(1,128)} %refs_0_.11), channel_id=1, source_target_pairs={{0,2},{2,0},{4,6},{6,4},{8,10},{10,8},{12,14},{14,12},{1,3},{3,1},... | collective-permute-start | bytes 104 | tf_op jit(solution)/shard_map/ppermute | solution.py:500
  3.0 3.7 %collective-permute-start.1 = (s32[1,8]{1,0:T(1,128)}, s32[1,8]{1,0:T(1,128)S(1)}, u32[]{:S(2)}, u32[]{:S(2)}) collective-permute-start(s32[1,8]{1,0:T(1,128)} %refs_0_.11), channel_id=1, source_target_pairs={{0,4},{2,6},{4,0},{6,2},{8,12},{10,14},{12,8},{14,10},{1,5},{3,7},... | collective-permute-start | bytes 104 | tf_op jit(solution)/shard_map/ppermute | solution.py:500
  4.5 4.6 %collective-permute-start.2 = (s32[1,8]{1,0:T(1,128)}, s32[1,8]{1,0:T(1,128)S(1)}, u32[]{:S(2)}, u32[]{:S(2)}) collective-permute-start(s32[1,8]{1,0:T(1,128)} %refs_0_.11), channel_id=1, source_target_pairs={{0,6},{2,4},{4,2},{6,0},{8,14},{10,12},{12,10},{14,8},{1,7},{3,5},... | collective-permute-start | bytes 104 | tf_op jit(solution)/shard_map/ppermute | solution.py:500
  5.8 3.4 %collective-permute-start.3 = (f32[5,24,256]{2,1,0:T(8,128)S(1)}, f32[5,24,256]{2,1,0:T(8,128)S(1)}, u32[]{:S(2)}, u32[]{:S(2)}) collective-permute-start(f32[5,24,256]{2,1,0:T(8,128)S(1)} %shard_map.100.refs_2_), channel_id=1, source_target_pairs={{0,1},{1,0},{2,3},{3,2},{4,5},{5,4},{6,7},{7,6},{8,9},{9,8},{10,11... | collective-permute-start | bytes 368648 | tf_op jit(solution)/shard_map/ppermute | solution.py:503
  9.1 31.1 %collective-permute-start.5 = (bf16[24,512,256]{2,1,0:T(8,128)(2,1)}, bf16[24,512,256]{2,1,0:T(8,128)(2,1)}, u32[]{:S(2)}, u32[]{:S(2)}) collective-permute-start(bf16[24,512,256]{2,1,0:T(8,128)(2,1)} %refs_0_.8), channel_id=1, source_target_pairs={{0,1},{1,0},{2,3},{3,2},{4,5},{5,4},{6,7},{7,6},{8,9},{9,8},{10,11... | collective-permute-start | bytes 18874376 | tf_op jit(solution)/shard_map/ppermute | solution.py:503
  9.1 26.5 %collective-permute-start.4 = (bf16[2,64,2048]{2,1,0:T(8,128)(2,1)S(1)}, bf16[2,64,2048]{2,1,0:T(8,128)(2,1)S(1)}, u32[]{:S(2)}, u32[]{:S(2)}) collective-permute-start(bf16[2,64,2048]{2,1,0:T(8,128)(2,1)S(1)} %dynamic-slice_bitcast_fusion.refs_4_), channel_id=1, source_target_pairs={{0,8},{2,10},{4,12},{6,14},{8,0},{10,2},{12,4},{14,6},{1,9},{3,11}... | collective-permute-start | bytes 1572872 | tf_op jit(solution)/shard_map/ppermute | solution.py:500
  13.5 23.1 %collective-permute-start.6 = (bf16[2,64,1024]{2,1,0:T(8,128)(2,1)}, bf16[2,64,1024]{2,1,0:T(8,128)(2,1)S(1)}, u32[]{:S(2)}, u32[]{:S(2)}) collective-permute-start(bf16[2,64,1024]{2,1,0:T(8,128)(2,1)} %get-tuple-element.68), channel_id=1, source_target_pairs={{0,2},{2,0},{4,6},{6,4},{8,10},{10,8},{12,14},{14,12},{1,3},{3,1},... | collective-permute-start | bytes 786440 | tf_op jit(solution)/shard_map/ppermute | solution.py:500
  14.0 24.7 %collective-permute-start.7 = (bf16[2,64,1024]{2,1,0:T(8,128)(2,1)}, bf16[2,64,1024]{2,1,0:T(8,128)(2,1)S(1)}, u32[]{:S(2)}, u32[]{:S(2)}) collective-permute-start(bf16[2,64,1024]{2,1,0:T(8,128)(2,1)} %get-tuple-element.69), channel_id=1, source_target_pairs={{0,4},{2,6},{4,0},{6,2},{8,12},{10,14},{12,8},{14,10},{1,5},{3,7},... | collective-permute-start | bytes 786440 | tf_op jit(solution)/shard_map/ppermute | solution.py:500
  15.1 25.1 %collective-permute-start.8 = (bf16[2,64,1024]{2,1,0:T(8,128)(2,1)}, bf16[2,64,1024]{2,1,0:T(8,128)(2,1)S(1)}, u32[]{:S(2)}, u32[]{:S(2)}) collective-permute-start(bf16[2,64,1024]{2,1,0:T(8,128)(2,1)} %get-tuple-element.70), channel_id=1, source_target_pairs={{0,6},{2,4},{4,2},{6,0},{8,14},{10,12},{12,10},{14,8},{1,7},{3,5},... | collective-permute-start | bytes 786440 | tf_op jit(solution)/shard_map/ppermute | solution.py:500
  36.5 18.3 %collective-permute-start.10 = (bf16[2,64,1024]{2,1,0:T(8,128)(2,1)S(1)}, bf16[2,64,1024]{2,1,0:T(8,128)(2,1)S(1)}, u32[]{:S(2)}, u32[]{:S(2)}) collective-permute-start(bf16[2,64,1024]{2,1,0:T(8,128)(2,1)S(1)} %get-tuple-element.74), channel_id=1, source_target_pairs={{0,4},{2,6},{4,0},{6,2},{8,12},{10,14},{12,8},{14,10},{1,5},{3,7},... | collective-permute-start | bytes 786440 | tf_op jit(solution)/shard_map/ppermute | solution.py:500
  36.6 21.3 %collective-permute-start.11 = (bf16[2,64,1024]{2,1,0:T(8,128)(2,1)S(1)}, bf16[2,64,1024]{2,1,0:T(8,128)(2,1)S(1)}, u32[]{:S(2)}, u32[]{:S(2)}) collective-permute-start(bf16[2,64,1024]{2,1,0:T(8,128)(2,1)S(1)} %get-tuple-element.75), channel_id=1, source_target_pairs={{0,6},{2,4},{4,2},{6,0},{8,14},{10,12},{12,10},{14,8},{1,7},{3,5},... | collective-permute-start | bytes 786440 | tf_op jit(solution)/shard_map/ppermute | solution.py:500
  38.7 19.2 %collective-permute-start.9 = (bf16[2,64,1024]{2,1,0:T(8,128)(2,1)S(1)}, bf16[2,64,1024]{2,1,0:T(8,128)(2,1)S(1)}, u32[]{:S(2)}, u32[]{:S(2)}) collective-permute-start(bf16[2,64,1024]{2,1,0:T(8,128)(2,1)S(1)} %get-tuple-element.73), channel_id=1, source_target_pairs={{0,2},{2,0},{4,6},{6,4},{8,10},{10,8},{12,14},{14,12},{1,3},{3,1},... | collective-permute-start | bytes 786440 | tf_op jit(solution)/shard_map/ppermute | solution.py:500
  54.4 17.7 %collective-permute-start.12 = (bf16[2,64,1024]{2,1,0:T(8,128)(2,1)S(1)}, bf16[2,64,1024]{2,1,0:T(8,128)(2,1)S(1)}, u32[]{:S(2)}, u32[]{:S(2)}) collective-permute-start(bf16[2,64,1024]{2,1,0:T(8,128)(2,1)S(1)} %get-tuple-element.84), channel_id=1, source_target_pairs={{0,2},{2,0},{4,6},{6,4},{8,10},{10,8},{12,14},{14,12},{1,3},{3,1},... | collective-permute-start | bytes 786440 | tf_op jit(solution)/shard_map/ppermute | solution.py:500
  54.8 17.3 %collective-permute-start.13 = (bf16[2,64,1024]{2,1,0:T(8,128)(2,1)S(1)}, bf16[2,64,1024]{2,1,0:T(8,128)(2,1)S(1)}, u32[]{:S(2)}, u32[]{:S(2)}) collective-permute-start(bf16[2,64,1024]{2,1,0:T(8,128)(2,1)S(1)} %get-tuple-element.85), channel_id=1, source_target_pairs={{0,4},{2,6},{4,0},{6,2},{8,12},{10,14},{12,8},{14,10},{1,5},{3,7},... | collective-permute-start | bytes 786440 | tf_op jit(solution)/shard_map/ppermute | solution.py:500
  54.8 17.3 %collective-permute-start.14 = (bf16[2,64,1024]{2,1,0:T(8,128)(2,1)S(1)}, bf16[2,64,1024]{2,1,0:T(8,128)(2,1)S(1)}, u32[]{:S(2)}, u32[]{:S(2)}) collective-permute-start(bf16[2,64,1024]{2,1,0:T(8,128)(2,1)S(1)} %get-tuple-element.86), channel_id=1, source_target_pairs={{0,6},{2,4},{4,2},{6,0},{8,14},{10,12},{12,10},{14,8},{1,7},{3,5},... | collective-permute-start | bytes 786440 | tf_op jit(solution)/shard_map/ppermute | solution.py:500
  72.1 6.3 %collective-permute-start.15 = (bf16[1,64,1024]{2,1,0:T(8,128)(2,1)S(1)}, bf16[1,64,1024]{2,1,0:T(8,128)(2,1)S(1)}, u32[]{:S(2)}, u32[]{:S(2)}) collective-permute-start(bf16[1,64,1024]{2,1,0:T(8,128)(2,1)S(1)} %get-tuple-element.93), channel_id=1, source_target_pairs={{0,2},{2,0},{4,6},{6,4},{8,10},{10,8},{12,14},{14,12},{1,3},{3,1},... | collective-permute-start | bytes 393224 | tf_op jit(solution)/shard_map/ppermute | solution.py:500
  72.4 5.9 %collective-permute-start.16 = (bf16[1,64,1024]{2,1,0:T(8,128)(2,1)S(1)}, bf16[1,64,1024]{2,1,0:T(8,128)(2,1)S(1)}, u32[]{:S(2)}, u32[]{:S(2)}) collective-permute-start(bf16[1,64,1024]{2,1,0:T(8,128)(2,1)S(1)} %get-tuple-element.95), channel_id=1, source_target_pairs={{0,4},{2,6},{4,0},{6,2},{8,12},{10,14},{12,8},{14,10},{1,5},{3,7},... | collective-permute-start | bytes 393224 | tf_op jit(solution)/shard_map/ppermute | solution.py:500
  72.5 7.6 %collective-permute-start.17 = (bf16[1,64,1024]{2,1,0:T(8,128)(2,1)S(1)}, bf16[1,64,1024]{2,1,0:T(8,128)(2,1)S(1)}, u32[]{:S(2)}, u32[]{:S(2)}) collective-permute-start(bf16[1,64,1024]{2,1,0:T(8,128)(2,1)S(1)} %get-tuple-element.97), channel_id=1, source_target_pairs={{0,6},{2,4},{4,2},{6,0},{8,14},{10,12},{12,10},{14,8},{1,7},{3,5},... | collective-permute-start | bytes 393224 | tf_op jit(solution)/shard_map/ppermute | solution.py:500
  81.0 5.5 %collective-permute-start.19 = (bf16[1,64,1024]{2,1,0:T(8,128)(2,1)S(1)}, bf16[1,64,1024]{2,1,0:T(8,128)(2,1)S(1)}, u32[]{:S(2)}, u32[]{:S(2)}) collective-permute-start(bf16[1,64,1024]{2,1,0:T(8,128)(2,1)S(1)} %get-tuple-element.101), channel_id=1, source_target_pairs={{0,2},{2,0},{4,6},{6,4},{8,10},{10,8},{12,14},{14,12},{1,3},{3,1},... | collective-permute-start | bytes 393224 | tf_op jit(solution)/shard_map/ppermute | solution.py:500
  81.3 5.8 %collective-permute-start.20 = (bf16[1,64,1024]{2,1,0:T(8,128)(2,1)S(1)}, bf16[1,64,1024]{2,1,0:T(8,128)(2,1)S(1)}, u32[]{:S(2)}, u32[]{:S(2)}) collective-permute-start(bf16[1,64,1024]{2,1,0:T(8,128)(2,1)S(1)} %get-tuple-element.102), channel_id=1, source_target_pairs={{0,4},{2,6},{4,0},{6,2},{8,12},{10,14},{12,8},{14,10},{1,5},{3,7},... | collective-permute-start | bytes 393224 | tf_op jit(solution)/shard_map/ppermute | solution.py:500
  83.1 8.7 %collective-permute-start.21 = (bf16[1,64,1024]{2,1,0:T(8,128)(2,1)S(1)}, bf16[1,64,1024]{2,1,0:T(8,128)(2,1)S(1)}, u32[]{:S(2)}, u32[]{:S(2)}) collective-permute-start(bf16[1,64,1024]{2,1,0:T(8,128)(2,1)S(1)} %get-tuple-element.103), channel_id=1, source_target_pairs={{0,6},{2,4},{4,2},{6,0},{8,14},{10,12},{12,10},{14,8},{1,7},{3,5},... | collective-permute-start | bytes 393224 | tf_op jit(solution)/shard_map/ppermute | solution.py:500
  84.5 18.4 %collective-permute-start.18 = (bf16[1,64,2048]{2,1,0:T(8,128)(2,1)S(1)}, bf16[1,64,2048]{2,1,0:T(8,128)(2,1)S(1)}, u32[]{:S(2)}, u32[]{:S(2)}) collective-permute-start(bf16[1,64,2048]{2,1,0:T(8,128)(2,1)S(1)} %shard_map.107), channel_id=1, source_target_pairs={{0,8},{2,10},{4,12},{6,14},{8,0},{10,2},{12,4},{14,6},{1,9},{3,11}... | collective-permute-start | bytes 786440 | tf_op jit(solution)/shard_map/ppermute | solution.py:500
  92.8 13.8 %collective-permute-start.22 = (bf16[1,64,2048]{2,1,0:T(8,128)(2,1)S(1)}, bf16[1,64,2048]{2,1,0:T(8,128)(2,1)S(1)}, u32[]{:S(2)}, u32[]{:S(2)}) collective-permute-start(bf16[1,64,2048]{2,1,0:T(8,128)(2,1)S(1)} %shard_map.108), channel_id=1, source_target_pairs={{0,8},{2,10},{4,12},{6,14},{8,0},{10,2},{12,4},{14,6},{1,9},{3,11}... | collective-permute-start | bytes 786440 | tf_op jit(solution)/shard_map/ppermute | solution.py:500
  108.0 1.6 %collective-permute-start.23 = (bf16[2,64,1024]{2,1,0:T(8,128)(2,1)S(1)}, bf16[2,64,1024]{2,1,0:T(8,128)(2,1)S(1)}, u32[]{:S(2)}, u32[]{:S(2)}) collective-permute-start(bf16[2,64,1024]{2,1,0:T(8,128)(2,1)S(1)} %get-tuple-element.106), channel_id=1, source_target_pairs={{0,1},{1,0},{2,3},{3,2},{4,5},{5,4},{6,7},{7,6},{8,9},{9,8},{10,11... | collective-permute-start | bytes 786440 | tf_op jit(solution)/shard_map/ppermute | solution.py:503
  (1 other events, 5.8 us)

commit v11 on v10

--- a/solution.py
+++ b/solution.py
@@ -373,13 +373,13 @@
     at_lives, at_near, at_far, at_pos, at_col, _ = table_places(batches, group)
     at_row = at_far if split else at_near
 
-    def fetch(j, act):
+    def fetch(j, sem):
         b = table[j]
         for side in (0, 1):
 
             @pl.when((b >= half) if side else (b < half))
             def _():
-                act(pltpu.make_async_copy(xs[side].at[b - half * side], xbuf.at[j], xsems.at[j]))
+                pltpu.make_async_copy(xs[side].at[b - half * side], xbuf.at[j], sem).start()
 
     copies = [
         pltpu.make_async_copy(part, dense.at[pl.ds(nb * k, nb), :, pl.ds(0, wide)], sems.at[k])
@@ -392,9 +392,10 @@
     for copy in copies:
         copy.start()
 
-    @pl.loop(0, batches)
-    def _(j):
-        fetch(j, lambda copy: copy.start())
+    @pl.loop(0, batches // group)
+    def _(h):
+        for u in range(group):
+            fetch(h * group + u, xsems.at[h])
 
     acc[...] = jnp.zeros(acc.shape, acc.dtype)
     dense[:, :, wide:] = jnp.zeros((spare + 1, sub, FB), dense.dtype)
@@ -432,10 +433,8 @@
 
     @pl.loop(0, batches // group)
     def _(h):
-        @pl.loop(0, group)
-        def _(u):
-            fetch(h * group + u, lambda copy: copy.wait())
-
+        arrived = xbuf.at[pl.ds(h * group, group)]
+        pltpu.make_async_copy(arrived, arrived, xsems.at[h]).wait()
         for live in range(2, TMAX + 1):
 
             @pl.when(table[at_lives + h] == live)
@@ -479,7 +478,7 @@
             pltpu.VMEM((4, batches, pts), jnp.float32),
             pltpu.VMEM(centre.shape, jnp.float32),
             pltpu.SemaphoreType.DMA((pieces + 3,)),
-            pltpu.SemaphoreType.DMA((batches,)),
+            pltpu.SemaphoreType.DMA((batches // group,)),
         ],
         cost=(flops, 2 * batches * width * pts),
     )
@@ -528,14 +527,15 @@
     sums = batch_sums(table, *common, parts, False)
     table, _ = lax.optimization_barrier((table, sums[0]))
     far_sums = batch_sums(table, *common, far_parts, True)
-    terms = [sums[0]] + [swap(sums[k], k) for k in range(1, near)]
+    terms = [sums[0], sums[1]] + [swap(sums[k], k) for k in range(2, near)]
     far_sums, terms = lax.optimization_barrier((far_sums, terms))
     far_terms = []
     for b in range(nb):
         chunk = [far_sums[b]] + [swap(far_sums[nb * k + b], k) for k in range(1, near)]
         merged = merge(sets, chunk, cols)
-        far_sums, merged = lax.optimization_barrier((far_sums, merged))
+        far_sums, merged, terms[1] = lax.optimization_barrier((far_sums, merged, terms[1]))
         far_terms.append(swap(merged, near))
+    terms[1] = swap(terms[1], 1)
     keep, give = finish(sets, core, terms, far_terms)
     got = across(give)
     pair = jnp.where(r == 0, jnp.stack([keep, got], axis=1), jnp.stack([got, keep], axis=1))

time: 111 us -> 108 us (0.973)
  Pallas kernels: 42.9 us -> 39.5 us
    pallas_call x10, Pallas kernels: 42.9 us -> 39.5 us  [call(): pl.pallas_call(kernel, grid_spec=pltpu.PrefetchScalarGridSpec(num_scalar_...]
  transfers between devices with their start and end apart: 24 -> 24, of which waited for: 12 -> 12; matrix products, arithmetic and copies ran while one was open for 0% -> 0% of each run, Pallas kernels for 37% -> 35%
where the time goes in v11:
time: 108 us; the launch traced here: 107 us
  Pallas kernels  39.5 us (37%)
  waiting for transfers between devices  37.9 us (35%)
  starting transfers between devices  28.9 us (27%)
    pallas_call x10, Pallas kernels, call(): pl.pallas_call(kernel, grid_spec=pltpu.PrefetchScalarGridSpec(num_scalar_...  39.5 us
    ppermute x21, waiting for transfers between devices, swap(): return lax.ppermute(x, 'dom', [(a, a ^ k) for a in range(n)])  36.4 us
    ppermute x21, starting transfers between devices, swap(): return lax.ppermute(x, 'dom', [(a, a ^ k) for a in range(n)])  28.8 us
  transfers between devices with their start and end apart: 24, of which 12 were waited for; matrix products, arithmetic and copies ran while one was open for 0% of the time, Pallas kernels for 35%

profile of v11, /device:TPU:0, one launch (start us, length us, event | category | flops | bytes accessed | tf_op | source)
XLA Modules:
  0.0 107.4 jit_solution(16036723432940705479)
XLA Ops:
  0.0 3.0 %collective-permute-start = (s32[1,8]{1,0:T(1,128)}, s32[1,8]{1,0:T(1,128)S(1)}, u32[]{:S(2)}, u32[]{:S(2)}) collective-permute-start(s32[1,8]{1,0:T(1,128)} %refs_0_.11), channel_id=1, source_target_pairs={{0,2},{2,0},{4,6},{6,4},{8,10},{10,8},{12,14},{14,12},{1,3},{3,1},... | collective-permute-start | bytes 104 | tf_op jit(solution)/shard_map/ppermute | solution.py:499
  3.0 1.6 %collective-permute-start.1 = (s32[1,8]{1,0:T(1,128)}, s32[1,8]{1,0:T(1,128)S(1)}, u32[]{:S(2)}, u32[]{:S(2)}) collective-permute-start(s32[1,8]{1,0:T(1,128)} %refs_0_.11), channel_id=1, source_target_pairs={{0,4},{2,6},{4,0},{6,2},{8,12},{10,14},{12,8},{14,10},{1,5},{3,7},... | collective-permute-start | bytes 104 | tf_op jit(solution)/shard_map/ppermute | solution.py:499
  6.6 2.5 %collective-permute-done.2.refs_3_ = s32[1,8]{1,0:T(1,128)S(1)} collective-permute-done((s32[1,8]{1,0:T(1,128)}, s32[1,8]{1,0:T(1,128)S(1)}, u32[]{:S(2)}, u32[]{:S(2)}) %collective-permute-start.2) | collective-permute-done | bytes 64 | tf_op jit(solution)/shard_map/ppermute | solution.py:499
  9.1 2.6 %collective-permute-start.4 = (bf16[2,64,2048]{2,1,0:T(8,128)(2,1)S(1)}, bf16[2,64,2048]{2,1,0:T(8,128)(2,1)S(1)}, u32[]{:S(2)}, u32[]{:S(2)}) collective-permute-start(bf16[2,64,2048]{2,1,0:T(8,128)(2,1)S(1)} %dynamic-slice_bitcast_fusion.refs_4_), channel_id=1, source_target_pairs={{0,8},{2,10},{4,12},{6,14},{8,0},{10,2},{12,4},{14,6},{1,9},{3,11}... | collective-permute-start | bytes 1572872 | tf_op jit(solution)/shard_map/ppermute | solution.py:499
  11.7 1.8 %shard_map.104 = (bf16[2,64,1024]{2,1,0:T(8,128)(2,1)S(1)}, bf16[2,64,1024]{2,1,0:T(8,128)(2,1)}, bf16[2,64,1024]{2,1,0:T(8,128)(2,1)}, bf16[2,64,1024]{2,1,0:T(8,128)(2,1)}) custom-call(s32[1,8]{1,0:T(1,128)} %refs_0_.11, s32[1,8]{1,0:T(1,128)S(1)} %collective-permute-done.refs_1_, s32[1,8]{1,0:T(1,128)S(1)} %collective-permute-done.1.refs_2_, ...), custom_call_target="tpu_custom_call" | custom-call | bytes 1572864 | tf_op jit(solution)/shard_map/pallas_call | solution.py:129
  15.2 1.8 %collective-permute-start.8 = (bf16[2,64,1024]{2,1,0:T(8,128)(2,1)}, bf16[2,64,1024]{2,1,0:T(8,128)(2,1)S(1)}, u32[]{:S(2)}, u32[]{:S(2)}) collective-permute-start(bf16[2,64,1024]{2,1,0:T(8,128)(2,1)} %get-tuple-element.72), channel_id=1, source_target_pairs={{0,6},{2,4},{4,2},{6,0},{8,14},{10,12},{12,10},{14,8},{1,7},{3,5},... | collective-permute-start | bytes 786440 | tf_op jit(solution)/shard_map/ppermute | solution.py:499
  17.0 2.1 %shard_map.102.refs_4_ = f32[4,8,64,128]{3,2,1,0:T(8,128)S(1)} custom-call(s32[1,8]{1,0:T(1,128)} %refs_0_.11, s32[1]{0:T(128)} %bitcast.4.core.refs_4_, f32[3,2048]{1,0:T(4,128)} %centers.1, f32[1,2048]{1,0:T(1,128)} %bitcast.17), custom_call_target="tpu_custom_call" | custom-call | bytes 2097152 | tf_op jit(solution)/shard_map/pallas_call | solution.py:129
  19.1 5.4 %shard_map.101.table = s32[824]{0:T(1024)S(1)} custom-call(s32[1]{0:T(128)} %bitcast.5.me, s32[16]{0:T(128)} %owner.1, s32[1,8]{1,0:T(1,128)} %refs_0_.11, s32[4,24]{1,0:T(4,128)} %bitcast.19, f32[5,24,256]{2,1,0:T(8,128)S(1)} %collective-permute-done.3.packed.refs_3_, s32[24]{0:T(128)} %counts.3), custom_call_target="tpu_custom_call" | custom-call | bytes 1536 | tf_op jit(solution)/shard_map/pallas_call | solution.py:129
  24.5 11.1 %collective-permute-done.4.refs_4_ = bf16[2,64,2048]{2,1,0:T(8,128)(2,1)S(1)} collective-permute-done((bf16[2,64,2048]{2,1,0:T(8,128)(2,1)S(1)}, bf16[2,64,2048]{2,1,0:T(8,128)(2,1)S(1)}, u32[]{:S(2)}, u32[]{:S(2)}) %collective-permute-start.4) | collective-permute-done | bytes 524320 | tf_op jit(solution)/shard_map/ppermute | solution.py:499
  36.6 2.1 %collective-permute-start.11 = (bf16[2,64,1024]{2,1,0:T(8,128)(2,1)S(1)}, bf16[2,64,1024]{2,1,0:T(8,128)(2,1)S(1)}, u32[]{:S(2)}, u32[]{:S(2)}) collective-permute-start(bf16[2,64,1024]{2,1,0:T(8,128)(2,1)S(1)} %get-tuple-element.77), channel_id=1, source_target_pairs={{0,6},{2,4},{4,2},{6,0},{8,14},{10,12},{12,10},{14,8},{1,7},{3,5},... | collective-permute-start | bytes 786440 | tf_op jit(solution)/shard_map/ppermute | solution.py:499
  38.7 1.4 %collective-permute-start.9 = (bf16[2,64,1024]{2,1,0:T(8,128)(2,1)S(1)}, bf16[2,64,1024]{2,1,0:T(8,128)(2,1)S(1)}, u32[]{:S(2)}, u32[]{:S(2)}) collective-permute-start(bf16[2,64,1024]{2,1,0:T(8,128)(2,1)S(1)} %get-tuple-element.75), channel_id=1, source_target_pairs={{0,2},{2,0},{4,6},{6,4},{8,10},{10,8},{12,14},{14,12},{1,3},{3,1},... | collective-permute-start | bytes 786440 | tf_op jit(solution)/shard_map/ppermute | solution.py:499
  40.2 12.4 %shard_map.105 = (f32[2,64,1024]{2,1,0:T(8,128)S(1)}, bf16[2,64,1024]{2,1,0:T(8,128)(2,1)S(1)}, bf16[2,64,1024]{2,1,0:T(8,128)(2,1)S(1)}, bf16[2,64,1024]{2,1,0:T(8,128)(2,1)S(1)}) custom-call(s32[824]{0:T(1024)S(1)} %shard_map.101.table, bf16[24,512,256]{2,1,0:T(8,128)(2,1)} %refs_0_.8, bf16[24,512,256]{2,1,0:T(8,128)(2,1)} %collective-permute-done.5.refs_1_, ...), custom_call_target="tpu_custom_call" | custom-call | flops 6442450944 | bytes 12582912 | tf_op jit(solution)/shard_map/pallas_call | solution.py:129
  53.4 2.0 %collective-permute-start.13 = (bf16[2,64,1024]{2,1,0:T(8,128)(2,1)S(1)}, bf16[2,64,1024]{2,1,0:T(8,128)(2,1)S(1)}, u32[]{:S(2)}, u32[]{:S(2)}) collective-permute-start(bf16[2,64,1024]{2,1,0:T(8,128)(2,1)S(1)} %get-tuple-element.88), channel_id=1, source_target_pairs={{0,6},{2,4},{4,2},{6,0},{8,14},{10,12},{12,10},{14,8},{1,7},{3,5},... | collective-permute-start | bytes 786440 | tf_op jit(solution)/shard_map/ppermute | solution.py:499
  55.4 12.4 %shard_map.106 = (f32[1,64,1024]{2,1,0:T(8,128)S(1)}, f32[1,64,1024]{2,1,0:T(8,128)S(1)}, bf16[1,64,1024]{2,1,0:T(8,128)(2,1)S(1)}, bf16[1,64,1024]{2,1,0:T(8,12...) custom-call(s32[824]{0:T(1024)S(1)} %shard_map.101.table, ...), custom_call_target="tpu_custom_call" | custom-call | flops 6442450944 | bytes 12582912 | tf_op jit(solution)/shard_map/pallas_call | solution.py:129
  67.9 1.6 %collective-permute-start.14 = (bf16[1,64,1024]{2,1,0:T(8,128)(2,1)S(1)}, bf16[1,64,1024]{2,1,0:T(8,128)(2,1)S(1)}, u32[]{:S(2)}, u32[]{:S(2)}) collective-permute-start(bf16[1,64,1024]{2,1,0:T(8,128)(2,1)S(1)} %get-tuple-element.92), channel_id=1, source_target_pairs={{0,2},{2,0},{4,6},{6,4},{8,10},{10,8},{12,14},{14,12},{1,3},{3,1},... | collective-permute-start | bytes 393224 | tf_op jit(solution)/shard_map/ppermute | solution.py:499
  71.5 2.9 %collective-permute-done.14.refs_5_ = bf16[1,64,1024]{2,1,0:T(8,128)(2,1)S(1)} collective-permute-done((bf16[1,64,1024]{2,1,0:T(8,128)(2,1)S(1)}, bf16[1,64,1024]{2,1,0:T(8,128)(2,1)S(1)}, u32[]{:S(2)}, u32[]{:S(2)}) %collective-permute-start.14) | collective-permute-done | bytes 131104 | tf_op jit(solution)/shard_map/ppermute | solution.py:499
  74.5 1.8 %collective-permute-done.16.refs_7_ = bf16[1,64,1024]{2,1,0:T(8,128)(2,1)S(1)} collective-permute-done((bf16[1,64,1024]{2,1,0:T(8,128)(2,1)S(1)}, bf16[1,64,1024]{2,1,0:T(8,128)(2,1)S(1)}, u32[]{:S(2)}, u32[]{:S(2)}) %collective-permute-start.16) | collective-permute-done | bytes 131104 | tf_op jit(solution)/shard_map/ppermute | solution.py:499
  80.9 2.2 %collective-permute-start.21 = (bf16[1,64,2048]{2,1,0:T(8,128)(2,1)S(1)}, bf16[1,64,2048]{2,1,0:T(8,128)(2,1)S(1)}, u32[]{:S(2)}, u32[]{:S(2)}) collective-permute-start(bf16[1,64,2048]{2,1,0:T(8,128)(2,1)S(1)} %shard_map.107), channel_id=1, source_target_pairs={{0,8},{2,10},{4,12},{6,14},{8,0},{10,2},{12,4},{14,6},{1,9},{3,11}... | collective-permute-start | bytes 786440 | tf_op jit(solution)/shard_map/ppermute | solution.py:499
  83.8 4.3 %collective-permute-done.19.refs_7_ = bf16[1,64,1024]{2,1,0:T(8,128)(2,1)S(1)} collective-permute-done((bf16[1,64,1024]{2,1,0:T(8,128)(2,1)S(1)}, bf16[1,64,1024]{2,1,0:T(8,128)(2,1)S(1)}, u32[]{:S(2)}, u32[]{:S(2)}) %collective-permute-start.19) | collective-permute-done | bytes 131104 | tf_op jit(solution)/shard_map/ppermute | solution.py:499
  89.3 2.5 %collective-permute-start.22 = (bf16[1,64,2048]{2,1,0:T(8,128)(2,1)S(1)}, bf16[1,64,2048]{2,1,0:T(8,128)(2,1)S(1)}, u32[]{:S(2)}, u32[]{:S(2)}) collective-permute-start(bf16[1,64,2048]{2,1,0:T(8,128)(2,1)S(1)} %shard_map.108), channel_id=1, source_target_pairs={{0,8},{2,10},{4,12},{6,14},{8,0},{10,2},{12,4},{14,6},{1,9},{3,11}... | collective-permute-start | bytes 786440 | tf_op jit(solution)/shard_map/ppermute | solution.py:499
  91.7 8.1 %collective-permute-done.21.refs_9_ = bf16[1,64,2048]{2,1,0:T(8,128)(2,1)S(1)} collective-permute-done((bf16[1,64,2048]{2,1,0:T(8,128)(2,1)S(1)}, bf16[1,64,2048]{2,1,0:T(8,128)(2,1)S(1)}, u32[]{:S(2)}, u32[]{:S(2)}) %collective-permute-start.21) | collective-permute-done | bytes 262176 | tf_op jit(solution)/shard_map/ppermute | solution.py:499
  99.9 3.7 %collective-permute-done.22.refs_10_ = bf16[1,64,2048]{2,1,0:T(8,128)(2,1)S(1)} collective-permute-done((bf16[1,64,2048]{2,1,0:T(8,128)(2,1)S(1)}, bf16[1,64,2048]{2,1,0:T(8,128)(2,1)S(1)}, u32[]{:S(2)}, u32[]{:S(2)}) %collective-permute-start.22) | collective-permute-done | bytes 262176 | tf_op jit(solution)/shard_map/ppermute | solution.py:499
  103.6 1.3 %shard_map.109 = (bf16[2,64,1024]{2,1,0:T(8,128)(2,1)S(1)}, bf16[2,64,1024]{2,1,0:T(8,128)(2,1)S(1)}) custom-call(s32[1,8]{1,0:T(1,128)} %refs_0_.11, s32[1,8]{1,0:T(1,128)S(1)} %collective-permute-done.refs_1_, s32[1,8]{1,0:T(1,128)S(1)} %collective-permute-done.1.refs_2_, s32[1,8]{1,0:T(1,128)S(1)} %collective-permute-done.2.refs_3_, ...), custom_call_target="tpu_custom_call" | custom-call | bytes 2359296 | tf_op jit(solution)/shard_map/pallas_call | solution.py:129
  105.0 1.5 %collective-permute-done.23 = bf16[2,64,1024]{2,1,0:T(8,128)(2,1)S(1)} collective-permute-done((bf16[2,64,1024]{2,1,0:T(8,128)(2,1)S(1)}, bf16[2,64,1024]{2,1,0:T(8,128)(2,1)S(1)}, u32[]{:S(2)}, u32[]{:S(2)}) %collective-permute-start.23) | collective-permute-done | bytes 262176 | tf_op jit(solution)/shard_map/ppermute | solution.py:502
  (39 shorter events, 15.2 us)
Async XLA Ops:
  0.0 5.9 %collective-permute-start = (s32[1,8]{1,0:T(1,128)}, s32[1,8]{1,0:T(1,128)S(1)}, u32[]{:S(2)}, u32[]{:S(2)}) collective-permute-start(s32[1,8]{1,0:T(1,128)} %refs_0_.11), channel_id=1, source_target_pairs={{0,2},{2,0},{4,6},{6,4},{8,10},{10,8},{12,14},{14,12},{1,3},{3,1},... | collective-permute-start | bytes 104 | tf_op jit(solution)/shard_map/ppermute | solution.py:499
  3.0 3.7 %collective-permute-start.1 = (s32[1,8]{1,0:T(1,128)}, s32[1,8]{1,0:T(1,128)S(1)}, u32[]{:S(2)}, u32[]{:S(2)}) collective-permute-start(s32[1,8]{1,0:T(1,128)} %refs_0_.11), channel_id=1, source_target_pairs={{0,4},{2,6},{4,0},{6,2},{8,12},{10,14},{12,8},{14,10},{1,5},{3,7},... | collective-permute-start | bytes 104 | tf_op jit(solution)/shard_map/ppermute | solution.py:499
  4.5 4.6 %collective-permute-start.2 = (s32[1,8]{1,0:T(1,128)}, s32[1,8]{1,0:T(1,128)S(1)}, u32[]{:S(2)}, u32[]{:S(2)}) collective-permute-start(s32[1,8]{1,0:T(1,128)} %refs_0_.11), channel_id=1, source_target_pairs={{0,6},{2,4},{4,2},{6,0},{8,14},{10,12},{12,10},{14,8},{1,7},{3,5},... | collective-permute-start | bytes 104 | tf_op jit(solution)/shard_map/ppermute | solution.py:499
  5.8 3.4 %collective-permute-start.3 = (f32[5,24,256]{2,1,0:T(8,128)S(1)}, f32[5,24,256]{2,1,0:T(8,128)S(1)}, u32[]{:S(2)}, u32[]{:S(2)}) collective-permute-start(f32[5,24,256]{2,1,0:T(8,128)S(1)} %shard_map.100.refs_2_), channel_id=1, source_target_pairs={{0,1},{1,0},{2,3},{3,2},{4,5},{5,4},{6,7},{7,6},{8,9},{9,8},{10,11... | collective-permute-start | bytes 368648 | tf_op jit(solution)/shard_map/ppermute | solution.py:502
  9.1 31.1 %collective-permute-start.5 = (bf16[24,512,256]{2,1,0:T(8,128)(2,1)}, bf16[24,512,256]{2,1,0:T(8,128)(2,1)}, u32[]{:S(2)}, u32[]{:S(2)}) collective-permute-start(bf16[24,512,256]{2,1,0:T(8,128)(2,1)} %refs_0_.8), channel_id=1, source_target_pairs={{0,1},{1,0},{2,3},{3,2},{4,5},{5,4},{6,7},{7,6},{8,9},{9,8},{10,11... | collective-permute-start | bytes 18874376 | tf_op jit(solution)/shard_map/ppermute | solution.py:502
  9.1 26.5 %collective-permute-start.4 = (bf16[2,64,2048]{2,1,0:T(8,128)(2,1)S(1)}, bf16[2,64,2048]{2,1,0:T(8,128)(2,1)S(1)}, u32[]{:S(2)}, u32[]{:S(2)}) collective-permute-start(bf16[2,64,2048]{2,1,0:T(8,128)(2,1)S(1)} %dynamic-slice_bitcast_fusion.refs_4_), channel_id=1, source_target_pairs={{0,8},{2,10},{4,12},{6,14},{8,0},{10,2},{12,4},{14,6},{1,9},{3,11}... | collective-permute-start | bytes 1572872 | tf_op jit(solution)/shard_map/ppermute | solution.py:499
  13.5 23.1 %collective-permute-start.6 = (bf16[2,64,1024]{2,1,0:T(8,128)(2,1)}, bf16[2,64,1024]{2,1,0:T(8,128)(2,1)S(1)}, u32[]{:S(2)}, u32[]{:S(2)}) collective-permute-start(bf16[2,64,1024]{2,1,0:T(8,128)(2,1)} %get-tuple-element.70), channel_id=1, source_target_pairs={{0,2},{2,0},{4,6},{6,4},{8,10},{10,8},{12,14},{14,12},{1,3},{3,1},... | collective-permute-start | bytes 786440 | tf_op jit(solution)/shard_map/ppermute | solution.py:499
  14.0 24.7 %collective-permute-start.7 = (bf16[2,64,1024]{2,1,0:T(8,128)(2,1)}, bf16[2,64,1024]{2,1,0:T(8,128)(2,1)S(1)}, u32[]{:S(2)}, u32[]{:S(2)}) collective-permute-start(bf16[2,64,1024]{2,1,0:T(8,128)(2,1)} %get-tuple-element.71), channel_id=1, source_target_pairs={{0,4},{2,6},{4,0},{6,2},{8,12},{10,14},{12,8},{14,10},{1,5},{3,7},... | collective-permute-start | bytes 786440 | tf_op jit(solution)/shard_map/ppermute | solution.py:499
  15.2 25.1 %collective-permute-start.8 = (bf16[2,64,1024]{2,1,0:T(8,128)(2,1)}, bf16[2,64,1024]{2,1,0:T(8,128)(2,1)S(1)}, u32[]{:S(2)}, u32[]{:S(2)}) collective-permute-start(bf16[2,64,1024]{2,1,0:T(8,128)(2,1)} %get-tuple-element.72), channel_id=1, source_target_pairs={{0,6},{2,4},{4,2},{6,0},{8,14},{10,12},{12,10},{14,8},{1,7},{3,5},... | collective-permute-start | bytes 786440 | tf_op jit(solution)/shard_map/ppermute | solution.py:499
  36.5 18.9 %collective-permute-start.10 = (bf16[2,64,1024]{2,1,0:T(8,128)(2,1)S(1)}, bf16[2,64,1024]{2,1,0:T(8,128)(2,1)S(1)}, u32[]{:S(2)}, u32[]{:S(2)}) collective-permute-start(bf16[2,64,1024]{2,1,0:T(8,128)(2,1)S(1)} %get-tuple-element.76), channel_id=1, source_target_pairs={{0,4},{2,6},{4,0},{6,2},{8,12},{10,14},{12,8},{14,10},{1,5},{3,7},... | collective-permute-start | bytes 786440 | tf_op jit(solution)/shard_map/ppermute | solution.py:499
  36.6 18.8 %collective-permute-start.11 = (bf16[2,64,1024]{2,1,0:T(8,128)(2,1)S(1)}, bf16[2,64,1024]{2,1,0:T(8,128)(2,1)S(1)}, u32[]{:S(2)}, u32[]{:S(2)}) collective-permute-start(bf16[2,64,1024]{2,1,0:T(8,128)(2,1)S(1)} %get-tuple-element.77), channel_id=1, source_target_pairs={{0,6},{2,4},{4,2},{6,0},{8,14},{10,12},{12,10},{14,8},{1,7},{3,5},... | collective-permute-start | bytes 786440 | tf_op jit(solution)/shard_map/ppermute | solution.py:499
  38.7 16.8 %collective-permute-start.9 = (bf16[2,64,1024]{2,1,0:T(8,128)(2,1)S(1)}, bf16[2,64,1024]{2,1,0:T(8,128)(2,1)S(1)}, u32[]{:S(2)}, u32[]{:S(2)}) collective-permute-start(bf16[2,64,1024]{2,1,0:T(8,128)(2,1)S(1)} %get-tuple-element.75), channel_id=1, source_target_pairs={{0,2},{2,0},{4,6},{6,4},{8,10},{10,8},{12,14},{14,12},{1,3},{3,1},... | collective-permute-start | bytes 786440 | tf_op jit(solution)/shard_map/ppermute | solution.py:499
  52.6 15.2 %collective-permute-start.12 = (bf16[2,64,1024]{2,1,0:T(8,128)(2,1)S(1)}, bf16[2,64,1024]{2,1,0:T(8,128)(2,1)S(1)}, u32[]{:S(2)}, u32[]{:S(2)}) collective-permute-start(bf16[2,64,1024]{2,1,0:T(8,128)(2,1)S(1)} %get-tuple-element.87), channel_id=1, source_target_pairs={{0,4},{2,6},{4,0},{6,2},{8,12},{10,14},{12,8},{14,10},{1,5},{3,7},... | collective-permute-start | bytes 786440 | tf_op jit(solution)/shard_map/ppermute | solution.py:499
  53.4 14.5 %collective-permute-start.13 = (bf16[2,64,1024]{2,1,0:T(8,128)(2,1)S(1)}, bf16[2,64,1024]{2,1,0:T(8,128)(2,1)S(1)}, u32[]{:S(2)}, u32[]{:S(2)}) collective-permute-start(bf16[2,64,1024]{2,1,0:T(8,128)(2,1)S(1)} %get-tuple-element.88), channel_id=1, source_target_pairs={{0,6},{2,4},{4,2},{6,0},{8,14},{10,12},{12,10},{14,8},{1,7},{3,5},... | collective-permute-start | bytes 786440 | tf_op jit(solution)/shard_map/ppermute | solution.py:499
  67.9 6.4 %collective-permute-start.14 = (bf16[1,64,1024]{2,1,0:T(8,128)(2,1)S(1)}, bf16[1,64,1024]{2,1,0:T(8,128)(2,1)S(1)}, u32[]{:S(2)}, u32[]{:S(2)}) collective-permute-start(bf16[1,64,1024]{2,1,0:T(8,128)(2,1)S(1)} %get-tuple-element.92), channel_id=1, source_target_pairs={{0,2},{2,0},{4,6},{6,4},{8,10},{10,8},{12,14},{14,12},{1,3},{3,1},... | collective-permute-start | bytes 393224 | tf_op jit(solution)/shard_map/ppermute | solution.py:499
  69.5 5.1 %collective-permute-start.15 = (bf16[1,64,1024]{2,1,0:T(8,128)(2,1)S(1)}, bf16[1,64,1024]{2,1,0:T(8,128)(2,1)S(1)}, u32[]{:S(2)}, u32[]{:S(2)}) collective-permute-start(bf16[1,64,1024]{2,1,0:T(8,128)(2,1)S(1)} %get-tuple-element.94), channel_id=1, source_target_pairs={{0,4},{2,6},{4,0},{6,2},{8,12},{10,14},{12,8},{14,10},{1,5},{3,7},... | collective-permute-start | bytes 393224 | tf_op jit(solution)/shard_map/ppermute | solution.py:499
  70.3 6.0 %collective-permute-start.16 = (bf16[1,64,1024]{2,1,0:T(8,128)(2,1)S(1)}, bf16[1,64,1024]{2,1,0:T(8,128)(2,1)S(1)}, u32[]{:S(2)}, u32[]{:S(2)}) collective-permute-start(bf16[1,64,1024]{2,1,0:T(8,128)(2,1)S(1)} %get-tuple-element.96), channel_id=1, source_target_pairs={{0,6},{2,4},{4,2},{6,0},{8,14},{10,12},{12,10},{14,8},{1,7},{3,5},... | collective-permute-start | bytes 393224 | tf_op jit(solution)/shard_map/ppermute | solution.py:499
  77.3 5.7 %collective-permute-start.17 = (bf16[1,64,1024]{2,1,0:T(8,128)(2,1)S(1)}, bf16[1,64,1024]{2,1,0:T(8,128)(2,1)S(1)}, u32[]{:S(2)}, u32[]{:S(2)}) collective-permute-start(bf16[1,64,1024]{2,1,0:T(8,128)(2,1)S(1)} %get-tuple-element.100), channel_id=1, source_target_pairs={{0,2},{2,0},{4,6},{6,4},{8,10},{10,8},{12,14},{14,12},{1,3},{3,1},... | collective-permute-start | bytes 393224 | tf_op jit(solution)/shard_map/ppermute | solution.py:499
  78.5 5.4 %collective-permute-start.18 = (bf16[1,64,1024]{2,1,0:T(8,128)(2,1)S(1)}, bf16[1,64,1024]{2,1,0:T(8,128)(2,1)S(1)}, u32[]{:S(2)}, u32[]{:S(2)}) collective-permute-start(bf16[1,64,1024]{2,1,0:T(8,128)(2,1)S(1)} %get-tuple-element.101), channel_id=1, source_target_pairs={{0,4},{2,6},{4,0},{6,2},{8,12},{10,14},{12,8},{14,10},{1,5},{3,7},... | collective-permute-start | bytes 393224 | tf_op jit(solution)/shard_map/ppermute | solution.py:499
  79.7 8.5 %collective-permute-start.19 = (bf16[1,64,1024]{2,1,0:T(8,128)(2,1)S(1)}, bf16[1,64,1024]{2,1,0:T(8,128)(2,1)S(1)}, u32[]{:S(2)}, u32[]{:S(2)}) collective-permute-start(bf16[1,64,1024]{2,1,0:T(8,128)(2,1)S(1)} %get-tuple-element.102), channel_id=1, source_target_pairs={{0,6},{2,4},{4,2},{6,0},{8,14},{10,12},{12,10},{14,8},{1,7},{3,5},... | collective-permute-start | bytes 393224 | tf_op jit(solution)/shard_map/ppermute | solution.py:499
  80.9 19.0 %collective-permute-start.21 = (bf16[1,64,2048]{2,1,0:T(8,128)(2,1)S(1)}, bf16[1,64,2048]{2,1,0:T(8,128)(2,1)S(1)}, u32[]{:S(2)}, u32[]{:S(2)}) collective-permute-start(bf16[1,64,2048]{2,1,0:T(8,128)(2,1)S(1)} %shard_map.107), channel_id=1, source_target_pairs={{0,8},{2,10},{4,12},{6,14},{8,0},{10,2},{12,4},{14,6},{1,9},{3,11}... | collective-permute-start | bytes 786440 | tf_op jit(solution)/shard_map/ppermute | solution.py:499
  89.2 10.7 %collective-permute-start.20 = (bf16[2,64,1024]{2,1,0:T(8,128)(2,1)S(1)}, bf16[2,64,1024]{2,1,0:T(8,128)(2,1)S(1)}, u32[]{:S(2)}, u32[]{:S(2)}) collective-permute-start(bf16[2,64,1024]{2,1,0:T(8,128)(2,1)S(1)} %get-tuple-element.104), channel_id=1, source_target_pairs={{0,2},{2,0},{4,6},{6,4},{8,10},{10,8},{12,14},{14,12},{1,3},{3,1},... | collective-permute-start | bytes 786440 | tf_op jit(solution)/shard_map/ppermute | solution.py:499
  89.3 14.3 %collective-permute-start.22 = (bf16[1,64,2048]{2,1,0:T(8,128)(2,1)S(1)}, bf16[1,64,2048]{2,1,0:T(8,128)(2,1)S(1)}, u32[]{:S(2)}, u32[]{:S(2)}) collective-permute-start(bf16[1,64,2048]{2,1,0:T(8,128)(2,1)S(1)} %shard_map.108), channel_id=1, source_target_pairs={{0,8},{2,10},{4,12},{6,14},{8,0},{10,2},{12,4},{14,6},{1,9},{3,11}... | collective-permute-start | bytes 786440 | tf_op jit(solution)/shard_map/ppermute | solution.py:499
  104.9 1.6 %collective-permute-start.23 = (bf16[2,64,1024]{2,1,0:T(8,128)(2,1)S(1)}, bf16[2,64,1024]{2,1,0:T(8,128)(2,1)S(1)}, u32[]{:S(2)}, u32[]{:S(2)}) collective-permute-start(bf16[2,64,1024]{2,1,0:T(8,128)(2,1)S(1)} %get-tuple-element.110), channel_id=1, source_target_pairs={{0,1},{1,0},{2,3},{3,2},{4,5},{5,4},{6,7},{7,6},{8,9},{9,8},{10,11... | collective-permute-start | bytes 786440 | tf_op jit(solution)/shard_map/ppermute | solution.py:502
  (1 other events, 5.8 us)

commit v12 on v11

--- a/solution.py
+++ b/solution.py
@@ -318,7 +318,7 @@
     out[...] = total[...].astype(out.dtype)
 
 
-def merge(sets, terms, cols):
+def merge(sets, terms, cols, dtype=jnp.bfloat16):
     nb, sub, wide = terms[0].shape
     shape = (nb, sub, cols)
     return call(
@@ -326,39 +326,61 @@
         sets,
         terms,
         [whole(t.shape) for t in terms],
-        jax.ShapeDtypeStruct(shape, jnp.bfloat16),
+        jax.ShapeDtypeStruct(shape, dtype),
         whole(shape),
         [pltpu.VMEM(shape, jnp.float32)],
         cost=(0, 2 * nb * sub * (cols + 5 * wide)),
     )
 
 
-def finish_kernel(peers, *refs):
-    sets, core = refs[:peers], refs[peers]
-    terms, fars = refs[peers + 1 : 2 * peers + 1], refs[2 * peers + 1 : -3]
-    keep, give, total = refs[-3:]
-    add_up(sets, terms, total)
-    half = keep.shape[2]
-    for out, side in ((keep, core[0]), (give, 1 - core[0])):
+def finish_kernel(core, near, *refs):
+    fars, (out, give, keep, sem) = refs[:-4], refs[-4:]
+    half = give.shape[2]
+    for part, side in ((keep, core[0]), (give, 1 - core[0])):
         cols = pl.ds(pl.multiple_of(side * half, FB), half)
         for b, far in enumerate(fars):
-            out[b] = (total[b, :, cols] + far[0, :, cols].astype(jnp.float32)).astype(out.dtype)
-
-
-def finish(sets, core, terms, fars):
-    nb, sub, wide = terms[0].shape
-    cols = fars[0].shape[2]
+            part[b] = (near[b, :, cols] + far[0, :, cols].astype(jnp.float32)).astype(part.dtype)
+        if part is keep:
+            copy = pltpu.make_async_copy(keep, out.at[:, side], sem)
+            copy.start()
+    copy.wait()
+
+
+def finish(core, near, fars):
+    nb, sub, cols = near.shape
     shape = (nb, sub, cols // 2)
     return call(
-        functools.partial(finish_kernel, len(terms)),
-        [*sets, core],
-        [*terms, *fars],
-        [whole(t.shape) for t in (*terms, *fars)],
-        [jax.ShapeDtypeStruct(shape, jnp.bfloat16)] * 2,
-        [whole(shape)] * 2,
-        [pltpu.VMEM((nb, sub, cols), jnp.float32)],
-        cost=(0, 2 * nb * sub * (2 * cols + 5 * wide)),
-    )
+        finish_kernel,
+        [core],
+        [near, *fars],
+        [whole(t.shape) for t in (near, *fars)],
+        [jax.ShapeDtypeStruct((nb, 2, *shape[1:]), jnp.bfloat16), jax.ShapeDtypeStruct(shape, jnp.bfloat16)],
+        [pl.BlockSpec(memory_space=pl.ANY), whole(shape)],
+        [pltpu.VMEM(shape, jnp.bfloat16), pltpu.SemaphoreType.DMA],
+        cost=(0, 2 * nb * sub * 4 * cols),
+    )
+
+
+def place_kernel(core, got, _, out, sem):
+    copy = pltpu.make_async_copy(got, out.at[:, 1 - core[0]], sem)
+    copy.start()
+    copy.wait()
+
+
+def place(core, got, out):
+    return pl.pallas_call(
+        place_kernel,
+        grid_spec=pltpu.PrefetchScalarGridSpec(
+            num_scalar_prefetch=1,
+            grid=(1,),
+            in_specs=[pl.BlockSpec(memory_space=pl.ANY)] * 2,
+            out_specs=pl.BlockSpec(memory_space=pl.ANY),
+            scratch_shapes=[pltpu.SemaphoreType.DMA],
+        ),
+        out_shape=jax.ShapeDtypeStruct(out.shape, out.dtype),
+        input_output_aliases={2: 0},
+        compiler_params=pltpu.CompilerParams(vmem_limit_bytes=36 * MIB),
+    )(core, got, out)
 
 
 def batch_kernel(group, pieces, split, table, *refs):
@@ -508,7 +530,7 @@
     sets = [touched] + [swap(touched, k) for k in range(1, near)]
     packed = pack(stay(points.transpose(1, 0, 2)), stay(weights), stay(blocks.T), stay(counts))
     packed_b = across(packed)
-    own, sets, basis, packed_b = lax.optimization_barrier((own, sets, basis, packed_b))
+    own, sets, basis = lax.optimization_barrier((own, sets, basis))
     far = swap(own, near)
     sets[0] = stay(touched)
     picked = pick(sets, own)
@@ -529,17 +551,18 @@
     far_sums = batch_sums(table, *common, far_parts, True)
     terms = [sums[0], sums[1]] + [swap(sums[k], k) for k in range(2, near)]
     far_sums, terms = lax.optimization_barrier((far_sums, terms))
+    terms[1] = swap(terms[1], 1)
+    near_sum = merge(sets, terms, cols, jnp.float32)
     far_terms = []
     for b in range(nb):
         chunk = [far_sums[b]] + [swap(far_sums[nb * k + b], k) for k in range(1, near)]
+        if b == nb - 1:
+            chunk, near_sum = lax.optimization_barrier((chunk, near_sum))
         merged = merge(sets, chunk, cols)
-        far_sums, merged, terms[1] = lax.optimization_barrier((far_sums, merged, terms[1]))
+        far_sums, merged = lax.optimization_barrier((far_sums, merged))
         far_terms.append(swap(merged, near))
-    terms[1] = swap(terms[1], 1)
-    keep, give = finish(sets, core, terms, far_terms)
-    got = across(give)
-    pair = jnp.where(r == 0, jnp.stack([keep, got], axis=1), jnp.stack([got, keep], axis=1))
-    return pair.reshape(nb * FB, cols // cores)
+    out, give = finish(core, near_sum, far_terms)
+    return place(core, across(give), out).reshape(nb * FB, cols // cores)
 
 
 def solution(mesh):

time: 108 us -> 108 us (level)
  Pallas kernels: 39.5 us -> 42.3 us
  waiting for transfers between devices: 37.9 us -> 35.2 us
    ppermute x21, waiting for transfers between devices: 36.4 us -> 31.3 us  [swap(): return lax.ppermute(x, 'dom', [(a, a ^ k) for a in range(n)])]
    ppermute x3, waiting for transfers between devices: 1.52 us -> 3.95 us  [across(): return lax.ppermute(x, 'rows', [(a, cores - 1 - a) for a in range(cores)])]
    pallas_call x10 -> x11, Pallas kernels: 39.5 us -> 41.6 us  [call(): pl.pallas_call(kernel, grid_spec=pltpu.PrefetchScalarGridSpec(num_scalar_...]
  transfers between devices with their start and end apart: 24 -> 24, of which waited for: 12 -> 13; matrix products, arithmetic and copies ran while one was open for 0% -> 0% of each run, Pallas kernels for 35% -> 38%
where the time goes in v12:
time: 108 us
  Pallas kernels  42.3 us (39%)
  waiting for transfers between devices  35.2 us (33%)
  starting transfers between devices  29.9 us (28%)
    pallas_call x11, Pallas kernels, call(): pl.pallas_call(kernel, grid_spec=pltpu.PrefetchScalarGridSpec(num_scalar_...  41.6 us
    ppermute x21, waiting for transfers between devices, swap(): return lax.ppermute(x, 'dom', [(a, a ^ k) for a in range(n)])  31.3 us
    ppermute x21, starting transfers between devices, swap(): return lax.ppermute(x, 'dom', [(a, a ^ k) for a in range(n)])  29.5 us
    ppermute x3, waiting for transfers between devices, across(): return lax.ppermute(x, 'rows', [(a, cores - 1 - a) for a in range(cores)])  3.95 us
  transfers between devices with their start and end apart: 24, of which 13 were waited for; matrix products, arithmetic and copies ran while one was open for 0% of the time, Pallas kernels for 38%

profile of v12, /device:TPU:0, one launch (start us, length us, event | category | flops | bytes accessed | tf_op | source)
XLA Modules:
  0.0 107.6 jit_solution(17017817144090553550)
XLA Ops:
  0.0 4.0 %collective-permute-start.2 = (s32[1,8]{1,0:T(1,128)}, s32[1,8]{1,0:T(1,128)S(1)}, u32[]{:S(2)}, u32[]{:S(2)}) collective-permute-start(s32[1,8]{1,0:T(1,128)} %refs_0_.11), channel_id=1, source_target_pairs={{0,6},{2,4},{4,2},{6,0},{8,14},{10,12},{12,10},{14,8},{1,7},{3,5},... | collective-permute-start | bytes 104 | tf_op jit(solution)/shard_map/ppermute | solution.py:521
  5.6 2.0 %collective-permute-done.1.refs_2_ = s32[1,8]{1,0:T(1,128)S(1)} collective-permute-done((s32[1,8]{1,0:T(1,128)}, s32[1,8]{1,0:T(1,128)S(1)}, u32[]{:S(2)}, u32[]{:S(2)}) %collective-permute-start.1) | collective-permute-done | bytes 64 | tf_op jit(solution)/shard_map/ppermute | solution.py:521
  8.1 2.6 %collective-permute-start.3 = (bf16[2,64,2048]{2,1,0:T(8,128)(2,1)S(1)}, bf16[2,64,2048]{2,1,0:T(8,128)(2,1)S(1)}, u32[]{:S(2)}, u32[]{:S(2)}) collective-permute-start(bf16[2,64,2048]{2,1,0:T(8,128)(2,1)S(1)} %dynamic-slice_bitcast_fusion.refs_4_), channel_id=1, source_target_pairs={{0,8},{2,10},{4,12},{6,14},{8,0},{10,2},{12,4},{14,6},{1,9},{3,11}... | collective-permute-start | bytes 1572872 | tf_op jit(solution)/shard_map/ppermute | solution.py:521
  12.2 1.7 %shard_map.104 = (bf16[2,64,1024]{2,1,0:T(8,128)(2,1)S(1)}, bf16[2,64,1024]{2,1,0:T(8,128)(2,1)}, bf16[2,64,1024]{2,1,0:T(8,128)(2,1)}, bf16[2,64,1024]{2,1,0:T(8,128)(2,1)S(1)}) custom-call(s32[1,8]{1,0:T(1,128)} %refs_0_.11, s32[1,8]{1,0:T(1,128)S(1)} %collective-permute-done.refs_1_, s32[1,8]{1,0:T(1,128)S(1)} %collective-permute-done.1.refs_2_, ...), custom_call_target="tpu_custom_call" | custom-call | bytes 1572864 | tf_op jit(solution)/shard_map/pallas_call | solution.py:129
  14.4 1.6 %collective-permute-start.7 = (bf16[2,64,1024]{2,1,0:T(8,128)(2,1)}, bf16[2,64,1024]{2,1,0:T(8,128)(2,1)S(1)}, u32[]{:S(2)}, u32[]{:S(2)}) collective-permute-start(bf16[2,64,1024]{2,1,0:T(8,128)(2,1)} %get-tuple-element.72), channel_id=1, source_target_pairs={{0,4},{2,6},{4,0},{6,2},{8,12},{10,14},{12,8},{14,10},{1,5},{3,7},... | collective-permute-start | bytes 786440 | tf_op jit(solution)/shard_map/ppermute | solution.py:521
  16.0 2.4 %collective-permute-done.4.packed.refs_3_ = f32[5,24,256]{2,1,0:T(8,128)S(1)} collective-permute-done((f32[5,24,256]{2,1,0:T(8,128)S(1)}, f32[5,24,256]{2,1,0:T(8,128)S(1)}, u32[]{:S(2)}, u32[]{:S(2)}) %collective-permute-start.4) | collective-permute-done | bytes 122912 | tf_op jit(solution)/shard_map/ppermute | solution.py:524
  20.0 2.1 %shard_map.102.refs_4_ = f32[4,8,64,128]{3,2,1,0:T(8,128)S(1)} custom-call(s32[1,8]{1,0:T(1,128)} %refs_0_.11, s32[1]{0:T(128)} %bitcast.core, f32[3,2048]{1,0:T(4,128)} %centers.1, f32[1,2048]{1,0:T(1,128)} %bitcast.13), custom_call_target="tpu_custom_call" | custom-call | bytes 2097152 | tf_op jit(solution)/shard_map/pallas_call | solution.py:129
  22.1 5.4 %shard_map.101.table = s32[824]{0:T(1024)S(1)} custom-call(s32[1]{0:T(128)} %bitcast.3.me, s32[16]{0:T(128)} %owner.1, s32[1,8]{1,0:T(1,128)} %refs_0_.11, s32[4,24]{1,0:T(4,128)} %bitcast.15, f32[5,24,256]{2,1,0:T(8,128)S(1)} %collective-permute-done.4.packed.refs_3_, s32[24]{0:T(128)} %counts.3), custom_call_target="tpu_custom_call" | custom-call | bytes 1536 | tf_op jit(solution)/shard_map/pallas_call | solution.py:129
  27.5 7.2 %collective-permute-done.3.refs_4_ = bf16[2,64,2048]{2,1,0:T(8,128)(2,1)S(1)} collective-permute-done((bf16[2,64,2048]{2,1,0:T(8,128)(2,1)S(1)}, bf16[2,64,2048]{2,1,0:T(8,128)(2,1)S(1)}, u32[]{:S(2)}, u32[]{:S(2)}) %collective-permute-start.3) | collective-permute-done | bytes 524320 | tf_op jit(solution)/shard_map/ppermute | solution.py:521
  36.9 2.3 %collective-permute-start.11 = (bf16[2,64,1024]{2,1,0:T(8,128)(2,1)S(1)}, bf16[2,64,1024]{2,1,0:T(8,128)(2,1)S(1)}, u32[]{:S(2)}, u32[]{:S(2)}) collective-permute-start(bf16[2,64,1024]{2,1,0:T(8,128)(2,1)S(1)} %get-tuple-element.78), channel_id=1, source_target_pairs={{0,6},{2,4},{4,2},{6,0},{8,14},{10,12},{12,10},{14,8},{1,7},{3,5},... | collective-permute-start | bytes 786440 | tf_op jit(solution)/shard_map/ppermute | solution.py:521
  39.9 13.1 %shard_map.105 = (f32[2,64,1024]{2,1,0:T(8,128)S(1)}, bf16[2,64,1024]{2,1,0:T(8,128)(2,1)S(1)}, bf16[2,64,1024]{2,1,0:T(8,128)(2,1)S(1)}, bf16[2,64,1024]{2,1,0:T(8,128)(2,1)S(1)}) custom-call(s32[824]{0:T(1024)S(1)} %shard_map.101.table, bf16[24,512,256]{2,1,0:T(8,128)(2,1)} %refs_0_.8, bf16[24,512,256]{2,1,0:T(8,128)(2,1)} %collective-permute-done.5.refs_1_, ...), custom_call_target="tpu_custom_call" | custom-call | flops 6442450944 | bytes 12582912 | tf_op jit(solution)/shard_map/pallas_call | solution.py:129
  53.1 1.9 %collective-permute-start.13 = (bf16[2,64,1024]{2,1,0:T(8,128)(2,1)S(1)}, bf16[2,64,1024]{2,1,0:T(8,128)(2,1)S(1)}, u32[]{:S(2)}, u32[]{:S(2)}) collective-permute-start(bf16[2,64,1024]{2,1,0:T(8,128)(2,1)S(1)} %get-tuple-element.89), channel_id=1, source_target_pairs={{0,6},{2,4},{4,2},{6,0},{8,14},{10,12},{12,10},{14,8},{1,7},{3,5},... | collective-permute-start | bytes 786440 | tf_op jit(solution)/shard_map/ppermute | solution.py:521
  55.1 13.2 %shard_map.106 = (f32[1,64,1024]{2,1,0:T(8,128)S(1)}, f32[1,64,1024]{2,1,0:T(8,128)S(1)}, bf16[1,64,1024]{2,1,0:T(8,128)(2,1)S(1)}, bf16[1,64,1024]{2,1,0:T(8,12...) custom-call(s32[824]{0:T(1024)S(1)} %shard_map.101.table, ...), custom_call_target="tpu_custom_call" | custom-call | flops 6442450944 | bytes 12582912 | tf_op jit(solution)/shard_map/pallas_call | solution.py:129
  68.3 1.7 %collective-permute-start.14 = (bf16[1,64,1024]{2,1,0:T(8,128)(2,1)S(1)}, bf16[1,64,1024]{2,1,0:T(8,128)(2,1)S(1)}, u32[]{:S(2)}, u32[]{:S(2)}) collective-permute-start(bf16[1,64,1024]{2,1,0:T(8,128)(2,1)S(1)} %get-tuple-element.92), channel_id=1, source_target_pairs={{0,2},{2,0},{4,6},{6,4},{8,10},{10,8},{12,14},{14,12},{1,3},{3,1},... | collective-permute-start | bytes 393224 | tf_op jit(solution)/shard_map/ppermute | solution.py:521
  70.0 1.8 %collective-permute-start.16 = (bf16[1,64,1024]{2,1,0:T(8,128)(2,1)S(1)}, bf16[1,64,1024]{2,1,0:T(8,128)(2,1)S(1)}, u32[]{:S(2)}, u32[]{:S(2)}) collective-permute-start(bf16[1,64,1024]{2,1,0:T(8,128)(2,1)S(1)} %get-tuple-element.96), channel_id=1, source_target_pairs={{0,6},{2,4},{4,2},{6,0},{8,14},{10,12},{12,10},{14,8},{1,7},{3,5},... | collective-permute-start | bytes 393224 | tf_op jit(solution)/shard_map/ppermute | solution.py:521
  71.8 1.6 %collective-permute-start.20 = (bf16[2,64,1024]{2,1,0:T(8,128)(2,1)S(1)}, bf16[2,64,1024]{2,1,0:T(8,128)(2,1)S(1)}, u32[]{:S(2)}, u32[]{:S(2)}) collective-permute-start(bf16[2,64,1024]{2,1,0:T(8,128)(2,1)S(1)} %get-tuple-element.103), channel_id=1, source_target_pairs={{0,2},{2,0},{4,6},{6,4},{8,10},{10,8},{12,14},{14,12},{1,3},{3,1},... | collective-permute-start | bytes 786440 | tf_op jit(solution)/shard_map/ppermute | solution.py:521
  73.5 3.8 %collective-permute-done.14.refs_5_ = bf16[1,64,1024]{2,1,0:T(8,128)(2,1)S(1)} collective-permute-done((bf16[1,64,1024]{2,1,0:T(8,128)(2,1)S(1)}, bf16[1,64,1024]{2,1,0:T(8,128)(2,1)S(1)}, u32[]{:S(2)}, u32[]{:S(2)}) %collective-permute-start.14) | collective-permute-done | bytes 131104 | tf_op jit(solution)/shard_map/ppermute | solution.py:521
  78.3 1.9 %collective-permute-start.17 = (bf16[1,64,1024]{2,1,0:T(8,128)(2,1)S(1)}, bf16[1,64,1024]{2,1,0:T(8,128)(2,1)S(1)}, u32[]{:S(2)}, u32[]{:S(2)}) collective-permute-start(bf16[1,64,1024]{2,1,0:T(8,128)(2,1)S(1)} %get-tuple-element.99), channel_id=1, source_target_pairs={{0,2},{2,0},{4,6},{6,4},{8,10},{10,8},{12,14},{14,12},{1,3},{3,1},... | collective-permute-start | bytes 393224 | tf_op jit(solution)/shard_map/ppermute | solution.py:521
  80.2 1.7 %collective-permute-start.19 = (bf16[1,64,1024]{2,1,0:T(8,128)(2,1)S(1)}, bf16[1,64,1024]{2,1,0:T(8,128)(2,1)S(1)}, u32[]{:S(2)}, u32[]{:S(2)}) collective-permute-start(bf16[1,64,1024]{2,1,0:T(8,128)(2,1)S(1)} %get-tuple-element.101), channel_id=1, source_target_pairs={{0,6},{2,4},{4,2},{6,0},{8,14},{10,12},{12,10},{14,8},{1,7},{3,5},... | collective-permute-start | bytes 393224 | tf_op jit(solution)/shard_map/ppermute | solution.py:521
  81.9 1.7 %collective-permute-start.21 = (bf16[1,64,2048]{2,1,0:T(8,128)(2,1)S(1)}, bf16[1,64,2048]{2,1,0:T(8,128)(2,1)S(1)}, u32[]{:S(2)}, u32[]{:S(2)}) collective-permute-start(bf16[1,64,2048]{2,1,0:T(8,128)(2,1)S(1)} %shard_map.107), channel_id=1, source_target_pairs={{0,8},{2,10},{4,12},{6,14},{8,0},{10,2},{12,4},{14,6},{1,9},{3,11}... | collective-permute-start | bytes 786440 | tf_op jit(solution)/shard_map/ppermute | solution.py:521
  86.0 1.6 %collective-permute-done.19.refs_7_ = bf16[1,64,1024]{2,1,0:T(8,128)(2,1)S(1)} collective-permute-done((bf16[1,64,1024]{2,1,0:T(8,128)(2,1)S(1)}, bf16[1,64,1024]{2,1,0:T(8,128)(2,1)S(1)}, u32[]{:S(2)}, u32[]{:S(2)}) %collective-permute-start.19) | collective-permute-done | bytes 131104 | tf_op jit(solution)/shard_map/ppermute | solution.py:521
  88.6 2.7 %collective-permute-start.22 = (bf16[1,64,2048]{2,1,0:T(8,128)(2,1)S(1)}, bf16[1,64,2048]{2,1,0:T(8,128)(2,1)S(1)}, u32[]{:S(2)}, u32[]{:S(2)}) collective-permute-start(bf16[1,64,2048]{2,1,0:T(8,128)(2,1)S(1)} %shard_map.109), channel_id=1, source_target_pairs={{0,8},{2,10},{4,12},{6,14},{8,0},{10,2},{12,4},{14,6},{1,9},{3,11}... | collective-permute-start | bytes 786440 | tf_op jit(solution)/shard_map/ppermute | solution.py:521
  91.3 8.7 %collective-permute-done.21.refs_0_ = bf16[1,64,2048]{2,1,0:T(8,128)(2,1)S(1)} collective-permute-done((bf16[1,64,2048]{2,1,0:T(8,128)(2,1)S(1)}, bf16[1,64,2048]{2,1,0:T(8,128)(2,1)S(1)}, u32[]{:S(2)}, u32[]{:S(2)}) %collective-permute-start.21) | collective-permute-done | bytes 262176 | tf_op jit(solution)/shard_map/ppermute | solution.py:521
  100.0 4.5 %collective-permute-done.22.refs_1_ = bf16[1,64,2048]{2,1,0:T(8,128)(2,1)S(1)} collective-permute-done((bf16[1,64,2048]{2,1,0:T(8,128)(2,1)S(1)}, bf16[1,64,2048]{2,1,0:T(8,128)(2,1)S(1)}, u32[]{:S(2)}, u32[]{:S(2)}) %collective-permute-start.22) | collective-permute-done | bytes 262176 | tf_op jit(solution)/shard_map/ppermute | solution.py:521
  (39 shorter events, 16.0 us)
Async XLA Ops:
  0.0 5.6 %collective-permute-start.2 = (s32[1,8]{1,0:T(1,128)}, s32[1,8]{1,0:T(1,128)S(1)}, u32[]{:S(2)}, u32[]{:S(2)}) collective-permute-start(s32[1,8]{1,0:T(1,128)} %refs_0_.11), channel_id=1, source_target_pairs={{0,6},{2,4},{4,2},{6,0},{8,14},{10,12},{12,10},{14,8},{1,7},{3,5},... | collective-permute-start | bytes 104 | tf_op jit(solution)/shard_map/ppermute | solution.py:521
  4.0 3.7 %collective-permute-start.1 = (s32[1,8]{1,0:T(1,128)}, s32[1,8]{1,0:T(1,128)S(1)}, u32[]{:S(2)}, u32[]{:S(2)}) collective-permute-start(s32[1,8]{1,0:T(1,128)} %refs_0_.11), channel_id=1, source_target_pairs={{0,4},{2,6},{4,0},{6,2},{8,12},{10,14},{12,8},{14,10},{1,5},{3,7},... | collective-permute-start | bytes 104 | tf_op jit(solution)/shard_map/ppermute | solution.py:521
  4.4 3.7 %collective-permute-start = (s32[1,8]{1,0:T(1,128)}, s32[1,8]{1,0:T(1,128)S(1)}, u32[]{:S(2)}, u32[]{:S(2)}) collective-permute-start(s32[1,8]{1,0:T(1,128)} %refs_0_.11), channel_id=1, source_target_pairs={{0,2},{2,0},{4,6},{6,4},{8,10},{10,8},{12,14},{14,12},{1,3},{3,1},... | collective-permute-start | bytes 104 | tf_op jit(solution)/shard_map/ppermute | solution.py:521
  8.1 31.8 %collective-permute-start.5 = (bf16[24,512,256]{2,1,0:T(8,128)(2,1)}, bf16[24,512,256]{2,1,0:T(8,128)(2,1)}, u32[]{:S(2)}, u32[]{:S(2)}) collective-permute-start(bf16[24,512,256]{2,1,0:T(8,128)(2,1)} %refs_0_.8), channel_id=1, source_target_pairs={{0,1},{1,0},{2,3},{3,2},{4,5},{5,4},{6,7},{7,6},{8,9},{9,8},{10,11... | collective-permute-start | bytes 18874376 | tf_op jit(solution)/shard_map/ppermute | solution.py:524
  8.1 26.6 %collective-permute-start.3 = (bf16[2,64,2048]{2,1,0:T(8,128)(2,1)S(1)}, bf16[2,64,2048]{2,1,0:T(8,128)(2,1)S(1)}, u32[]{:S(2)}, u32[]{:S(2)}) collective-permute-start(bf16[2,64,2048]{2,1,0:T(8,128)(2,1)S(1)} %dynamic-slice_bitcast_fusion.refs_4_), channel_id=1, source_target_pairs={{0,8},{2,10},{4,12},{6,14},{8,0},{10,2},{12,4},{14,6},{1,9},{3,11}... | collective-permute-start | bytes 1572872 | tf_op jit(solution)/shard_map/ppermute | solution.py:521
  11.9 6.5 %collective-permute-start.4 = (f32[5,24,256]{2,1,0:T(8,128)S(1)}, f32[5,24,256]{2,1,0:T(8,128)S(1)}, u32[]{:S(2)}, u32[]{:S(2)}) collective-permute-start(f32[5,24,256]{2,1,0:T(8,128)S(1)} %shard_map.100.refs_2_), channel_id=1, source_target_pairs={{0,1},{1,0},{2,3},{3,2},{4,5},{5,4},{6,7},{7,6},{8,9},{9,8},{10,11... | collective-permute-start | bytes 368648 | tf_op jit(solution)/shard_map/ppermute | solution.py:524
  13.9 22.2 %collective-permute-start.6 = (bf16[2,64,1024]{2,1,0:T(8,128)(2,1)}, bf16[2,64,1024]{2,1,0:T(8,128)(2,1)S(1)}, u32[]{:S(2)}, u32[]{:S(2)}) collective-permute-start(bf16[2,64,1024]{2,1,0:T(8,128)(2,1)} %get-tuple-element.71), channel_id=1, source_target_pairs={{0,2},{2,0},{4,6},{6,4},{8,10},{10,8},{12,14},{14,12},{1,3},{3,1},... | collective-permute-start | bytes 786440 | tf_op jit(solution)/shard_map/ppermute | solution.py:521
  14.4 22.4 %collective-permute-start.7 = (bf16[2,64,1024]{2,1,0:T(8,128)(2,1)}, bf16[2,64,1024]{2,1,0:T(8,128)(2,1)S(1)}, u32[]{:S(2)}, u32[]{:S(2)}) collective-permute-start(bf16[2,64,1024]{2,1,0:T(8,128)(2,1)} %get-tuple-element.72), channel_id=1, source_target_pairs={{0,4},{2,6},{4,0},{6,2},{8,12},{10,14},{12,8},{14,10},{1,5},{3,7},... | collective-permute-start | bytes 786440 | tf_op jit(solution)/shard_map/ppermute | solution.py:521
  18.4 21.5 %collective-permute-start.8 = (bf16[2,64,1024]{2,1,0:T(8,128)(2,1)S(1)}, bf16[2,64,1024]{2,1,0:T(8,128)(2,1)}, u32[]{:S(2)}, u32[]{:S(2)}) collective-permute-start(bf16[2,64,1024]{2,1,0:T(8,128)(2,1)S(1)} %get-tuple-element.73), channel_id=1, source_target_pairs={{0,6},{2,4},{4,2},{6,0},{8,14},{10,12},{12,10},{14,8},{1,7},{3,5},... | collective-permute-start | bytes 786440 | tf_op jit(solution)/shard_map/ppermute | solution.py:521
  35.6 19.5 %collective-permute-start.9 = (bf16[2,64,1024]{2,1,0:T(8,128)(2,1)S(1)}, bf16[2,64,1024]{2,1,0:T(8,128)(2,1)S(1)}, u32[]{:S(2)}, u32[]{:S(2)}) collective-permute-start(bf16[2,64,1024]{2,1,0:T(8,128)(2,1)S(1)} %get-tuple-element.76), channel_id=1, source_target_pairs={{0,2},{2,0},{4,6},{6,4},{8,10},{10,8},{12,14},{14,12},{1,3},{3,1},... | collective-permute-start | bytes 786440 | tf_op jit(solution)/shard_map/ppermute | solution.py:521
  36.2 18.9 %collective-permute-start.10 = (bf16[2,64,1024]{2,1,0:T(8,128)(2,1)S(1)}, bf16[2,64,1024]{2,1,0:T(8,128)(2,1)S(1)}, u32[]{:S(2)}, u32[]{:S(2)}) collective-permute-start(bf16[2,64,1024]{2,1,0:T(8,128)(2,1)S(1)} %get-tuple-element.77), channel_id=1, source_target_pairs={{0,4},{2,6},{4,0},{6,2},{8,12},{10,14},{12,8},{14,10},{1,5},{3,7},... | collective-permute-start | bytes 786440 | tf_op jit(solution)/shard_map/ppermute | solution.py:521
  36.9 18.2 %collective-permute-start.11 = (bf16[2,64,1024]{2,1,0:T(8,128)(2,1)S(1)}, bf16[2,64,1024]{2,1,0:T(8,128)(2,1)S(1)}, u32[]{:S(2)}, u32[]{:S(2)}) collective-permute-start(bf16[2,64,1024]{2,1,0:T(8,128)(2,1)S(1)} %get-tuple-element.78), channel_id=1, source_target_pairs={{0,6},{2,4},{4,2},{6,0},{8,14},{10,12},{12,10},{14,8},{1,7},{3,5},... | collective-permute-start | bytes 786440 | tf_op jit(solution)/shard_map/ppermute | solution.py:521
  53.1 15.2 %collective-permute-start.12 = (bf16[2,64,1024]{2,1,0:T(8,128)(2,1)S(1)}, bf16[2,64,1024]{2,1,0:T(8,128)(2,1)S(1)}, u32[]{:S(2)}, u32[]{:S(2)}) collective-permute-start(bf16[2,64,1024]{2,1,0:T(8,128)(2,1)S(1)} %get-tuple-element.88), channel_id=1, source_target_pairs={{0,4},{2,6},{4,0},{6,2},{8,12},{10,14},{12,8},{14,10},{1,5},{3,7},... | collective-permute-start | bytes 786440 | tf_op jit(solution)/shard_map/ppermute | solution.py:521
  53.1 15.1 %collective-permute-start.13 = (bf16[2,64,1024]{2,1,0:T(8,128)(2,1)S(1)}, bf16[2,64,1024]{2,1,0:T(8,128)(2,1)S(1)}, u32[]{:S(2)}, u32[]{:S(2)}) collective-permute-start(bf16[2,64,1024]{2,1,0:T(8,128)(2,1)S(1)} %get-tuple-element.89), channel_id=1, source_target_pairs={{0,6},{2,4},{4,2},{6,0},{8,14},{10,12},{12,10},{14,8},{1,7},{3,5},... | collective-permute-start | bytes 786440 | tf_op jit(solution)/shard_map/ppermute | solution.py:521
  68.3 9.0 %collective-permute-start.14 = (bf16[1,64,1024]{2,1,0:T(8,128)(2,1)S(1)}, bf16[1,64,1024]{2,1,0:T(8,128)(2,1)S(1)}, u32[]{:S(2)}, u32[]{:S(2)}) collective-permute-start(bf16[1,64,1024]{2,1,0:T(8,128)(2,1)S(1)} %get-tuple-element.92), channel_id=1, source_target_pairs={{0,2},{2,0},{4,6},{6,4},{8,10},{10,8},{12,14},{14,12},{1,3},{3,1},... | collective-permute-start | bytes 393224 | tf_op jit(solution)/shard_map/ppermute | solution.py:521
  70.0 7.3 %collective-permute-start.15 = (bf16[1,64,1024]{2,1,0:T(8,128)(2,1)S(1)}, bf16[1,64,1024]{2,1,0:T(8,128)(2,1)S(1)}, u32[]{:S(2)}, u32[]{:S(2)}) collective-permute-start(bf16[1,64,1024]{2,1,0:T(8,128)(2,1)S(1)} %get-tuple-element.94), channel_id=1, source_target_pairs={{0,4},{2,6},{4,0},{6,2},{8,12},{10,14},{12,8},{14,10},{1,5},{3,7},... | collective-permute-start | bytes 393224 | tf_op jit(solution)/shard_map/ppermute | solution.py:521
  70.0 7.3 %collective-permute-start.16 = (bf16[1,64,1024]{2,1,0:T(8,128)(2,1)S(1)}, bf16[1,64,1024]{2,1,0:T(8,128)(2,1)S(1)}, u32[]{:S(2)}, u32[]{:S(2)}) collective-permute-start(bf16[1,64,1024]{2,1,0:T(8,128)(2,1)S(1)} %get-tuple-element.96), channel_id=1, source_target_pairs={{0,6},{2,4},{4,2},{6,0},{8,14},{10,12},{12,10},{14,8},{1,7},{3,5},... | collective-permute-start | bytes 393224 | tf_op jit(solution)/shard_map/ppermute | solution.py:521
  71.8 12.5 %collective-permute-start.20 = (bf16[2,64,1024]{2,1,0:T(8,128)(2,1)S(1)}, bf16[2,64,1024]{2,1,0:T(8,128)(2,1)S(1)}, u32[]{:S(2)}, u32[]{:S(2)}) collective-permute-start(bf16[2,64,1024]{2,1,0:T(8,128)(2,1)S(1)} %get-tuple-element.103), channel_id=1, source_target_pairs={{0,2},{2,0},{4,6},{6,4},{8,10},{10,8},{12,14},{14,12},{1,3},{3,1},... | collective-permute-start | bytes 786440 | tf_op jit(solution)/shard_map/ppermute | solution.py:521
  78.3 7.6 %collective-permute-start.17 = (bf16[1,64,1024]{2,1,0:T(8,128)(2,1)S(1)}, bf16[1,64,1024]{2,1,0:T(8,128)(2,1)S(1)}, u32[]{:S(2)}, u32[]{:S(2)}) collective-permute-start(bf16[1,64,1024]{2,1,0:T(8,128)(2,1)S(1)} %get-tuple-element.99), channel_id=1, source_target_pairs={{0,2},{2,0},{4,6},{6,4},{8,10},{10,8},{12,14},{14,12},{1,3},{3,1},... | collective-permute-start | bytes 393224 | tf_op jit(solution)/shard_map/ppermute | solution.py:521
  80.2 5.8 %collective-permute-start.18 = (bf16[1,64,1024]{2,1,0:T(8,128)(2,1)S(1)}, bf16[1,64,1024]{2,1,0:T(8,128)(2,1)S(1)}, u32[]{:S(2)}, u32[]{:S(2)}) collective-permute-start(bf16[1,64,1024]{2,1,0:T(8,128)(2,1)S(1)} %get-tuple-element.100), channel_id=1, source_target_pairs={{0,4},{2,6},{4,0},{6,2},{8,12},{10,14},{12,8},{14,10},{1,5},{3,7},... | collective-permute-start | bytes 393224 | tf_op jit(solution)/shard_map/ppermute | solution.py:521
  80.2 7.4 %collective-permute-start.19 = (bf16[1,64,1024]{2,1,0:T(8,128)(2,1)S(1)}, bf16[1,64,1024]{2,1,0:T(8,128)(2,1)S(1)}, u32[]{:S(2)}, u32[]{:S(2)}) collective-permute-start(bf16[1,64,1024]{2,1,0:T(8,128)(2,1)S(1)} %get-tuple-element.101), channel_id=1, source_target_pairs={{0,6},{2,4},{4,2},{6,0},{8,14},{10,12},{12,10},{14,8},{1,7},{3,5},... | collective-permute-start | bytes 393224 | tf_op jit(solution)/shard_map/ppermute | solution.py:521
  81.9 18.1 %collective-permute-start.21 = (bf16[1,64,2048]{2,1,0:T(8,128)(2,1)S(1)}, bf16[1,64,2048]{2,1,0:T(8,128)(2,1)S(1)}, u32[]{:S(2)}, u32[]{:S(2)}) collective-permute-start(bf16[1,64,2048]{2,1,0:T(8,128)(2,1)S(1)} %shard_map.107), channel_id=1, source_target_pairs={{0,8},{2,10},{4,12},{6,14},{8,0},{10,2},{12,4},{14,6},{1,9},{3,11}... | collective-permute-start | bytes 786440 | tf_op jit(solution)/shard_map/ppermute | solution.py:521
  88.6 15.9 %collective-permute-start.22 = (bf16[1,64,2048]{2,1,0:T(8,128)(2,1)S(1)}, bf16[1,64,2048]{2,1,0:T(8,128)(2,1)S(1)}, u32[]{:S(2)}, u32[]{:S(2)}) collective-permute-start(bf16[1,64,2048]{2,1,0:T(8,128)(2,1)S(1)} %shard_map.109), channel_id=1, source_target_pairs={{0,8},{2,10},{4,12},{6,14},{8,0},{10,2},{12,4},{14,6},{1,9},{3,11}... | collective-permute-start | bytes 786440 | tf_op jit(solution)/shard_map/ppermute | solution.py:521
  105.3 1.6 %collective-permute-start.23 = (bf16[2,64,1024]{2,1,0:T(8,128)(2,1)S(1)}, bf16[2,64,1024]{2,1,0:T(8,128)(2,1)S(1)}, u32[]{:S(2)}, u32[]{:S(2)}) collective-permute-start(bf16[2,64,1024]{2,1,0:T(8,128)(2,1)S(1)} %get-tuple-element.113), channel_id=1, source_target_pairs={{0,1},{1,0},{2,3},{3,2},{4,5},{5,4},{6,7},{7,6},{8,9},{9,8},{10,11... | collective-permute-start | bytes 786440 | tf_op jit(solution)/shard_map/ppermute | solution.py:524
  (1 other events, 4.6 us)
